TPU v7x, 32 devices: a whole 2x2x4 slice. The times are simulated.
32 devices in a mesh: grid: 4 (over y, x), band: 8 (over z, core).
Axes of the slice: x: 2, y: 2, z: 4, core: 2. Of those that a mesh axis runs over, the one named last changes fastest.
Arguments:
- psi: float32 [2, 8, 2048, 96], P(None, 'band', 'grid'), may hold values from -6 to 6
- col_map: int32 [2048], P('grid'), may hold values from 0 to 9215, as said below
- potential: float32 [96, 9216], P('grid'), may hold values from -3 to 3
- lower: float32 [1], replicated, may hold values from 0.2 to 0.6
- upper: float32 [1], replicated, may hold values from 2.6 to 3.2
Outputs:
- filtered: float32 [2, 8, 2048, 96], P(None, 'band', 'grid')
- gram: float32 [2, 8, 8], P(None, 'band', 'grid')
Inputs may be any that keep to these rules, and one draw needn't show every extreme that they name: `col_map`: the entries are distinct; every column with gx^2 + gy^2 <= 24^2 appears once, the remaining entries are other columns of the grid.
All inputs are finite; a program needn't handle non-finite values.
Results may differ from a plain program's by a relative error of at most 0.0003.
Values may be sent and summed in bfloat16 or wider, within the bound.
No kernel may reach another device: no remote copies, remote signals or barrier semaphores. Data moves between devices by JAX's collectives and lax.ppermute only.
A program may use at most 64 MiB of HBM per device.

v0:
```python
import math

import jax
import jax.numpy as jnp
from jax import lax
from jax.sharding import PartitionSpec as P


def folded(index, size):
    return jnp.where(index < size // 2, index, index - size)


def tables(size, sign):
    index = jnp.arange(size, dtype=jnp.int32)
    angle = (index[:, None] * index[None, :] % size).astype(jnp.float32) * (2.0 * math.pi / size)
    cosine = jnp.cos(angle)
    sine = jnp.sin(angle) * sign
    top = jnp.stack([cosine, sine], axis=1)
    bottom = jnp.stack([-sine, cosine], axis=1)
    return jnp.stack([top, bottom])


def transform(stacked, table, form):
    return jnp.einsum(form, stacked, table, precision=lax.Precision.HIGHEST)


def correlation(rows, cols):
    dims = (((1,), (1,)), ((), ()))
    real_part = lax.dot_general(
        rows[0], cols[0], dims, preferred_element_type=jnp.float32
    ) + lax.dot_general(rows[1], cols[1], dims, preferred_element_type=jnp.float32)
    imag_part = lax.dot_general(
        rows[0], cols[1], dims, preferred_element_type=jnp.float32
    ) - lax.dot_general(rows[1], cols[0], dims, preferred_element_type=jnp.float32)
    return jnp.stack([real_part, imag_part])


def body(psi, col_map, potential, lower, upper):
    bands_dev = psi.shape[1]
    cols_dev = psi.shape[2]
    size = psi.shape[3]
    radius = size // 4
    forward = tables(size, 1.0)
    backward = tables(size, -1.0)
    freq_x = folded(col_map // size, size)
    freq_y = folded(col_map % size, size)
    freq_z = folded(jnp.arange(size, dtype=jnp.int32), size)
    radius2 = (freq_x * freq_x + freq_y * freq_y)[:, None] + (freq_z * freq_z)[None, :]
    inside = (radius2 <= radius * radius).astype(jnp.float32)
    kinetic = 2.0 * radius2.astype(jnp.float32) / (radius * radius)
    full_map = lax.all_gather(col_map, "grid", axis=0, tiled=True)
    scaled = (potential / float(size**3)).reshape(potential.shape[0], size, size)

    def planes_work(block):
        count = block.shape[1]
        depth = block.shape[2]
        dense = (
            jnp.zeros((2, count, depth, size * size), jnp.float32)
            .at[:, :, :, full_map]
            .set(block)
            .reshape(2, count, depth, size, size)
        )
        dense = transform(dense, forward, "pbzxy,pxqu->qbzuy")
        dense = transform(dense, forward, "pbzxy,pyqv->qbzxv")
        dense = dense * scaled[None, None]
        dense = transform(dense, backward, "pbzxy,pxqu->qbzuy")
        dense = transform(dense, backward, "pbzxy,pyqv->qbzxv")
        picked = dense.reshape(2, count, depth, size * size)[:, :, :, full_map]
        return lax.all_to_all(picked, "grid", split_axis=3, concat_axis=2, tiled=True)

    def apply_h(coeff):
        stacked = transform(coeff, forward, "pbck,pkqz->qbzc")
        back = planes_work(lax.all_to_all(stacked, "grid", split_axis=2, concat_axis=3, tiled=True))
        back = transform(back, backward, "pbzc,pzqk->qbck")
        return jnp.stack(
            [kinetic * coeff[0] + inside * back[0], kinetic * coeff[1] + inside * back[1]]
        )

    center = (upper[0] + lower[0]) / 2.0
    half = (upper[0] - lower[0]) / 2.0
    start = inside * psi
    first = (apply_h(start) - center * start) / half
    filtered = 2.0 * (apply_h(first) - center * first) / half - start
    rounded = filtered.astype(jnp.bfloat16).reshape(2, bands_dev, cols_dev * size)
    partial_sum = correlation(rounded, lax.all_gather(rounded, "band", axis=1, tiled=True))
    gram = lax.psum_scatter(partial_sum, "grid", scatter_dimension=2, tiled=True) / (
        4.0 * radius**3
    )
    return (filtered, gram)


def solution(mesh):
    return jax.shard_map(
        body,
        mesh=mesh,
        in_specs=(P(None, "band", "grid", None), P("grid"), P("grid", None), P(), P()),
        out_specs=(P(None, "band", "grid", None), P(None, "band", "grid")),
        check_vma=False,
    )
```

profile of v0, /device:TPU:0, one launch (start us, length us, event | category | flops | bytes accessed | tf_op | source)
XLA Modules:
  0.0 627.1 jit_solution(12987956038167116893)
XLA Ops:
  7.8 0.7 fusion.91
  8.6 0.6 copy-done.28
  9.2 1.1 bitcast_multiply_fusion.2
  10.4 0.8 fusion.79
  11.1 0.6 copy-done.6
  11.8 0.5 convolution_bitcast_fusion.3
  12.4 1.1 copy.89
  13.4 5.2 all-to-all-start
  18.7 0.5 mul.270
  19.1 0.4 copy.93
  19.5 8.8 %all-gather = s32[4,1,512]{2,1,0:T(1,128)S(1)} all-gather(s32[1,1,512]{2,1,0:T(1,128)S(1)} %bitcast.278), channel_id=1, replica_groups=mesh['grid'=4,'band'=8] {'grid'}, dimensions={0}, use_global_device_ids=true | all-gather | bytes 10240 | tf_op jit(solution)/shard_map/all_gather | solution.py:51
  28.4 0.7 copy-done.26
  29.1 2.5 copy.90
  31.6 3.9 broadcast.367.clone
  35.6 187.2 %scatter_fusion = f32[2,24,9216]{1,0,2:T(2,128)} fusion(f32[2,24,9216]{1,0,2:T(2,128)} %broadcast.367.clone, s32[2048]{0:T(1024)S(1)} %get-tuple-element.25, f32[2048,2,24]{2,1,0:T(2,128)S(1)} %bitcast.269), kind=kCustom, calls=%fused_computation.2 | custom fusion | bytes 1187840 | tf_op jit(solution)/shard_map/scatter | solution.py:60
  222.8 9.1 %copy.91 = f32[2,24,96,96]{3,2,0,1:T(8,128)S(1)} copy(f32[2,24,96,96]{1,0,3,2:T(2,128)} %bitcast.263) | data formatting | bytes 3538944 | tf_op jit(solution)/shard_map/reshape.4
  231.9 3.2 fusion.22
  235.1 2.8 fusion.1
  238.0 2.7 fusion.27
  240.7 2.8 fusion.30
  243.5 8.2 %copy.147 = f32[2,1,24,96,96]{2,0,4,3,1:T(2,128)} copy(f32[2,1,24,96,96]{3,4,2,0,1:T(8,128)S(1)} %fusion.30) | data formatting | bytes 3538944 | tf_op jit(solution)/shard_map/reshape | solution.py:68
  251.7 18.1 %gather_fusion = f32[2048,2,24]{2,1,0:T(2,128)} fusion(f32[2,24,9216]{1,0,2:T(2,128)} %bitcast.264, s32[2048]{0:T(1024)S(1)} %get-tuple-element.24), kind=kCustom, calls=%fused_computation | custom fusion | bytes 794624 | tf_op jit(solution)/shard_map/gather | solution.py:68
  269.8 1.8 bitcast_bitcast_fusion.1
  271.7 4.5 reshape.488
  276.2 3.5 all-to-all-start.1
  281.0 4.5 all-to-all-done.1
  285.5 0.5 broadcast.398
  286.0 2.4 reduce
  288.4 4.4 reshape.489
  292.8 1.9 copy.148
  294.7 1.2 copy.102
  296.0 0.5 convolution_bitcast_fusion.2
  296.5 1.2 fusion.58
  297.9 0.5 convolution_bitcast_fusion.1
  298.9 9.9 %all_to_all.66 = f32[2,1,96,512]{3,0,1,2:T(2,128)} all-to-all(f32[2,1,96,512]{3,0,1,2:T(2,128)S(1)} %copy.103), channel_id=1, replica_groups=mesh['grid'=4,'band'=8] {'grid'}, dimensions={2} | all-to-all | bytes 786432 | tf_op jit(solution)/shard_map/all_to_all | solution.py:73
  308.8 2.5 copy.104
  311.4 3.9 broadcast.367
  315.3 187.2 %scatter_fusion.1 = f32[2,24,9216]{1,0,2:T(2,128)} fusion(f32[2,24,9216]{1,0,2:T(2,128)} %broadcast.367, s32[2048]{0:T(1024)S(1)} %get-tuple-element.25, f32[2048,2,24]{2,1,0:T(2,128)S(1)} %bitcast.268), kind=kCustom, calls=%fused_computation.3 | custom fusion | bytes 1187840 | tf_op jit(solution)/shard_map/scatter | solution.py:60
  502.5 9.1 %copy.105 = f32[2,24,96,96]{3,2,0,1:T(8,128)S(1)} copy(f32[2,24,96,96]{1,0,3,2:T(2,128)} %bitcast.262) | data formatting | bytes 3538944 | tf_op jit(solution)/shard_map/reshape.25
  511.6 3.2 fusion.33
  514.8 2.8 fusion
  517.7 2.7 fusion.38
  520.4 2.8 fusion.41
  523.2 8.2 %copy.155 = f32[2,1,24,96,96]{2,0,4,3,1:T(2,128)} copy(f32[2,1,24,96,96]{3,4,2,0,1:T(8,128)S(1)} %fusion.41) | data formatting | bytes 3538944 | tf_op jit(solution)/shard_map/reshape | solution.py:68
  531.5 18.1 %gather_fusion.1 = f32[2048,2,24]{2,1,0:T(2,128)} fusion(f32[2,24,9216]{1,0,2:T(2,128)} %bitcast.265, s32[2048]{0:T(1024)S(1)} %get-tuple-element.24), kind=kCustom, calls=%fused_computation.1 | custom fusion | bytes 794624 | tf_op jit(solution)/shard_map/gather | solution.py:68
  549.5 1.8 bitcast_bitcast_fusion
  551.3 3.7 reshape.490
  555.1 8.8 %all_to_all.67 = f32[4,1,24576]{2,1,0:T(1,128)S(1)} all-to-all(f32[4,1,24576]{2,1,0:T(1,128)S(1)} %reshape.490), channel_id=1, replica_groups=mesh['grid'=4,'band'=8] {'grid'}, dimensions={0} | all-to-all | bytes 786432 | tf_op jit(solution)/shard_map/all_to_all | solution.py:69
  563.9 1.7 reduce.1
  565.6 3.3 reshape.491
  569.0 1.9 copy.156
  570.9 1.2 copy.115
  572.1 0.5 convolution_bitcast_fusion
  572.8 0.9 fusion.103
  573.9 1.1 reshape.390
  575.1 0.6 dynamic-slice
  576.4 23.7 %all-gather.3.cloned.1.call-done = bf16[2,8,49152]{2,0,1:T(2,128)(2,1)} async-done(((bf16[2,1,49152]{2,0,1:T(2,128)(2,1)}), bf16[2,8,49152]{2,0,1:T(2,128)(2,1)}) %all-gather.3.cloned.1.call-update) | async-done | bytes 1572880 | tf_op jit(solution)/shard_map/all_gather | solution.py:85
  600.0 4.7 fusion.105
  604.7 1.0 convolution_bitcast_fusion.6
  605.8 1.0 convolution_bitcast_fusion.4
  606.8 1.1 fusion.45
  607.8 1.0 fusion.47
  609.5 9.8 %all-reduce = f32[2,1,8]{2,1,0:T(1,128)S(1)} all-reduce(f32[2,1,8]{2,1,0:T(1,128)S(1)} %pad_maximum_fusion.14), channel_id=2, replica_groups=mesh['grid'=4,'band'=8] {'grid'}, use_global_device_ids=true, to_apply=%region_2.3.clone | all-reduce | flops 16 | bytes 128
  619.4 0.6 dynamic-slice_multiply_fusion
  (89 shorter events, 2.7 us)
Async XLA Ops:
  7.2 11.4 %copy-start.27 = (f32[24,9216]{1,0:T(8,128)S(1)}, f32[24,9216]{1,0:T(8,128)}, u32[]{:S(2)}) copy-start(f32[24,9216]{1,0:T(8,128)} %param.7) | copy-start | bytes 2654212
  7.8 0.7 copy-start.32
  8.6 0.6 copy-start.28
  9.2 3.1 copy-start.19
  10.4 2.0 copy-start.16
  11.1 0.6 copy-start.6
  11.1 0.7 copy-start.10
  13.4 14.9 %all-to-all-start = ((f32[2,1,96,512]{3,0,1,2:T(2,128)}), f32[2,1,96,512]{3,0,1,2:T(2,128)S(1)}, u32[]{:S(2)}, u32[]{:S(2)}) async-start(f32[2,1,96,512]{3,0,1,2:T(2,128)} %copy.89), calls=%async_computation | async-start | bytes 786432 | tf_op jit(solution)/shard_map/all_to_all | solution.py:73
  18.7 0.9 copy-start.31
  28.4 0.7 copy-start.26
  231.9 3.2 copy-start.7
  231.9 3.2 copy-start.11
  235.1 2.9 copy-start
  235.1 2.9 copy-start.3
  276.2 9.3 %all-to-all-start.1 = ((f32[4,1,24576]{2,1,0:T(1,128)}), f32[4,1,24576]{2,1,0:T(1,128)S(1)}, u32[]{:S(2)}, u32[]{:S(2)}) async-start(f32[4,1,24576]{2,1,0:T(1,128)} %reshape.488), calls=%async_computation.1 | async-start | bytes 786432 | tf_op jit(solution)/shard_map/all_to_all | solution.py:69
  279.6 320.4 %all-gather.3.cloned.1.call-start = ((), (), s32[]{:S(2)}) async-start(), calls=%async_computation.4 | async-start | bytes 1769472 | tf_op jit(solution)/shard_map/all_gather | solution.py:85
  288.4 7.5 %copy-start.1 = (f32[1,96,2,96]{1,3,2,0:T(8,128)S(1)}, f32[1,96,2,96]{1,3,2,0:T(8,128)}, u32[]{:S(2)}) copy-start(f32[1,96,2,96]{1,3,2,0:T(8,128)} %get-tuple-element.20) | copy-start | bytes 221188
  288.4 7.6 %copy-start.4 = (f32[1,96,2,96]{1,3,2,0:T(8,128)S(1)}, f32[1,96,2,96]{1,3,2,0:T(8,128)}, u32[]{:S(2)}) copy-start(f32[1,96,2,96]{1,3,2,0:T(8,128)} %get-tuple-element.23) | copy-start | bytes 221188
  292.8 3.7 copy-start.29
  292.8 3.7 copy-start.33
  294.7 3.0 copy-start.14
  294.7 3.0 copy-start.20
  294.7 3.1 copy-start.8
  294.7 3.1 copy-start.12
  297.7 11.1 %copy-start.22 = (f32[1,1,512,96]{2,3,0,1:T(8,128)}, f32[1,1,512,96]{2,3,0,1:T(8,128)S(1)}, u32[]{:S(2)}) copy-start(f32[1,1,512,96]{2,3,0,1:T(8,128)S(1)} %get-tuple-element.16) | copy-start | bytes 589828
  297.7 11.1 %copy-start.24 = (f32[1,1,512,96]{2,3,0,1:T(8,128)}, f32[1,1,512,96]{2,3,0,1:T(8,128)S(1)}, u32[]{:S(2)}) copy-start(f32[1,1,512,96]{2,3,0,1:T(8,128)S(1)} %get-tuple-element.17) | copy-start | bytes 589828
  297.8 0.8 copy-start.17
  511.6 3.2 copy-start.9
  511.6 3.2 copy-start.13
  514.8 2.9 copy-start.2
  514.8 2.9 copy-start.5
  568.9 3.7 copy-start.18
  568.9 3.7 copy-start.30
  568.9 3.7 copy-start.34
  569.0 3.8 copy-start.15
  569.0 3.8 copy-start.21
  569.0 3.8 copy-start.23
  570.9 1.9 copy-start.25
  572.6 2.5 copy-start.35
Sparse Core Ops, SparseCore 0:
  575.2 24.7 all-gather.2
where the time goes:
time: 635 us; the launch traced here: 627 us
  local copies, waits for them, and re-layouts  496 us (78%)
  blocking collectives  37.4 us (6%)
  matrix products  29.3 us (5%)
  waiting for transfers between devices  28.2 us (4%)
  between operations  16.9 us (3%)
  other arithmetic  10.4 us (2%)
  starting transfers between devices  8.66 us (1%)
    scatter x2, local copies, waits for them, and re-layouts, planes_work(): dense = jnp.zeros((2, count, depth, size * size), jnp.float32).at[:, :, :...  374 us
    gather x2, local copies, waits for them, and re-layouts, planes_work(): picked = dense.reshape(2, count, depth, size * size)[:, :, :, full_map]  36.2 us
    another operation x6, local copies, waits for them, and re-layouts  26.4 us
    dot_general x12, matrix products, transform(): return jnp.einsum(form, stacked, table, precision=lax.Precision.HIGHEST)  25.2 us
    all_gather x1, waiting for transfers between devices, body(): lax.all_gather(rounded, 'band', axis=1, tiled=True)  23.7 us
    unnamed x79, local copies, waits for them, and re-layouts  22.5 us
    reshape x2, local copies, waits for them, and re-layouts, planes_work(): picked = dense.reshape(2, count, depth, size * size)[:, :, :, full_map]  16.5 us
  transfers between devices with their start and end apart: 3, of which 2 were waited for; matrix products, arithmetic and copies ran while one was open for 0% of the time, Pallas kernels for 0%

commit v1 on v0

v1 whole, which is shorter than its diff:
```python
import functools

import jax
import jax.numpy as jnp
import ml_dtypes
import numpy as np
from jax import lax
from jax.experimental import pallas as pl
from jax.experimental.pallas import tpu as pltpu
from jax.sharding import PartitionSpec as P

GY = 64
GX = 56
F32 = jnp.float32
BF16 = jnp.bfloat16
VMEM_LIMIT = 60 * 1024 * 1024


def round_up(value, unit):
    return -(-value // unit) * unit


def halves(table):
    table = np.asarray(table, np.float32)
    high = table.astype(ml_dtypes.bfloat16)
    low = (table - high.astype(np.float32)).astype(ml_dtypes.bfloat16)
    return np.stack([high, low])


def folded(index, size):
    return np.where(index < size // 2, index, index - size)


def z_tables(size, devices, pad):
    depth = size // devices
    radius = size // 4
    freq = np.arange(size)
    keep = np.abs(folded(freq, size)) <= radius
    ahead = np.zeros((devices, 2, 2 * pad, size))
    back = np.zeros((devices, 2 * pad, 256))
    for d in range(devices):
        plane = d * depth + np.arange(depth)
        angle = 2 * np.pi * ((plane[:, None] * freq[None, :]) % size) / size
        c, s = np.cos(angle) * keep, np.sin(angle) * keep
        ahead[d, 0, :depth], ahead[d, 0, pad : pad + depth] = c, s
        ahead[d, 1, :depth], ahead[d, 1, pad : pad + depth] = -s, c
        back[d, :depth, :size], back[d, :depth, 128 : 128 + size] = c, -s
        back[d, pad : pad + depth, :size], back[d, pad : pad + depth, 128 : 128 + size] = s, c
    return halves(ahead), halves(back)


def plane_tables(size):
    radius = size // 4
    count = 2 * radius + 1
    freq = np.arange(count) - radius
    angle = 2 * np.pi * ((freq[:, None] * np.arange(size)[None, :]) % size) / size
    c, s = np.cos(angle), np.sin(angle)
    ty = np.zeros((2 * GY, 256))
    ty[:count, :size], ty[:count, 128 : 128 + size] = c, s
    ty[GY : GY + count, :size], ty[GY : GY + count, 128 : 128 + size] = -s, c
    tyb = np.zeros((256, 2 * GY))
    tyb[:size, :count], tyb[:size, GY : GY + count] = c.T, -s.T
    tyb[128 : 128 + size, :count], tyb[128 : 128 + size, GY : GY + count] = s.T, c.T
    tx = np.zeros((2 * size, 2 * GX))
    tx[:size, :count], tx[:size, GX : GX + count] = c.T, -s.T
    tx[size:, :count], tx[size:, GX : GX + count] = s.T, c.T
    txb = np.zeros((2 * GX, 2 * size))
    txb[:count, :size], txb[:count, size:] = c, s
    txb[GX : GX + count, :size], txb[GX : GX + count, size:] = -s, c
    return halves(ty), halves(tx), halves(txb), halves(tyb)


def split(value):
    high = value.astype(BF16)
    low = (value - high.astype(F32)).astype(BF16)
    return high, low


def dot(a, b, dims=((1,), (0,))):
    return lax.dot_general(a, b, (dims, ((), ())), preferred_element_type=F32)


def dot3(a, b, dims=((1,), (0,))):
    return dot(a[0], b[0], dims) + dot(a[0], b[1], dims) + dot(a[1], b[0], dims)


def call(kernel, out_shape, in_specs, scratch=()):
    return pl.pallas_call(
        kernel,
        out_shape=out_shape,
        in_specs=in_specs,
        scratch_shapes=list(scratch),
        compiler_params=pltpu.CompilerParams(vmem_limit_bytes=VMEM_LIMIT),
    )


SMEM = pl.BlockSpec(memory_space=pltpu.SMEM)
VMEM = pl.BlockSpec(memory_space=pltpu.VMEM)


def column_values(row, lanes):
    return jnp.transpose(jnp.broadcast_to(row, (lanes, row.shape[1])))


def sphere(radius_row, size):
    cols = radius_row.shape[1]
    radius = size // 4
    flat = column_values(radius_row, 128)[:, :size]
    lane = lax.broadcasted_iota(jnp.int32, (cols, size), 1)
    freq = jnp.where(lane < size // 2, lane, lane - size).astype(F32)
    radius2 = flat + freq * freq
    return radius2 <= float(radius * radius), radius2 * (2.0 / (radius * radius))


def to_planes(me, parts, table_ref, outs, step):
    count = len(outs)
    total = None
    for p in range(2):
        high, low = split(parts[p])
        ta = jnp.concatenate([table_ref[0, step(me, k), p] for k in range(count)], axis=0)
        tb = jnp.concatenate([table_ref[1, step(me, k), p] for k in range(count)], axis=0)
        piece = dot3((ta, tb), (high, low), ((1,), (1,)))
        total = piece if total is None else total + piece
    rows = outs[0].shape[0]
    for k in range(count):
        outs[k][...] = total[k * rows : (k + 1) * rows]


def from_planes(me, planes, table_ref, step, size):
    count = len(planes)
    stacked = jnp.concatenate([ref[...] for ref in planes], axis=0)
    high, low = split(jnp.transpose(stacked))
    ta = jnp.concatenate([table_ref[0, step(me, k)] for k in range(count)], axis=0)
    tb = jnp.concatenate([table_ref[1, step(me, k)] for k in range(count)], axis=0)
    total = dot3((high, low), (ta, tb))
    return total[:, :size], total[:, 128 : 128 + size]


def first_kernel(devices, step, size, me_ref, psi_ref, radius_ref, ahead_ref, *outs):
    inside, _ = sphere(radius_ref[...], size)
    parts = [jnp.where(inside, psi_ref[p], 0.0) for p in range(2)]
    to_planes(me_ref[0], parts, ahead_ref, outs, step)


def middle_kernel(devices, step, size, me_ref, low_ref, up_ref, *refs):
    planes, refs = refs[:devices], refs[devices:]
    psi_ref, radius_ref, ahead_ref, back_ref, first_ref = refs[:5]
    outs = refs[5:]
    center = (up_ref[0] + low_ref[0]) / 2.0
    half = (up_ref[0] - low_ref[0]) / 2.0
    inside, kinetic = sphere(radius_ref[...], size)
    back = from_planes(me_ref[0], planes, back_ref, step, size)
    parts = []
    for p in range(2):
        value = jnp.where(inside, ((kinetic - center) * psi_ref[p] + back[p]) / half, 0.0)
        first_ref[p] = value
        parts.append(value)
    to_planes(me_ref[0], parts, ahead_ref, outs, step)


def last_kernel(devices, step, size, me_ref, low_ref, up_ref, *refs):
    planes, refs = refs[:devices], refs[devices:]
    psi_ref, first_ref, radius_ref, back_ref, pick_ref, filtered_ref, packed_ref = refs
    center = (up_ref[0] + low_ref[0]) / 2.0
    half = (up_ref[0] - low_ref[0]) / 2.0
    inside, kinetic = sphere(radius_ref[...], size)
    back = from_planes(me_ref[0], planes, back_ref, step, size)
    packed = None
    for p in range(2):
        value = 2.0 * ((kinetic - center) * first_ref[p] + back[p]) / half - psi_ref[p]
        value = jnp.where(inside, value, 0.0)
        filtered_ref[p] = value
        piece = dot(value.astype(BF16), pick_ref[p])
        packed = piece if packed is None else packed + piece
    packed_ref[...] = packed.astype(BF16)


def slab_kernel(devices, size, depth, *refs):
    planes, refs = refs[:devices], refs[devices:]
    place_ref, pot_ref, ty_ref, tx_ref, txb_ref, tyb_ref = refs[:6]
    outs = refs[6 : 6 + devices]
    y0_ref, y1_ref, q_ref, box_ref, gxc_ref, oy_ref = refs[6 + devices :]
    pad = planes[0].shape[0] // 2
    cols = planes[0].shape[1]
    total = cols * devices
    radius = size // 4
    tiles = -(-(2 * radius + 1) // 4)
    gx_row, gy_row = place_ref[0:1, :], place_ref[1:2, :]
    lane = lax.broadcasted_iota(jnp.int32, (total, 128), 1)
    gxc_ref[...] = column_values(gx_row, 128).astype(BF16)
    oy_ref[...] = jnp.where(column_values(gy_row, 128) == (lane % GY).astype(F32), 1.0, 0.0).astype(BF16)
    side = (lax.broadcasted_iota(jnp.int32, (total, 128), 1) // GY).astype(BF16)
    near = lax.broadcasted_iota(jnp.int32, (pad, 128), 1) < GY

    stacked = jnp.concatenate([ref[...] for ref in planes], axis=1)
    lhs = jnp.concatenate(split(stacked), axis=0)
    ty = (ty_ref[0], ty_ref[1])
    zero = jnp.zeros((), BF16)
    for t in range(tiles):
        hot = []
        for u in range(2):
            hot.append(jnp.where(gxc_ref[...] - side == float(4 * t + 2 * u), oy_ref[...], zero))
        got = dot(lhs, jnp.concatenate(hot, axis=1))
        got = got[: 2 * pad] + got[2 * pad :]
        rows = []
        for u in range(2):
            re, im = got[:pad, 128 * u : 128 * u + 128], got[pad:, 128 * u : 128 * u + 128]
            rows.append(jnp.where(near, re, pltpu.roll(im, GY, 1)))
            rows.append(jnp.where(near, pltpu.roll(re, GY, 1), im))
        moved = dot3(split(jnp.concatenate(rows, axis=0)), ty)
        y0_ref[4 * t * pad : 4 * (t + 1) * pad] = moved[:, :128]
        y1_ref[4 * t * pad : 4 * (t + 1) * pad] = moved[:, 128:]
    if tiles * 4 < GX:
        rest = jnp.zeros(((GX - 4 * tiles) * pad, 128), F32)
        y0_ref[4 * tiles * pad :] = rest
        y1_ref[4 * tiles * pad :] = rest
    if depth < pad:
        q_ref[depth * GX :] = jnp.zeros(((pad - depth) * GX, 128), F32)

    tx = (tx_ref[0], tx_ref[1])
    txb = (txb_ref[0], txb_ref[1])
    tyb = (tyb_ref[0], tyb_ref[1])
    for z in range(0, depth, 2):
        sides = []
        for w in range(2):
            rows = pl.ds(z + w, GX, stride=pad)
            sides.append(jnp.concatenate([y0_ref[rows, :], y1_ref[rows, :]], axis=0))
        field = dot3(tx, split(jnp.concatenate(sides, axis=1)))
        pot = jnp.concatenate([pot_ref[z], pot_ref[z + 1]], axis=1)
        field = field * jnp.concatenate([pot, pot], axis=0)
        back = dot3(txb, split(field))
        rows = [
            jnp.concatenate([back[:GX, 128 * w : 128 * w + 128], back[GX:, 128 * w : 128 * w + 128]], axis=1)
            for w in range(2)
        ]
        q_ref[z * GX : (z + 2) * GX] = dot3(split(jnp.concatenate(rows, axis=0)), tyb)

    for t in range(tiles):
        for u in range(2):
            a = q_ref[pl.ds(4 * t + 2 * u, pad, stride=GX), :]
            b = q_ref[pl.ds(4 * t + 2 * u + 1, pad, stride=GX), :]
            re = jnp.where(near, a, pltpu.roll(b, GY, 1))
            im = jnp.where(near, pltpu.roll(a, GY, 1), b)
            at = 256 * t + 128 * u
            box_ref[:, at : at + 128] = jnp.concatenate(split(jnp.concatenate([re, im], axis=0)), axis=0)

    box = box_ref[...]
    wide = min(256, cols)
    down = lax.broadcasted_iota(jnp.int32, (GY, wide), 0).astype(F32)
    for k in range(devices):
        for at in range(0, cols, wide):
            here = k * cols + at
            gx = jnp.broadcast_to(gx_row[:, here : here + wide], (GY, wide)).astype(BF16)
            hot = jnp.where(jnp.broadcast_to(gy_row[:, here : here + wide], (GY, wide)) == down, 1.0, 0.0).astype(BF16)
            tall = jnp.concatenate([jnp.where(gx == float(v), hot, zero) for v in range(4 * tiles)], axis=0)
            got = dot(box, tall)
            outs[k][:, at : at + wide] = got[: 2 * pad] + got[2 * pad :]


def body(devices, bands, psi, col_map, potential, lower, upper):
    cols, size = psi.shape[2], psi.shape[3]
    radius = size // 4
    depth = size // devices
    pad = round_up(depth, 8)
    rows = 2 * pad
    me = lax.axis_index("grid")
    me_arg = me.astype(jnp.int32).reshape(1)
    if devices & (devices - 1) == 0:
        step = lambda at, k: at ^ k
        back_step = step
    else:
        raise ValueError("grid size")

    def exchange(values):
        return [values[0]] + [
            lax.ppermute(values[k], "grid", [(d, step(d, k)) for d in range(devices)]) for k in range(1, devices)
        ]

    ahead, back = z_tables(size, devices, pad)
    ty, tx, txb, tyb = plane_tables(size)
    count = 2 * radius + 1
    pick = np.zeros((2, size, 128), ml_dtypes.bfloat16)
    for j in range(count):
        pick[0, (j - radius) % size, j] = 1
        pick[1, (j - radius) % size, GY + j] = 1

    kx, ky = col_map // size, col_map % size
    gx = jnp.where(kx < size // 2, kx, kx - size)
    gy = jnp.where(ky < size // 2, ky, ky - size)
    radius2 = gx * gx + gy * gy
    used = radius2 <= radius * radius
    place = jnp.stack([jnp.where(used, gx + radius, -9), jnp.where(used, gy + radius, -9)]).astype(F32)
    radius_row = radius2.astype(F32).reshape(1, cols)
    places = jnp.concatenate(exchange([place] * devices), axis=1)
    pot = (potential * (1.0 / float(size**3))).reshape(depth, size, size)
    pot = jnp.pad(pot, ((0, 0), (0, 0), (0, 128 - size)))

    psi2 = psi.reshape(2, cols, size)
    plane_shape = [jax.ShapeDtypeStruct((rows, cols), F32)] * devices
    sent = call(
        functools.partial(first_kernel, devices, step, size),
        plane_shape,
        [SMEM, VMEM, VMEM, VMEM],
    )(me_arg, psi2, radius_row, ahead)

    def slab(values):
        return call(
            functools.partial(slab_kernel, devices, size, depth),
            plane_shape,
            [VMEM] * (devices + 6),
            [
                pltpu.VMEM((GX * pad, 128), F32),
                pltpu.VMEM((GX * pad, 128), F32),
                pltpu.VMEM((pad * GX, 128), F32),
                pltpu.VMEM((2 * rows, 256 * (-(-count // 4))), BF16),
                pltpu.VMEM((cols * devices, 128), BF16),
                pltpu.VMEM((cols * devices, 128), BF16),
            ],
        )(*values, places, pot, ty, tx, txb, tyb)

    planes = exchange(slab(exchange(sent)))
    first, *sent = call(
        functools.partial(middle_kernel, devices, step, size),
        [jax.ShapeDtypeStruct((2, cols, size), F32)] + plane_shape,
        [SMEM] * 3 + [VMEM] * (devices + 4),
    )(me_arg, lower, upper, *planes, psi2, radius_row, ahead, back)
    planes = exchange(slab(exchange(sent)))
    filtered, packed = call(
        functools.partial(last_kernel, devices, step, size),
        [jax.ShapeDtypeStruct((2, cols, size), F32), jax.ShapeDtypeStruct((cols, 128), BF16)],
        [SMEM] * 3 + [VMEM] * (devices + 5),
    )(me_arg, lower, upper, *planes, psi2, first, radius_row, back, pick)

    part = cols // bands
    spread = lax.all_to_all(packed.reshape(bands, part, 128), "band", split_axis=0, concat_axis=0, tiled=True)
    real, imag = spread[:, :, :GY], spread[:, :, GY:]
    dims = (((1, 2), (1, 2)), ((), ()))
    real_part = lax.dot_general(spread, spread, dims, preferred_element_type=F32)
    cross = lax.dot_general(real, imag, dims, preferred_element_type=F32)
    sums = lax.psum(jnp.stack([real_part, cross - cross.T]), ("grid", "band"))
    own = bands // devices
    gram = lax.dynamic_slice(sums, (0, lax.axis_index("band"), me * own), (2, 1, own)) / (4.0 * radius**3)
    return filtered.reshape(psi.shape), gram


def solution(mesh):
    return jax.shard_map(
        functools.partial(body, mesh.shape["grid"], mesh.shape["band"]),
        mesh=mesh,
        in_specs=(P(None, "band", "grid", None), P("grid"), P("grid", None), P(), P()),
        out_specs=(P(None, "band", "grid", None), P(None, "band", "grid")),
        check_vma=False,
    )
```

time: 635 us -> 143 us (0.23); the launches traced: 627 us -> 142 us
  local copies, waits for them, and re-layouts: 496 us -> 8.27 us
  Pallas kernels: 0 us -> 45.1 us
  matrix products: 29.3 us -> 0.49 us
  between operations: 16.9 us -> 2 us
  starting transfers between devices: 8.66 us -> 23.4 us
  waiting for transfers between devices: 28.2 us -> 20.7 us
  other arithmetic: 10.4 us -> 3.4 us
    scatter x2 -> x0, local copies, waits for them, and re-layouts: 374 us -> none  [planes_work(): dense = jnp.zeros((2, count, depth, size * size), jnp.float32).at[:, :, :...]
    pallas_call x0 -> x5, Pallas kernels: none -> 45.1 us  [the longest x2 36.6 us: slab(): call(functools.partial(slab_kernel, devices, size, depth), plane_shape, [...]
    psum x0 -> x1, blocking collectives: none -> 38.6 us  [body(): sums = lax.psum(jnp.stack([real_part, cross - cross.T]), ('grid', 'band'))]
    gather x2 -> x0, local copies, waits for them, and re-layouts: 36.2 us -> none  [planes_work(): picked = dense.reshape(2, count, depth, size * size)[:, :, :, full_map]]
    dot_general x16 -> x2, matrix products: 29.3 us -> 0.49 us  [the longest x1 0.27 us: body(): cross = lax.dot_general(real, imag, dims, preferred_element_type=F32)]
    another operation x6 -> x0, local copies, waits for them, and re-layouts: 26.4 us -> none
    all_gather x1 -> x0, waiting for transfers between devices: 23.7 us -> none  [body(): lax.all_gather(rounded, 'band', axis=1, tiled=True)]
    all_to_all x2 -> x0, blocking collectives: 18.7 us -> none  [the longest x1 9.9 us: apply_h(): lax.all_to_all(stacked, 'grid', split_axis=2, concat_axis=3, tiled=True)]
  transfers between devices with their start and end apart: 3 -> 16, of which waited for: 2 -> 11; matrix products, arithmetic and copies ran while one was open for 0% -> 4% of each run, Pallas kernels for 0% -> 2%
where the time goes in v1:
time: 143 us; the launch traced here: 142 us
  Pallas kernels  45.1 us (32%)
  blocking collectives  38.6 us (27%)
  starting transfers between devices  23.4 us (16%)
  waiting for transfers between devices  20.7 us (14%)
  local copies, waits for them, and re-layouts  8.27 us (6%)
  other arithmetic  3.4 us (2%)
  between operations  2 us (1%)
    psum x1, blocking collectives, body(): sums = lax.psum(jnp.stack([real_part, cross - cross.T]), ('grid', 'band'))  38.6 us
    pallas_call x2, Pallas kernels, slab(): call(functools.partial(slab_kernel, devices, size, depth), plane_shape, [...  36.6 us
    ppermute x15, starting transfers between devices, exchange(): lax.ppermute(values[k], 'grid', [(d, step(d, k)) for d in range(devices)])  18.5 us
    ppermute x15, waiting for transfers between devices, exchange(): lax.ppermute(values[k], 'grid', [(d, step(d, k)) for d in range(devices)])  15.9 us
    unnamed x30, local copies, waits for them, and re-layouts  6.52 us
    all_to_all x1, starting transfers between devices, body(): lax.all_to_all(packed.reshape(bands, part, 128), 'band', split_axis=0, co...  4.88 us
    all_to_all x1, waiting for transfers between devices, body(): lax.all_to_all(packed.reshape(bands, part, 128), 'band', split_axis=0, co...  4.8 us
    pallas_call x1, Pallas kernels, body(): call(functools.partial(middle_kernel, devices, step, size), [jax.ShapeDty...  3.43 us
  transfers between devices with their start and end apart: 16, of which 11 were waited for; matrix products, arithmetic and copies ran while one was open for 4% of the time, Pallas kernels for 2%

profile of v1, /device:TPU:0, one launch (start us, length us, event | category | flops | bytes accessed | tf_op | source)
XLA Modules:
  0.0 142.1 jit_solution(13518441649644918019)
XLA Ops:
  0.6 0.0 copy-start
  0.6 0.8 add_select_fusion.3
  1.4 1.3 add_select_fusion.2
  2.7 3.0 %collective-permute-start.3 = (f32[2,512]{1,0:T(2,128)S(1)}, f32[2,512]{1,0:T(2,128)S(1)}, u32[]{:S(2)}, u32[]{:S(2)}) collective-permute-start(f32[2,512]{1,0:T(2,128)S(1)} %add_convert_fusion), channel_id=1, source_target_pairs={{0,8},{8,0},{16,24},{24,16},{1,9},{9,1},{17,25},{25,17},{2,10},{10... | collective-permute-start | bytes 12296 | tf_op jit(solution)/shard_map/ppermute | solution.py:276
  5.7 1.5 %collective-permute-start.4 = (f32[2,512]{1,0:T(2,128)S(1)}, f32[2,512]{1,0:T(2,128)S(1)}, u32[]{:S(2)}, u32[]{:S(2)}) collective-permute-start(f32[2,512]{1,0:T(2,128)S(1)} %add_convert_fusion), channel_id=1, source_target_pairs={{0,16},{8,24},{16,0},{24,8},{1,17},{9,25},{17,1},{25,9},{2,18},{10... | collective-permute-start | bytes 12296 | tf_op jit(solution)/shard_map/ppermute | solution.py:276
  7.2 0.0 collective-permute-start.5
  7.2 2.0 %copy.18 = f32[2,1,512,96]{3,2,0,1:T(8,128)} copy(f32[2,1,512,96]{2,3,1,0:T(8,128)} %param.12) | data formatting | bytes 786432 | tf_op args[0]
  9.2 2.4 %shard_map.131 = (f32[48,512]{1,0:T(8,128)}, f32[48,512]{1,0:T(8,128)}, f32[48,512]{1,0:T(8,128)}, f32[48,512]{1,0:T(8,128)}) custom-call(s32[1]{0:T(128)} %bitcast.me_ref, f32[2,512,96]{2,1,0:T(8,128)} %bitcast.18, f32[1,512]{1,0:T(1,128)} %bitcast.23, bf16[2,4,2,48,96]{4,3,2,1,0:T(8,128)(2,1)} %constant.66.clone.ahead_ref.refs_6_), custom_call_target="tpu_custom_call" | custom-call | tf_op jit(solution)/shard_map/pallas_call | solution.py:300
  11.6 1.9 %collective-permute-start = (f32[48,512]{1,0:T(8,128)}, f32[48,512]{1,0:T(8,128)S(1)}, u32[]{:S(2)}, u32[]{:S(2)}) collective-permute-start(f32[48,512]{1,0:T(8,128)} %get-tuple-element.22), channel_id=1, source_target_pairs={{0,8},{8,0},{16,24},{24,16},{1,9},{9,1},{17,25},{25,17},{2,10},{10... | collective-permute-start | bytes 294920 | tf_op jit(solution)/shard_map/ppermute | solution.py:276
  13.6 1.5 %collective-permute-start.1 = (f32[48,512]{1,0:T(8,128)}, f32[48,512]{1,0:T(8,128)S(1)}, u32[]{:S(2)}, u32[]{:S(2)}) collective-permute-start(f32[48,512]{1,0:T(8,128)} %get-tuple-element.23), channel_id=1, source_target_pairs={{0,16},{8,24},{16,0},{24,8},{1,17},{9,25},{17,1},{25,9},{2,18},{10... | collective-permute-start | bytes 294920 | tf_op jit(solution)/shard_map/ppermute | solution.py:276
  15.1 0.0 copy-done
  15.1 0.1 broadcast_multiply_fusion
  15.2 0.5 reshape.25
  15.6 0.0 copy-start.13
  15.6 1.1 pad.4.refs_5_
  16.8 0.0 collective-permute-done.3
  16.8 0.0 copy-done.13
  16.8 0.0 collective-permute-start.2
  16.8 0.0 collective-permute-done.4
  16.8 0.0 collective-permute-done.5
  16.8 0.6 pad_maximum_fusion.refs_4_
  17.4 0.0 collective-permute-done.refs_1_
  17.4 1.2 collective-permute-done.1.refs_2_
  18.6 3.7 %collective-permute-done.2.refs_3_ = f32[48,512]{1,0:T(8,128)S(1)} collective-permute-done((f32[48,512]{1,0:T(8,128)S(1)}, f32[48,512]{1,0:T(8,128)S(1)}, u32[]{:S(2)}, u32[]{:S(2)}) %collective-permute-start.2) | collective-permute-done | bytes 98336 | tf_op jit(solution)/shard_map/ppermute | solution.py:276
  22.3 0.0 copy-done.1
  22.3 0.0 copy-done.2
  22.3 0.6 copy-done.3
  22.9 18.3 %shard_map.132 = (f32[48,512]{1,0:T(8,128)}, f32[48,512]{1,0:T(8,128)}, f32[48,512]{1,0:T(8,128)}, f32[48,512]{1,0:T(8,128)}) custom-call(f32[48,512]{1,0:T(8,128)} %get-tuple-element.21.refs_0_, f32[48,512]{1,0:T(8,128)} %copy-done.1, f32[48,512]{1,0:T(8,128)} %copy-done.2, f32[48,512]{1,0:T(8,128)} %copy-done.3, f32[2,2048]{1,0:T(2,128)} %pad_maximum_fusion.refs_4_, ...), custom_call_target="tpu_custom_call" | custom-call | tf_op jit(solution)/shard_map/pallas_call | solution.py:307
  41.2 0.5 collective-permute-start.6
  41.7 0.1 collective-permute-start.7
  41.8 2.9 %collective-permute-start.8 = (f32[48,512]{1,0:T(8,128)}, f32[48,512]{1,0:T(8,128)S(1)}, u32[]{:S(2)}, u32[]{:S(2)}) collective-permute-start(f32[48,512]{1,0:T(8,128)} %get-tuple-element.28), channel_id=1, source_target_pairs={{0,24},{8,16},{16,8},{24,0},{1,25},{9,17},{17,9},{25,1},{2,26},{10... | collective-permute-start | bytes 294920 | tf_op jit(solution)/shard_map/ppermute | solution.py:276
  46.0 0.0 collective-permute-done.6.refs_1_
  46.0 0.5 collective-permute-done.7.refs_2_
  46.6 1.0 collective-permute-done.8.refs_3_
  47.6 0.0 copy-done.8
  47.6 0.6 copy-done.12
  48.2 3.4 %shard_map.133 = (f32[2,512,96]{2,1,0:T(8,128)}, f32[48,512]{1,0:T(8,128)}, f32[48,512]{1,0:T(8,128)}, f32[48,512]{1,0:T(8,128)}, f32[48,512]{1,0:T(8,128)}) custom-call(s32[1]{0:T(128)} %bitcast.me_ref, f32[1]{0:T(128)S(6)} %copy.27.low_ref, f32[1]{0:T(128)S(6)} %copy.28.up_ref, f32[48,512]{1,0:T(8,128)} %get-tuple-element.25.refs_0_, f32[48,512]{1,0:T(8,128)} %copy-done.8, ...), custom_call_target="tpu_custom_call" | custom-call | tf_op jit(solution)/shard_map/pallas_call | solution.py:322
  51.7 1.9 %collective-permute-start.10 = (f32[48,512]{1,0:T(8,128)}, f32[48,512]{1,0:T(8,128)S(1)}, u32[]{:S(2)}, u32[]{:S(2)}) collective-permute-start(f32[48,512]{1,0:T(8,128)} %get-tuple-element.31), channel_id=1, source_target_pairs={{0,16},{8,24},{16,0},{24,8},{1,17},{9,25},{17,1},{25,9},{2,18},{10... | collective-permute-start | bytes 294920 | tf_op jit(solution)/shard_map/ppermute | solution.py:276
  53.5 1.4 %collective-permute-start.11 = (f32[48,512]{1,0:T(8,128)}, f32[48,512]{1,0:T(8,128)S(1)}, u32[]{:S(2)}, u32[]{:S(2)}) collective-permute-start(f32[48,512]{1,0:T(8,128)} %get-tuple-element.32), channel_id=1, source_target_pairs={{0,24},{8,16},{16,8},{24,0},{1,25},{9,17},{17,9},{25,1},{2,26},{10... | collective-permute-start | bytes 294920 | tf_op jit(solution)/shard_map/ppermute | solution.py:276
  55.0 0.2 collective-permute-start.9
  55.2 1.3 collective-permute-done.10.refs_2_
  56.5 2.8 %collective-permute-done.11.refs_3_ = f32[48,512]{1,0:T(8,128)S(1)} collective-permute-done((f32[48,512]{1,0:T(8,128)}, f32[48,512]{1,0:T(8,128)S(1)}, u32[]{:S(2)}, u32[]{:S(2)}) %collective-permute-start.11) | collective-permute-done | bytes 98336 | tf_op jit(solution)/shard_map/ppermute | solution.py:276
  59.3 0.5 collective-permute-done.9.refs_1_
  59.8 0.1 copy-done.5
  59.9 0.5 copy-done.6
  60.4 18.3 %shard_map.134 = (f32[48,512]{1,0:T(8,128)}, f32[48,512]{1,0:T(8,128)}, f32[48,512]{1,0:T(8,128)}, f32[48,512]{1,0:T(8,128)}) custom-call(f32[48,512]{1,0:T(8,128)} %get-tuple-element.29.refs_0_, f32[48,512]{1,0:T(8,128)} %copy-done.6, f32[48,512]{1,0:T(8,128)} %copy-done.4, f32[48,512]{1,0:T(8,128)} %copy-done.5, f32[2,2048]{1,0:T(2,128)} %pad_maximum_fusion.refs_4_, ...), custom_call_target="tpu_custom_call" | custom-call | tf_op jit(solution)/shard_map/pallas_call | solution.py:307
  78.7 1.1 collective-permute-start.12
  79.8 1.5 %collective-permute-start.13 = (f32[48,512]{1,0:T(8,128)}, f32[48,512]{1,0:T(8,128)S(1)}, u32[]{:S(2)}, u32[]{:S(2)}) collective-permute-start(f32[48,512]{1,0:T(8,128)} %get-tuple-element.35), channel_id=1, source_target_pairs={{0,16},{8,24},{16,0},{24,8},{1,17},{9,25},{17,1},{25,9},{2,18},{10... | collective-permute-start | bytes 294920 | tf_op jit(solution)/shard_map/ppermute | solution.py:276
  81.3 0.9 collective-permute-start.14
  82.2 1.3 collective-permute-done.12.refs_1_
  83.6 1.0 collective-permute-done.13.refs_2_
  84.6 2.4 %collective-permute-done.14.refs_3_ = f32[48,512]{1,0:T(8,128)S(1)} collective-permute-done((f32[48,512]{1,0:T(8,128)}, f32[48,512]{1,0:T(8,128)S(1)}, u32[]{:S(2)}, u32[]{:S(2)}) %collective-permute-start.14) | collective-permute-done | bytes 98336 | tf_op jit(solution)/shard_map/ppermute | solution.py:276
  87.0 0.0 copy-done.9
  87.0 0.6 copy-done.11
  87.7 2.8 %shard_map.135 = (f32[2,512,96]{2,1,0:T(8,128)}, bf16[512,128]{1,0:T(8,128)(2,1)}) custom-call(s32[1]{0:T(128)} %bitcast.me_ref, f32[1]{0:T(128)S(6)} %copy.27.low_ref, f32[1]{0:T(128)S(6)} %copy.28.up_ref, f32[48,512]{1,0:T(8,128)} %get-tuple-element.33.refs_0_, f32[48,512]{1,0:T(8,128)} %copy-done.7, f32[48,512]{1,0:T(8,128)} %copy-done.9, ...), custom_call_target="tpu_custom_call" | custom-call | tf_op jit(solution)/shard_map/pallas_call | solution.py:328
  90.5 4.9 %all-to-all-start = ((bf16[8,64,128]{2,1,0:T(8,128)(2,1)}), bf16[8,64,128]{2,1,0:T(8,128)(2,1)S(1)}, u32[]{:S(2)}, u32[]{:S(2)}) async-start(bf16[8,64,128]{2,1,0:T(8,128)(2,1)} %bitcast.22), calls=%async_computation | async-start | bytes 262144 | tf_op jit(solution)/shard_map/all_to_all | solution.py:335
  95.3 2.0 %copy.24 = f32[2,1,512,96]{2,3,1,0:T(8,128)} copy(f32[2,1,512,96]{3,2,0,1:T(8,128)} %bitcast.21) | data formatting | bytes 786432
  97.3 4.8 %all-to-all-done = bf16[8,64,128]{2,1,0:T(8,128)(2,1)S(1)} async-done(((bf16[8,64,128]{2,1,0:T(8,128)(2,1)}), bf16[8,64,128]{2,1,0:T(8,128)(2,1)S(1)}, u32[]{:S(2)}, u32[]{:S(2)}) %all-to-all-start) | async-done | bytes 131104 | tf_op jit(solution)/shard_map/all_to_all | solution.py:335
  102.1 0.1 copy.19
  102.2 0.3 convolution_bitcast_fusion
  102.5 0.1 copy.23
  102.6 0.2 convolution_bitcast_fusion.1
  102.8 38.6 %psum.7 = f32[2,8,8]{2,1,0:T(8,128)S(1)} all-reduce(f32[2,8,8]{2,1,0:T(8,128)S(1)} %pad_maximum_fusion.1), channel_id=1, replica_groups=mesh['grid'=4,'band'=8] {'grid','band'}, use_global_device_ids=true, to_apply=%region_0.1 | all-reduce | flops 128 | bytes 1024 | tf_op jit(solution)/shard_map/psum | solution.py:340
  141.4 0.6 dynamic-slice_multiply_fusion
  (18 shorter events, 0.0 us)
Async XLA Ops:
  0.6 14.5 %copy-start = (f32[24,9216]{1,0:T(8,128)S(1)}, f32[24,9216]{1,0:T(8,128)}, u32[]{:S(2)}) copy-start(f32[24,9216]{1,0:T(8,128)} %param.14) | copy-start | bytes 2654212
  2.7 14.1 %collective-permute-start.3 = (f32[2,512]{1,0:T(2,128)S(1)}, f32[2,512]{1,0:T(2,128)S(1)}, u32[]{:S(2)}, u32[]{:S(2)}) collective-permute-start(f32[2,512]{1,0:T(2,128)S(1)} %add_convert_fusion), channel_id=1, source_target_pairs={{0,8},{8,0},{16,24},{24,16},{1,9},{9,1},{17,25},{25,17},{2,10},{10... | collective-permute-start | bytes 12296 | tf_op jit(solution)/shard_map/ppermute | solution.py:276
  5.7 11.1 %collective-permute-start.4 = (f32[2,512]{1,0:T(2,128)S(1)}, f32[2,512]{1,0:T(2,128)S(1)}, u32[]{:S(2)}, u32[]{:S(2)}) collective-permute-start(f32[2,512]{1,0:T(2,128)S(1)} %add_convert_fusion), channel_id=1, source_target_pairs={{0,16},{8,24},{16,0},{24,8},{1,17},{9,25},{17,1},{25,9},{2,18},{10... | collective-permute-start | bytes 12296 | tf_op jit(solution)/shard_map/ppermute | solution.py:276
  7.2 9.6 %collective-permute-start.5 = (f32[2,512]{1,0:T(2,128)S(1)}, f32[2,512]{1,0:T(2,128)S(1)}, u32[]{:S(2)}, u32[]{:S(2)}) collective-permute-start(f32[2,512]{1,0:T(2,128)S(1)} %add_convert_fusion), channel_id=1, source_target_pairs={{0,24},{8,16},{16,8},{24,0},{1,25},{9,17},{17,9},{25,1},{2,26},{10... | collective-permute-start | bytes 12296 | tf_op jit(solution)/shard_map/ppermute | solution.py:276
  11.6 5.8 %collective-permute-start = (f32[48,512]{1,0:T(8,128)}, f32[48,512]{1,0:T(8,128)S(1)}, u32[]{:S(2)}, u32[]{:S(2)}) collective-permute-start(f32[48,512]{1,0:T(8,128)} %get-tuple-element.22), channel_id=1, source_target_pairs={{0,8},{8,0},{16,24},{24,16},{1,9},{9,1},{17,25},{25,17},{2,10},{10... | collective-permute-start | bytes 294920 | tf_op jit(solution)/shard_map/ppermute | solution.py:276
  13.6 5.1 %collective-permute-start.1 = (f32[48,512]{1,0:T(8,128)}, f32[48,512]{1,0:T(8,128)S(1)}, u32[]{:S(2)}, u32[]{:S(2)}) collective-permute-start(f32[48,512]{1,0:T(8,128)} %get-tuple-element.23), channel_id=1, source_target_pairs={{0,16},{8,24},{16,0},{24,8},{1,17},{9,25},{17,1},{25,9},{2,18},{10... | collective-permute-start | bytes 294920 | tf_op jit(solution)/shard_map/ppermute | solution.py:276
  15.6 1.1 copy-start.13
  16.8 5.5 %collective-permute-start.2 = (f32[48,512]{1,0:T(8,128)S(1)}, f32[48,512]{1,0:T(8,128)S(1)}, u32[]{:S(2)}, u32[]{:S(2)}) collective-permute-start(f32[48,512]{1,0:T(8,128)S(1)} %copy-done.13), channel_id=1, source_target_pairs={{0,24},{8,16},{16,8},{24,0},{1,25},{9,17},{17,9},{25,1},{2,26},{10... | collective-permute-start | bytes 294920 | tf_op jit(solution)/shard_map/ppermute | solution.py:276
  17.4 4.9 %copy-start.1 = (f32[48,512]{1,0:T(8,128)}, f32[48,512]{1,0:T(8,128)S(1)}, u32[]{:S(2)}) copy-start(f32[48,512]{1,0:T(8,128)S(1)} %collective-permute-done.refs_1_) | copy-start | bytes 294916
  18.6 3.7 %copy-start.2 = (f32[48,512]{1,0:T(8,128)}, f32[48,512]{1,0:T(8,128)S(1)}, u32[]{:S(2)}) copy-start(f32[48,512]{1,0:T(8,128)S(1)} %collective-permute-done.1.refs_2_) | copy-start | bytes 294916
  22.3 0.6 copy-start.3
  41.2 4.8 %collective-permute-start.6 = (f32[48,512]{1,0:T(8,128)}, f32[48,512]{1,0:T(8,128)S(1)}, u32[]{:S(2)}, u32[]{:S(2)}) collective-permute-start(f32[48,512]{1,0:T(8,128)} %get-tuple-element.26), channel_id=1, source_target_pairs={{0,8},{8,0},{16,24},{24,16},{1,9},{9,1},{17,25},{25,17},{2,10},{10... | collective-permute-start | bytes 294920 | tf_op jit(solution)/shard_map/ppermute | solution.py:276
  41.7 4.8 %collective-permute-start.7 = (f32[48,512]{1,0:T(8,128)}, f32[48,512]{1,0:T(8,128)S(1)}, u32[]{:S(2)}, u32[]{:S(2)}) collective-permute-start(f32[48,512]{1,0:T(8,128)} %get-tuple-element.27), channel_id=1, source_target_pairs={{0,16},{8,24},{16,0},{24,8},{1,17},{9,25},{17,1},{25,9},{2,18},{10... | collective-permute-start | bytes 294920 | tf_op jit(solution)/shard_map/ppermute | solution.py:276
  41.8 5.8 %collective-permute-start.8 = (f32[48,512]{1,0:T(8,128)}, f32[48,512]{1,0:T(8,128)S(1)}, u32[]{:S(2)}, u32[]{:S(2)}) collective-permute-start(f32[48,512]{1,0:T(8,128)} %get-tuple-element.28), channel_id=1, source_target_pairs={{0,24},{8,16},{16,8},{24,0},{1,25},{9,17},{17,9},{25,1},{2,26},{10... | collective-permute-start | bytes 294920 | tf_op jit(solution)/shard_map/ppermute | solution.py:276
  46.0 1.6 %copy-start.8 = (f32[48,512]{1,0:T(8,128)}, f32[48,512]{1,0:T(8,128)S(1)}, u32[]{:S(2)}) copy-start(f32[48,512]{1,0:T(8,128)S(1)} %collective-permute-done.6.refs_1_) | copy-start | bytes 294916
  46.6 1.0 copy-start.10
  47.6 0.6 copy-start.12
  51.7 4.8 %collective-permute-start.10 = (f32[48,512]{1,0:T(8,128)}, f32[48,512]{1,0:T(8,128)S(1)}, u32[]{:S(2)}, u32[]{:S(2)}) collective-permute-start(f32[48,512]{1,0:T(8,128)} %get-tuple-element.31), channel_id=1, source_target_pairs={{0,16},{8,24},{16,0},{24,8},{1,17},{9,25},{17,1},{25,9},{2,18},{10... | collective-permute-start | bytes 294920 | tf_op jit(solution)/shard_map/ppermute | solution.py:276
  53.5 5.7 %collective-permute-start.11 = (f32[48,512]{1,0:T(8,128)}, f32[48,512]{1,0:T(8,128)S(1)}, u32[]{:S(2)}, u32[]{:S(2)}) collective-permute-start(f32[48,512]{1,0:T(8,128)} %get-tuple-element.32), channel_id=1, source_target_pairs={{0,24},{8,16},{16,8},{24,0},{1,25},{9,17},{17,9},{25,1},{2,26},{10... | collective-permute-start | bytes 294920 | tf_op jit(solution)/shard_map/ppermute | solution.py:276
  55.0 4.8 %collective-permute-start.9 = (f32[48,512]{1,0:T(8,128)}, f32[48,512]{1,0:T(8,128)S(1)}, u32[]{:S(2)}, u32[]{:S(2)}) collective-permute-start(f32[48,512]{1,0:T(8,128)} %get-tuple-element.30), channel_id=1, source_target_pairs={{0,8},{8,0},{16,24},{24,16},{1,9},{9,1},{17,25},{25,17},{2,10},{10... | collective-permute-start | bytes 294920 | tf_op jit(solution)/shard_map/ppermute | solution.py:276
  56.5 3.3 %copy-start.4 = (f32[48,512]{1,0:T(8,128)}, f32[48,512]{1,0:T(8,128)S(1)}, u32[]{:S(2)}) copy-start(f32[48,512]{1,0:T(8,128)S(1)} %collective-permute-done.10.refs_2_) | copy-start | bytes 294916
  59.3 0.6 copy-start.5
  59.8 0.6 copy-start.6
  78.7 4.8 %collective-permute-start.12 = (f32[48,512]{1,0:T(8,128)}, f32[48,512]{1,0:T(8,128)S(1)}, u32[]{:S(2)}, u32[]{:S(2)}) collective-permute-start(f32[48,512]{1,0:T(8,128)} %get-tuple-element.34), channel_id=1, source_target_pairs={{0,8},{8,0},{16,24},{24,16},{1,9},{9,1},{17,25},{25,17},{2,10},{10... | collective-permute-start | bytes 294920 | tf_op jit(solution)/shard_map/ppermute | solution.py:276
  79.8 4.8 %collective-permute-start.13 = (f32[48,512]{1,0:T(8,128)}, f32[48,512]{1,0:T(8,128)S(1)}, u32[]{:S(2)}, u32[]{:S(2)}) collective-permute-start(f32[48,512]{1,0:T(8,128)} %get-tuple-element.35), channel_id=1, source_target_pairs={{0,16},{8,24},{16,0},{24,8},{1,17},{9,25},{17,1},{25,9},{2,18},{10... | collective-permute-start | bytes 294920 | tf_op jit(solution)/shard_map/ppermute | solution.py:276
  81.3 5.7 %collective-permute-start.14 = (f32[48,512]{1,0:T(8,128)}, f32[48,512]{1,0:T(8,128)S(1)}, u32[]{:S(2)}, u32[]{:S(2)}) collective-permute-start(f32[48,512]{1,0:T(8,128)} %get-tuple-element.36), channel_id=1, source_target_pairs={{0,24},{8,16},{16,8},{24,0},{1,25},{9,17},{17,9},{25,1},{2,26},{10... | collective-permute-start | bytes 294920 | tf_op jit(solution)/shard_map/ppermute | solution.py:276
  83.6 3.5 %copy-start.7 = (f32[48,512]{1,0:T(8,128)}, f32[48,512]{1,0:T(8,128)S(1)}, u32[]{:S(2)}) copy-start(f32[48,512]{1,0:T(8,128)S(1)} %collective-permute-done.12.refs_1_) | copy-start | bytes 294916
  84.6 2.4 %copy-start.9 = (f32[48,512]{1,0:T(8,128)}, f32[48,512]{1,0:T(8,128)S(1)}, u32[]{:S(2)}) copy-start(f32[48,512]{1,0:T(8,128)S(1)} %collective-permute-done.13.refs_2_) | copy-start | bytes 294916
  87.0 0.6 copy-start.11
  90.5 11.7 %all-to-all-start = ((bf16[8,64,128]{2,1,0:T(8,128)(2,1)}), bf16[8,64,128]{2,1,0:T(8,128)(2,1)S(1)}, u32[]{:S(2)}, u32[]{:S(2)}) async-start(bf16[8,64,128]{2,1,0:T(8,128)(2,1)} %bitcast.22), calls=%async_computation | async-start | bytes 262144 | tf_op jit(solution)/shard_map/all_to_all | solution.py:335

commit v2 on v1

v2 whole, which is shorter than its diff:
```python
import functools

import jax
import jax.numpy as jnp
import ml_dtypes
import numpy as np
from jax import lax
from jax.experimental import pallas as pl
from jax.experimental.pallas import tpu as pltpu
from jax.sharding import PartitionSpec as P

GY = 64
GX = 56
F32 = jnp.float32
BF16 = jnp.bfloat16
MIB = 1024 * 1024


def round_up(value, unit):
    return -(-value // unit) * unit


def halves(table):
    table = np.asarray(table, np.float32)
    high = table.astype(ml_dtypes.bfloat16)
    low = (table - high.astype(np.float32)).astype(ml_dtypes.bfloat16)
    return high, low


def stacked_table(table, axis):
    high, low = halves(table)
    return np.concatenate([high, high, low], axis=axis)


def folded(index, size):
    return np.where(index < size // 2, index, index - size)


def z_tables(size, devices, pad):
    depth = size // devices
    rows = 2 * pad
    freq = np.arange(size)
    ahead = np.zeros((devices, rows, 2 * size))
    back = np.zeros((2 * size, devices * rows))
    for d in range(devices):
        plane = d * depth + np.arange(depth)
        angle = 2 * np.pi * ((plane[:, None] * freq[None, :]) % size) / size
        c, s = np.cos(angle), np.sin(angle)
        ahead[d, :depth, :size], ahead[d, :depth, size:] = c, -s
        ahead[d, pad : pad + depth, :size], ahead[d, pad : pad + depth, size:] = s, c
        at = d * rows
        back[:size, at : at + depth], back[:size, at + pad : at + pad + depth] = c.T, s.T
        back[size:, at : at + depth], back[size:, at + pad : at + pad + depth] = -s.T, c.T
    return stacked_table(ahead, 2), stacked_table(back, 1)


def plane_tables(size):
    radius = size // 4
    count = 2 * radius + 1
    freq = np.arange(count) - radius
    angle = 2 * np.pi * ((freq[:, None] * np.arange(size)[None, :]) % size) / size
    c, s = np.cos(angle), np.sin(angle)
    ty = np.zeros((2 * GY, 256))
    ty[:count, :size], ty[:count, 128 : 128 + size] = c, s
    ty[GY : GY + count, :size], ty[GY : GY + count, 128 : 128 + size] = -s, c
    tyb = np.zeros((256, 2 * GY))
    tyb[:size, :count], tyb[:size, GY : GY + count] = c.T, -s.T
    tyb[128 : 128 + size, :count], tyb[128 : 128 + size, GY : GY + count] = s.T, c.T
    tx = np.zeros((2 * size, 2 * GX))
    tx[:size, :count], tx[:size, GX : GX + count] = c.T, -s.T
    tx[size:, :count], tx[size:, GX : GX + count] = s.T, c.T
    txb = np.zeros((2 * GX, 2 * size))
    txb[:count, :size], txb[:count, size:] = c, s
    txb[GX : GX + count, :size], txb[GX : GX + count, size:] = -s, c
    return stacked_table(ty, 0), stacked_table(tx, 1), stacked_table(txb, 1), stacked_table(tyb, 0)


def split(value):
    high = value.astype(BF16)
    low = (value - high.astype(F32)).astype(BF16)
    return high, low


def tripled(value, axis):
    high, low = split(value)
    return jnp.concatenate([high, low, high], axis=axis)


def dot(a, b, dims=((1,), (0,))):
    return lax.dot_general(a, b, (dims, ((), ())), preferred_element_type=F32)


SMEM = pl.BlockSpec(memory_space=pltpu.SMEM)
VMEM = pl.BlockSpec(memory_space=pltpu.VMEM)


def call(kernel, out_shape, scalars, arrays, scratch=(), limit=24):
    arrays = [pltpu.with_memory_space_constraint(value, pltpu.VMEM) if keep else value for value, keep in arrays]
    return pl.pallas_call(
        kernel,
        out_shape=out_shape,
        in_specs=[SMEM] * len(scalars) + [VMEM] * len(arrays),
        out_specs=[VMEM] * len(out_shape),
        scratch_shapes=list(scratch),
        compiler_params=pltpu.CompilerParams(vmem_limit_bytes=limit * MIB),
    )(*scalars, *arrays)


def position(col_row, size):
    place = col_row.astype(F32)
    kx = jnp.floor((place + 0.5) * (1.0 / size))
    ky = place - kx * size
    half = float(size // 2)
    return jnp.where(kx < half, kx, kx - size), jnp.where(ky < half, ky, ky - size)


def sphere(col_row, size):
    cols = col_row.shape[1]
    radius = size // 4
    gx, gy = position(col_row, size)
    index = lax.broadcasted_iota(jnp.int32, (size, cols), 0)
    freq = jnp.where(index < size // 2, index, index - size).astype(F32)
    radius2 = (gx * gx + gy * gy) + freq * freq
    return radius2 <= float(radius * radius), radius2 * (2.0 / (radius * radius))


def to_planes(me, parts, table_ref, outs, step):
    value = tripled(jnp.concatenate(parts, axis=0), 0)
    table = jnp.concatenate([table_ref[step(me, k)] for k in range(len(outs))], axis=0)
    total = dot(table, value)
    rows = table_ref.shape[1]
    for k in range(len(outs)):
        outs[k][:rows] = total[k * rows : (k + 1) * rows]


def from_planes(me, planes, table_ref, held, step, size):
    rows = planes[0].shape[0]
    third = rows * len(planes)
    for k in range(len(planes)):
        high, low = split(planes[k][...])
        at = step(me, k) * rows
        for j, value in enumerate((high, low, high)):
            held[pl.ds(pl.multiple_of(j * third + at, 16), rows), :] = value
    total = dot(table_ref[...], held[...])
    return total[:size], total[size:]


def first_kernel(devices, step, size, me_ref, psi_ref, col_ref, ahead_ref, *outs):
    inside, _ = sphere(col_ref[...], size)
    parts = [jnp.where(inside, psi_ref[p], 0.0) for p in range(2)]
    to_planes(me_ref[0], parts, ahead_ref, outs, step)
    radius = size // 4
    gx, gy = position(col_ref[...], size)
    used = gx * gx + gy * gy <= float(radius * radius)
    rows = ahead_ref.shape[1]
    row = lax.broadcasted_iota(jnp.int32, (8, gx.shape[1]), 0)
    place = jnp.where(used, jnp.where(row == 0, gx, gy) + float(radius), -9.0)
    for k in range(devices):
        outs[k][rows:] = place


def middle_kernel(devices, step, size, me_ref, low_ref, up_ref, *refs):
    planes, refs = refs[:devices], refs[devices:]
    psi_ref, col_ref, ahead_ref, back_ref, first_ref = refs[:5]
    outs, held = refs[5 : 5 + devices], refs[5 + devices]
    center = (up_ref[0] + low_ref[0]) / 2.0
    half = (up_ref[0] - low_ref[0]) / 2.0
    inside, kinetic = sphere(col_ref[...], size)
    back = from_planes(me_ref[0], planes, back_ref, held, step, size)
    parts = []
    for p in range(2):
        value = jnp.where(inside, ((kinetic - center) * psi_ref[p] + back[p]) / half, 0.0)
        first_ref[p] = value
        parts.append(value)
    to_planes(me_ref[0], parts, ahead_ref, outs, step)


def last_kernel(devices, bands, step, band_step, size, me_ref, band_ref, low_ref, up_ref, *refs):
    planes, refs = refs[:devices], refs[devices:]
    psi_ref, first_ref, col_ref, back_ref, pick_ref, filtered_ref = refs[:6]
    outs, (held, packed) = refs[6 : 6 + bands], refs[6 + bands :]
    center = (up_ref[0] + low_ref[0]) / 2.0
    half = (up_ref[0] - low_ref[0]) / 2.0
    inside, kinetic = sphere(col_ref[...], size)
    back = from_planes(me_ref[0], planes, back_ref, held, step, size)
    total = None
    for p in range(2):
        value = 2.0 * ((kinetic - center) * first_ref[p] + back[p]) / half - psi_ref[p]
        value = jnp.where(inside, value, 0.0)
        filtered_ref[p] = value
        piece = dot(pick_ref[p], value.astype(BF16))
        total = piece if total is None else total + piece
    packed[...] = total.astype(BF16)
    rows = packed.shape[0] // bands
    for k in range(bands):
        outs[k][...] = packed[pl.ds(pl.multiple_of(band_step(band_ref[0], k) * rows, 16), rows), :]


def gram_kernel(bands, band_step, band_ref, *refs):
    parts, sum_ref, held = refs[:bands], refs[bands], refs[bands + 1]
    rows, cols = parts[0].shape
    blocks = cols // 128
    for k in range(bands):
        at = pl.multiple_of(band_step(band_ref[0], k) * rows, 16)
        value = parts[k][...].astype(F32)
        for j in range(blocks):
            held[j, pl.ds(at, rows), :] = value[:, 128 * j : 128 * j + 128]
    lines = [[held[j, pl.ds(r, bands, stride=rows), :] for j in range(blocks)] for r in range(rows)]
    real = jnp.concatenate([v for r in range(rows // 2) for v in lines[r]], axis=1)
    imag = jnp.concatenate([v for r in range(rows // 2, rows) for v in lines[r]], axis=1)
    left = jnp.concatenate([real, imag], axis=1).astype(BF16)
    right = jnp.concatenate([imag, -real], axis=1).astype(BF16)
    sum_ref[0] = dot(left, left, ((1,), (1,)))
    sum_ref[1] = dot(left, right, ((1,), (1,)))


def slab_kernel(devices, size, depth, again, *refs):
    planes, refs = refs[:devices], refs[devices:]
    marks = planes
    if again:
        marks, refs = refs[:devices], refs[devices:]
    pot_ref, ty_ref, tx_ref, txb_ref, tyb_ref = refs[:5]
    outs = refs[5 : 5 + devices]
    y0_ref, y1_ref, q_ref, box_ref = refs[5 + devices :]
    pad = round_up(depth, 8)
    rows = 2 * pad
    cols = planes[0].shape[1]
    radius = size // 4
    tiles = -(-(2 * radius + 1) // 4)
    zero = jnp.zeros((), BF16)
    near = lax.broadcasted_iota(jnp.int32, (pad, 128), 1) < GY

    def one_hot(k, at, wide):
        gx = jnp.broadcast_to(marks[k][rows : rows + 1, at : at + wide], (16, wide)).astype(BF16)
        gy = jnp.broadcast_to(marks[k][rows + 1 : rows + 2, at : at + wide], (GY, wide))
        down = lax.broadcasted_iota(jnp.int32, (GY, wide), 0).astype(F32)
        hot = jnp.where(gy == down, 1.0, 0.0).astype(BF16)
        return gx, [hot[16 * i : 16 * i + 16] for i in range(GY // 16)]

    def expand(pieces, first, count):
        gx, hot = pieces
        tall = []
        for v in range(first, first + count):
            here = gx == float(v)
            tall += [jnp.where(here, piece, zero) for piece in hot]
        return jnp.concatenate(tall, axis=0)

    lhs = jnp.concatenate(split(jnp.concatenate([ref[:rows] for ref in planes], axis=1)), axis=0)
    sources = [one_hot(k, 0, cols) for k in range(devices)]
    whole = (
        jnp.concatenate([s[0] for s in sources], axis=1),
        [jnp.concatenate([s[1][i] for s in sources], axis=1) for i in range(GY // 16)],
    )
    for t in range(tiles):
        got = dot(lhs, expand(whole, 4 * t, 4), ((1,), (1,)))
        got = got[:rows] + got[rows:]
        mixed = []
        for u in range(2):
            re, im = got[:pad, 128 * u : 128 * u + 128], got[pad:, 128 * u : 128 * u + 128]
            mixed.append(jnp.where(near, re, pltpu.roll(im, GY, 1)))
            mixed.append(jnp.where(near, pltpu.roll(re, GY, 1), im))
        moved = dot(tripled(jnp.concatenate(mixed, axis=0), 1), ty_ref[...])
        y0_ref[4 * t * pad : 4 * (t + 1) * pad] = moved[:, :128]
        y1_ref[4 * t * pad : 4 * (t + 1) * pad] = moved[:, 128:]
    if tiles * 4 < GX:
        rest = jnp.zeros(((GX - 4 * tiles) * pad, 128), F32)
        y0_ref[4 * tiles * pad :] = rest
        y1_ref[4 * tiles * pad :] = rest
    if depth < pad:
        q_ref[depth * GX :] = jnp.zeros(((pad - depth) * GX, 128), F32)

    for z in range(0, depth, 2):
        sides = []
        for w in range(2):
            line = pl.ds(z + w, GX, stride=pad)
            sides.append(jnp.concatenate([y0_ref[line, :], y1_ref[line, :]], axis=0))
        field = dot(tx_ref[...], tripled(jnp.concatenate(sides, axis=1), 0))
        pot = jnp.concatenate([pot_ref[z], pot_ref[z + 1]], axis=1)
        field = field * jnp.concatenate([pot, pot], axis=0)
        back = dot(txb_ref[...], tripled(field, 0))
        turned = [
            jnp.concatenate([back[:GX, 128 * w : 128 * w + 128], back[GX:, 128 * w : 128 * w + 128]], axis=1)
            for w in range(2)
        ]
        q_ref[z * GX : (z + 2) * GX] = dot(tripled(jnp.concatenate(turned, axis=0), 1), tyb_ref[...])

    for t in range(2 * tiles):
        a = q_ref[pl.ds(2 * t, pad, stride=GX), :]
        b = q_ref[pl.ds(2 * t + 1, pad, stride=GX), :]
        re = jnp.where(near, a, pltpu.roll(b, GY, 1))
        im = jnp.where(near, pltpu.roll(a, GY, 1), b)
        box_ref[:, 128 * t : 128 * t + 128] = jnp.concatenate(split(jnp.concatenate([re, im], axis=0)), axis=0)

    box = box_ref[...]
    wide = min(256, cols)
    for k in range(devices):
        for at in range(0, cols, wide):
            got = dot(box, expand(one_hot(k, at, wide), 0, 4 * tiles))
            outs[k][:, at : at + wide] = got[:rows] + got[rows:]


def body(devices, bands, psi, col_map, potential, lower, upper):
    cols, size = psi.shape[2], psi.shape[3]
    radius = size // 4
    depth = size // devices
    pad = round_up(depth, 8)
    rows = 2 * pad
    me, band = lax.axis_index("grid"), lax.axis_index("band")
    me_arg = me.astype(jnp.int32).reshape(1)
    band_arg = band.astype(jnp.int32).reshape(1)
    if devices & (devices - 1) or bands & (bands - 1):
        raise ValueError("mesh size")

    def step(at, k):
        return at ^ k

    def exchange(values, axis="grid"):
        size = len(values)
        return [values[0]] + [
            lax.ppermute(values[k], axis, [(d, step(d, k)) for d in range(size)]) for k in range(1, size)
        ]

    def total(value, axis, size):
        bit = 1
        while bit < size:
            value = value + lax.ppermute(value, axis, [(d, d ^ bit) for d in range(size)])
            bit *= 2
        return value

    ahead, back = z_tables(size, devices, pad)
    tables = plane_tables(size)
    count = 2 * radius + 1
    slots = round_up(-(-count // bands), 8)
    pick = np.zeros((2, bands * 2 * slots, size), ml_dtypes.bfloat16)
    for j in range(count):
        at = (j % bands) * 2 * slots + j // bands
        pick[0, at, (j - radius) % size] = 1
        pick[1, at + slots, (j - radius) % size] = 1

    pot = (potential * (1.0 / float(size**3))).reshape(depth, size, size)
    pot = jnp.pad(pot, ((0, 0), (0, 0), (0, 128 - size)))
    psi_t = jnp.transpose(psi.reshape(2, cols, size), (0, 2, 1))
    col_row = col_map.reshape(1, cols)

    def vmem(shape, dtype=F32):
        return pltpu.VMEM(shape, dtype)

    marks = exchange(
        call(
            functools.partial(first_kernel, devices, step, size),
            [vmem((rows + 8, cols))] * devices,
            [me_arg],
            [(psi_t, False), (col_row, False), (ahead, False)],
        )
    )

    def slab(values, again):
        given = values + (marks if again else [])
        return call(
            functools.partial(slab_kernel, devices, size, depth, again),
            [vmem((rows, cols))] * devices,
            [],
            [(value, True) for value in given] + [(pot, False)] + [(table, False) for table in tables],
            [
                pltpu.VMEM((GX * pad, 128), F32),
                pltpu.VMEM((GX * pad, 128), F32),
                pltpu.VMEM((pad * GX, 128), F32),
                pltpu.VMEM((2 * rows, 256 * (-(-count // 4))), BF16),
            ],
        )

    held = pltpu.VMEM((3 * devices * rows, cols), BF16)
    planes = exchange(slab(marks, False))
    first, *sent = call(
        functools.partial(middle_kernel, devices, step, size),
        [vmem((2, size, cols))] + [vmem((rows, cols))] * devices,
        [me_arg, lower, upper],
        [(value, True) for value in planes] + [(psi_t, False), (col_row, False), (ahead, False), (back, False)],
        [held],
    )
    planes = exchange(slab(exchange(sent), True))
    filtered, *packed = call(
        functools.partial(last_kernel, devices, bands, step, step, size),
        [jax.ShapeDtypeStruct((2, size, cols), F32)] + [vmem((2 * slots, cols), BF16)] * bands,
        [me_arg, band_arg, lower, upper],
        [(value, True) for value in planes]
        + [(psi_t, False), (first, True), (col_row, False), (back, False), (pick, False)],
        [held, pltpu.VMEM((bands * 2 * slots, cols), BF16)],
    )
    (partial_sum,) = call(
        functools.partial(gram_kernel, bands, step),
        [vmem((2, bands, bands))],
        [band_arg],
        [(value, True) for value in exchange(packed, "band")],
        [pltpu.VMEM((cols // 128, bands * 2 * slots, 128), F32)],
    )
    sums = total(total(partial_sum, "grid", devices), "band", bands)
    own = bands // devices
    gram = lax.dynamic_slice(sums, (0, band, me * own), (2, 1, own)) / (4.0 * radius**3)
    return jnp.transpose(filtered, (0, 2, 1)).reshape(psi.shape), gram


def solution(mesh):
    return jax.shard_map(
        functools.partial(body, mesh.shape["grid"], mesh.shape["band"]),
        mesh=mesh,
        in_specs=(P(None, "band", "grid", None), P("grid"), P("grid", None), P(), P()),
        out_specs=(P(None, "band", "grid", None), P(None, "band", "grid")),
        check_vma=False,
    )
```

time: 143 us -> 107 us (0.75)
  blocking collectives: 38.6 us -> 0 us
  waiting for transfers between devices: 20.7 us -> 33.3 us
  local copies, waits for them, and re-layouts: 8.27 us -> 3.22 us
  Pallas kernels: 45.1 us -> 40.5 us
  starting transfers between devices: 23.4 us -> 25.8 us
  other arithmetic: 3.4 us -> 1.89 us
    psum x1 -> x0, blocking collectives: 38.6 us -> none  [body(): sums = lax.psum(jnp.stack([real_part, cross - cross.T]), ('grid', 'band'))]
    ppermute x15 -> x24, waiting for transfers between devices: 15.9 us -> 33.3 us  [the longest x19 19 us: exchange(): lax.ppermute(values[k], axis, [(d, step(d, k)) for d in range(size)])]
    ppermute x15 -> x24, starting transfers between devices: 18.5 us -> 25.8 us  [the longest x19 23.4 us: exchange(): lax.ppermute(values[k], axis, [(d, step(d, k)) for d in range(size)])]
    all_to_all x1 -> x0, starting transfers between devices: 4.88 us -> none  [body(): lax.all_to_all(packed.reshape(bands, part, 128), 'band', split_axis=0, co...]
    all_to_all x1 -> x0, waiting for transfers between devices: 4.8 us -> none  [body(): lax.all_to_all(packed.reshape(bands, part, 128), 'band', split_axis=0, co...]
    pallas_call x5 -> x6, Pallas kernels: 45.1 us -> 40.5 us  [call(): pl.pallas_call(kernel, out_shape=out_shape, in_specs=[SMEM] * len(scalars...]
    unnamed x30 -> x24, local copies, waits for them, and re-layouts: 6.52 us -> 2.67 us
    select_n x2 -> x0, other arithmetic: 2.05 us -> none  [the longest x1 1.27 us: body(): jnp.where(used, gy + radius, -9)]
  transfers between devices with their start and end apart: 16 -> 24, of which waited for: 11 -> 20; matrix products, arithmetic and copies ran while one was open for 4% -> 2% of each run, Pallas kernels for 2% -> 0%
where the time goes in v2:
time: 107 us
  Pallas kernels  40.5 us (38%)
  waiting for transfers between devices  33.3 us (31%)
  starting transfers between devices  25.8 us (24%)
  local copies, waits for them, and re-layouts  3.22 us (3%)
  between operations  2.12 us (2%)
  other arithmetic  1.89 us (2%)
    pallas_call x6, Pallas kernels, call(): pl.pallas_call(kernel, out_shape=out_shape, in_specs=[SMEM] * len(scalars...  40.5 us
    ppermute x19, starting transfers between devices, exchange(): lax.ppermute(values[k], axis, [(d, step(d, k)) for d in range(size)])  23.4 us
    ppermute x19, waiting for transfers between devices, exchange(): lax.ppermute(values[k], axis, [(d, step(d, k)) for d in range(size)])  19 us
    ppermute x5, waiting for transfers between devices, total(): lax.ppermute(value, axis, [(d, d ^ bit) for d in range(size)])  14.3 us
    unnamed x24, local copies, waits for them, and re-layouts  2.67 us
    ppermute x5, starting transfers between devices, total(): lax.ppermute(value, axis, [(d, d ^ bit) for d in range(size)])  2.43 us
  transfers between devices with their start and end apart: 24, of which 20 were waited for; matrix products, arithmetic and copies ran while one was open for 2% of the time, Pallas kernels for 0%

profile of v2, /device:TPU:0, one launch (start us, length us, event | category | flops | bytes accessed | tf_op | source)
XLA Modules:
  0.0 106.8 jit_solution(15026221498897430938)
XLA Ops:
  0.6 0.0 copy-start
  0.6 1.0 copy-done
  1.6 0.9 copy-done.3
  2.6 0.7 copy-done.10
  3.3 0.4 shard_map.131
  3.6 3.0 %collective-permute-start = (f32[56,512]{1,0:T(8,128)S(1)}, f32[56,512]{1,0:T(8,128)S(1)}, u32[]{:S(2)}, u32[]{:S(2)}) collective-permute-start(f32[56,512]{1,0:T(8,128)S(1)} %get-tuple-element.29), channel_id=1, source_target_pairs={{0,8},{8,0},{16,24},{24,16},{1,9},{9,1},{17,25},{25,17},{2,10},{10... | collective-permute-start | bytes 344072 | tf_op jit(solution)/shard_map/ppermute | solution.py:320
  6.7 1.5 %collective-permute-start.1 = (f32[56,512]{1,0:T(8,128)S(1)}, f32[56,512]{1,0:T(8,128)S(1)}, u32[]{:S(2)}, u32[]{:S(2)}) collective-permute-start(f32[56,512]{1,0:T(8,128)S(1)} %get-tuple-element.30), channel_id=1, source_target_pairs={{0,16},{8,24},{16,0},{24,8},{1,17},{9,25},{17,1},{25,9},{2,18},{10... | collective-permute-start | bytes 344072 | tf_op jit(solution)/shard_map/ppermute | solution.py:320
  8.2 0.0 collective-permute-start.2
  8.2 1.2 %broadcast_multiply_fusion = f32[24,9216]{1,0:T(8,128)S(1)} fusion(f32[24,9216]{1,0:T(8,128)} %param.14), kind=kLoop, calls=%fused_computation | loop fusion | flops 221184 | bytes 1769472 | tf_op jit(solution)/shard_map/mul | solution.py:340
  9.4 0.5 reshape.26
  9.9 0.0 copy-start.5
  9.9 0.0 copy-start.6
  9.9 0.0 copy-start.7
  10.0 0.0 copy-start.8
  10.0 0.1 pad.4.refs_4_.refs_8_
  10.1 0.0 copy-start.1
  10.1 0.0 copy-start.2
  10.1 0.0 copy-start.4
  10.1 0.0 copy-start.11
  10.1 0.1 collective-permute-done.refs_1_.refs_5_
  10.2 2.8 %collective-permute-done.1.refs_2_.refs_6_ = f32[56,512]{1,0:T(8,128)S(1)} collective-permute-done((f32[56,512]{1,0:T(8,128)S(1)}, f32[56,512]{1,0:T(8,128)S(1)}, u32[]{:S(2)}, u32[]{:S(2)}) %collective-permute-start.1) | collective-permute-done | bytes 114720 | tf_op jit(solution)/shard_map/ppermute | solution.py:320
  13.0 0.9 collective-permute-done.2.refs_3_.refs_7_
  13.9 18.9 %shard_map.132 = (f32[48,512]{1,0:T(8,128)S(1)}, f32[48,512]{1,0:T(8,128)S(1)}, f32[48,512]{1,0:T(8,128)S(1)}, f32[48,512]{1,0:T(8,128)S(1)}) custom-call(f32[56,512]{1,0:T(8,128)S(1)} %get-tuple-element.28.refs_0_.refs_4_, f32[56,512]{1,0:T(8,128)S(1)} %collective-permute-done.refs_1_.refs_5_, f32[56,512]{1,0:T(8,128)S(1)} %collective-permute-done.1.refs_2_.refs_6_, ...), custom_call_target="tpu_custom_call" | custom-call | tf_op jit(solution)/shard_map/pallas_call | solution.py:99
  32.8 1.1 %collective-permute-start.3 = (f32[48,512]{1,0:T(8,128)S(1)}, f32[48,512]{1,0:T(8,128)S(1)}, u32[]{:S(2)}, u32[]{:S(2)}) collective-permute-start(f32[48,512]{1,0:T(8,128)S(1)} %get-tuple-element.33), channel_id=1, source_target_pairs={{0,8},{8,0},{16,24},{24,16},{1,9},{9,1},{17,25},{25,17},{2,10},{10... | collective-permute-start | bytes 294920 | tf_op jit(solution)/shard_map/ppermute | solution.py:320
  33.9 0.8 collective-permute-start.4
  34.7 1.6 %collective-permute-start.5 = (f32[48,512]{1,0:T(8,128)S(1)}, f32[48,512]{1,0:T(8,128)S(1)}, u32[]{:S(2)}, u32[]{:S(2)}) collective-permute-start(f32[48,512]{1,0:T(8,128)S(1)} %get-tuple-element.35), channel_id=1, source_target_pairs={{0,24},{8,16},{16,8},{24,0},{1,25},{9,17},{17,9},{25,1},{2,26},{10... | collective-permute-start | bytes 294920 | tf_op jit(solution)/shard_map/ppermute | solution.py:320
  37.6 0.8 collective-permute-done.3.refs_1_
  38.5 0.1 collective-permute-done.4.refs_2_
  38.6 1.7 %collective-permute-done.5.refs_3_ = f32[48,512]{1,0:T(8,128)S(1)} collective-permute-done((f32[48,512]{1,0:T(8,128)S(1)}, f32[48,512]{1,0:T(8,128)S(1)}, u32[]{:S(2)}, u32[]{:S(2)}) %collective-permute-start.5) | collective-permute-done | bytes 98336 | tf_op jit(solution)/shard_map/ppermute | solution.py:320
  40.3 0.7 shard_map.133
  41.0 1.5 %collective-permute-start.6 = (f32[48,512]{1,0:T(8,128)S(1)}, f32[48,512]{1,0:T(8,128)S(1)}, u32[]{:S(2)}, u32[]{:S(2)}) collective-permute-start(f32[48,512]{1,0:T(8,128)S(1)} %get-tuple-element.37), channel_id=1, source_target_pairs={{0,8},{8,0},{16,24},{24,16},{1,9},{9,1},{17,25},{25,17},{2,10},{10... | collective-permute-start | bytes 294920 | tf_op jit(solution)/shard_map/ppermute | solution.py:320
  42.6 0.7 collective-permute-start.7
  43.2 1.3 %collective-permute-start.8 = (f32[48,512]{1,0:T(8,128)S(1)}, f32[48,512]{1,0:T(8,128)S(1)}, u32[]{:S(2)}, u32[]{:S(2)}) collective-permute-start(f32[48,512]{1,0:T(8,128)S(1)} %get-tuple-element.39), channel_id=1, source_target_pairs={{0,24},{8,16},{16,8},{24,0},{1,25},{9,17},{17,9},{25,1},{2,26},{10... | collective-permute-start | bytes 294920 | tf_op jit(solution)/shard_map/ppermute | solution.py:320
  44.6 1.1 %collective-permute-done.6.refs_1_ = f32[48,512]{1,0:T(8,128)S(1)} collective-permute-done((f32[48,512]{1,0:T(8,128)S(1)}, f32[48,512]{1,0:T(8,128)S(1)}, u32[]{:S(2)}, u32[]{:S(2)}) %collective-permute-start.6) | collective-permute-done | bytes 98336 | tf_op jit(solution)/shard_map/ppermute | solution.py:320
  45.7 1.5 %collective-permute-done.7.refs_2_ = f32[48,512]{1,0:T(8,128)S(1)} collective-permute-done((f32[48,512]{1,0:T(8,128)S(1)}, f32[48,512]{1,0:T(8,128)S(1)}, u32[]{:S(2)}, u32[]{:S(2)}) %collective-permute-start.7) | collective-permute-done | bytes 98336 | tf_op jit(solution)/shard_map/ppermute | solution.py:320
  47.2 1.6 %collective-permute-done.8.refs_3_ = f32[48,512]{1,0:T(8,128)S(1)} collective-permute-done((f32[48,512]{1,0:T(8,128)S(1)}, f32[48,512]{1,0:T(8,128)S(1)}, u32[]{:S(2)}, u32[]{:S(2)}) %collective-permute-start.8) | collective-permute-done | bytes 98336 | tf_op jit(solution)/shard_map/ppermute | solution.py:320
  48.8 19.0 %shard_map.134 = (f32[48,512]{1,0:T(8,128)S(1)}, f32[48,512]{1,0:T(8,128)S(1)}, f32[48,512]{1,0:T(8,128)S(1)}, f32[48,512]{1,0:T(8,128)S(1)}) custom-call(f32[48,512]{1,0:T(8,128)S(1)} %get-tuple-element.36.refs_0_, f32[48,512]{1,0:T(8,128)S(1)} %collective-permute-done.6.refs_1_, f32[48,512]{1,0:T(8,128)S(1)} %collective-permute-done.7.refs_2_, ...), custom_call_target="tpu_custom_call" | custom-call | tf_op jit(solution)/shard_map/pallas_call | solution.py:99
  67.8 1.4 %collective-permute-start.10 = (f32[48,512]{1,0:T(8,128)S(1)}, f32[48,512]{1,0:T(8,128)S(1)}, u32[]{:S(2)}, u32[]{:S(2)}) collective-permute-start(f32[48,512]{1,0:T(8,128)S(1)} %get-tuple-element.42), channel_id=1, source_target_pairs={{0,16},{8,24},{16,0},{24,8},{1,17},{9,25},{17,1},{25,9},{2,18},{10... | collective-permute-start | bytes 294920 | tf_op jit(solution)/shard_map/ppermute | solution.py:320
  69.2 1.2 %collective-permute-start.11 = (f32[48,512]{1,0:T(8,128)S(1)}, f32[48,512]{1,0:T(8,128)S(1)}, u32[]{:S(2)}, u32[]{:S(2)}) collective-permute-start(f32[48,512]{1,0:T(8,128)S(1)} %get-tuple-element.43), channel_id=1, source_target_pairs={{0,24},{8,16},{16,8},{24,0},{1,25},{9,17},{17,9},{25,1},{2,26},{10... | collective-permute-start | bytes 294920 | tf_op jit(solution)/shard_map/ppermute | solution.py:320
  70.4 1.0 collective-permute-start.9
  71.3 1.1 %collective-permute-done.10.refs_2_ = f32[48,512]{1,0:T(8,128)S(1)} collective-permute-done((f32[48,512]{1,0:T(8,128)S(1)}, f32[48,512]{1,0:T(8,128)S(1)}, u32[]{:S(2)}, u32[]{:S(2)}) %collective-permute-start.10) | collective-permute-done | bytes 98336 | tf_op jit(solution)/shard_map/ppermute | solution.py:320
  72.5 2.2 %collective-permute-done.11.refs_3_ = f32[48,512]{1,0:T(8,128)S(1)} collective-permute-done((f32[48,512]{1,0:T(8,128)S(1)}, f32[48,512]{1,0:T(8,128)S(1)}, u32[]{:S(2)}, u32[]{:S(2)}) %collective-permute-start.11) | collective-permute-done | bytes 98336 | tf_op jit(solution)/shard_map/ppermute | solution.py:320
  74.7 0.3 collective-permute-done.9.refs_1_
  75.0 1.2 %shard_map.135 = (f32[2,96,512]{2,1,0:T(8,128)}, bf16[16,512]{1,0:T(8,128)(2,1)S(1)}, bf16[16,512]{1,0:T(8,128)(2,1)S(1)}, bf16[16,512]{1,0:T(8,128)(2,1)S(1)}, ...) custom-call(s32[1]{0:T(128)} %bitcast.me_ref, ...), custom_call_target="tpu_custom_call" | custom-call | tf_op jit(solution)/shard_map/pallas_call | solution.py:99
  76.1 0.0 collective-permute-start.12
  76.2 1.6 %collective-permute-start.13 = (bf16[16,512]{1,0:T(8,128)(2,1)S(1)}, bf16[16,512]{1,0:T(8,128)(2,1)S(1)}, u32[]{:S(2)}, u32[]{:S(2)}) collective-permute-start(bf16[16,512]{1,0:T(8,128)(2,1)S(1)} %get-tuple-element.48), channel_id=1, source_target_pairs={{0,2},{1,3},{2,0},{3,1},{4,6},{5,7},{6,4},{7,5},{8,10},{9,11},{10,... | collective-permute-start | bytes 49160 | tf_op jit(solution)/shard_map/ppermute | solution.py:320
  77.7 0.3 collective-permute-start.14
  78.0 2.6 %collective-permute-start.15 = (bf16[16,512]{1,0:T(8,128)(2,1)S(1)}, bf16[16,512]{1,0:T(8,128)(2,1)S(1)}, u32[]{:S(2)}, u32[]{:S(2)}) collective-permute-start(bf16[16,512]{1,0:T(8,128)(2,1)S(1)} %get-tuple-element.50), channel_id=1, source_target_pairs={{0,4},{1,5},{2,6},{3,7},{4,0},{5,1},{6,2},{7,3},{8,12},{9,13},{10,... | collective-permute-start | bytes 49160 | tf_op jit(solution)/shard_map/ppermute | solution.py:320
  80.6 3.5 %collective-permute-start.17 = (bf16[16,512]{1,0:T(8,128)(2,1)S(1)}, bf16[16,512]{1,0:T(8,128)(2,1)S(1)}, u32[]{:S(2)}, u32[]{:S(2)}) collective-permute-start(bf16[16,512]{1,0:T(8,128)(2,1)S(1)} %get-tuple-element.52), channel_id=1, source_target_pairs={{0,6},{1,7},{2,4},{3,5},{4,2},{5,3},{6,0},{7,1},{8,14},{9,15},{10,... | collective-permute-start | bytes 49160 | tf_op jit(solution)/shard_map/ppermute | solution.py:320
  84.2 0.0 collective-permute-done.13.refs_2_
  84.2 0.2 collective-permute-start.18
  84.4 0.3 collective-permute-done.16.refs_5_
  84.7 1.5 %collective-permute-done.17.refs_6_ = bf16[16,512]{1,0:T(8,128)(2,1)S(1)} collective-permute-done((bf16[16,512]{1,0:T(8,128)(2,1)S(1)}, bf16[16,512]{1,0:T(8,128)(2,1)S(1)}, u32[]{:S(2)}, u32[]{:S(2)}) %collective-permute-start.17) | collective-permute-done | bytes 16416 | tf_op jit(solution)/shard_map/ppermute | solution.py:320
  86.2 2.9 %collective-permute-done.18.refs_7_ = bf16[16,512]{1,0:T(8,128)(2,1)S(1)} collective-permute-done((bf16[16,512]{1,0:T(8,128)(2,1)S(1)}, bf16[16,512]{1,0:T(8,128)(2,1)S(1)}, u32[]{:S(2)}, u32[]{:S(2)}) %collective-permute-start.18) | collective-permute-done | bytes 16416 | tf_op jit(solution)/shard_map/ppermute | solution.py:320
  89.1 0.3 shard_map.136
  89.5 1.1 %collective-permute-start.19 = (f32[2,8,8]{2,1,0:T(8,128)S(1)}, f32[2,8,8]{2,1,0:T(8,128)S(1)}, u32[]{:S(2)}, u32[]{:S(2)}) collective-permute-start(f32[2,8,8]{2,1,0:T(8,128)S(1)} %shard_map.136), channel_id=1, source_target_pairs={{0,8},{8,0},{16,24},{24,16},{1,9},{9,1},{17,25},{25,17},{2,10},{10... | collective-permute-start | bytes 1544 | tf_op jit(solution)/shard_map/ppermute | solution.py:326
  90.5 2.6 %collective-permute-done.19 = f32[2,8,8]{2,1,0:T(8,128)S(1)} collective-permute-done((f32[2,8,8]{2,1,0:T(8,128)S(1)}, f32[2,8,8]{2,1,0:T(8,128)S(1)}, u32[]{:S(2)}, u32[]{:S(2)}) %collective-permute-start.19) | collective-permute-done | bytes 544 | tf_op jit(solution)/shard_map/ppermute | solution.py:326
  93.1 1.3 %collective-permute-start.20 = (f32[2,8,8]{2,1,0:T(8,128)S(1)}, f32[2,8,8]{2,1,0:T(8,128)S(1)}, u32[]{:S(2)}, u32[]{:S(2)}) collective-permute-start(f32[2,8,8]{2,1,0:T(8,128)S(1)} %add.23), channel_id=1, source_target_pairs={{0,16},{8,24},{16,0},{24,8},{1,17},{9,25},{17,1},{25,9},{2,18},{10... | collective-permute-start | bytes 1544 | tf_op jit(solution)/shard_map/ppermute | solution.py:326
  94.5 2.3 %collective-permute-done.20 = f32[2,8,8]{2,1,0:T(8,128)S(1)} collective-permute-done((f32[2,8,8]{2,1,0:T(8,128)S(1)}, f32[2,8,8]{2,1,0:T(8,128)S(1)}, u32[]{:S(2)}, u32[]{:S(2)}) %collective-permute-start.20) | collective-permute-done | bytes 544 | tf_op jit(solution)/shard_map/ppermute | solution.py:326
  96.8 0.0 collective-permute-start.21
  96.8 1.2 %collective-permute-done.21 = f32[2,8,8]{2,1,0:T(8,128)S(1)} collective-permute-done((f32[2,8,8]{2,1,0:T(8,128)S(1)}, f32[2,8,8]{2,1,0:T(8,128)S(1)}, u32[]{:S(2)}, u32[]{:S(2)}) %collective-permute-start.21) | collective-permute-done | bytes 544 | tf_op jit(solution)/shard_map/ppermute | solution.py:326
  98.0 3.6 %collective-permute-done.22 = f32[2,8,8]{2,1,0:T(8,128)S(1)} collective-permute-done((f32[2,8,8]{2,1,0:T(8,128)S(1)}, f32[2,8,8]{2,1,0:T(8,128)S(1)}, u32[]{:S(2)}, u32[]{:S(2)}) %collective-permute-start.22) | collective-permute-done | bytes 544 | tf_op jit(solution)/shard_map/ppermute | solution.py:326
  101.6 4.5 %collective-permute-done.23 = f32[2,8,8]{2,1,0:T(8,128)S(1)} collective-permute-done((f32[2,8,8]{2,1,0:T(8,128)S(1)}, f32[2,8,8]{2,1,0:T(8,128)S(1)}, u32[]{:S(2)}, u32[]{:S(2)}) %collective-permute-start.23) | collective-permute-done | bytes 544 | tf_op jit(solution)/shard_map/ppermute | solution.py:326
  106.2 0.6 fusion
  (22 shorter events, 0.1 us)
Async XLA Ops:
  0.6 1.0 copy-start
  1.6 0.9 copy-start.3
  2.6 0.7 copy-start.10
  3.6 6.6 %collective-permute-start = (f32[56,512]{1,0:T(8,128)S(1)}, f32[56,512]{1,0:T(8,128)S(1)}, u32[]{:S(2)}, u32[]{:S(2)}) collective-permute-start(f32[56,512]{1,0:T(8,128)S(1)} %get-tuple-element.29), channel_id=1, source_target_pairs={{0,8},{8,0},{16,24},{24,16},{1,9},{9,1},{17,25},{25,17},{2,10},{10... | collective-permute-start | bytes 344072 | tf_op jit(solution)/shard_map/ppermute | solution.py:320
  6.7 6.4 %collective-permute-start.1 = (f32[56,512]{1,0:T(8,128)S(1)}, f32[56,512]{1,0:T(8,128)S(1)}, u32[]{:S(2)}, u32[]{:S(2)}) collective-permute-start(f32[56,512]{1,0:T(8,128)S(1)} %get-tuple-element.30), channel_id=1, source_target_pairs={{0,16},{8,24},{16,0},{24,8},{1,17},{9,25},{17,1},{25,9},{2,18},{10... | collective-permute-start | bytes 344072 | tf_op jit(solution)/shard_map/ppermute | solution.py:320
  8.2 5.7 %collective-permute-start.2 = (f32[56,512]{1,0:T(8,128)S(1)}, f32[56,512]{1,0:T(8,128)S(1)}, u32[]{:S(2)}, u32[]{:S(2)}) collective-permute-start(f32[56,512]{1,0:T(8,128)S(1)} %get-tuple-element.31), channel_id=1, source_target_pairs={{0,24},{8,16},{16,8},{24,0},{1,25},{9,17},{17,9},{25,1},{2,26},{10... | collective-permute-start | bytes 344072 | tf_op jit(solution)/shard_map/ppermute | solution.py:320
  9.9 4.0 %copy-start.5 = (bf16[384,256]{1,0:T(8,128)(2,1)S(1)}, bf16[384,256]{1,0:T(8,128)(2,1)}, u32[]{:S(2)}) copy-start(bf16[384,256]{1,0:T(8,128)(2,1)} %constant.36.clone.refs_5_.refs_9_) | copy-start | bytes 589828
  9.9 4.0 %copy-start.6 = (bf16[768,128]{1,0:T(8,128)(2,1)S(1)}, bf16[768,128]{1,0:T(8,128)(2,1)}, u32[]{:S(2)}) copy-start(bf16[768,128]{1,0:T(8,128)(2,1)} %constant.39.clone.refs_8_.refs_12_) | copy-start | bytes 589828
  9.9 4.0 %copy-start.7 = (bf16[192,336]{1,0:T(8,128)(2,1)S(1)}, bf16[192,336]{1,0:T(8,128)(2,1)}, u32[]{:S(2)}) copy-start(bf16[192,336]{1,0:T(8,128)(2,1)} %constant.37.clone.refs_6_.refs_10_) | copy-start | bytes 387076
  10.0 4.0 %copy-start.8 = (bf16[112,576]{1,0:T(8,128)(2,1)S(1)}, bf16[112,576]{1,0:T(8,128)(2,1)}, u32[]{:S(2)}) copy-start(bf16[112,576]{1,0:T(8,128)(2,1)} %constant.38.clone.refs_7_.refs_11_) | copy-start | bytes 387076
  10.1 30.2 %copy-start.1 = (f32[2,1,512,96]{2,3,1,0:T(8,128)S(1)}, f32[2,1,512,96]{2,3,1,0:T(8,128)}, u32[]{:S(2)}) copy-start(f32[2,1,512,96]{2,3,1,0:T(8,128)} %param.12) | copy-start | bytes 1179652
  10.1 30.2 %copy-start.2 = (bf16[192,576]{1,0:T(8,128)(2,1)S(1)}, bf16[192,576]{1,0:T(8,128)(2,1)}, u32[]{:S(2)}) copy-start(bf16[192,576]{1,0:T(8,128)(2,1)} %constant.40.clone.refs_7_) | copy-start | bytes 663556
  10.1 30.2 %copy-start.4 = (bf16[4,48,576]{2,1,0:T(8,128)(2,1)S(1)}, bf16[4,48,576]{2,1,0:T(8,128)(2,1)}, u32[]{:S(2)}) copy-start(bf16[4,48,576]{2,1,0:T(8,128)(2,1)} %constant.35.clone.ahead_ref.refs_6_) | copy-start | bytes 663556
  10.1 30.2 %copy-start.11 = (s32[512]{0:T(512)S(1)}, s32[512]{0:T(512)}, u32[]{:S(2)}) copy-start(s32[512]{0:T(512)} %param.13) | copy-start | bytes 6148
  32.8 5.7 %collective-permute-start.3 = (f32[48,512]{1,0:T(8,128)S(1)}, f32[48,512]{1,0:T(8,128)S(1)}, u32[]{:S(2)}, u32[]{:S(2)}) collective-permute-start(f32[48,512]{1,0:T(8,128)S(1)} %get-tuple-element.33), channel_id=1, source_target_pairs={{0,8},{8,0},{16,24},{24,16},{1,9},{9,1},{17,25},{25,17},{2,10},{10... | collective-permute-start | bytes 294920 | tf_op jit(solution)/shard_map/ppermute | solution.py:320
  33.9 4.7 %collective-permute-start.4 = (f32[48,512]{1,0:T(8,128)S(1)}, f32[48,512]{1,0:T(8,128)S(1)}, u32[]{:S(2)}, u32[]{:S(2)}) collective-permute-start(f32[48,512]{1,0:T(8,128)S(1)} %get-tuple-element.34), channel_id=1, source_target_pairs={{0,16},{8,24},{16,0},{24,8},{1,17},{9,25},{17,1},{25,9},{2,18},{10... | collective-permute-start | bytes 294920 | tf_op jit(solution)/shard_map/ppermute | solution.py:320
  34.7 5.5 %collective-permute-start.5 = (f32[48,512]{1,0:T(8,128)S(1)}, f32[48,512]{1,0:T(8,128)S(1)}, u32[]{:S(2)}, u32[]{:S(2)}) collective-permute-start(f32[48,512]{1,0:T(8,128)S(1)} %get-tuple-element.35), channel_id=1, source_target_pairs={{0,24},{8,16},{16,8},{24,0},{1,25},{9,17},{17,9},{25,1},{2,26},{10... | collective-permute-start | bytes 294920 | tf_op jit(solution)/shard_map/ppermute | solution.py:320
  41.0 4.7 %collective-permute-start.6 = (f32[48,512]{1,0:T(8,128)S(1)}, f32[48,512]{1,0:T(8,128)S(1)}, u32[]{:S(2)}, u32[]{:S(2)}) collective-permute-start(f32[48,512]{1,0:T(8,128)S(1)} %get-tuple-element.37), channel_id=1, source_target_pairs={{0,8},{8,0},{16,24},{24,16},{1,9},{9,1},{17,25},{25,17},{2,10},{10... | collective-permute-start | bytes 294920 | tf_op jit(solution)/shard_map/ppermute | solution.py:320
  42.6 4.6 %collective-permute-start.7 = (f32[48,512]{1,0:T(8,128)S(1)}, f32[48,512]{1,0:T(8,128)S(1)}, u32[]{:S(2)}, u32[]{:S(2)}) collective-permute-start(f32[48,512]{1,0:T(8,128)S(1)} %get-tuple-element.38), channel_id=1, source_target_pairs={{0,16},{8,24},{16,0},{24,8},{1,17},{9,25},{17,1},{25,9},{2,18},{10... | collective-permute-start | bytes 294920 | tf_op jit(solution)/shard_map/ppermute | solution.py:320
  43.2 5.5 %collective-permute-start.8 = (f32[48,512]{1,0:T(8,128)S(1)}, f32[48,512]{1,0:T(8,128)S(1)}, u32[]{:S(2)}, u32[]{:S(2)}) collective-permute-start(f32[48,512]{1,0:T(8,128)S(1)} %get-tuple-element.39), channel_id=1, source_target_pairs={{0,24},{8,16},{16,8},{24,0},{1,25},{9,17},{17,9},{25,1},{2,26},{10... | collective-permute-start | bytes 294920 | tf_op jit(solution)/shard_map/ppermute | solution.py:320
  48.8 26.2 %copy-start.9 = (bf16[2,128,96]{2,1,0:T(8,128)(2,1)S(1)}, bf16[2,128,96]{2,1,0:T(8,128)(2,1)}, u32[]{:S(2)}) copy-start(bf16[2,128,96]{2,1,0:T(8,128)(2,1)} %constant.41.clone.refs_8_) | copy-start | bytes 147460
  67.8 4.7 %collective-permute-start.10 = (f32[48,512]{1,0:T(8,128)S(1)}, f32[48,512]{1,0:T(8,128)S(1)}, u32[]{:S(2)}, u32[]{:S(2)}) collective-permute-start(f32[48,512]{1,0:T(8,128)S(1)} %get-tuple-element.42), channel_id=1, source_target_pairs={{0,16},{8,24},{16,0},{24,8},{1,17},{9,25},{17,1},{25,9},{2,18},{10... | collective-permute-start | bytes 294920 | tf_op jit(solution)/shard_map/ppermute | solution.py:320
  69.2 5.5 %collective-permute-start.11 = (f32[48,512]{1,0:T(8,128)S(1)}, f32[48,512]{1,0:T(8,128)S(1)}, u32[]{:S(2)}, u32[]{:S(2)}) collective-permute-start(f32[48,512]{1,0:T(8,128)S(1)} %get-tuple-element.43), channel_id=1, source_target_pairs={{0,24},{8,16},{16,8},{24,0},{1,25},{9,17},{17,9},{25,1},{2,26},{10... | collective-permute-start | bytes 294920 | tf_op jit(solution)/shard_map/ppermute | solution.py:320
  70.4 4.6 %collective-permute-start.9 = (f32[48,512]{1,0:T(8,128)S(1)}, f32[48,512]{1,0:T(8,128)S(1)}, u32[]{:S(2)}, u32[]{:S(2)}) collective-permute-start(f32[48,512]{1,0:T(8,128)S(1)} %get-tuple-element.41), channel_id=1, source_target_pairs={{0,8},{8,0},{16,24},{24,16},{1,9},{9,1},{17,25},{25,17},{2,10},{10... | collective-permute-start | bytes 294920 | tf_op jit(solution)/shard_map/ppermute | solution.py:320
  76.1 4.5 %collective-permute-start.12 = (bf16[16,512]{1,0:T(8,128)(2,1)S(1)}, bf16[16,512]{1,0:T(8,128)(2,1)S(1)}, u32[]{:S(2)}, u32[]{:S(2)}) collective-permute-start(bf16[16,512]{1,0:T(8,128)(2,1)S(1)} %get-tuple-element.47), channel_id=1, source_target_pairs={{0,1},{1,0},{2,3},{3,2},{4,5},{5,4},{6,7},{7,6},{8,9},{9,8},{10,11... | collective-permute-start | bytes 49160 | tf_op jit(solution)/shard_map/ppermute | solution.py:320
  76.2 8.0 %collective-permute-start.13 = (bf16[16,512]{1,0:T(8,128)(2,1)S(1)}, bf16[16,512]{1,0:T(8,128)(2,1)S(1)}, u32[]{:S(2)}, u32[]{:S(2)}) collective-permute-start(bf16[16,512]{1,0:T(8,128)(2,1)S(1)} %get-tuple-element.48), channel_id=1, source_target_pairs={{0,2},{1,3},{2,0},{3,1},{4,6},{5,7},{6,4},{7,5},{8,10},{9,11},{10,... | collective-permute-start | bytes 49160 | tf_op jit(solution)/shard_map/ppermute | solution.py:320
  77.7 6.6 %collective-permute-start.14 = (bf16[16,512]{1,0:T(8,128)(2,1)S(1)}, bf16[16,512]{1,0:T(8,128)(2,1)S(1)}, u32[]{:S(2)}, u32[]{:S(2)}) collective-permute-start(bf16[16,512]{1,0:T(8,128)(2,1)S(1)} %get-tuple-element.49), channel_id=1, source_target_pairs={{0,3},{1,2},{2,1},{3,0},{4,7},{5,6},{6,5},{7,4},{8,11},{9,10},{10,... | collective-permute-start | bytes 49160 | tf_op jit(solution)/shard_map/ppermute | solution.py:320
  78.0 6.3 %collective-permute-start.15 = (bf16[16,512]{1,0:T(8,128)(2,1)S(1)}, bf16[16,512]{1,0:T(8,128)(2,1)S(1)}, u32[]{:S(2)}, u32[]{:S(2)}) collective-permute-start(bf16[16,512]{1,0:T(8,128)(2,1)S(1)} %get-tuple-element.50), channel_id=1, source_target_pairs={{0,4},{1,5},{2,6},{3,7},{4,0},{5,1},{6,2},{7,3},{8,12},{9,13},{10,... | collective-permute-start | bytes 49160 | tf_op jit(solution)/shard_map/ppermute | solution.py:320
  80.6 4.1 %collective-permute-start.16 = (bf16[16,512]{1,0:T(8,128)(2,1)S(1)}, bf16[16,512]{1,0:T(8,128)(2,1)S(1)}, u32[]{:S(2)}, u32[]{:S(2)}) collective-permute-start(bf16[16,512]{1,0:T(8,128)(2,1)S(1)} %get-tuple-element.51), channel_id=1, source_target_pairs={{0,5},{1,4},{2,7},{3,6},{4,1},{5,0},{6,3},{7,2},{8,13},{9,12},{10,... | collective-permute-start | bytes 49160 | tf_op jit(solution)/shard_map/ppermute | solution.py:320
  80.6 5.6 %collective-permute-start.17 = (bf16[16,512]{1,0:T(8,128)(2,1)S(1)}, bf16[16,512]{1,0:T(8,128)(2,1)S(1)}, u32[]{:S(2)}, u32[]{:S(2)}) collective-permute-start(bf16[16,512]{1,0:T(8,128)(2,1)S(1)} %get-tuple-element.52), channel_id=1, source_target_pairs={{0,6},{1,7},{2,4},{3,5},{4,2},{5,3},{6,0},{7,1},{8,14},{9,15},{10,... | collective-permute-start | bytes 49160 | tf_op jit(solution)/shard_map/ppermute | solution.py:320
  84.2 5.0 %collective-permute-start.18 = (bf16[16,512]{1,0:T(8,128)(2,1)S(1)}, bf16[16,512]{1,0:T(8,128)(2,1)S(1)}, u32[]{:S(2)}, u32[]{:S(2)}) collective-permute-start(bf16[16,512]{1,0:T(8,128)(2,1)S(1)} %get-tuple-element.53), channel_id=1, source_target_pairs={{0,7},{1,6},{2,5},{3,4},{4,3},{5,2},{6,1},{7,0},{8,15},{9,14},{10,... | collective-permute-start | bytes 49160 | tf_op jit(solution)/shard_map/ppermute | solution.py:320
  89.5 3.7 %collective-permute-start.19 = (f32[2,8,8]{2,1,0:T(8,128)S(1)}, f32[2,8,8]{2,1,0:T(8,128)S(1)}, u32[]{:S(2)}, u32[]{:S(2)}) collective-permute-start(f32[2,8,8]{2,1,0:T(8,128)S(1)} %shard_map.136), channel_id=1, source_target_pairs={{0,8},{8,0},{16,24},{24,16},{1,9},{9,1},{17,25},{25,17},{2,10},{10... | collective-permute-start | bytes 1544 | tf_op jit(solution)/shard_map/ppermute | solution.py:326
  93.1 3.7 %collective-permute-start.20 = (f32[2,8,8]{2,1,0:T(8,128)S(1)}, f32[2,8,8]{2,1,0:T(8,128)S(1)}, u32[]{:S(2)}, u32[]{:S(2)}) collective-permute-start(f32[2,8,8]{2,1,0:T(8,128)S(1)} %add.23), channel_id=1, source_target_pairs={{0,16},{8,24},{16,0},{24,8},{1,17},{9,25},{17,1},{25,9},{2,18},{10... | collective-permute-start | bytes 1544 | tf_op jit(solution)/shard_map/ppermute | solution.py:326
  96.8 1.2 %collective-permute-start.21 = (f32[2,8,8]{2,1,0:T(8,128)S(1)}, f32[2,8,8]{2,1,0:T(8,128)S(1)}, u32[]{:S(2)}, u32[]{:S(2)}) collective-permute-start(f32[2,8,8]{2,1,0:T(8,128)S(1)} %add.24), channel_id=1, source_target_pairs={{0,1},{1,0},{2,3},{3,2},{4,5},{5,4},{6,7},{7,6},{8,9},{9,8},{10,11... | collective-permute-start | bytes 1544 | tf_op jit(solution)/shard_map/ppermute | solution.py:326
  98.0 3.7 %collective-permute-start.22 = (f32[2,8,8]{2,1,0:T(8,128)S(1)}, f32[2,8,8]{2,1,0:T(8,128)S(1)}, u32[]{:S(2)}, u32[]{:S(2)}) collective-permute-start(f32[2,8,8]{2,1,0:T(8,128)S(1)} %add.25), channel_id=1, source_target_pairs={{0,2},{1,3},{2,0},{3,1},{4,6},{5,7},{6,4},{7,5},{8,10},{9,11},{10,... | collective-permute-start | bytes 1544 | tf_op jit(solution)/shard_map/ppermute | solution.py:326
  101.6 4.5 %collective-permute-start.23 = (f32[2,8,8]{2,1,0:T(8,128)S(1)}, f32[2,8,8]{2,1,0:T(8,128)S(1)}, u32[]{:S(2)}, u32[]{:S(2)}) collective-permute-start(f32[2,8,8]{2,1,0:T(8,128)S(1)} %add.26), channel_id=1, source_target_pairs={{0,4},{1,5},{2,6},{3,7},{4,0},{5,1},{6,2},{7,3},{8,12},{9,13},{10,... | collective-permute-start | bytes 1544 | tf_op jit(solution)/shard_map/ppermute | solution.py:326

commit v3 on v2

--- a/solution.py
+++ b/solution.py
@@ -75,6 +75,22 @@
     return stacked_table(ty, 0), stacked_table(tx, 1), stacked_table(txb, 1), stacked_table(tyb, 0)
 
 
+def packing(size):
+    radius = size // 4
+    widths = [int(np.sqrt(radius * radius - g * g)) for g in range(-radius, radius + 1)]
+    slots, free = [None] * len(widths), []
+    for i in sorted(range(len(widths)), key=lambda j: (-widths[j], j)):
+        span = 2 * widths[i] + 1
+        for s in range(len(free) + 1):
+            if s == len(free):
+                free.append(128)
+            if free[s] >= span:
+                slots[i] = (widths[i], s, 128 - free[s] + widths[i])
+                free[s] -= span
+                break
+    return slots, round_up(len(free), 2)
+
+
 def split(value):
     high = value.astype(BF16)
     low = (value - high.astype(F32)).astype(BF16)
@@ -154,7 +170,11 @@
     used = gx * gx + gy * gy <= float(radius * radius)
     rows = ahead_ref.shape[1]
     row = lax.broadcasted_iota(jnp.int32, (8, gx.shape[1]), 0)
-    place = jnp.where(used, jnp.where(row == 0, gx, gy) + float(radius), -9.0)
+    slot, lane = jnp.zeros(row.shape, F32), jnp.zeros(row.shape, F32)
+    for i, (_, s, middle) in enumerate(packing(size)[0]):
+        here = gx == float(i - radius)
+        slot, lane = jnp.where(here, float(s), slot), jnp.where(here, float(middle), lane)
+    place = jnp.where(used, jnp.where(row == 0, slot, lane + gy), -9.0)
     for k in range(devices):
         outs[k][rows:] = place
 
@@ -221,27 +241,30 @@
         marks, refs = refs[:devices], refs[devices:]
     pot_ref, ty_ref, tx_ref, txb_ref, tyb_ref = refs[:5]
     outs = refs[5 : 5 + devices]
-    y0_ref, y1_ref, q_ref, box_ref = refs[5 + devices :]
+    in_ref, y0_ref, y1_ref, back_ref, q_ref, box_ref = refs[5 + devices :]
     pad = round_up(depth, 8)
     rows = 2 * pad
     cols = planes[0].shape[1]
     radius = size // 4
-    tiles = -(-(2 * radius + 1) // 4)
+    places, slots = packing(size)
     zero = jnp.zeros((), BF16)
-    near = lax.broadcasted_iota(jnp.int32, (pad, 128), 1) < GY
+    lane = lax.broadcasted_iota(jnp.int32, (pad, 128), 1)
+
+    def between(first, last):
+        return (lane >= first) & (lane <= last)
 
     def one_hot(k, at, wide):
-        gx = jnp.broadcast_to(marks[k][rows : rows + 1, at : at + wide], (16, wide)).astype(BF16)
-        gy = jnp.broadcast_to(marks[k][rows + 1 : rows + 2, at : at + wide], (GY, wide))
-        down = lax.broadcasted_iota(jnp.int32, (GY, wide), 0).astype(F32)
-        hot = jnp.where(gy == down, 1.0, 0.0).astype(BF16)
-        return gx, [hot[16 * i : 16 * i + 16] for i in range(GY // 16)]
+        slot = jnp.broadcast_to(marks[k][rows : rows + 1, at : at + wide], (16, wide)).astype(BF16)
+        spot = jnp.broadcast_to(marks[k][rows + 1 : rows + 2, at : at + wide], (128, wide))
+        down = lax.broadcasted_iota(jnp.int32, (128, wide), 0).astype(F32)
+        hot = jnp.where(spot == down, 1.0, 0.0).astype(BF16)
+        return slot, [hot[16 * i : 16 * i + 16] for i in range(8)]
 
     def expand(pieces, first, count):
-        gx, hot = pieces
+        slot, hot = pieces
         tall = []
         for v in range(first, first + count):
-            here = gx == float(v)
+            here = slot == float(v)
             tall += [jnp.where(here, piece, zero) for piece in hot]
         return jnp.concatenate(tall, axis=0)
 
@@ -249,53 +272,62 @@
     sources = [one_hot(k, 0, cols) for k in range(devices)]
     whole = (
         jnp.concatenate([s[0] for s in sources], axis=1),
-        [jnp.concatenate([s[1][i] for s in sources], axis=1) for i in range(GY // 16)],
-    )
-    for t in range(tiles):
-        got = dot(lhs, expand(whole, 4 * t, 4), ((1,), (1,)))
+        [jnp.concatenate([s[1][i] for s in sources], axis=1) for i in range(8)],
+    )
+    for t in range(0, slots, 2):
+        got = dot(lhs, expand(whole, t, 2), ((1,), (1,)))
         got = got[:rows] + got[rows:]
-        mixed = []
-        for u in range(2):
-            re, im = got[:pad, 128 * u : 128 * u + 128], got[pad:, 128 * u : 128 * u + 128]
-            mixed.append(jnp.where(near, re, pltpu.roll(im, GY, 1)))
-            mixed.append(jnp.where(near, pltpu.roll(re, GY, 1), im))
-        moved = dot(tripled(jnp.concatenate(mixed, axis=0), 1), ty_ref[...])
-        y0_ref[4 * t * pad : 4 * (t + 1) * pad] = moved[:, :128]
-        y1_ref[4 * t * pad : 4 * (t + 1) * pad] = moved[:, 128:]
-    if tiles * 4 < GX:
-        rest = jnp.zeros(((GX - 4 * tiles) * pad, 128), F32)
-        y0_ref[4 * tiles * pad :] = rest
-        y1_ref[4 * tiles * pad :] = rest
+        for i, (width, slot, middle) in enumerate(places):
+            if slot // 2 * 2 != t:
+                continue
+            at = 128 * (slot - t)
+            re = pltpu.roll(got[:pad, at : at + 128], (radius - middle) % 128, 1)
+            im = pltpu.roll(got[pad:, at : at + 128], (radius + GY - middle) % 128, 1)
+            im = jnp.where(between(GY + radius - width, GY + radius + width), im, 0.0)
+            in_ref[i * pad : (i + 1) * pad] = jnp.where(between(radius - width, radius + width), re, im)
+    in_ref[len(places) * pad :] = jnp.zeros(((GX - len(places)) * pad, 128), F32)
+    moved = dot(tripled(in_ref[...], 1), ty_ref[...])
+    y0_ref[...] = moved[:, :128]
+    y1_ref[...] = moved[:, 128:]
     if depth < pad:
         q_ref[depth * GX :] = jnp.zeros(((pad - depth) * GX, 128), F32)
 
-    for z in range(0, depth, 2):
-        sides = []
-        for w in range(2):
-            line = pl.ds(z + w, GX, stride=pad)
-            sides.append(jnp.concatenate([y0_ref[line, :], y1_ref[line, :]], axis=0))
-        field = dot(tx_ref[...], tripled(jnp.concatenate(sides, axis=1), 0))
-        pot = jnp.concatenate([pot_ref[z], pot_ref[z + 1]], axis=1)
-        field = field * jnp.concatenate([pot, pot], axis=0)
-        back = dot(txb_ref[...], tripled(field, 0))
-        turned = [
-            jnp.concatenate([back[:GX, 128 * w : 128 * w + 128], back[GX:, 128 * w : 128 * w + 128]], axis=1)
-            for w in range(2)
-        ]
-        q_ref[z * GX : (z + 2) * GX] = dot(tripled(jnp.concatenate(turned, axis=0), 1), tyb_ref[...])
-
-    for t in range(2 * tiles):
-        a = q_ref[pl.ds(2 * t, pad, stride=GX), :]
-        b = q_ref[pl.ds(2 * t + 1, pad, stride=GX), :]
-        re = jnp.where(near, a, pltpu.roll(b, GY, 1))
-        im = jnp.where(near, pltpu.roll(a, GY, 1), b)
-        box_ref[:, 128 * t : 128 * t + 128] = jnp.concatenate(split(jnp.concatenate([re, im], axis=0)), axis=0)
+    chunk = 8
+    for first in range(0, depth, chunk):
+        last = min(depth, first + chunk)
+        for z in range(first, last, 2):
+            sides = []
+            for w in range(2):
+                line = pl.ds(z + w, GX, stride=pad)
+                sides.append(jnp.concatenate([y0_ref[line, :], y1_ref[line, :]], axis=0))
+            field = dot(tx_ref[...], tripled(jnp.concatenate(sides, axis=1), 0))
+            pot = jnp.concatenate([pot_ref[z], pot_ref[z + 1]], axis=1)
+            field = field * jnp.concatenate([pot, pot], axis=0)
+            back = dot(txb_ref[...], tripled(field, 0))
+            for w in range(2):
+                for p in range(2):
+                    back_ref[(z + w) * GX : (z + w + 1) * GX, 128 * p : 128 * p + 128] = back[
+                        p * GX : (p + 1) * GX, 128 * w : 128 * w + 128
+                    ]
+        part = slice(first * GX, last * GX)
+        q_ref[part] = dot(tripled(back_ref[part], 1), tyb_ref[...])
+
+    for s in range(slots):
+        re, im = jnp.zeros((pad, 128), F32), jnp.zeros((pad, 128), F32)
+        for i, (width, slot, middle) in enumerate(places):
+            if slot != s:
+                continue
+            value = q_ref[pl.ds(i, pad, stride=GX), :]
+            here = between(middle - width, middle + width)
+            re = jnp.where(here, pltpu.roll(value, (middle - radius) % 128, 1), re)
+            im = jnp.where(here, pltpu.roll(value, (middle - radius - GY) % 128, 1), im)
+        box_ref[:, 128 * s : 128 * s + 128] = jnp.concatenate(split(jnp.concatenate([re, im], axis=0)), axis=0)
 
     box = box_ref[...]
     wide = min(256, cols)
     for k in range(devices):
         for at in range(0, cols, wide):
-            got = dot(box, expand(one_hot(k, at, wide), 0, 4 * tiles))
+            got = dot(box, expand(one_hot(k, at, wide), 0, slots))
             outs[k][:, at : at + wide] = got[:rows] + got[rows:]
 
 
@@ -321,11 +353,7 @@
         ]
 
     def total(value, axis, size):
-        bit = 1
-        while bit < size:
-            value = value + lax.ppermute(value, axis, [(d, d ^ bit) for d in range(size)])
-            bit *= 2
-        return value
+        return functools.reduce(jnp.add, exchange([value] * size, axis))
 
     ahead, back = z_tables(size, devices, pad)
     tables = plane_tables(size)
@@ -364,8 +392,10 @@
             [
                 pltpu.VMEM((GX * pad, 128), F32),
                 pltpu.VMEM((GX * pad, 128), F32),
+                pltpu.VMEM((GX * pad, 128), F32),
+                pltpu.VMEM((pad * GX, 256), F32),
                 pltpu.VMEM((pad * GX, 128), F32),
-                pltpu.VMEM((2 * rows, 256 * (-(-count // 4))), BF16),
+                pltpu.VMEM((2 * rows, 128 * packing(size)[1]), BF16),
             ],
         )
 

time: 107 us -> 86.8 us (0.81)
  Pallas kernels: 40.5 us -> 20 us
  starting transfers between devices: 25.8 us -> 35 us
  waiting for transfers between devices: 33.3 us -> 24.3 us
    pallas_call x6, Pallas kernels: 40.5 us -> 20 us  [call(): pl.pallas_call(kernel, out_shape=out_shape, in_specs=[SMEM] * len(scalars...]
    ppermute x5 -> x0, waiting for transfers between devices: 14.3 us -> none  [total(): lax.ppermute(value, axis, [(d, d ^ bit) for d in range(size)])]
    ppermute x19 -> x29, starting transfers between devices: 23.4 us -> 35 us  [exchange(): lax.ppermute(values[k], axis, [(d, step(d, k)) for d in range(size)])]
    ppermute x19 -> x29, waiting for transfers between devices: 19 us -> 24.3 us  [exchange(): lax.ppermute(values[k], axis, [(d, step(d, k)) for d in range(size)])]
    ppermute x5 -> x0, starting transfers between devices: 2.43 us -> none  [total(): lax.ppermute(value, axis, [(d, d ^ bit) for d in range(size)])]
  transfers between devices with their start and end apart: 24 -> 29, of which waited for: 20 -> 19; matrix products, arithmetic and copies ran while one was open for 2% -> 2% of each run, Pallas kernels for 0% -> 0%
where the time goes in v3:
time: 86.8 us; the launch traced here: 86.5 us
  starting transfers between devices  35 us (40%)
  waiting for transfers between devices  24.3 us (28%)
  Pallas kernels  20 us (23%)
  local copies, waits for them, and re-layouts  3.22 us (4%)
  between operations  2.14 us (2%)
  other arithmetic  1.9 us (2%)
    ppermute x29, starting transfers between devices, exchange(): lax.ppermute(values[k], axis, [(d, step(d, k)) for d in range(size)])  35 us
    ppermute x29, waiting for transfers between devices, exchange(): lax.ppermute(values[k], axis, [(d, step(d, k)) for d in range(size)])  24.3 us
    pallas_call x6, Pallas kernels, call(): pl.pallas_call(kernel, out_shape=out_shape, in_specs=[SMEM] * len(scalars...  20 us
    unnamed x24, local copies, waits for them, and re-layouts  2.67 us
  transfers between devices with their start and end apart: 29, of which 19 were waited for; matrix products, arithmetic and copies ran while one was open for 2% of the time, Pallas kernels for 0%

profile of v3, /device:TPU:0, one launch (start us, length us, event | category | flops | bytes accessed | tf_op | source)
XLA Modules:
  0.0 86.5 jit_solution(13771950931049484736)
XLA Ops:
  0.6 1.0 %copy-done = f32[2,1,512,96]{2,3,1,0:T(8,128)S(1)} copy-done((f32[2,1,512,96]{2,3,1,0:T(8,128)S(1)}, f32[2,1,512,96]{2,3,1,0:T(8,128)}, u32[]{:S(2)}) %copy-start) | copy-done | bytes 393240
  1.6 0.9 %copy-done.3 = bf16[4,48,576]{2,1,0:T(8,128)(2,1)S(1)} copy-done((bf16[4,48,576]{2,1,0:T(8,128)(2,1)S(1)}, bf16[4,48,576]{2,1,0:T(8,128)(2,1)}, u32[]{:S(2)}) %copy-start.3) | copy-done | bytes 221208
  2.6 0.7 copy-done.10
  3.3 0.5 shard_map.131
  3.8 3.0 %collective-permute-start = (f32[56,512]{1,0:T(8,128)S(1)}, f32[56,512]{1,0:T(8,128)S(1)}, u32[]{:S(2)}, u32[]{:S(2)}) collective-permute-start(f32[56,512]{1,0:T(8,128)S(1)} %get-tuple-element.29), channel_id=1, source_target_pairs={{0,8},{8,0},{16,24},{24,16},{1,9},{9,1},{17,25},{25,17},{2,10},{10... | collective-permute-start | bytes 344072 | tf_op jit(solution)/shard_map/ppermute | solution.py:352
  6.8 1.5 %collective-permute-start.1 = (f32[56,512]{1,0:T(8,128)S(1)}, f32[56,512]{1,0:T(8,128)S(1)}, u32[]{:S(2)}, u32[]{:S(2)}) collective-permute-start(f32[56,512]{1,0:T(8,128)S(1)} %get-tuple-element.30), channel_id=1, source_target_pairs={{0,16},{8,24},{16,0},{24,8},{1,17},{9,25},{17,1},{25,9},{2,18},{10... | collective-permute-start | bytes 344072 | tf_op jit(solution)/shard_map/ppermute | solution.py:352
  8.3 0.0 collective-permute-start.2
  8.3 1.2 %broadcast_multiply_fusion = f32[24,9216]{1,0:T(8,128)S(1)} fusion(f32[24,9216]{1,0:T(8,128)} %param.14), kind=kLoop, calls=%fused_computation | loop fusion | flops 221184 | bytes 1769472 | tf_op jit(solution)/shard_map/mul | solution.py:368
  9.6 0.5 reshape.26
  10.0 0.0 copy-start.5
  10.0 0.0 copy-start.6
  10.0 0.0 copy-start.7
  10.1 0.0 copy-start.8
  10.1 0.1 pad.4.refs_4_.refs_8_
  10.2 0.0 copy-start.2
  10.2 0.0 copy-start.4
  10.2 0.1 collective-permute-done.refs_1_.refs_5_
  10.3 2.8 %collective-permute-done.1.refs_2_.refs_6_ = f32[56,512]{1,0:T(8,128)S(1)} collective-permute-done((f32[56,512]{1,0:T(8,128)S(1)}, f32[56,512]{1,0:T(8,128)S(1)}, u32[]{:S(2)}, u32[]{:S(2)}) %collective-permute-start.1) | collective-permute-done | bytes 114720 | tf_op jit(solution)/shard_map/ppermute | solution.py:352
  13.1 0.9 %collective-permute-done.2.refs_3_.refs_7_ = f32[56,512]{1,0:T(8,128)S(1)} collective-permute-done((f32[56,512]{1,0:T(8,128)S(1)}, f32[56,512]{1,0:T(8,128)S(1)}, u32[]{:S(2)}, u32[]{:S(2)}) %collective-permute-start.2) | collective-permute-done | bytes 114720 | tf_op jit(solution)/shard_map/ppermute | solution.py:352
  14.0 8.6 %shard_map.132 = (f32[48,512]{1,0:T(8,128)S(1)}, f32[48,512]{1,0:T(8,128)S(1)}, f32[48,512]{1,0:T(8,128)S(1)}, f32[48,512]{1,0:T(8,128)S(1)}) custom-call(f32[56,512]{1,0:T(8,128)S(1)} %get-tuple-element.28.refs_0_.refs_4_, f32[56,512]{1,0:T(8,128)S(1)} %collective-permute-done.refs_1_.refs_5_, f32[56,512]{1,0:T(8,128)S(1)} %collective-permute-done.1.refs_2_.refs_6_, ...), custom_call_target="tpu_custom_call" | custom-call | tf_op jit(solution)/shard_map/pallas_call | solution.py:115
  22.6 1.1 %collective-permute-start.3 = (f32[48,512]{1,0:T(8,128)S(1)}, f32[48,512]{1,0:T(8,128)S(1)}, u32[]{:S(2)}, u32[]{:S(2)}) collective-permute-start(f32[48,512]{1,0:T(8,128)S(1)} %get-tuple-element.33), channel_id=1, source_target_pairs={{0,8},{8,0},{16,24},{24,16},{1,9},{9,1},{17,25},{25,17},{2,10},{10... | collective-permute-start | bytes 294920 | tf_op jit(solution)/shard_map/ppermute | solution.py:352
  23.7 0.8 collective-permute-start.4
  24.6 1.6 %collective-permute-start.5 = (f32[48,512]{1,0:T(8,128)S(1)}, f32[48,512]{1,0:T(8,128)S(1)}, u32[]{:S(2)}, u32[]{:S(2)}) collective-permute-start(f32[48,512]{1,0:T(8,128)S(1)} %get-tuple-element.35), channel_id=1, source_target_pairs={{0,24},{8,16},{16,8},{24,0},{1,25},{9,17},{17,9},{25,1},{2,26},{10... | collective-permute-start | bytes 294920 | tf_op jit(solution)/shard_map/ppermute | solution.py:352
  27.5 0.8 collective-permute-done.3.refs_1_
  28.3 0.1 collective-permute-done.4.refs_2_
  28.4 1.7 %collective-permute-done.5.refs_3_ = f32[48,512]{1,0:T(8,128)S(1)} collective-permute-done((f32[48,512]{1,0:T(8,128)S(1)}, f32[48,512]{1,0:T(8,128)S(1)}, u32[]{:S(2)}, u32[]{:S(2)}) %collective-permute-start.5) | collective-permute-done | bytes 98336 | tf_op jit(solution)/shard_map/ppermute | solution.py:352
  30.1 0.7 shard_map.133
  30.8 1.5 %collective-permute-start.6 = (f32[48,512]{1,0:T(8,128)S(1)}, f32[48,512]{1,0:T(8,128)S(1)}, u32[]{:S(2)}, u32[]{:S(2)}) collective-permute-start(f32[48,512]{1,0:T(8,128)S(1)} %get-tuple-element.37), channel_id=1, source_target_pairs={{0,8},{8,0},{16,24},{24,16},{1,9},{9,1},{17,25},{25,17},{2,10},{10... | collective-permute-start | bytes 294920 | tf_op jit(solution)/shard_map/ppermute | solution.py:352
  32.4 0.7 collective-permute-start.7
  33.1 1.3 %collective-permute-start.8 = (f32[48,512]{1,0:T(8,128)S(1)}, f32[48,512]{1,0:T(8,128)S(1)}, u32[]{:S(2)}, u32[]{:S(2)}) collective-permute-start(f32[48,512]{1,0:T(8,128)S(1)} %get-tuple-element.39), channel_id=1, source_target_pairs={{0,24},{8,16},{16,8},{24,0},{1,25},{9,17},{17,9},{25,1},{2,26},{10... | collective-permute-start | bytes 294920 | tf_op jit(solution)/shard_map/ppermute | solution.py:352
  34.4 1.1 %collective-permute-done.6.refs_1_ = f32[48,512]{1,0:T(8,128)S(1)} collective-permute-done((f32[48,512]{1,0:T(8,128)S(1)}, f32[48,512]{1,0:T(8,128)S(1)}, u32[]{:S(2)}, u32[]{:S(2)}) %collective-permute-start.6) | collective-permute-done | bytes 98336 | tf_op jit(solution)/shard_map/ppermute | solution.py:352
  35.5 1.5 %collective-permute-done.7.refs_2_ = f32[48,512]{1,0:T(8,128)S(1)} collective-permute-done((f32[48,512]{1,0:T(8,128)S(1)}, f32[48,512]{1,0:T(8,128)S(1)}, u32[]{:S(2)}, u32[]{:S(2)}) %collective-permute-start.7) | collective-permute-done | bytes 98336 | tf_op jit(solution)/shard_map/ppermute | solution.py:352
  37.0 1.6 %collective-permute-done.8.refs_3_ = f32[48,512]{1,0:T(8,128)S(1)} collective-permute-done((f32[48,512]{1,0:T(8,128)S(1)}, f32[48,512]{1,0:T(8,128)S(1)}, u32[]{:S(2)}, u32[]{:S(2)}) %collective-permute-start.8) | collective-permute-done | bytes 98336 | tf_op jit(solution)/shard_map/ppermute | solution.py:352
  38.6 8.7 %shard_map.134 = (f32[48,512]{1,0:T(8,128)S(1)}, f32[48,512]{1,0:T(8,128)S(1)}, f32[48,512]{1,0:T(8,128)S(1)}, f32[48,512]{1,0:T(8,128)S(1)}) custom-call(f32[48,512]{1,0:T(8,128)S(1)} %get-tuple-element.36.refs_0_, f32[48,512]{1,0:T(8,128)S(1)} %collective-permute-done.6.refs_1_, f32[48,512]{1,0:T(8,128)S(1)} %collective-permute-done.7.refs_2_, ...), custom_call_target="tpu_custom_call" | custom-call | tf_op jit(solution)/shard_map/pallas_call | solution.py:115
  47.3 1.4 %collective-permute-start.10 = (f32[48,512]{1,0:T(8,128)S(1)}, f32[48,512]{1,0:T(8,128)S(1)}, u32[]{:S(2)}, u32[]{:S(2)}) collective-permute-start(f32[48,512]{1,0:T(8,128)S(1)} %get-tuple-element.42), channel_id=1, source_target_pairs={{0,16},{8,24},{16,0},{24,8},{1,17},{9,25},{17,1},{25,9},{2,18},{10... | collective-permute-start | bytes 294920 | tf_op jit(solution)/shard_map/ppermute | solution.py:352
  48.7 1.2 %collective-permute-start.11 = (f32[48,512]{1,0:T(8,128)S(1)}, f32[48,512]{1,0:T(8,128)S(1)}, u32[]{:S(2)}, u32[]{:S(2)}) collective-permute-start(f32[48,512]{1,0:T(8,128)S(1)} %get-tuple-element.43), channel_id=1, source_target_pairs={{0,24},{8,16},{16,8},{24,0},{1,25},{9,17},{17,9},{25,1},{2,26},{10... | collective-permute-start | bytes 294920 | tf_op jit(solution)/shard_map/ppermute | solution.py:352
  49.9 1.0 %collective-permute-start.9 = (f32[48,512]{1,0:T(8,128)S(1)}, f32[48,512]{1,0:T(8,128)S(1)}, u32[]{:S(2)}, u32[]{:S(2)}) collective-permute-start(f32[48,512]{1,0:T(8,128)S(1)} %get-tuple-element.41), channel_id=1, source_target_pairs={{0,8},{8,0},{16,24},{24,16},{1,9},{9,1},{17,25},{25,17},{2,10},{10... | collective-permute-start | bytes 294920 | tf_op jit(solution)/shard_map/ppermute | solution.py:352
  50.8 1.1 %collective-permute-done.10.refs_2_ = f32[48,512]{1,0:T(8,128)S(1)} collective-permute-done((f32[48,512]{1,0:T(8,128)S(1)}, f32[48,512]{1,0:T(8,128)S(1)}, u32[]{:S(2)}, u32[]{:S(2)}) %collective-permute-start.10) | collective-permute-done | bytes 98336 | tf_op jit(solution)/shard_map/ppermute | solution.py:352
  52.0 2.2 %collective-permute-done.11.refs_3_ = f32[48,512]{1,0:T(8,128)S(1)} collective-permute-done((f32[48,512]{1,0:T(8,128)S(1)}, f32[48,512]{1,0:T(8,128)S(1)}, u32[]{:S(2)}, u32[]{:S(2)}) %collective-permute-start.11) | collective-permute-done | bytes 98336 | tf_op jit(solution)/shard_map/ppermute | solution.py:352
  54.2 0.3 collective-permute-done.9.refs_1_
  54.5 1.2 %shard_map.135 = (f32[2,96,512]{2,1,0:T(8,128)}, bf16[16,512]{1,0:T(8,128)(2,1)S(1)}, bf16[16,512]{1,0:T(8,128)(2,1)S(1)}, bf16[16,512]{1,0:T(8,128)(2,1)S(1)}, ...) custom-call(s32[1]{0:T(128)} %bitcast.me_ref, ...), custom_call_target="tpu_custom_call" | custom-call | tf_op jit(solution)/shard_map/pallas_call | solution.py:115
  55.7 1.6 %collective-permute-start.13 = (bf16[16,512]{1,0:T(8,128)(2,1)S(1)}, bf16[16,512]{1,0:T(8,128)(2,1)S(1)}, u32[]{:S(2)}, u32[]{:S(2)}) collective-permute-start(bf16[16,512]{1,0:T(8,128)(2,1)S(1)} %get-tuple-element.48), channel_id=1, source_target_pairs={{0,2},{1,3},{2,0},{3,1},{4,6},{5,7},{6,4},{7,5},{8,10},{9,11},{10,... | collective-permute-start | bytes 49160 | tf_op jit(solution)/shard_map/ppermute | solution.py:352
  57.2 0.3 collective-permute-start.14
  57.5 2.6 %collective-permute-start.15 = (bf16[16,512]{1,0:T(8,128)(2,1)S(1)}, bf16[16,512]{1,0:T(8,128)(2,1)S(1)}, u32[]{:S(2)}, u32[]{:S(2)}) collective-permute-start(bf16[16,512]{1,0:T(8,128)(2,1)S(1)} %get-tuple-element.50), channel_id=1, source_target_pairs={{0,4},{1,5},{2,6},{3,7},{4,0},{5,1},{6,2},{7,3},{8,12},{9,13},{10,... | collective-permute-start | bytes 49160 | tf_op jit(solution)/shard_map/ppermute | solution.py:352
  60.1 3.6 %collective-permute-start.17 = (bf16[16,512]{1,0:T(8,128)(2,1)S(1)}, bf16[16,512]{1,0:T(8,128)(2,1)S(1)}, u32[]{:S(2)}, u32[]{:S(2)}) collective-permute-start(bf16[16,512]{1,0:T(8,128)(2,1)S(1)} %get-tuple-element.52), channel_id=1, source_target_pairs={{0,6},{1,7},{2,4},{3,5},{4,2},{5,3},{6,0},{7,1},{8,14},{9,15},{10,... | collective-permute-start | bytes 49160 | tf_op jit(solution)/shard_map/ppermute | solution.py:352
  63.7 0.2 collective-permute-start.18
  63.8 0.3 collective-permute-done.16.refs_5_
  64.2 1.6 %collective-permute-done.17.refs_6_ = bf16[16,512]{1,0:T(8,128)(2,1)S(1)} collective-permute-done((bf16[16,512]{1,0:T(8,128)(2,1)S(1)}, bf16[16,512]{1,0:T(8,128)(2,1)S(1)}, u32[]{:S(2)}, u32[]{:S(2)}) %collective-permute-start.17) | collective-permute-done | bytes 16416 | tf_op jit(solution)/shard_map/ppermute | solution.py:352
  65.7 2.9 %collective-permute-done.18.refs_7_ = bf16[16,512]{1,0:T(8,128)(2,1)S(1)} collective-permute-done((bf16[16,512]{1,0:T(8,128)(2,1)S(1)}, bf16[16,512]{1,0:T(8,128)(2,1)S(1)}, u32[]{:S(2)}, u32[]{:S(2)}) %collective-permute-start.18) | collective-permute-done | bytes 16416 | tf_op jit(solution)/shard_map/ppermute | solution.py:352
  68.6 0.3 shard_map.136
  69.0 1.1 %collective-permute-start.19 = (f32[2,8,8]{2,1,0:T(8,128)S(1)}, f32[2,8,8]{2,1,0:T(8,128)S(1)}, u32[]{:S(2)}, u32[]{:S(2)}) collective-permute-start(f32[2,8,8]{2,1,0:T(8,128)S(1)} %shard_map.136), channel_id=1, source_target_pairs={{0,8},{8,0},{16,24},{24,16},{1,9},{9,1},{17,25},{25,17},{2,10},{10... | collective-permute-start | bytes 1544 | tf_op jit(solution)/shard_map/ppermute | solution.py:352
  70.0 1.3 %collective-permute-start.20 = (f32[2,8,8]{2,1,0:T(8,128)S(1)}, f32[2,8,8]{2,1,0:T(8,128)S(1)}, u32[]{:S(2)}, u32[]{:S(2)}) collective-permute-start(f32[2,8,8]{2,1,0:T(8,128)S(1)} %shard_map.136), channel_id=1, source_target_pairs={{0,16},{8,24},{16,0},{24,8},{1,17},{9,25},{17,1},{25,9},{2,18},{10... | collective-permute-start | bytes 1544 | tf_op jit(solution)/shard_map/ppermute | solution.py:352
  71.3 1.2 %collective-permute-start.21 = (f32[2,8,8]{2,1,0:T(8,128)S(1)}, f32[2,8,8]{2,1,0:T(8,128)S(1)}, u32[]{:S(2)}, u32[]{:S(2)}) collective-permute-start(f32[2,8,8]{2,1,0:T(8,128)S(1)} %shard_map.136), channel_id=1, source_target_pairs={{0,24},{8,16},{16,8},{24,0},{1,25},{9,17},{17,9},{25,1},{2,26},{10... | collective-permute-start | bytes 1544 | tf_op jit(solution)/shard_map/ppermute | solution.py:352
  72.5 0.2 collective-permute-done.19
  72.6 1.0 %collective-permute-done.20 = f32[2,8,8]{2,1,0:T(8,128)S(1)} collective-permute-done((f32[2,8,8]{2,1,0:T(8,128)S(1)}, f32[2,8,8]{2,1,0:T(8,128)S(1)}, u32[]{:S(2)}, u32[]{:S(2)}) %collective-permute-start.20) | collective-permute-done | bytes 544 | tf_op jit(solution)/shard_map/ppermute | solution.py:352
  73.7 2.2 %collective-permute-done.21 = f32[2,8,8]{2,1,0:T(8,128)S(1)} collective-permute-done((f32[2,8,8]{2,1,0:T(8,128)S(1)}, f32[2,8,8]{2,1,0:T(8,128)S(1)}, u32[]{:S(2)}, u32[]{:S(2)}) %collective-permute-start.21) | collective-permute-done | bytes 544 | tf_op jit(solution)/shard_map/ppermute | solution.py:352
  75.9 0.1 collective-permute-start.23
  75.9 1.8 %collective-permute-start.24 = (f32[2,8,8]{2,1,0:T(8,128)S(1)}, f32[2,8,8]{2,1,0:T(8,128)S(1)}, u32[]{:S(2)}, u32[]{:S(2)}) collective-permute-start(f32[2,8,8]{2,1,0:T(8,128)S(1)} %add_add_fusion), channel_id=1, source_target_pairs={{0,3},{1,2},{2,1},{3,0},{4,7},{5,6},{6,5},{7,4},{8,11},{9,10},{10,... | collective-permute-start | bytes 1544 | tf_op jit(solution)/shard_map/ppermute | solution.py:352
  77.7 2.6 %collective-permute-start.26 = (f32[2,8,8]{2,1,0:T(8,128)S(1)}, f32[2,8,8]{2,1,0:T(8,128)S(1)}, u32[]{:S(2)}, u32[]{:S(2)}) collective-permute-start(f32[2,8,8]{2,1,0:T(8,128)S(1)} %add_add_fusion), channel_id=1, source_target_pairs={{0,5},{1,4},{2,7},{3,6},{4,1},{5,0},{6,3},{7,2},{8,13},{9,12},{10,... | collective-permute-start | bytes 1544 | tf_op jit(solution)/shard_map/ppermute | solution.py:352
  80.3 0.6 collective-permute-start.27
  80.9 3.0 %collective-permute-start.28 = (f32[2,8,8]{2,1,0:T(8,128)S(1)}, f32[2,8,8]{2,1,0:T(8,128)S(1)}, u32[]{:S(2)}, u32[]{:S(2)}) collective-permute-start(f32[2,8,8]{2,1,0:T(8,128)S(1)} %add_add_fusion), channel_id=1, source_target_pairs={{0,7},{1,6},{2,5},{3,4},{4,3},{5,2},{6,1},{7,0},{8,15},{9,14},{10,... | collective-permute-start | bytes 1544 | tf_op jit(solution)/shard_map/ppermute | solution.py:352
  84.0 1.9 %collective-permute-done.27 = f32[2,8,8]{2,1,0:T(8,128)S(1)} collective-permute-done((f32[2,8,8]{2,1,0:T(8,128)S(1)}, f32[2,8,8]{2,1,0:T(8,128)S(1)}, u32[]{:S(2)}, u32[]{:S(2)}) %collective-permute-start.27) | collective-permute-done | bytes 544 | tf_op jit(solution)/shard_map/ppermute | solution.py:352
  85.9 0.0 collective-permute-done.28
  85.9 0.6 fusion.1
  (30 shorter events, 0.1 us)
Async XLA Ops:
  0.6 1.0 %copy-start = (f32[2,1,512,96]{2,3,1,0:T(8,128)S(1)}, f32[2,1,512,96]{2,3,1,0:T(8,128)}, u32[]{:S(2)}) copy-start(f32[2,1,512,96]{2,3,1,0:T(8,128)} %param.12) | copy-start | bytes 1179652
  1.6 0.9 %copy-start.3 = (bf16[4,48,576]{2,1,0:T(8,128)(2,1)S(1)}, bf16[4,48,576]{2,1,0:T(8,128)(2,1)}, u32[]{:S(2)}) copy-start(bf16[4,48,576]{2,1,0:T(8,128)(2,1)} %constant.35.clone.ahead_ref.refs_6_) | copy-start | bytes 663556
  2.6 0.7 copy-start.10
  3.8 6.6 %collective-permute-start = (f32[56,512]{1,0:T(8,128)S(1)}, f32[56,512]{1,0:T(8,128)S(1)}, u32[]{:S(2)}, u32[]{:S(2)}) collective-permute-start(f32[56,512]{1,0:T(8,128)S(1)} %get-tuple-element.29), channel_id=1, source_target_pairs={{0,8},{8,0},{16,24},{24,16},{1,9},{9,1},{17,25},{25,17},{2,10},{10... | collective-permute-start | bytes 344072 | tf_op jit(solution)/shard_map/ppermute | solution.py:352
  6.8 6.3 %collective-permute-start.1 = (f32[56,512]{1,0:T(8,128)S(1)}, f32[56,512]{1,0:T(8,128)S(1)}, u32[]{:S(2)}, u32[]{:S(2)}) collective-permute-start(f32[56,512]{1,0:T(8,128)S(1)} %get-tuple-element.30), channel_id=1, source_target_pairs={{0,16},{8,24},{16,0},{24,8},{1,17},{9,25},{17,1},{25,9},{2,18},{10... | collective-permute-start | bytes 344072 | tf_op jit(solution)/shard_map/ppermute | solution.py:352
  8.3 5.7 %collective-permute-start.2 = (f32[56,512]{1,0:T(8,128)S(1)}, f32[56,512]{1,0:T(8,128)S(1)}, u32[]{:S(2)}, u32[]{:S(2)}) collective-permute-start(f32[56,512]{1,0:T(8,128)S(1)} %get-tuple-element.31), channel_id=1, source_target_pairs={{0,24},{8,16},{16,8},{24,0},{1,25},{9,17},{17,9},{25,1},{2,26},{10... | collective-permute-start | bytes 344072 | tf_op jit(solution)/shard_map/ppermute | solution.py:352
  10.0 4.0 %copy-start.5 = (bf16[384,256]{1,0:T(8,128)(2,1)S(1)}, bf16[384,256]{1,0:T(8,128)(2,1)}, u32[]{:S(2)}) copy-start(bf16[384,256]{1,0:T(8,128)(2,1)} %constant.36.clone.refs_5_.refs_9_) | copy-start | bytes 589828
  10.0 4.0 %copy-start.6 = (bf16[768,128]{1,0:T(8,128)(2,1)S(1)}, bf16[768,128]{1,0:T(8,128)(2,1)}, u32[]{:S(2)}) copy-start(bf16[768,128]{1,0:T(8,128)(2,1)} %constant.39.clone.refs_8_.refs_12_) | copy-start | bytes 589828
  10.0 4.0 %copy-start.7 = (bf16[192,336]{1,0:T(8,128)(2,1)S(1)}, bf16[192,336]{1,0:T(8,128)(2,1)}, u32[]{:S(2)}) copy-start(bf16[192,336]{1,0:T(8,128)(2,1)} %constant.37.clone.refs_6_.refs_10_) | copy-start | bytes 387076
  10.1 4.0 %copy-start.8 = (bf16[112,576]{1,0:T(8,128)(2,1)S(1)}, bf16[112,576]{1,0:T(8,128)(2,1)}, u32[]{:S(2)}) copy-start(bf16[112,576]{1,0:T(8,128)(2,1)} %constant.38.clone.refs_7_.refs_11_) | copy-start | bytes 387076
  10.2 19.9 %copy-start.1 = (f32[2,1,512,96]{2,3,1,0:T(8,128)S(1)}, f32[2,1,512,96]{2,3,1,0:T(8,128)}, u32[]{:S(2)}) copy-start(f32[2,1,512,96]{2,3,1,0:T(8,128)} %param.12) | copy-start | bytes 1179652
  10.2 19.9 %copy-start.2 = (bf16[192,576]{1,0:T(8,128)(2,1)S(1)}, bf16[192,576]{1,0:T(8,128)(2,1)}, u32[]{:S(2)}) copy-start(bf16[192,576]{1,0:T(8,128)(2,1)} %constant.40.clone.refs_7_) | copy-start | bytes 663556
  10.2 19.9 %copy-start.4 = (bf16[4,48,576]{2,1,0:T(8,128)(2,1)S(1)}, bf16[4,48,576]{2,1,0:T(8,128)(2,1)}, u32[]{:S(2)}) copy-start(bf16[4,48,576]{2,1,0:T(8,128)(2,1)} %constant.35.clone.ahead_ref.refs_6_) | copy-start | bytes 663556
  10.2 19.9 %copy-start.11 = (s32[512]{0:T(512)S(1)}, s32[512]{0:T(512)}, u32[]{:S(2)}) copy-start(s32[512]{0:T(512)} %param.13) | copy-start | bytes 6148
  22.6 5.7 %collective-permute-start.3 = (f32[48,512]{1,0:T(8,128)S(1)}, f32[48,512]{1,0:T(8,128)S(1)}, u32[]{:S(2)}, u32[]{:S(2)}) collective-permute-start(f32[48,512]{1,0:T(8,128)S(1)} %get-tuple-element.33), channel_id=1, source_target_pairs={{0,8},{8,0},{16,24},{24,16},{1,9},{9,1},{17,25},{25,17},{2,10},{10... | collective-permute-start | bytes 294920 | tf_op jit(solution)/shard_map/ppermute | solution.py:352
  23.7 4.7 %collective-permute-start.4 = (f32[48,512]{1,0:T(8,128)S(1)}, f32[48,512]{1,0:T(8,128)S(1)}, u32[]{:S(2)}, u32[]{:S(2)}) collective-permute-start(f32[48,512]{1,0:T(8,128)S(1)} %get-tuple-element.34), channel_id=1, source_target_pairs={{0,16},{8,24},{16,0},{24,8},{1,17},{9,25},{17,1},{25,9},{2,18},{10... | collective-permute-start | bytes 294920 | tf_op jit(solution)/shard_map/ppermute | solution.py:352
  24.6 5.5 %collective-permute-start.5 = (f32[48,512]{1,0:T(8,128)S(1)}, f32[48,512]{1,0:T(8,128)S(1)}, u32[]{:S(2)}, u32[]{:S(2)}) collective-permute-start(f32[48,512]{1,0:T(8,128)S(1)} %get-tuple-element.35), channel_id=1, source_target_pairs={{0,24},{8,16},{16,8},{24,0},{1,25},{9,17},{17,9},{25,1},{2,26},{10... | collective-permute-start | bytes 294920 | tf_op jit(solution)/shard_map/ppermute | solution.py:352
  30.8 4.7 %collective-permute-start.6 = (f32[48,512]{1,0:T(8,128)S(1)}, f32[48,512]{1,0:T(8,128)S(1)}, u32[]{:S(2)}, u32[]{:S(2)}) collective-permute-start(f32[48,512]{1,0:T(8,128)S(1)} %get-tuple-element.37), channel_id=1, source_target_pairs={{0,8},{8,0},{16,24},{24,16},{1,9},{9,1},{17,25},{25,17},{2,10},{10... | collective-permute-start | bytes 294920 | tf_op jit(solution)/shard_map/ppermute | solution.py:352
  32.4 4.6 %collective-permute-start.7 = (f32[48,512]{1,0:T(8,128)S(1)}, f32[48,512]{1,0:T(8,128)S(1)}, u32[]{:S(2)}, u32[]{:S(2)}) collective-permute-start(f32[48,512]{1,0:T(8,128)S(1)} %get-tuple-element.38), channel_id=1, source_target_pairs={{0,16},{8,24},{16,0},{24,8},{1,17},{9,25},{17,1},{25,9},{2,18},{10... | collective-permute-start | bytes 294920 | tf_op jit(solution)/shard_map/ppermute | solution.py:352
  33.1 5.5 %collective-permute-start.8 = (f32[48,512]{1,0:T(8,128)S(1)}, f32[48,512]{1,0:T(8,128)S(1)}, u32[]{:S(2)}, u32[]{:S(2)}) collective-permute-start(f32[48,512]{1,0:T(8,128)S(1)} %get-tuple-element.39), channel_id=1, source_target_pairs={{0,24},{8,16},{16,8},{24,0},{1,25},{9,17},{17,9},{25,1},{2,26},{10... | collective-permute-start | bytes 294920 | tf_op jit(solution)/shard_map/ppermute | solution.py:352
  38.6 15.9 %copy-start.9 = (bf16[2,128,96]{2,1,0:T(8,128)(2,1)S(1)}, bf16[2,128,96]{2,1,0:T(8,128)(2,1)}, u32[]{:S(2)}) copy-start(bf16[2,128,96]{2,1,0:T(8,128)(2,1)} %constant.41.clone.refs_8_) | copy-start | bytes 147460
  47.3 4.7 %collective-permute-start.10 = (f32[48,512]{1,0:T(8,128)S(1)}, f32[48,512]{1,0:T(8,128)S(1)}, u32[]{:S(2)}, u32[]{:S(2)}) collective-permute-start(f32[48,512]{1,0:T(8,128)S(1)} %get-tuple-element.42), channel_id=1, source_target_pairs={{0,16},{8,24},{16,0},{24,8},{1,17},{9,25},{17,1},{25,9},{2,18},{10... | collective-permute-start | bytes 294920 | tf_op jit(solution)/shard_map/ppermute | solution.py:352
  48.7 5.5 %collective-permute-start.11 = (f32[48,512]{1,0:T(8,128)S(1)}, f32[48,512]{1,0:T(8,128)S(1)}, u32[]{:S(2)}, u32[]{:S(2)}) collective-permute-start(f32[48,512]{1,0:T(8,128)S(1)} %get-tuple-element.43), channel_id=1, source_target_pairs={{0,24},{8,16},{16,8},{24,0},{1,25},{9,17},{17,9},{25,1},{2,26},{10... | collective-permute-start | bytes 294920 | tf_op jit(solution)/shard_map/ppermute | solution.py:352
  49.9 4.6 %collective-permute-start.9 = (f32[48,512]{1,0:T(8,128)S(1)}, f32[48,512]{1,0:T(8,128)S(1)}, u32[]{:S(2)}, u32[]{:S(2)}) collective-permute-start(f32[48,512]{1,0:T(8,128)S(1)} %get-tuple-element.41), channel_id=1, source_target_pairs={{0,8},{8,0},{16,24},{24,16},{1,9},{9,1},{17,25},{25,17},{2,10},{10... | collective-permute-start | bytes 294920 | tf_op jit(solution)/shard_map/ppermute | solution.py:352
  55.7 4.4 %collective-permute-start.12 = (bf16[16,512]{1,0:T(8,128)(2,1)S(1)}, bf16[16,512]{1,0:T(8,128)(2,1)S(1)}, u32[]{:S(2)}, u32[]{:S(2)}) collective-permute-start(bf16[16,512]{1,0:T(8,128)(2,1)S(1)} %get-tuple-element.47), channel_id=1, source_target_pairs={{0,1},{1,0},{2,3},{3,2},{4,5},{5,4},{6,7},{7,6},{8,9},{9,8},{10,11... | collective-permute-start | bytes 49160 | tf_op jit(solution)/shard_map/ppermute | solution.py:352
  55.7 8.0 %collective-permute-start.13 = (bf16[16,512]{1,0:T(8,128)(2,1)S(1)}, bf16[16,512]{1,0:T(8,128)(2,1)S(1)}, u32[]{:S(2)}, u32[]{:S(2)}) collective-permute-start(bf16[16,512]{1,0:T(8,128)(2,1)S(1)} %get-tuple-element.48), channel_id=1, source_target_pairs={{0,2},{1,3},{2,0},{3,1},{4,6},{5,7},{6,4},{7,5},{8,10},{9,11},{10,... | collective-permute-start | bytes 49160 | tf_op jit(solution)/shard_map/ppermute | solution.py:352
  57.2 6.6 %collective-permute-start.14 = (bf16[16,512]{1,0:T(8,128)(2,1)S(1)}, bf16[16,512]{1,0:T(8,128)(2,1)S(1)}, u32[]{:S(2)}, u32[]{:S(2)}) collective-permute-start(bf16[16,512]{1,0:T(8,128)(2,1)S(1)} %get-tuple-element.49), channel_id=1, source_target_pairs={{0,3},{1,2},{2,1},{3,0},{4,7},{5,6},{6,5},{7,4},{8,11},{9,10},{10,... | collective-permute-start | bytes 49160 | tf_op jit(solution)/shard_map/ppermute | solution.py:352
  57.5 6.3 %collective-permute-start.15 = (bf16[16,512]{1,0:T(8,128)(2,1)S(1)}, bf16[16,512]{1,0:T(8,128)(2,1)S(1)}, u32[]{:S(2)}, u32[]{:S(2)}) collective-permute-start(bf16[16,512]{1,0:T(8,128)(2,1)S(1)} %get-tuple-element.50), channel_id=1, source_target_pairs={{0,4},{1,5},{2,6},{3,7},{4,0},{5,1},{6,2},{7,3},{8,12},{9,13},{10,... | collective-permute-start | bytes 49160 | tf_op jit(solution)/shard_map/ppermute | solution.py:352
  60.1 4.1 %collective-permute-start.16 = (bf16[16,512]{1,0:T(8,128)(2,1)S(1)}, bf16[16,512]{1,0:T(8,128)(2,1)S(1)}, u32[]{:S(2)}, u32[]{:S(2)}) collective-permute-start(bf16[16,512]{1,0:T(8,128)(2,1)S(1)} %get-tuple-element.51), channel_id=1, source_target_pairs={{0,5},{1,4},{2,7},{3,6},{4,1},{5,0},{6,3},{7,2},{8,13},{9,12},{10,... | collective-permute-start | bytes 49160 | tf_op jit(solution)/shard_map/ppermute | solution.py:352
  60.1 5.6 %collective-permute-start.17 = (bf16[16,512]{1,0:T(8,128)(2,1)S(1)}, bf16[16,512]{1,0:T(8,128)(2,1)S(1)}, u32[]{:S(2)}, u32[]{:S(2)}) collective-permute-start(bf16[16,512]{1,0:T(8,128)(2,1)S(1)} %get-tuple-element.52), channel_id=1, source_target_pairs={{0,6},{1,7},{2,4},{3,5},{4,2},{5,3},{6,0},{7,1},{8,14},{9,15},{10,... | collective-permute-start | bytes 49160 | tf_op jit(solution)/shard_map/ppermute | solution.py:352
  63.7 5.0 %collective-permute-start.18 = (bf16[16,512]{1,0:T(8,128)(2,1)S(1)}, bf16[16,512]{1,0:T(8,128)(2,1)S(1)}, u32[]{:S(2)}, u32[]{:S(2)}) collective-permute-start(bf16[16,512]{1,0:T(8,128)(2,1)S(1)} %get-tuple-element.53), channel_id=1, source_target_pairs={{0,7},{1,6},{2,5},{3,4},{4,3},{5,2},{6,1},{7,0},{8,15},{9,14},{10,... | collective-permute-start | bytes 49160 | tf_op jit(solution)/shard_map/ppermute | solution.py:352
  69.0 3.7 %collective-permute-start.19 = (f32[2,8,8]{2,1,0:T(8,128)S(1)}, f32[2,8,8]{2,1,0:T(8,128)S(1)}, u32[]{:S(2)}, u32[]{:S(2)}) collective-permute-start(f32[2,8,8]{2,1,0:T(8,128)S(1)} %shard_map.136), channel_id=1, source_target_pairs={{0,8},{8,0},{16,24},{24,16},{1,9},{9,1},{17,25},{25,17},{2,10},{10... | collective-permute-start | bytes 1544 | tf_op jit(solution)/shard_map/ppermute | solution.py:352
  70.0 3.7 %collective-permute-start.20 = (f32[2,8,8]{2,1,0:T(8,128)S(1)}, f32[2,8,8]{2,1,0:T(8,128)S(1)}, u32[]{:S(2)}, u32[]{:S(2)}) collective-permute-start(f32[2,8,8]{2,1,0:T(8,128)S(1)} %shard_map.136), channel_id=1, source_target_pairs={{0,16},{8,24},{16,0},{24,8},{1,17},{9,25},{17,1},{25,9},{2,18},{10... | collective-permute-start | bytes 1544 | tf_op jit(solution)/shard_map/ppermute | solution.py:352
  71.3 4.5 %collective-permute-start.21 = (f32[2,8,8]{2,1,0:T(8,128)S(1)}, f32[2,8,8]{2,1,0:T(8,128)S(1)}, u32[]{:S(2)}, u32[]{:S(2)}) collective-permute-start(f32[2,8,8]{2,1,0:T(8,128)S(1)} %shard_map.136), channel_id=1, source_target_pairs={{0,24},{8,16},{16,8},{24,0},{1,25},{9,17},{17,9},{25,1},{2,26},{10... | collective-permute-start | bytes 1544 | tf_op jit(solution)/shard_map/ppermute | solution.py:352
  75.9 4.5 %collective-permute-start.22 = (f32[2,8,8]{2,1,0:T(8,128)S(1)}, f32[2,8,8]{2,1,0:T(8,128)S(1)}, u32[]{:S(2)}, u32[]{:S(2)}) collective-permute-start(f32[2,8,8]{2,1,0:T(8,128)S(1)} %add_add_fusion), channel_id=1, source_target_pairs={{0,1},{1,0},{2,3},{3,2},{4,5},{5,4},{6,7},{7,6},{8,9},{9,8},{10,11... | collective-permute-start | bytes 1544 | tf_op jit(solution)/shard_map/ppermute | solution.py:352
  75.9 5.0 %collective-permute-start.23 = (f32[2,8,8]{2,1,0:T(8,128)S(1)}, f32[2,8,8]{2,1,0:T(8,128)S(1)}, u32[]{:S(2)}, u32[]{:S(2)}) collective-permute-start(f32[2,8,8]{2,1,0:T(8,128)S(1)} %add_add_fusion), channel_id=1, source_target_pairs={{0,2},{1,3},{2,0},{3,1},{4,6},{5,7},{6,4},{7,5},{8,10},{9,11},{10,... | collective-permute-start | bytes 1544 | tf_op jit(solution)/shard_map/ppermute | solution.py:352
  75.9 8.0 %collective-permute-start.24 = (f32[2,8,8]{2,1,0:T(8,128)S(1)}, f32[2,8,8]{2,1,0:T(8,128)S(1)}, u32[]{:S(2)}, u32[]{:S(2)}) collective-permute-start(f32[2,8,8]{2,1,0:T(8,128)S(1)} %add_add_fusion), channel_id=1, source_target_pairs={{0,3},{1,2},{2,1},{3,0},{4,7},{5,6},{6,5},{7,4},{8,11},{9,10},{10,... | collective-permute-start | bytes 1544 | tf_op jit(solution)/shard_map/ppermute | solution.py:352
  77.7 6.2 %collective-permute-start.25 = (f32[2,8,8]{2,1,0:T(8,128)S(1)}, f32[2,8,8]{2,1,0:T(8,128)S(1)}, u32[]{:S(2)}, u32[]{:S(2)}) collective-permute-start(f32[2,8,8]{2,1,0:T(8,128)S(1)} %add_add_fusion), channel_id=1, source_target_pairs={{0,4},{1,5},{2,6},{3,7},{4,0},{5,1},{6,2},{7,3},{8,12},{9,13},{10,... | collective-permute-start | bytes 1544 | tf_op jit(solution)/shard_map/ppermute | solution.py:352
  77.7 6.2 %collective-permute-start.26 = (f32[2,8,8]{2,1,0:T(8,128)S(1)}, f32[2,8,8]{2,1,0:T(8,128)S(1)}, u32[]{:S(2)}, u32[]{:S(2)}) collective-permute-start(f32[2,8,8]{2,1,0:T(8,128)S(1)} %add_add_fusion), channel_id=1, source_target_pairs={{0,5},{1,4},{2,7},{3,6},{4,1},{5,0},{6,3},{7,2},{8,13},{9,12},{10,... | collective-permute-start | bytes 1544 | tf_op jit(solution)/shard_map/ppermute | solution.py:352
  80.3 5.5 %collective-permute-start.27 = (f32[2,8,8]{2,1,0:T(8,128)S(1)}, f32[2,8,8]{2,1,0:T(8,128)S(1)}, u32[]{:S(2)}, u32[]{:S(2)}) collective-permute-start(f32[2,8,8]{2,1,0:T(8,128)S(1)} %add_add_fusion), channel_id=1, source_target_pairs={{0,6},{1,7},{2,4},{3,5},{4,2},{5,3},{6,0},{7,1},{8,14},{9,15},{10,... | collective-permute-start | bytes 1544 | tf_op jit(solution)/shard_map/ppermute | solution.py:352
  80.9 5.0 %collective-permute-start.28 = (f32[2,8,8]{2,1,0:T(8,128)S(1)}, f32[2,8,8]{2,1,0:T(8,128)S(1)}, u32[]{:S(2)}, u32[]{:S(2)}) collective-permute-start(f32[2,8,8]{2,1,0:T(8,128)S(1)} %add_add_fusion), channel_id=1, source_target_pairs={{0,7},{1,6},{2,5},{3,4},{4,3},{5,2},{6,1},{7,0},{8,15},{9,14},{10,... | collective-permute-start | bytes 1544 | tf_op jit(solution)/shard_map/ppermute | solution.py:352

commit v4 on v3

--- a/solution.py
+++ b/solution.py
@@ -108,14 +108,15 @@
 
 SMEM = pl.BlockSpec(memory_space=pltpu.SMEM)
 VMEM = pl.BlockSpec(memory_space=pltpu.VMEM)
-
-
-def call(kernel, out_shape, scalars, arrays, scratch=(), limit=24):
+HBM = pl.BlockSpec(memory_space=pltpu.HBM)
+
+
+def call(kernel, out_shape, scalars, arrays, scratch=(), limit=24, far=False):
     arrays = [pltpu.with_memory_space_constraint(value, pltpu.VMEM) if keep else value for value, keep in arrays]
     return pl.pallas_call(
         kernel,
         out_shape=out_shape,
-        in_specs=[SMEM] * len(scalars) + [VMEM] * len(arrays),
+        in_specs=[SMEM] * len(scalars) + [HBM if far else VMEM] * len(arrays),
         out_specs=[VMEM] * len(out_shape),
         scratch_shapes=list(scratch),
         compiler_params=pltpu.CompilerParams(vmem_limit_bytes=limit * MIB),
@@ -161,7 +162,14 @@
     return total[:size], total[size:]
 
 
-def first_kernel(devices, step, size, me_ref, psi_ref, col_ref, ahead_ref, *outs):
+def first_kernel(devices, step, size, me_ref, *refs):
+    far, refs = refs[:3], refs[3:]
+    outs, (psi_ref, col_ref, ahead_ref, sems) = refs[:devices], refs[devices:]
+    copies = [pltpu.make_async_copy(far[i], refs[devices + i], sems.at[i]) for i in range(3)]
+    for copy in copies:
+        copy.start()
+    for copy in copies:
+        copy.wait()
     inside, _ = sphere(col_ref[...], size)
     parts = [jnp.where(inside, psi_ref[p], 0.0) for p in range(2)]
     to_planes(me_ref[0], parts, ahead_ref, outs, step)
@@ -230,8 +238,12 @@
     imag = jnp.concatenate([v for r in range(rows // 2, rows) for v in lines[r]], axis=1)
     left = jnp.concatenate([real, imag], axis=1).astype(BF16)
     right = jnp.concatenate([imag, -real], axis=1).astype(BF16)
-    sum_ref[0] = dot(left, left, ((1,), (1,)))
-    sum_ref[1] = dot(left, right, ((1,), (1,)))
+    wide = lax.broadcasted_iota(jnp.int32, (bands, 128), 1) < bands
+    for p, other in enumerate((left, right)):
+        tall = jnp.concatenate([other, jnp.zeros((128 - bands, other.shape[1]), BF16)], axis=0)
+        value = jnp.where(wide, dot(left, tall, ((1,), (1,))), 0.0)
+        for g in range(sum_ref.shape[0] // bands):
+            sum_ref[g * bands : (g + 1) * bands, p, :] = value
 
 
 def slab_kernel(devices, size, depth, again, *refs):
@@ -352,9 +364,6 @@
             lax.ppermute(values[k], axis, [(d, step(d, k)) for d in range(size)]) for k in range(1, size)
         ]
 
-    def total(value, axis, size):
-        return functools.reduce(jnp.add, exchange([value] * size, axis))
-
     ahead, back = z_tables(size, devices, pad)
     tables = plane_tables(size)
     count = 2 * radius + 1
@@ -379,6 +388,13 @@
             [vmem((rows + 8, cols))] * devices,
             [me_arg],
             [(psi_t, False), (col_row, False), (ahead, False)],
+            [
+                pltpu.VMEM(psi_t.shape, F32),
+                pltpu.VMEM(col_row.shape, jnp.int32),
+                pltpu.VMEM(ahead.shape, BF16),
+                pltpu.SemaphoreType.DMA((3,)),
+            ],
+            far=True,
         )
     )
 
@@ -419,14 +435,14 @@
     )
     (partial_sum,) = call(
         functools.partial(gram_kernel, bands, step),
-        [vmem((2, bands, bands))],
+        [vmem((devices * bands, 8, 128))],
         [band_arg],
         [(value, True) for value in exchange(packed, "band")],
         [pltpu.VMEM((cols // 128, bands * 2 * slots, 128), F32)],
     )
-    sums = total(total(partial_sum, "grid", devices), "band", bands)
+    sums = jnp.sum(lax.all_to_all(partial_sum, ("grid", "band"), 0, 0, tiled=True), axis=0)
     own = bands // devices
-    gram = lax.dynamic_slice(sums, (0, band, me * own), (2, 1, own)) / (4.0 * radius**3)
+    gram = lax.dynamic_slice(sums, (0, me * own), (2, own)).reshape(2, 1, own) / (4.0 * radius**3)
     return jnp.transpose(filtered, (0, 2, 1)).reshape(psi.shape), gram
 
 

time: 86.8 us -> 81.9 us (0.944)
  starting transfers between devices: 35 us -> 26 us
  waiting for transfers between devices: 24.3 us -> 27.2 us
  Pallas kernels: 20 us -> 21.2 us
    ppermute x29 -> x19, starting transfers between devices: 35 us -> 23.4 us  [exchange(): lax.ppermute(values[k], axis, [(d, step(d, k)) for d in range(size)])]
    all_to_all x0 -> x1, waiting for transfers between devices: none -> 8.17 us  [body(): lax.all_to_all(partial_sum, ('grid', 'band'), 0, 0, tiled=True)]
    ppermute x29 -> x19, waiting for transfers between devices: 24.3 us -> 19 us  [exchange(): lax.ppermute(values[k], axis, [(d, step(d, k)) for d in range(size)])]
    all_to_all x0 -> x1, starting transfers between devices: none -> 2.57 us  [body(): lax.all_to_all(partial_sum, ('grid', 'band'), 0, 0, tiled=True)]
    pallas_call x6, Pallas kernels: 20 us -> 21.2 us  [call(): pl.pallas_call(kernel, out_shape=out_shape, in_specs=[SMEM] * len(scalars...]
  transfers between devices with their start and end apart: 29 -> 20, of which waited for: 19 -> 16; matrix products, arithmetic and copies ran while one was open for 2% -> 2% of each run, Pallas kernels for 0% -> 0%
where the time goes in v4:
time: 81.9 us; the launch traced here: 81.6 us
  waiting for transfers between devices  27.2 us (33%)
  starting transfers between devices  26 us (32%)
  Pallas kernels  21.2 us (26%)
  local copies, waits for them, and re-layouts  3.22 us (4%)
  between operations  2.12 us (3%)
  other arithmetic  1.92 us (2%)
    ppermute x19, starting transfers between devices, exchange(): lax.ppermute(values[k], axis, [(d, step(d, k)) for d in range(size)])  23.4 us
    pallas_call x6, Pallas kernels, call(): pl.pallas_call(kernel, out_shape=out_shape, in_specs=[SMEM] * len(scalars...  21.2 us
    ppermute x19, waiting for transfers between devices, exchange(): lax.ppermute(values[k], axis, [(d, step(d, k)) for d in range(size)])  19 us
    all_to_all x1, waiting for transfers between devices, body(): lax.all_to_all(partial_sum, ('grid', 'band'), 0, 0, tiled=True)  8.17 us
    unnamed x24, local copies, waits for them, and re-layouts  2.67 us
    all_to_all x1, starting transfers between devices, body(): lax.all_to_all(partial_sum, ('grid', 'band'), 0, 0, tiled=True)  2.57 us
  transfers between devices with their start and end apart: 20, of which 16 were waited for; matrix products, arithmetic and copies ran while one was open for 2% of the time, Pallas kernels for 0%

profile of v4, /device:TPU:0, one launch (start us, length us, event | category | flops | bytes accessed | tf_op | source)
XLA Modules:
  0.0 81.6 jit_solution(10123973372794092057)
XLA Ops:
  0.6 0.0 copy-start
  0.6 1.0 %copy-done = f32[2,1,512,96]{2,3,1,0:T(8,128)S(1)} copy-done((f32[2,1,512,96]{2,3,1,0:T(8,128)S(1)}, f32[2,1,512,96]{2,3,1,0:T(8,128)}, u32[]{:S(2)}) %copy-start) | copy-done | bytes 393240
  1.6 0.9 %copy-done.3 = bf16[4,48,576]{2,1,0:T(8,128)(2,1)S(1)} copy-done((bf16[4,48,576]{2,1,0:T(8,128)(2,1)S(1)}, bf16[4,48,576]{2,1,0:T(8,128)(2,1)}, u32[]{:S(2)}) %copy-start.3) | copy-done | bytes 221208
  2.6 0.7 copy-done.10
  3.3 1.0 %shard_map.131 = (f32[56,512]{1,0:T(8,128)S(1)}, f32[56,512]{1,0:T(8,128)S(1)}, f32[56,512]{1,0:T(8,128)S(1)}, f32[56,512]{1,0:T(8,128)S(1)}) custom-call(s32[1]{0:T(128)} %bitcast.me_ref, f32[2,96,512]{2,1,0:T(8,128)S(1)} %bitcast.14, s32[1,512]{1,0:T(1,128)S(1)} %bitcast.17, bf16[4,48,576]{2,1,0:T(8,128)(2,1)S(1)} %copy-done.3), custom_call_target="tpu_custom_call" | custom-call | tf_op jit(solution)/shard_map/pallas_call | solution.py:116
  4.3 3.0 %collective-permute-start = (f32[56,512]{1,0:T(8,128)S(1)}, f32[56,512]{1,0:T(8,128)S(1)}, u32[]{:S(2)}, u32[]{:S(2)}) collective-permute-start(f32[56,512]{1,0:T(8,128)S(1)} %get-tuple-element.29), channel_id=1, source_target_pairs={{0,8},{8,0},{16,24},{24,16},{1,9},{9,1},{17,25},{25,17},{2,10},{10... | collective-permute-start | bytes 344072 | tf_op jit(solution)/shard_map/ppermute | solution.py:364
  7.3 1.5 %collective-permute-start.1 = (f32[56,512]{1,0:T(8,128)S(1)}, f32[56,512]{1,0:T(8,128)S(1)}, u32[]{:S(2)}, u32[]{:S(2)}) collective-permute-start(f32[56,512]{1,0:T(8,128)S(1)} %get-tuple-element.30), channel_id=1, source_target_pairs={{0,16},{8,24},{16,0},{24,8},{1,17},{9,25},{17,1},{25,9},{2,18},{10... | collective-permute-start | bytes 344072 | tf_op jit(solution)/shard_map/ppermute | solution.py:364
  8.8 0.0 collective-permute-start.2
  8.8 1.2 %broadcast_multiply_fusion = f32[24,9216]{1,0:T(8,128)S(1)} fusion(f32[24,9216]{1,0:T(8,128)} %param.14), kind=kLoop, calls=%fused_computation | loop fusion | flops 221184 | bytes 1769472 | tf_op jit(solution)/shard_map/mul | solution.py:377
  10.1 0.5 reshape.28
  10.6 0.0 copy-start.5
  10.6 0.0 copy-start.6
  10.6 0.0 copy-start.7
  10.6 0.0 copy-start.8
  10.6 0.1 pad.4.refs_4_.refs_8_
  10.7 0.0 copy-start.1
  10.7 0.0 copy-start.2
  10.7 0.0 copy-start.4
  10.7 0.0 copy-start.11
  10.8 0.1 collective-permute-done.refs_1_.refs_5_
  10.8 2.8 %collective-permute-done.1.refs_2_.refs_6_ = f32[56,512]{1,0:T(8,128)S(1)} collective-permute-done((f32[56,512]{1,0:T(8,128)S(1)}, f32[56,512]{1,0:T(8,128)S(1)}, u32[]{:S(2)}, u32[]{:S(2)}) %collective-permute-start.1) | collective-permute-done | bytes 114720 | tf_op jit(solution)/shard_map/ppermute | solution.py:364
  13.6 0.9 %collective-permute-done.2.refs_3_.refs_7_ = f32[56,512]{1,0:T(8,128)S(1)} collective-permute-done((f32[56,512]{1,0:T(8,128)S(1)}, f32[56,512]{1,0:T(8,128)S(1)}, u32[]{:S(2)}, u32[]{:S(2)}) %collective-permute-start.2) | collective-permute-done | bytes 114720 | tf_op jit(solution)/shard_map/ppermute | solution.py:364
  14.6 0.0 copy-done.6
  14.6 8.6 %shard_map.132 = (f32[48,512]{1,0:T(8,128)S(1)}, f32[48,512]{1,0:T(8,128)S(1)}, f32[48,512]{1,0:T(8,128)S(1)}, f32[48,512]{1,0:T(8,128)S(1)}) custom-call(f32[56,512]{1,0:T(8,128)S(1)} %get-tuple-element.28.refs_0_.refs_4_, f32[56,512]{1,0:T(8,128)S(1)} %collective-permute-done.refs_1_.refs_5_, f32[56,512]{1,0:T(8,128)S(1)} %collective-permute-done.1.refs_2_.refs_6_, ...), custom_call_target="tpu_custom_call" | custom-call | tf_op jit(solution)/shard_map/pallas_call | solution.py:116
  23.1 1.1 %collective-permute-start.3 = (f32[48,512]{1,0:T(8,128)S(1)}, f32[48,512]{1,0:T(8,128)S(1)}, u32[]{:S(2)}, u32[]{:S(2)}) collective-permute-start(f32[48,512]{1,0:T(8,128)S(1)} %get-tuple-element.33), channel_id=1, source_target_pairs={{0,8},{8,0},{16,24},{24,16},{1,9},{9,1},{17,25},{25,17},{2,10},{10... | collective-permute-start | bytes 294920 | tf_op jit(solution)/shard_map/ppermute | solution.py:364
  24.2 0.8 %collective-permute-start.4 = (f32[48,512]{1,0:T(8,128)S(1)}, f32[48,512]{1,0:T(8,128)S(1)}, u32[]{:S(2)}, u32[]{:S(2)}) collective-permute-start(f32[48,512]{1,0:T(8,128)S(1)} %get-tuple-element.34), channel_id=1, source_target_pairs={{0,16},{8,24},{16,0},{24,8},{1,17},{9,25},{17,1},{25,9},{2,18},{10... | collective-permute-start | bytes 294920 | tf_op jit(solution)/shard_map/ppermute | solution.py:364
  25.1 1.6 %collective-permute-start.5 = (f32[48,512]{1,0:T(8,128)S(1)}, f32[48,512]{1,0:T(8,128)S(1)}, u32[]{:S(2)}, u32[]{:S(2)}) collective-permute-start(f32[48,512]{1,0:T(8,128)S(1)} %get-tuple-element.35), channel_id=1, source_target_pairs={{0,24},{8,16},{16,8},{24,0},{1,25},{9,17},{17,9},{25,1},{2,26},{10... | collective-permute-start | bytes 294920 | tf_op jit(solution)/shard_map/ppermute | solution.py:364
  28.0 0.8 collective-permute-done.3.refs_1_
  28.8 0.1 collective-permute-done.4.refs_2_
  28.9 1.7 %collective-permute-done.5.refs_3_ = f32[48,512]{1,0:T(8,128)S(1)} collective-permute-done((f32[48,512]{1,0:T(8,128)S(1)}, f32[48,512]{1,0:T(8,128)S(1)}, u32[]{:S(2)}, u32[]{:S(2)}) %collective-permute-start.5) | collective-permute-done | bytes 98336 | tf_op jit(solution)/shard_map/ppermute | solution.py:364
  30.6 0.0 copy-done.2
  30.6 0.7 shard_map.133
  31.3 1.6 %collective-permute-start.6 = (f32[48,512]{1,0:T(8,128)S(1)}, f32[48,512]{1,0:T(8,128)S(1)}, u32[]{:S(2)}, u32[]{:S(2)}) collective-permute-start(f32[48,512]{1,0:T(8,128)S(1)} %get-tuple-element.37), channel_id=1, source_target_pairs={{0,8},{8,0},{16,24},{24,16},{1,9},{9,1},{17,25},{25,17},{2,10},{10... | collective-permute-start | bytes 294920 | tf_op jit(solution)/shard_map/ppermute | solution.py:364
  32.9 0.7 collective-permute-start.7
  33.6 1.3 %collective-permute-start.8 = (f32[48,512]{1,0:T(8,128)S(1)}, f32[48,512]{1,0:T(8,128)S(1)}, u32[]{:S(2)}, u32[]{:S(2)}) collective-permute-start(f32[48,512]{1,0:T(8,128)S(1)} %get-tuple-element.39), channel_id=1, source_target_pairs={{0,24},{8,16},{16,8},{24,0},{1,25},{9,17},{17,9},{25,1},{2,26},{10... | collective-permute-start | bytes 294920 | tf_op jit(solution)/shard_map/ppermute | solution.py:364
  34.9 1.1 %collective-permute-done.6.refs_1_ = f32[48,512]{1,0:T(8,128)S(1)} collective-permute-done((f32[48,512]{1,0:T(8,128)S(1)}, f32[48,512]{1,0:T(8,128)S(1)}, u32[]{:S(2)}, u32[]{:S(2)}) %collective-permute-start.6) | collective-permute-done | bytes 98336 | tf_op jit(solution)/shard_map/ppermute | solution.py:364
  36.0 1.5 %collective-permute-done.7.refs_2_ = f32[48,512]{1,0:T(8,128)S(1)} collective-permute-done((f32[48,512]{1,0:T(8,128)S(1)}, f32[48,512]{1,0:T(8,128)S(1)}, u32[]{:S(2)}, u32[]{:S(2)}) %collective-permute-start.7) | collective-permute-done | bytes 98336 | tf_op jit(solution)/shard_map/ppermute | solution.py:364
  37.5 1.6 %collective-permute-done.8.refs_3_ = f32[48,512]{1,0:T(8,128)S(1)} collective-permute-done((f32[48,512]{1,0:T(8,128)S(1)}, f32[48,512]{1,0:T(8,128)S(1)}, u32[]{:S(2)}, u32[]{:S(2)}) %collective-permute-start.8) | collective-permute-done | bytes 98336 | tf_op jit(solution)/shard_map/ppermute | solution.py:364
  39.1 8.7 %shard_map.134 = (f32[48,512]{1,0:T(8,128)S(1)}, f32[48,512]{1,0:T(8,128)S(1)}, f32[48,512]{1,0:T(8,128)S(1)}, f32[48,512]{1,0:T(8,128)S(1)}) custom-call(f32[48,512]{1,0:T(8,128)S(1)} %get-tuple-element.36.refs_0_, f32[48,512]{1,0:T(8,128)S(1)} %collective-permute-done.6.refs_1_, f32[48,512]{1,0:T(8,128)S(1)} %collective-permute-done.7.refs_2_, ...), custom_call_target="tpu_custom_call" | custom-call | tf_op jit(solution)/shard_map/pallas_call | solution.py:116
  47.8 1.4 %collective-permute-start.10 = (f32[48,512]{1,0:T(8,128)S(1)}, f32[48,512]{1,0:T(8,128)S(1)}, u32[]{:S(2)}, u32[]{:S(2)}) collective-permute-start(f32[48,512]{1,0:T(8,128)S(1)} %get-tuple-element.42), channel_id=1, source_target_pairs={{0,16},{8,24},{16,0},{24,8},{1,17},{9,25},{17,1},{25,9},{2,18},{10... | collective-permute-start | bytes 294920 | tf_op jit(solution)/shard_map/ppermute | solution.py:364
  49.2 1.2 %collective-permute-start.11 = (f32[48,512]{1,0:T(8,128)S(1)}, f32[48,512]{1,0:T(8,128)S(1)}, u32[]{:S(2)}, u32[]{:S(2)}) collective-permute-start(f32[48,512]{1,0:T(8,128)S(1)} %get-tuple-element.43), channel_id=1, source_target_pairs={{0,24},{8,16},{16,8},{24,0},{1,25},{9,17},{17,9},{25,1},{2,26},{10... | collective-permute-start | bytes 294920 | tf_op jit(solution)/shard_map/ppermute | solution.py:364
  50.4 1.0 %collective-permute-start.9 = (f32[48,512]{1,0:T(8,128)S(1)}, f32[48,512]{1,0:T(8,128)S(1)}, u32[]{:S(2)}, u32[]{:S(2)}) collective-permute-start(f32[48,512]{1,0:T(8,128)S(1)} %get-tuple-element.41), channel_id=1, source_target_pairs={{0,8},{8,0},{16,24},{24,16},{1,9},{9,1},{17,25},{25,17},{2,10},{10... | collective-permute-start | bytes 294920 | tf_op jit(solution)/shard_map/ppermute | solution.py:364
  51.4 1.1 %collective-permute-done.10.refs_2_ = f32[48,512]{1,0:T(8,128)S(1)} collective-permute-done((f32[48,512]{1,0:T(8,128)S(1)}, f32[48,512]{1,0:T(8,128)S(1)}, u32[]{:S(2)}, u32[]{:S(2)}) %collective-permute-start.10) | collective-permute-done | bytes 98336 | tf_op jit(solution)/shard_map/ppermute | solution.py:364
  52.5 2.2 %collective-permute-done.11.refs_3_ = f32[48,512]{1,0:T(8,128)S(1)} collective-permute-done((f32[48,512]{1,0:T(8,128)S(1)}, f32[48,512]{1,0:T(8,128)S(1)}, u32[]{:S(2)}, u32[]{:S(2)}) %collective-permute-start.11) | collective-permute-done | bytes 98336 | tf_op jit(solution)/shard_map/ppermute | solution.py:364
  54.8 0.3 collective-permute-done.9.refs_1_
  55.0 1.2 %shard_map.135 = (f32[2,96,512]{2,1,0:T(8,128)}, bf16[16,512]{1,0:T(8,128)(2,1)S(1)}, bf16[16,512]{1,0:T(8,128)(2,1)S(1)}, bf16[16,512]{1,0:T(8,128)(2,1)S(1)}, ...) custom-call(s32[1]{0:T(128)} %bitcast.me_ref, ...), custom_call_target="tpu_custom_call" | custom-call | tf_op jit(solution)/shard_map/pallas_call | solution.py:116
  56.2 0.0 collective-permute-start.12
  56.2 1.6 %collective-permute-start.13 = (bf16[16,512]{1,0:T(8,128)(2,1)S(1)}, bf16[16,512]{1,0:T(8,128)(2,1)S(1)}, u32[]{:S(2)}, u32[]{:S(2)}) collective-permute-start(bf16[16,512]{1,0:T(8,128)(2,1)S(1)} %get-tuple-element.48), channel_id=1, source_target_pairs={{0,2},{1,3},{2,0},{3,1},{4,6},{5,7},{6,4},{7,5},{8,10},{9,11},{10,... | collective-permute-start | bytes 49160 | tf_op jit(solution)/shard_map/ppermute | solution.py:364
  57.8 0.3 collective-permute-start.14
  58.1 2.6 %collective-permute-start.15 = (bf16[16,512]{1,0:T(8,128)(2,1)S(1)}, bf16[16,512]{1,0:T(8,128)(2,1)S(1)}, u32[]{:S(2)}, u32[]{:S(2)}) collective-permute-start(bf16[16,512]{1,0:T(8,128)(2,1)S(1)} %get-tuple-element.50), channel_id=1, source_target_pairs={{0,4},{1,5},{2,6},{3,7},{4,0},{5,1},{6,2},{7,3},{8,12},{9,13},{10,... | collective-permute-start | bytes 49160 | tf_op jit(solution)/shard_map/ppermute | solution.py:364
  60.7 0.0 collective-permute-start.16
  60.7 0.0 collective-permute-done.12.refs_1_
  60.7 3.5 %collective-permute-start.17 = (bf16[16,512]{1,0:T(8,128)(2,1)S(1)}, bf16[16,512]{1,0:T(8,128)(2,1)S(1)}, u32[]{:S(2)}, u32[]{:S(2)}) collective-permute-start(bf16[16,512]{1,0:T(8,128)(2,1)S(1)} %get-tuple-element.52), channel_id=1, source_target_pairs={{0,6},{1,7},{2,4},{3,5},{4,2},{5,3},{6,0},{7,1},{8,14},{9,15},{10,... | collective-permute-start | bytes 49160 | tf_op jit(solution)/shard_map/ppermute | solution.py:364
  64.2 0.0 collective-permute-done.13.refs_2_
  64.2 0.2 collective-permute-start.18
  64.4 0.0 collective-permute-done.14.refs_3_
  64.4 0.0 collective-permute-done.15.refs_4_
  64.4 0.3 collective-permute-done.16.refs_5_
  64.7 1.5 %collective-permute-done.17.refs_6_ = bf16[16,512]{1,0:T(8,128)(2,1)S(1)} collective-permute-done((bf16[16,512]{1,0:T(8,128)(2,1)S(1)}, bf16[16,512]{1,0:T(8,128)(2,1)S(1)}, u32[]{:S(2)}, u32[]{:S(2)}) %collective-permute-start.17) | collective-permute-done | bytes 16416 | tf_op jit(solution)/shard_map/ppermute | solution.py:364
  66.3 2.9 %collective-permute-done.18.refs_7_ = bf16[16,512]{1,0:T(8,128)(2,1)S(1)} collective-permute-done((bf16[16,512]{1,0:T(8,128)(2,1)S(1)}, bf16[16,512]{1,0:T(8,128)(2,1)S(1)}, u32[]{:S(2)}, u32[]{:S(2)}) %collective-permute-start.18) | collective-permute-done | bytes 16416 | tf_op jit(solution)/shard_map/ppermute | solution.py:364
  69.2 1.0 %shard_map.136 = f32[32,8,128]{2,1,0:T(8,128)} custom-call(s32[1]{0:T(128)} %bitcast.1.band_ref, bf16[16,512]{1,0:T(8,128)(2,1)S(1)} %get-tuple-element.46.refs_0_, bf16[16,512]{1,0:T(8,128)(2,1)S(1)} %collective-permute-done.12.refs_1_, bf16[16,512]{1,0:T(8,128)(2,1)S(1)} %collective-permute-done.13.refs_2_, ...), custom_call_target="tpu_custom_call" | custom-call | tf_op jit(solution)/shard_map/pallas_call | solution.py:116
  70.2 2.6 %all-to-all-start = ((f32[32,8,128]{2,1,0:T(8,128)}), f32[32,8,128]{2,1,0:T(8,128)S(1)}, u32[]{:S(2)}, u32[]{:S(2)}) async-start(f32[32,8,128]{2,1,0:T(8,128)} %shard_map.136), calls=%async_computation | async-start | bytes 262144 | tf_op jit(solution)/shard_map/all_to_all | solution.py:443
  72.8 8.2 %all-to-all-done = f32[32,8,128]{2,1,0:T(8,128)S(1)} async-done(((f32[32,8,128]{2,1,0:T(8,128)}), f32[32,8,128]{2,1,0:T(8,128)S(1)}, u32[]{:S(2)}, u32[]{:S(2)}) %all-to-all-start) | async-done | bytes 131104 | tf_op jit(solution)/shard_map/all_to_all | solution.py:443
  81.0 0.6 dynamic-slice_multiply_fusion
  (11 shorter events, 0.1 us)
Async XLA Ops:
  0.6 1.0 %copy-start = (f32[2,1,512,96]{2,3,1,0:T(8,128)S(1)}, f32[2,1,512,96]{2,3,1,0:T(8,128)}, u32[]{:S(2)}) copy-start(f32[2,1,512,96]{2,3,1,0:T(8,128)} %param.12) | copy-start | bytes 1179652
  1.6 0.9 %copy-start.3 = (bf16[4,48,576]{2,1,0:T(8,128)(2,1)S(1)}, bf16[4,48,576]{2,1,0:T(8,128)(2,1)}, u32[]{:S(2)}) copy-start(bf16[4,48,576]{2,1,0:T(8,128)(2,1)} %constant.36.clone.refs_2_.refs_6_) | copy-start | bytes 663556
  2.6 0.7 copy-start.10
  4.3 6.6 %collective-permute-start = (f32[56,512]{1,0:T(8,128)S(1)}, f32[56,512]{1,0:T(8,128)S(1)}, u32[]{:S(2)}, u32[]{:S(2)}) collective-permute-start(f32[56,512]{1,0:T(8,128)S(1)} %get-tuple-element.29), channel_id=1, source_target_pairs={{0,8},{8,0},{16,24},{24,16},{1,9},{9,1},{17,25},{25,17},{2,10},{10... | collective-permute-start | bytes 344072 | tf_op jit(solution)/shard_map/ppermute | solution.py:364
  7.3 6.3 %collective-permute-start.1 = (f32[56,512]{1,0:T(8,128)S(1)}, f32[56,512]{1,0:T(8,128)S(1)}, u32[]{:S(2)}, u32[]{:S(2)}) collective-permute-start(f32[56,512]{1,0:T(8,128)S(1)} %get-tuple-element.30), channel_id=1, source_target_pairs={{0,16},{8,24},{16,0},{24,8},{1,17},{9,25},{17,1},{25,9},{2,18},{10... | collective-permute-start | bytes 344072 | tf_op jit(solution)/shard_map/ppermute | solution.py:364
  8.8 5.7 %collective-permute-start.2 = (f32[56,512]{1,0:T(8,128)S(1)}, f32[56,512]{1,0:T(8,128)S(1)}, u32[]{:S(2)}, u32[]{:S(2)}) collective-permute-start(f32[56,512]{1,0:T(8,128)S(1)} %get-tuple-element.31), channel_id=1, source_target_pairs={{0,24},{8,16},{16,8},{24,0},{1,25},{9,17},{17,9},{25,1},{2,26},{10... | collective-permute-start | bytes 344072 | tf_op jit(solution)/shard_map/ppermute | solution.py:364
  10.6 4.0 %copy-start.5 = (bf16[384,256]{1,0:T(8,128)(2,1)S(1)}, bf16[384,256]{1,0:T(8,128)(2,1)}, u32[]{:S(2)}) copy-start(bf16[384,256]{1,0:T(8,128)(2,1)} %constant.37.clone.refs_5_.refs_9_) | copy-start | bytes 589828
  10.6 4.0 %copy-start.6 = (bf16[768,128]{1,0:T(8,128)(2,1)S(1)}, bf16[768,128]{1,0:T(8,128)(2,1)}, u32[]{:S(2)}) copy-start(bf16[768,128]{1,0:T(8,128)(2,1)} %constant.40.clone.refs_8_.refs_12_) | copy-start | bytes 589828
  10.6 4.0 %copy-start.7 = (bf16[192,336]{1,0:T(8,128)(2,1)S(1)}, bf16[192,336]{1,0:T(8,128)(2,1)}, u32[]{:S(2)}) copy-start(bf16[192,336]{1,0:T(8,128)(2,1)} %constant.38.clone.refs_6_.refs_10_) | copy-start | bytes 387076
  10.6 4.0 %copy-start.8 = (bf16[112,576]{1,0:T(8,128)(2,1)S(1)}, bf16[112,576]{1,0:T(8,128)(2,1)}, u32[]{:S(2)}) copy-start(bf16[112,576]{1,0:T(8,128)(2,1)} %constant.39.clone.refs_7_.refs_11_) | copy-start | bytes 387076
  10.7 19.9 %copy-start.1 = (f32[2,1,512,96]{2,3,1,0:T(8,128)S(1)}, f32[2,1,512,96]{2,3,1,0:T(8,128)}, u32[]{:S(2)}) copy-start(f32[2,1,512,96]{2,3,1,0:T(8,128)} %param.12) | copy-start | bytes 1179652
  10.7 19.9 %copy-start.2 = (bf16[192,576]{1,0:T(8,128)(2,1)S(1)}, bf16[192,576]{1,0:T(8,128)(2,1)}, u32[]{:S(2)}) copy-start(bf16[192,576]{1,0:T(8,128)(2,1)} %constant.41.clone.refs_7_) | copy-start | bytes 663556
  10.7 19.9 %copy-start.4 = (bf16[4,48,576]{2,1,0:T(8,128)(2,1)S(1)}, bf16[4,48,576]{2,1,0:T(8,128)(2,1)}, u32[]{:S(2)}) copy-start(bf16[4,48,576]{2,1,0:T(8,128)(2,1)} %constant.36.clone.refs_2_.refs_6_) | copy-start | bytes 663556
  10.7 19.9 %copy-start.11 = (s32[512]{0:T(512)S(1)}, s32[512]{0:T(512)}, u32[]{:S(2)}) copy-start(s32[512]{0:T(512)} %param.13) | copy-start | bytes 6148
  23.1 5.7 %collective-permute-start.3 = (f32[48,512]{1,0:T(8,128)S(1)}, f32[48,512]{1,0:T(8,128)S(1)}, u32[]{:S(2)}, u32[]{:S(2)}) collective-permute-start(f32[48,512]{1,0:T(8,128)S(1)} %get-tuple-element.33), channel_id=1, source_target_pairs={{0,8},{8,0},{16,24},{24,16},{1,9},{9,1},{17,25},{25,17},{2,10},{10... | collective-permute-start | bytes 294920 | tf_op jit(solution)/shard_map/ppermute | solution.py:364
  24.2 4.7 %collective-permute-start.4 = (f32[48,512]{1,0:T(8,128)S(1)}, f32[48,512]{1,0:T(8,128)S(1)}, u32[]{:S(2)}, u32[]{:S(2)}) collective-permute-start(f32[48,512]{1,0:T(8,128)S(1)} %get-tuple-element.34), channel_id=1, source_target_pairs={{0,16},{8,24},{16,0},{24,8},{1,17},{9,25},{17,1},{25,9},{2,18},{10... | collective-permute-start | bytes 294920 | tf_op jit(solution)/shard_map/ppermute | solution.py:364
  25.1 5.5 %collective-permute-start.5 = (f32[48,512]{1,0:T(8,128)S(1)}, f32[48,512]{1,0:T(8,128)S(1)}, u32[]{:S(2)}, u32[]{:S(2)}) collective-permute-start(f32[48,512]{1,0:T(8,128)S(1)} %get-tuple-element.35), channel_id=1, source_target_pairs={{0,24},{8,16},{16,8},{24,0},{1,25},{9,17},{17,9},{25,1},{2,26},{10... | collective-permute-start | bytes 294920 | tf_op jit(solution)/shard_map/ppermute | solution.py:364
  31.3 4.7 %collective-permute-start.6 = (f32[48,512]{1,0:T(8,128)S(1)}, f32[48,512]{1,0:T(8,128)S(1)}, u32[]{:S(2)}, u32[]{:S(2)}) collective-permute-start(f32[48,512]{1,0:T(8,128)S(1)} %get-tuple-element.37), channel_id=1, source_target_pairs={{0,8},{8,0},{16,24},{24,16},{1,9},{9,1},{17,25},{25,17},{2,10},{10... | collective-permute-start | bytes 294920 | tf_op jit(solution)/shard_map/ppermute | solution.py:364
  32.9 4.6 %collective-permute-start.7 = (f32[48,512]{1,0:T(8,128)S(1)}, f32[48,512]{1,0:T(8,128)S(1)}, u32[]{:S(2)}, u32[]{:S(2)}) collective-permute-start(f32[48,512]{1,0:T(8,128)S(1)} %get-tuple-element.38), channel_id=1, source_target_pairs={{0,16},{8,24},{16,0},{24,8},{1,17},{9,25},{17,1},{25,9},{2,18},{10... | collective-permute-start | bytes 294920 | tf_op jit(solution)/shard_map/ppermute | solution.py:364
  33.6 5.5 %collective-permute-start.8 = (f32[48,512]{1,0:T(8,128)S(1)}, f32[48,512]{1,0:T(8,128)S(1)}, u32[]{:S(2)}, u32[]{:S(2)}) collective-permute-start(f32[48,512]{1,0:T(8,128)S(1)} %get-tuple-element.39), channel_id=1, source_target_pairs={{0,24},{8,16},{16,8},{24,0},{1,25},{9,17},{17,9},{25,1},{2,26},{10... | collective-permute-start | bytes 294920 | tf_op jit(solution)/shard_map/ppermute | solution.py:364
  39.1 15.9 %copy-start.9 = (bf16[2,128,96]{2,1,0:T(8,128)(2,1)S(1)}, bf16[2,128,96]{2,1,0:T(8,128)(2,1)}, u32[]{:S(2)}) copy-start(bf16[2,128,96]{2,1,0:T(8,128)(2,1)} %constant.42.clone.refs_8_) | copy-start | bytes 147460
  47.8 4.7 %collective-permute-start.10 = (f32[48,512]{1,0:T(8,128)S(1)}, f32[48,512]{1,0:T(8,128)S(1)}, u32[]{:S(2)}, u32[]{:S(2)}) collective-permute-start(f32[48,512]{1,0:T(8,128)S(1)} %get-tuple-element.42), channel_id=1, source_target_pairs={{0,16},{8,24},{16,0},{24,8},{1,17},{9,25},{17,1},{25,9},{2,18},{10... | collective-permute-start | bytes 294920 | tf_op jit(solution)/shard_map/ppermute | solution.py:364
  49.2 5.5 %collective-permute-start.11 = (f32[48,512]{1,0:T(8,128)S(1)}, f32[48,512]{1,0:T(8,128)S(1)}, u32[]{:S(2)}, u32[]{:S(2)}) collective-permute-start(f32[48,512]{1,0:T(8,128)S(1)} %get-tuple-element.43), channel_id=1, source_target_pairs={{0,24},{8,16},{16,8},{24,0},{1,25},{9,17},{17,9},{25,1},{2,26},{10... | collective-permute-start | bytes 294920 | tf_op jit(solution)/shard_map/ppermute | solution.py:364
  50.4 4.6 %collective-permute-start.9 = (f32[48,512]{1,0:T(8,128)S(1)}, f32[48,512]{1,0:T(8,128)S(1)}, u32[]{:S(2)}, u32[]{:S(2)}) collective-permute-start(f32[48,512]{1,0:T(8,128)S(1)} %get-tuple-element.41), channel_id=1, source_target_pairs={{0,8},{8,0},{16,24},{24,16},{1,9},{9,1},{17,25},{25,17},{2,10},{10... | collective-permute-start | bytes 294920 | tf_op jit(solution)/shard_map/ppermute | solution.py:364
  56.2 4.5 %collective-permute-start.12 = (bf16[16,512]{1,0:T(8,128)(2,1)S(1)}, bf16[16,512]{1,0:T(8,128)(2,1)S(1)}, u32[]{:S(2)}, u32[]{:S(2)}) collective-permute-start(bf16[16,512]{1,0:T(8,128)(2,1)S(1)} %get-tuple-element.47), channel_id=1, source_target_pairs={{0,1},{1,0},{2,3},{3,2},{4,5},{5,4},{6,7},{7,6},{8,9},{9,8},{10,11... | collective-permute-start | bytes 49160 | tf_op jit(solution)/shard_map/ppermute | solution.py:364
  56.2 8.0 %collective-permute-start.13 = (bf16[16,512]{1,0:T(8,128)(2,1)S(1)}, bf16[16,512]{1,0:T(8,128)(2,1)S(1)}, u32[]{:S(2)}, u32[]{:S(2)}) collective-permute-start(bf16[16,512]{1,0:T(8,128)(2,1)S(1)} %get-tuple-element.48), channel_id=1, source_target_pairs={{0,2},{1,3},{2,0},{3,1},{4,6},{5,7},{6,4},{7,5},{8,10},{9,11},{10,... | collective-permute-start | bytes 49160 | tf_op jit(solution)/shard_map/ppermute | solution.py:364
  57.8 6.6 %collective-permute-start.14 = (bf16[16,512]{1,0:T(8,128)(2,1)S(1)}, bf16[16,512]{1,0:T(8,128)(2,1)S(1)}, u32[]{:S(2)}, u32[]{:S(2)}) collective-permute-start(bf16[16,512]{1,0:T(8,128)(2,1)S(1)} %get-tuple-element.49), channel_id=1, source_target_pairs={{0,3},{1,2},{2,1},{3,0},{4,7},{5,6},{6,5},{7,4},{8,11},{9,10},{10,... | collective-permute-start | bytes 49160 | tf_op jit(solution)/shard_map/ppermute | solution.py:364
  58.1 6.3 %collective-permute-start.15 = (bf16[16,512]{1,0:T(8,128)(2,1)S(1)}, bf16[16,512]{1,0:T(8,128)(2,1)S(1)}, u32[]{:S(2)}, u32[]{:S(2)}) collective-permute-start(bf16[16,512]{1,0:T(8,128)(2,1)S(1)} %get-tuple-element.50), channel_id=1, source_target_pairs={{0,4},{1,5},{2,6},{3,7},{4,0},{5,1},{6,2},{7,3},{8,12},{9,13},{10,... | collective-permute-start | bytes 49160 | tf_op jit(solution)/shard_map/ppermute | solution.py:364
  60.7 4.1 %collective-permute-start.16 = (bf16[16,512]{1,0:T(8,128)(2,1)S(1)}, bf16[16,512]{1,0:T(8,128)(2,1)S(1)}, u32[]{:S(2)}, u32[]{:S(2)}) collective-permute-start(bf16[16,512]{1,0:T(8,128)(2,1)S(1)} %get-tuple-element.51), channel_id=1, source_target_pairs={{0,5},{1,4},{2,7},{3,6},{4,1},{5,0},{6,3},{7,2},{8,13},{9,12},{10,... | collective-permute-start | bytes 49160 | tf_op jit(solution)/shard_map/ppermute | solution.py:364
  60.7 5.6 %collective-permute-start.17 = (bf16[16,512]{1,0:T(8,128)(2,1)S(1)}, bf16[16,512]{1,0:T(8,128)(2,1)S(1)}, u32[]{:S(2)}, u32[]{:S(2)}) collective-permute-start(bf16[16,512]{1,0:T(8,128)(2,1)S(1)} %get-tuple-element.52), channel_id=1, source_target_pairs={{0,6},{1,7},{2,4},{3,5},{4,2},{5,3},{6,0},{7,1},{8,14},{9,15},{10,... | collective-permute-start | bytes 49160 | tf_op jit(solution)/shard_map/ppermute | solution.py:364
  64.2 5.0 %collective-permute-start.18 = (bf16[16,512]{1,0:T(8,128)(2,1)S(1)}, bf16[16,512]{1,0:T(8,128)(2,1)S(1)}, u32[]{:S(2)}, u32[]{:S(2)}) collective-permute-start(bf16[16,512]{1,0:T(8,128)(2,1)S(1)} %get-tuple-element.53), channel_id=1, source_target_pairs={{0,7},{1,6},{2,5},{3,4},{4,3},{5,2},{6,1},{7,0},{8,15},{9,14},{10,... | collective-permute-start | bytes 49160 | tf_op jit(solution)/shard_map/ppermute | solution.py:364
  70.2 10.8 %all-to-all-start = ((f32[32,8,128]{2,1,0:T(8,128)}), f32[32,8,128]{2,1,0:T(8,128)S(1)}, u32[]{:S(2)}, u32[]{:S(2)}) async-start(f32[32,8,128]{2,1,0:T(8,128)} %shard_map.136), calls=%async_computation | async-start | bytes 262144 | tf_op jit(solution)/shard_map/all_to_all | solution.py:443

commit v5 on v4

--- a/solution.py
+++ b/solution.py
@@ -72,7 +72,9 @@
     txb = np.zeros((2 * GX, 2 * size))
     txb[:count, :size], txb[:count, size:] = c, s
     txb[GX : GX + count, :size], txb[GX : GX + count, size:] = -s, c
-    return stacked_table(ty, 0), stacked_table(tx, 1), stacked_table(txb, 1), stacked_table(tyb, 0)
+    high, low = halves(tx)
+    tx = np.concatenate([np.concatenate([high, high], 1), np.concatenate([low, 0 * low], 1)], 0)
+    return stacked_table(ty, 0), tx, np.concatenate(halves(txb), 0), stacked_table(tyb, 0)
 
 
 def packing(size):
@@ -112,7 +114,8 @@
 
 
 def call(kernel, out_shape, scalars, arrays, scratch=(), limit=24, far=False):
-    arrays = [pltpu.with_memory_space_constraint(value, pltpu.VMEM) if keep else value for value, keep in arrays]
+    space = pltpu.HBM if far else pltpu.VMEM
+    arrays = [pltpu.with_memory_space_constraint(value, space) if keep else value for value, keep in arrays]
     return pl.pallas_call(
         kernel,
         out_shape=out_shape,
@@ -203,10 +206,9 @@
     to_planes(me_ref[0], parts, ahead_ref, outs, step)
 
 
-def last_kernel(devices, bands, step, band_step, size, me_ref, band_ref, low_ref, up_ref, *refs):
+def last_kernel(devices, bands, step, size, me_ref, low_ref, up_ref, *refs):
     planes, refs = refs[:devices], refs[devices:]
-    psi_ref, first_ref, col_ref, back_ref, pick_ref, filtered_ref = refs[:6]
-    outs, (held, packed) = refs[6 : 6 + bands], refs[6 + bands :]
+    psi_ref, first_ref, col_ref, back_ref, pick_ref, filtered_ref, packed_ref, held = refs
     center = (up_ref[0] + low_ref[0]) / 2.0
     half = (up_ref[0] - low_ref[0]) / 2.0
     inside, kinetic = sphere(col_ref[...], size)
@@ -218,32 +220,28 @@
         filtered_ref[p] = value
         piece = dot(pick_ref[p], value.astype(BF16))
         total = piece if total is None else total + piece
-    packed[...] = total.astype(BF16)
-    rows = packed.shape[0] // bands
+    rows = packed_ref.shape[1]
     for k in range(bands):
-        outs[k][...] = packed[pl.ds(pl.multiple_of(band_step(band_ref[0], k) * rows, 16), rows), :]
-
-
-def gram_kernel(bands, band_step, band_ref, *refs):
-    parts, sum_ref, held = refs[:bands], refs[bands], refs[bands + 1]
-    rows, cols = parts[0].shape
+        packed_ref[k] = total[k * rows : (k + 1) * rows].astype(BF16)
+
+
+def gram_kernel(bands, parts_ref, sum_ref, held):
+    rows, cols = parts_ref.shape[1:]
     blocks = cols // 128
     for k in range(bands):
-        at = pl.multiple_of(band_step(band_ref[0], k) * rows, 16)
-        value = parts[k][...].astype(F32)
+        value = parts_ref[k].astype(F32)
         for j in range(blocks):
-            held[j, pl.ds(at, rows), :] = value[:, 128 * j : 128 * j + 128]
+            held[j, k * rows : (k + 1) * rows, :] = value[:, 128 * j : 128 * j + 128]
     lines = [[held[j, pl.ds(r, bands, stride=rows), :] for j in range(blocks)] for r in range(rows)]
     real = jnp.concatenate([v for r in range(rows // 2) for v in lines[r]], axis=1)
     imag = jnp.concatenate([v for r in range(rows // 2, rows) for v in lines[r]], axis=1)
     left = jnp.concatenate([real, imag], axis=1).astype(BF16)
     right = jnp.concatenate([imag, -real], axis=1).astype(BF16)
-    wide = lax.broadcasted_iota(jnp.int32, (bands, 128), 1) < bands
-    for p, other in enumerate((left, right)):
-        tall = jnp.concatenate([other, jnp.zeros((128 - bands, other.shape[1]), BF16)], axis=0)
-        value = jnp.where(wide, dot(left, tall, ((1,), (1,))), 0.0)
-        for g in range(sum_ref.shape[0] // bands):
-            sum_ref[g * bands : (g + 1) * bands, p, :] = value
+    none = jnp.zeros((GY - bands, left.shape[1]), BF16)
+    tall = jnp.concatenate([left, none, right, none], axis=0)
+    value = dot(left, tall, ((1,), (1,)))
+    for g in range(sum_ref.shape[0] // bands):
+        sum_ref[g * bands : (g + 1) * bands, 0, :] = value
 
 
 def slab_kernel(devices, size, depth, again, *refs):
@@ -304,22 +302,26 @@
     if depth < pad:
         q_ref[depth * GX :] = jnp.zeros(((pad - depth) * GX, 128), F32)
 
-    chunk = 8
+    chunk, group = 8, 4
     for first in range(0, depth, chunk):
         last = min(depth, first + chunk)
-        for z in range(first, last, 2):
+        for z in range(first, last, group):
+            near = range(z, min(z + group, last))
             sides = []
-            for w in range(2):
-                line = pl.ds(z + w, GX, stride=pad)
+            for w in near:
+                line = pl.ds(w, GX, stride=pad)
                 sides.append(jnp.concatenate([y0_ref[line, :], y1_ref[line, :]], axis=0))
-            field = dot(tx_ref[...], tripled(jnp.concatenate(sides, axis=1), 0))
-            pot = jnp.concatenate([pot_ref[z], pot_ref[z + 1]], axis=1)
-            field = field * jnp.concatenate([pot, pot], axis=0)
-            back = dot(txb_ref[...], tripled(field, 0))
-            for w in range(2):
+            field = dot(tx_ref[...], jnp.concatenate(split(jnp.concatenate(sides, axis=1)), axis=0))
+            pot = jnp.concatenate([pot_ref[w] for w in near], axis=1)
+            field = (field[: 2 * size] + field[2 * size :]) * jnp.concatenate([pot, pot], axis=0)
+            high, low = split(field)
+            back = dot(txb_ref[...], high)
+            back = back[: 2 * GX] + back[2 * GX :] + dot(txb_ref[: 2 * GX], low)
+            for w in near:
                 for p in range(2):
-                    back_ref[(z + w) * GX : (z + w + 1) * GX, 128 * p : 128 * p + 128] = back[
-                        p * GX : (p + 1) * GX, 128 * w : 128 * w + 128
+                    at = 128 * (w - z)
+                    back_ref[w * GX : (w + 1) * GX, 128 * p : 128 * p + 128] = back[
+                        p * GX : (p + 1) * GX, at : at + 128
                     ]
         part = slice(first * GX, last * GX)
         q_ref[part] = dot(tripled(back_ref[part], 1), tyb_ref[...])
@@ -349,19 +351,17 @@
     depth = size // devices
     pad = round_up(depth, 8)
     rows = 2 * pad
-    me, band = lax.axis_index("grid"), lax.axis_index("band")
+    me = lax.axis_index("grid")
     me_arg = me.astype(jnp.int32).reshape(1)
-    band_arg = band.astype(jnp.int32).reshape(1)
-    if devices & (devices - 1) or bands & (bands - 1):
+    if devices & (devices - 1):
         raise ValueError("mesh size")
 
     def step(at, k):
         return at ^ k
 
-    def exchange(values, axis="grid"):
-        size = len(values)
+    def exchange(values):
         return [values[0]] + [
-            lax.ppermute(values[k], axis, [(d, step(d, k)) for d in range(size)]) for k in range(1, size)
+            lax.ppermute(values[k], "grid", [(d, step(d, k)) for d in range(devices)]) for k in range(1, devices)
         ]
 
     ahead, back = z_tables(size, devices, pad)
@@ -387,7 +387,7 @@
             functools.partial(first_kernel, devices, step, size),
             [vmem((rows + 8, cols))] * devices,
             [me_arg],
-            [(psi_t, False), (col_row, False), (ahead, False)],
+            [(psi_t, True), (col_row, True), (ahead, True)],
             [
                 pltpu.VMEM(psi_t.shape, F32),
                 pltpu.VMEM(col_row.shape, jnp.int32),
@@ -425,24 +425,25 @@
         [held],
     )
     planes = exchange(slab(exchange(sent), True))
-    filtered, *packed = call(
-        functools.partial(last_kernel, devices, bands, step, step, size),
-        [jax.ShapeDtypeStruct((2, size, cols), F32)] + [vmem((2 * slots, cols), BF16)] * bands,
-        [me_arg, band_arg, lower, upper],
+    filtered, packed = call(
+        functools.partial(last_kernel, devices, bands, step, size),
+        [vmem((2, size, cols)), vmem((bands, 2 * slots, cols), BF16)],
+        [me_arg, lower, upper],
         [(value, True) for value in planes]
         + [(psi_t, False), (first, True), (col_row, False), (back, False), (pick, False)],
-        [held, pltpu.VMEM((bands * 2 * slots, cols), BF16)],
+        [held],
     )
     (partial_sum,) = call(
-        functools.partial(gram_kernel, bands, step),
-        [vmem((devices * bands, 8, 128))],
-        [band_arg],
-        [(value, True) for value in exchange(packed, "band")],
+        functools.partial(gram_kernel, bands),
+        [vmem((devices * bands, 1, 128))],
+        [],
+        [(lax.all_to_all(packed, "band", 0, 0, tiled=True), True)],
         [pltpu.VMEM((cols // 128, bands * 2 * slots, 128), F32)],
     )
     sums = jnp.sum(lax.all_to_all(partial_sum, ("grid", "band"), 0, 0, tiled=True), axis=0)
     own = bands // devices
-    gram = lax.dynamic_slice(sums, (0, me * own), (2, own)).reshape(2, 1, own) / (4.0 * radius**3)
+    sums = sums.reshape(2, 1, GY)
+    gram = lax.dynamic_slice(sums, (0, 0, me * own), (2, 1, own)) / (4.0 * radius**3)
     return jnp.transpose(filtered, (0, 2, 1)).reshape(psi.shape), gram
 
 

time: 81.9 us -> 76.8 us (0.938)
  blocking collectives: 0 us -> 11.5 us
  starting transfers between devices: 26 us -> 18.1 us
  waiting for transfers between devices: 27.2 us -> 20.6 us
  local copies, waits for them, and re-layouts: 3.22 us -> 1.44 us
    all_to_all x0 -> x1, blocking collectives: none -> 11.5 us  [body(): lax.all_to_all(packed, 'band', 0, 0, tiled=True)]
    ppermute x19 -> x12, starting transfers between devices: 23.4 us -> 15.1 us  [exchange(): lax.ppermute(values[k], 'grid', [(d, step(d, k)) for d in range(devices)])]
    ppermute x19 -> x12, waiting for transfers between devices: 19 us -> 14.2 us  [exchange(): lax.ppermute(values[k], 'grid', [(d, step(d, k)) for d in range(devices)])]
    unnamed x24 -> x19, local copies, waits for them, and re-layouts: 2.67 us -> 0.81 us
    all_to_all x1, waiting for transfers between devices: 8.17 us -> 6.39 us  [body(): lax.all_to_all(partial_sum, ('grid', 'band'), 0, 0, tiled=True)]
  transfers between devices with their start and end apart: 20 -> 13, of which waited for: 16 -> 13; matrix products, arithmetic and copies ran while one was open for 2% -> 3% of each run, Pallas kernels for 0% -> 0%
where the time goes in v5:
time: 76.8 us; the launch traced here: 76.5 us
  Pallas kernels  20.9 us (27%)
  waiting for transfers between devices  20.6 us (27%)
  starting transfers between devices  18.1 us (24%)
  blocking collectives  11.5 us (15%)
  between operations  2.09 us (3%)
  other arithmetic  1.93 us (3%)
  local copies, waits for them, and re-layouts  1.44 us (2%)
    pallas_call x6, Pallas kernels, call(): pl.pallas_call(kernel, out_shape=out_shape, in_specs=[SMEM] * len(scalars...  20.9 us
    ppermute x12, starting transfers between devices, exchange(): lax.ppermute(values[k], 'grid', [(d, step(d, k)) for d in range(devices)])  15.1 us
    ppermute x12, waiting for transfers between devices, exchange(): lax.ppermute(values[k], 'grid', [(d, step(d, k)) for d in range(devices)])  14.2 us
    all_to_all x1, blocking collectives, body(): lax.all_to_all(packed, 'band', 0, 0, tiled=True)  11.5 us
    all_to_all x1, waiting for transfers between devices, body(): lax.all_to_all(partial_sum, ('grid', 'band'), 0, 0, tiled=True)  6.39 us
    all_to_all x1, starting transfers between devices, body(): lax.all_to_all(partial_sum, ('grid', 'band'), 0, 0, tiled=True)  2.96 us
  transfers between devices with their start and end apart: 13, of which 13 were waited for; matrix products, arithmetic and copies ran while one was open for 3% of the time, Pallas kernels for 0%

profile of v5, /device:TPU:0, one launch (start us, length us, event | category | flops | bytes accessed | tf_op | source)
XLA Modules:
  0.0 76.5 jit_solution(7637690004948874843)
XLA Ops:
  0.6 1.6 %shard_map.131 = (f32[56,512]{1,0:T(8,128)S(1)}, f32[56,512]{1,0:T(8,128)S(1)}, f32[56,512]{1,0:T(8,128)S(1)}, f32[56,512]{1,0:T(8,128)S(1)}) custom-call(s32[1]{0:T(128)} %bitcast.me_ref, f32[2,96,512]{2,1,0:T(8,128)} %bitcast.12, s32[1,512]{1,0:T(1,128)} %bitcast.15, bf16[4,48,576]{2,1,0:T(8,128)(2,1)} %constant.33.clone.refs_2_.refs_6_), custom_call_target="tpu_custom_call" | custom-call | tf_op jit(solution)/shard_map/pallas_call | solution.py:119
  2.2 3.0 %collective-permute-start = (f32[56,512]{1,0:T(8,128)S(1)}, f32[56,512]{1,0:T(8,128)S(1)}, u32[]{:S(2)}, u32[]{:S(2)}) collective-permute-start(f32[56,512]{1,0:T(8,128)S(1)} %get-tuple-element.22), channel_id=1, source_target_pairs={{0,8},{8,0},{16,24},{24,16},{1,9},{9,1},{17,25},{25,17},{2,10},{10... | collective-permute-start | bytes 344072 | tf_op jit(solution)/shard_map/ppermute | solution.py:364
  5.2 1.5 %collective-permute-start.1 = (f32[56,512]{1,0:T(8,128)S(1)}, f32[56,512]{1,0:T(8,128)S(1)}, u32[]{:S(2)}, u32[]{:S(2)}) collective-permute-start(f32[56,512]{1,0:T(8,128)S(1)} %get-tuple-element.23), channel_id=1, source_target_pairs={{0,16},{8,24},{16,0},{24,8},{1,17},{9,25},{17,1},{25,9},{2,18},{10... | collective-permute-start | bytes 344072 | tf_op jit(solution)/shard_map/ppermute | solution.py:364
  6.8 0.0 collective-permute-start.2
  6.8 1.2 %broadcast_multiply_fusion = f32[24,9216]{1,0:T(8,128)S(1)} fusion(f32[24,9216]{1,0:T(8,128)} %param.14), kind=kLoop, calls=%fused_computation | loop fusion | flops 221184 | bytes 1769472 | tf_op jit(solution)/shard_map/mul | solution.py:377
  8.0 0.5 reshape.27
  8.5 0.0 copy-start.3
  8.5 0.0 copy-start.4
  8.5 0.0 copy-start.5
  8.5 0.0 copy-start.6
  8.6 0.1 pad.4.refs_4_.refs_8_
  8.7 0.0 copy-start
  8.7 0.0 copy-start.1
  8.7 0.0 copy-start.2
  8.7 0.0 copy-start.8
  8.7 0.1 collective-permute-done.refs_1_.refs_5_
  8.8 2.8 %collective-permute-done.1.refs_2_.refs_6_ = f32[56,512]{1,0:T(8,128)S(1)} collective-permute-done((f32[56,512]{1,0:T(8,128)S(1)}, f32[56,512]{1,0:T(8,128)S(1)}, u32[]{:S(2)}, u32[]{:S(2)}) %collective-permute-start.1) | collective-permute-done | bytes 114720 | tf_op jit(solution)/shard_map/ppermute | solution.py:364
  11.6 0.9 %collective-permute-done.2.refs_3_.refs_7_ = f32[56,512]{1,0:T(8,128)S(1)} collective-permute-done((f32[56,512]{1,0:T(8,128)S(1)}, f32[56,512]{1,0:T(8,128)S(1)}, u32[]{:S(2)}, u32[]{:S(2)}) %collective-permute-start.2) | collective-permute-done | bytes 114720 | tf_op jit(solution)/shard_map/ppermute | solution.py:364
  12.5 0.0 copy-done.3
  12.5 0.0 copy-done.4
  12.5 0.0 copy-done.5
  12.5 0.0 copy-done.6
  12.5 8.4 %shard_map.132 = (f32[48,512]{1,0:T(8,128)S(1)}, f32[48,512]{1,0:T(8,128)S(1)}, f32[48,512]{1,0:T(8,128)S(1)}, f32[48,512]{1,0:T(8,128)S(1)}) custom-call(f32[56,512]{1,0:T(8,128)S(1)} %get-tuple-element.21.refs_0_.refs_4_, f32[56,512]{1,0:T(8,128)S(1)} %collective-permute-done.refs_1_.refs_5_, f32[56,512]{1,0:T(8,128)S(1)} %collective-permute-done.1.refs_2_.refs_6_, ...), custom_call_target="tpu_custom_call" | custom-call | tf_op jit(solution)/shard_map/pallas_call | solution.py:119
  20.9 1.1 %collective-permute-start.3 = (f32[48,512]{1,0:T(8,128)S(1)}, f32[48,512]{1,0:T(8,128)S(1)}, u32[]{:S(2)}, u32[]{:S(2)}) collective-permute-start(f32[48,512]{1,0:T(8,128)S(1)} %get-tuple-element.26), channel_id=1, source_target_pairs={{0,8},{8,0},{16,24},{24,16},{1,9},{9,1},{17,25},{25,17},{2,10},{10... | collective-permute-start | bytes 294920 | tf_op jit(solution)/shard_map/ppermute | solution.py:364
  22.0 0.8 %collective-permute-start.4 = (f32[48,512]{1,0:T(8,128)S(1)}, f32[48,512]{1,0:T(8,128)S(1)}, u32[]{:S(2)}, u32[]{:S(2)}) collective-permute-start(f32[48,512]{1,0:T(8,128)S(1)} %get-tuple-element.27), channel_id=1, source_target_pairs={{0,16},{8,24},{16,0},{24,8},{1,17},{9,25},{17,1},{25,9},{2,18},{10... | collective-permute-start | bytes 294920 | tf_op jit(solution)/shard_map/ppermute | solution.py:364
  22.8 1.6 %collective-permute-start.5 = (f32[48,512]{1,0:T(8,128)S(1)}, f32[48,512]{1,0:T(8,128)S(1)}, u32[]{:S(2)}, u32[]{:S(2)}) collective-permute-start(f32[48,512]{1,0:T(8,128)S(1)} %get-tuple-element.28), channel_id=1, source_target_pairs={{0,24},{8,16},{16,8},{24,0},{1,25},{9,17},{17,9},{25,1},{2,26},{10... | collective-permute-start | bytes 294920 | tf_op jit(solution)/shard_map/ppermute | solution.py:364
  25.7 0.8 %collective-permute-done.3.refs_1_ = f32[48,512]{1,0:T(8,128)S(1)} collective-permute-done((f32[48,512]{1,0:T(8,128)S(1)}, f32[48,512]{1,0:T(8,128)S(1)}, u32[]{:S(2)}, u32[]{:S(2)}) %collective-permute-start.3) | collective-permute-done | bytes 98336 | tf_op jit(solution)/shard_map/ppermute | solution.py:364
  26.5 0.1 collective-permute-done.4.refs_2_
  26.6 1.7 %collective-permute-done.5.refs_3_ = f32[48,512]{1,0:T(8,128)S(1)} collective-permute-done((f32[48,512]{1,0:T(8,128)S(1)}, f32[48,512]{1,0:T(8,128)S(1)}, u32[]{:S(2)}, u32[]{:S(2)}) %collective-permute-start.5) | collective-permute-done | bytes 98336 | tf_op jit(solution)/shard_map/ppermute | solution.py:364
  28.3 0.0 copy-done
  28.3 0.0 copy-done.1
  28.3 0.0 copy-done.2
  28.3 0.0 copy-done.8
  28.3 0.7 shard_map.133
  29.1 1.6 %collective-permute-start.6 = (f32[48,512]{1,0:T(8,128)S(1)}, f32[48,512]{1,0:T(8,128)S(1)}, u32[]{:S(2)}, u32[]{:S(2)}) collective-permute-start(f32[48,512]{1,0:T(8,128)S(1)} %get-tuple-element.30), channel_id=1, source_target_pairs={{0,8},{8,0},{16,24},{24,16},{1,9},{9,1},{17,25},{25,17},{2,10},{10... | collective-permute-start | bytes 294920 | tf_op jit(solution)/shard_map/ppermute | solution.py:364
  30.6 0.7 collective-permute-start.7
  31.3 1.3 %collective-permute-start.8 = (f32[48,512]{1,0:T(8,128)S(1)}, f32[48,512]{1,0:T(8,128)S(1)}, u32[]{:S(2)}, u32[]{:S(2)}) collective-permute-start(f32[48,512]{1,0:T(8,128)S(1)} %get-tuple-element.32), channel_id=1, source_target_pairs={{0,24},{8,16},{16,8},{24,0},{1,25},{9,17},{17,9},{25,1},{2,26},{10... | collective-permute-start | bytes 294920 | tf_op jit(solution)/shard_map/ppermute | solution.py:364
  32.6 1.1 %collective-permute-done.6.refs_1_ = f32[48,512]{1,0:T(8,128)S(1)} collective-permute-done((f32[48,512]{1,0:T(8,128)S(1)}, f32[48,512]{1,0:T(8,128)S(1)}, u32[]{:S(2)}, u32[]{:S(2)}) %collective-permute-start.6) | collective-permute-done | bytes 98336 | tf_op jit(solution)/shard_map/ppermute | solution.py:364
  33.8 1.5 %collective-permute-done.7.refs_2_ = f32[48,512]{1,0:T(8,128)S(1)} collective-permute-done((f32[48,512]{1,0:T(8,128)S(1)}, f32[48,512]{1,0:T(8,128)S(1)}, u32[]{:S(2)}, u32[]{:S(2)}) %collective-permute-start.7) | collective-permute-done | bytes 98336 | tf_op jit(solution)/shard_map/ppermute | solution.py:364
  35.3 1.6 %collective-permute-done.8.refs_3_ = f32[48,512]{1,0:T(8,128)S(1)} collective-permute-done((f32[48,512]{1,0:T(8,128)S(1)}, f32[48,512]{1,0:T(8,128)S(1)}, u32[]{:S(2)}, u32[]{:S(2)}) %collective-permute-start.8) | collective-permute-done | bytes 98336 | tf_op jit(solution)/shard_map/ppermute | solution.py:364
  36.8 0.0 copy-start.7
  36.8 8.5 %shard_map.134 = (f32[48,512]{1,0:T(8,128)S(1)}, f32[48,512]{1,0:T(8,128)S(1)}, f32[48,512]{1,0:T(8,128)S(1)}, f32[48,512]{1,0:T(8,128)S(1)}) custom-call(f32[48,512]{1,0:T(8,128)S(1)} %get-tuple-element.29.refs_0_, f32[48,512]{1,0:T(8,128)S(1)} %collective-permute-done.6.refs_1_, f32[48,512]{1,0:T(8,128)S(1)} %collective-permute-done.7.refs_2_, ...), custom_call_target="tpu_custom_call" | custom-call | tf_op jit(solution)/shard_map/pallas_call | solution.py:119
  45.3 1.4 %collective-permute-start.10 = (f32[48,512]{1,0:T(8,128)S(1)}, f32[48,512]{1,0:T(8,128)S(1)}, u32[]{:S(2)}, u32[]{:S(2)}) collective-permute-start(f32[48,512]{1,0:T(8,128)S(1)} %get-tuple-element.35), channel_id=1, source_target_pairs={{0,16},{8,24},{16,0},{24,8},{1,17},{9,25},{17,1},{25,9},{2,18},{10... | collective-permute-start | bytes 294920 | tf_op jit(solution)/shard_map/ppermute | solution.py:364
  46.7 1.2 %collective-permute-start.11 = (f32[48,512]{1,0:T(8,128)S(1)}, f32[48,512]{1,0:T(8,128)S(1)}, u32[]{:S(2)}, u32[]{:S(2)}) collective-permute-start(f32[48,512]{1,0:T(8,128)S(1)} %get-tuple-element.36), channel_id=1, source_target_pairs={{0,24},{8,16},{16,8},{24,0},{1,25},{9,17},{17,9},{25,1},{2,26},{10... | collective-permute-start | bytes 294920 | tf_op jit(solution)/shard_map/ppermute | solution.py:364
  47.9 1.0 %collective-permute-start.9 = (f32[48,512]{1,0:T(8,128)S(1)}, f32[48,512]{1,0:T(8,128)S(1)}, u32[]{:S(2)}, u32[]{:S(2)}) collective-permute-start(f32[48,512]{1,0:T(8,128)S(1)} %get-tuple-element.34), channel_id=1, source_target_pairs={{0,8},{8,0},{16,24},{24,16},{1,9},{9,1},{17,25},{25,17},{2,10},{10... | collective-permute-start | bytes 294920 | tf_op jit(solution)/shard_map/ppermute | solution.py:364
  48.9 1.1 %collective-permute-done.10.refs_2_ = f32[48,512]{1,0:T(8,128)S(1)} collective-permute-done((f32[48,512]{1,0:T(8,128)S(1)}, f32[48,512]{1,0:T(8,128)S(1)}, u32[]{:S(2)}, u32[]{:S(2)}) %collective-permute-start.10) | collective-permute-done | bytes 98336 | tf_op jit(solution)/shard_map/ppermute | solution.py:364
  50.0 2.2 %collective-permute-done.11.refs_3_ = f32[48,512]{1,0:T(8,128)S(1)} collective-permute-done((f32[48,512]{1,0:T(8,128)S(1)}, f32[48,512]{1,0:T(8,128)S(1)}, u32[]{:S(2)}, u32[]{:S(2)}) %collective-permute-start.11) | collective-permute-done | bytes 98336 | tf_op jit(solution)/shard_map/ppermute | solution.py:364
  52.2 0.3 collective-permute-done.9.refs_1_
  52.5 0.0 copy-done.7
  52.5 0.6 shard_map.135
  53.1 11.5 %all_to_all.10.parts_ref = bf16[8,16,512]{2,1,0:T(8,128)(2,1)S(1)} all-to-all(bf16[8,16,512]{2,1,0:T(8,128)(2,1)S(1)} %get-tuple-element.39), channel_id=1, replica_groups=mesh['grid'=4,'band'=8] {'band'}, dimensions={0} | all-to-all | bytes 262144 | tf_op jit(solution)/shard_map/all_to_all | solution.py:440
  64.6 1.1 %shard_map.136 = f32[32,1,128]{2,1,0:T(1,128)} custom-call(bf16[8,16,512]{2,1,0:T(8,128)(2,1)S(1)} %all_to_all.10.parts_ref), custom_call_target="tpu_custom_call" | custom-call | tf_op jit(solution)/shard_map/pallas_call | solution.py:119
  65.7 3.0 %all-to-all-start.1 = ((f32[32,1,128]{2,1,0:T(1,128)}), f32[32,1,128]{2,1,0:T(1,128)S(1)}, u32[]{:S(2)}, u32[]{:S(2)}) async-start(f32[32,1,128]{2,1,0:T(1,128)} %shard_map.136), calls=%async_computation.1 | async-start | bytes 32768 | tf_op jit(solution)/shard_map/all_to_all | solution.py:443
  68.6 0.7 copy.16
  69.4 6.4 %all-to-all-done.1 = f32[32,1,128]{2,1,0:T(1,128)S(1)} async-done(((f32[32,1,128]{2,1,0:T(1,128)}), f32[32,1,128]{2,1,0:T(1,128)S(1)}, u32[]{:S(2)}, u32[]{:S(2)}) %all-to-all-start.1) | async-done | bytes 16416 | tf_op jit(solution)/shard_map/all_to_all | solution.py:443
  75.8 0.1 reduce_sum.9
  75.8 0.1 reshape.29
  75.9 0.6 dynamic-slice_multiply_fusion
Async XLA Ops:
  2.2 6.6 %collective-permute-start = (f32[56,512]{1,0:T(8,128)S(1)}, f32[56,512]{1,0:T(8,128)S(1)}, u32[]{:S(2)}, u32[]{:S(2)}) collective-permute-start(f32[56,512]{1,0:T(8,128)S(1)} %get-tuple-element.22), channel_id=1, source_target_pairs={{0,8},{8,0},{16,24},{24,16},{1,9},{9,1},{17,25},{25,17},{2,10},{10... | collective-permute-start | bytes 344072 | tf_op jit(solution)/shard_map/ppermute | solution.py:364
  5.2 6.4 %collective-permute-start.1 = (f32[56,512]{1,0:T(8,128)S(1)}, f32[56,512]{1,0:T(8,128)S(1)}, u32[]{:S(2)}, u32[]{:S(2)}) collective-permute-start(f32[56,512]{1,0:T(8,128)S(1)} %get-tuple-element.23), channel_id=1, source_target_pairs={{0,16},{8,24},{16,0},{24,8},{1,17},{9,25},{17,1},{25,9},{2,18},{10... | collective-permute-start | bytes 344072 | tf_op jit(solution)/shard_map/ppermute | solution.py:364
  6.8 5.7 %collective-permute-start.2 = (f32[56,512]{1,0:T(8,128)S(1)}, f32[56,512]{1,0:T(8,128)S(1)}, u32[]{:S(2)}, u32[]{:S(2)}) collective-permute-start(f32[56,512]{1,0:T(8,128)S(1)} %get-tuple-element.24), channel_id=1, source_target_pairs={{0,24},{8,16},{16,8},{24,0},{1,25},{9,17},{17,9},{25,1},{2,26},{10... | collective-permute-start | bytes 344072 | tf_op jit(solution)/shard_map/ppermute | solution.py:364
  8.5 4.0 %copy-start.3 = (bf16[384,256]{1,0:T(8,128)(2,1)S(1)}, bf16[384,256]{1,0:T(8,128)(2,1)}, u32[]{:S(2)}) copy-start(bf16[384,256]{1,0:T(8,128)(2,1)} %constant.34.clone.refs_5_.refs_9_) | copy-start | bytes 589828
  8.5 4.0 %copy-start.4 = (bf16[384,224]{1,0:T(8,128)(2,1)S(1)}, bf16[384,224]{1,0:T(8,128)(2,1)}, u32[]{:S(2)}) copy-start(bf16[384,224]{1,0:T(8,128)(2,1)} %constant.35.clone.refs_6_.refs_10_) | copy-start | bytes 516100
  8.5 4.0 %copy-start.5 = (bf16[768,128]{1,0:T(8,128)(2,1)S(1)}, bf16[768,128]{1,0:T(8,128)(2,1)}, u32[]{:S(2)}) copy-start(bf16[768,128]{1,0:T(8,128)(2,1)} %constant.37.clone.refs_8_.refs_12_) | copy-start | bytes 589828
  8.5 4.0 %copy-start.6 = (bf16[224,192]{1,0:T(8,128)(2,1)S(1)}, bf16[224,192]{1,0:T(8,128)(2,1)}, u32[]{:S(2)}) copy-start(bf16[224,192]{1,0:T(8,128)(2,1)} %constant.36.clone.refs_7_.refs_11_) | copy-start | bytes 258052
  8.7 19.7 %copy-start = (f32[2,1,512,96]{2,3,1,0:T(8,128)S(1)}, f32[2,1,512,96]{2,3,1,0:T(8,128)}, u32[]{:S(2)}) copy-start(f32[2,1,512,96]{2,3,1,0:T(8,128)} %param.12) | copy-start | bytes 1179652
  8.7 19.7 %copy-start.1 = (bf16[192,576]{1,0:T(8,128)(2,1)S(1)}, bf16[192,576]{1,0:T(8,128)(2,1)}, u32[]{:S(2)}) copy-start(bf16[192,576]{1,0:T(8,128)(2,1)} %constant.38.clone.refs_7_) | copy-start | bytes 663556
  8.7 19.7 %copy-start.2 = (bf16[4,48,576]{2,1,0:T(8,128)(2,1)S(1)}, bf16[4,48,576]{2,1,0:T(8,128)(2,1)}, u32[]{:S(2)}) copy-start(bf16[4,48,576]{2,1,0:T(8,128)(2,1)} %constant.33.clone.refs_2_.refs_6_) | copy-start | bytes 663556
  8.7 19.6 %copy-start.8 = (s32[512]{0:T(512)S(1)}, s32[512]{0:T(512)}, u32[]{:S(2)}) copy-start(s32[512]{0:T(512)} %param.13) | copy-start | bytes 6148
  20.9 5.6 %collective-permute-start.3 = (f32[48,512]{1,0:T(8,128)S(1)}, f32[48,512]{1,0:T(8,128)S(1)}, u32[]{:S(2)}, u32[]{:S(2)}) collective-permute-start(f32[48,512]{1,0:T(8,128)S(1)} %get-tuple-element.26), channel_id=1, source_target_pairs={{0,8},{8,0},{16,24},{24,16},{1,9},{9,1},{17,25},{25,17},{2,10},{10... | collective-permute-start | bytes 294920 | tf_op jit(solution)/shard_map/ppermute | solution.py:364
  22.0 4.7 %collective-permute-start.4 = (f32[48,512]{1,0:T(8,128)S(1)}, f32[48,512]{1,0:T(8,128)S(1)}, u32[]{:S(2)}, u32[]{:S(2)}) collective-permute-start(f32[48,512]{1,0:T(8,128)S(1)} %get-tuple-element.27), channel_id=1, source_target_pairs={{0,16},{8,24},{16,0},{24,8},{1,17},{9,25},{17,1},{25,9},{2,18},{10... | collective-permute-start | bytes 294920 | tf_op jit(solution)/shard_map/ppermute | solution.py:364
  22.8 5.5 %collective-permute-start.5 = (f32[48,512]{1,0:T(8,128)S(1)}, f32[48,512]{1,0:T(8,128)S(1)}, u32[]{:S(2)}, u32[]{:S(2)}) collective-permute-start(f32[48,512]{1,0:T(8,128)S(1)} %get-tuple-element.28), channel_id=1, source_target_pairs={{0,24},{8,16},{16,8},{24,0},{1,25},{9,17},{17,9},{25,1},{2,26},{10... | collective-permute-start | bytes 294920 | tf_op jit(solution)/shard_map/ppermute | solution.py:364
  29.1 4.7 %collective-permute-start.6 = (f32[48,512]{1,0:T(8,128)S(1)}, f32[48,512]{1,0:T(8,128)S(1)}, u32[]{:S(2)}, u32[]{:S(2)}) collective-permute-start(f32[48,512]{1,0:T(8,128)S(1)} %get-tuple-element.30), channel_id=1, source_target_pairs={{0,8},{8,0},{16,24},{24,16},{1,9},{9,1},{17,25},{25,17},{2,10},{10... | collective-permute-start | bytes 294920 | tf_op jit(solution)/shard_map/ppermute | solution.py:364
  30.6 4.6 %collective-permute-start.7 = (f32[48,512]{1,0:T(8,128)S(1)}, f32[48,512]{1,0:T(8,128)S(1)}, u32[]{:S(2)}, u32[]{:S(2)}) collective-permute-start(f32[48,512]{1,0:T(8,128)S(1)} %get-tuple-element.31), channel_id=1, source_target_pairs={{0,16},{8,24},{16,0},{24,8},{1,17},{9,25},{17,1},{25,9},{2,18},{10... | collective-permute-start | bytes 294920 | tf_op jit(solution)/shard_map/ppermute | solution.py:364
  31.3 5.5 %collective-permute-start.8 = (f32[48,512]{1,0:T(8,128)S(1)}, f32[48,512]{1,0:T(8,128)S(1)}, u32[]{:S(2)}, u32[]{:S(2)}) collective-permute-start(f32[48,512]{1,0:T(8,128)S(1)} %get-tuple-element.32), channel_id=1, source_target_pairs={{0,24},{8,16},{16,8},{24,0},{1,25},{9,17},{17,9},{25,1},{2,26},{10... | collective-permute-start | bytes 294920 | tf_op jit(solution)/shard_map/ppermute | solution.py:364
  36.8 15.7 %copy-start.7 = (bf16[2,128,96]{2,1,0:T(8,128)(2,1)S(1)}, bf16[2,128,96]{2,1,0:T(8,128)(2,1)}, u32[]{:S(2)}) copy-start(bf16[2,128,96]{2,1,0:T(8,128)(2,1)} %constant.39.clone.refs_8_) | copy-start | bytes 147460
  45.3 4.6 %collective-permute-start.10 = (f32[48,512]{1,0:T(8,128)S(1)}, f32[48,512]{1,0:T(8,128)S(1)}, u32[]{:S(2)}, u32[]{:S(2)}) collective-permute-start(f32[48,512]{1,0:T(8,128)S(1)} %get-tuple-element.35), channel_id=1, source_target_pairs={{0,16},{8,24},{16,0},{24,8},{1,17},{9,25},{17,1},{25,9},{2,18},{10... | collective-permute-start | bytes 294920 | tf_op jit(solution)/shard_map/ppermute | solution.py:364
  46.7 5.5 %collective-permute-start.11 = (f32[48,512]{1,0:T(8,128)S(1)}, f32[48,512]{1,0:T(8,128)S(1)}, u32[]{:S(2)}, u32[]{:S(2)}) collective-permute-start(f32[48,512]{1,0:T(8,128)S(1)} %get-tuple-element.36), channel_id=1, source_target_pairs={{0,24},{8,16},{16,8},{24,0},{1,25},{9,17},{17,9},{25,1},{2,26},{10... | collective-permute-start | bytes 294920 | tf_op jit(solution)/shard_map/ppermute | solution.py:364
  47.9 4.6 %collective-permute-start.9 = (f32[48,512]{1,0:T(8,128)S(1)}, f32[48,512]{1,0:T(8,128)S(1)}, u32[]{:S(2)}, u32[]{:S(2)}) collective-permute-start(f32[48,512]{1,0:T(8,128)S(1)} %get-tuple-element.34), channel_id=1, source_target_pairs={{0,8},{8,0},{16,24},{24,16},{1,9},{9,1},{17,25},{25,17},{2,10},{10... | collective-permute-start | bytes 294920 | tf_op jit(solution)/shard_map/ppermute | solution.py:364
  65.7 10.1 %all-to-all-start.1 = ((f32[32,1,128]{2,1,0:T(1,128)}), f32[32,1,128]{2,1,0:T(1,128)S(1)}, u32[]{:S(2)}, u32[]{:S(2)}) async-start(f32[32,1,128]{2,1,0:T(1,128)} %shard_map.136), calls=%async_computation.1 | async-start | bytes 32768 | tf_op jit(solution)/shard_map/all_to_all | solution.py:443

commit v6 on v5

--- a/solution.py
+++ b/solution.py
@@ -251,7 +251,7 @@
         marks, refs = refs[:devices], refs[devices:]
     pot_ref, ty_ref, tx_ref, txb_ref, tyb_ref = refs[:5]
     outs = refs[5 : 5 + devices]
-    in_ref, y0_ref, y1_ref, back_ref, q_ref, box_ref = refs[5 + devices :]
+    in_ref, y0_ref, y1_ref, back_ref, q_ref, box_ref, slot_ref, spot_ref = refs[5 + devices :]
     pad = round_up(depth, 8)
     rows = 2 * pad
     cols = planes[0].shape[1]
@@ -279,13 +279,17 @@
         return jnp.concatenate(tall, axis=0)
 
     lhs = jnp.concatenate(split(jnp.concatenate([ref[:rows] for ref in planes], axis=1)), axis=0)
-    sources = [one_hot(k, 0, cols) for k in range(devices)]
-    whole = (
-        jnp.concatenate([s[0] for s in sources], axis=1),
-        [jnp.concatenate([s[1][i] for s in sources], axis=1) for i in range(8)],
-    )
+    row = lax.broadcasted_iota(jnp.int32, (8, 256), 0)
+    side = lax.broadcasted_iota(jnp.int32, (8, 256), 1) // 128
+    spread = jnp.where(row == side, 1.0, 0.0).astype(BF16)
+    both = dot(jnp.concatenate([ref[rows : rows + 8].astype(BF16) for ref in marks], axis=1), spread, ((0,), (0,)))
+    slot_ref[...] = both[:, :128].astype(BF16)
+    along = lax.broadcasted_iota(jnp.int32, (cols * devices, 128), 1).astype(F32)
+    spot_ref[...] = jnp.where(both[:, 128:] == along, 1.0, 0.0).astype(BF16)
+    in_ref[...] = jnp.zeros(in_ref.shape, F32)
     for t in range(0, slots, 2):
-        got = dot(lhs, expand(whole, t, 2), ((1,), (1,)))
+        hot = [jnp.where(slot_ref[...] == float(v), spot_ref[...], zero) for v in (t, t + 1)]
+        got = dot(lhs, jnp.concatenate(hot, axis=1))
         got = got[:rows] + got[rows:]
         for i, (width, slot, middle) in enumerate(places):
             if slot // 2 * 2 != t:
@@ -294,8 +298,7 @@
             re = pltpu.roll(got[:pad, at : at + 128], (radius - middle) % 128, 1)
             im = pltpu.roll(got[pad:, at : at + 128], (radius + GY - middle) % 128, 1)
             im = jnp.where(between(GY + radius - width, GY + radius + width), im, 0.0)
-            in_ref[i * pad : (i + 1) * pad] = jnp.where(between(radius - width, radius + width), re, im)
-    in_ref[len(places) * pad :] = jnp.zeros(((GX - len(places)) * pad, 128), F32)
+            in_ref[pl.ds(i, pad, stride=GX), :] = jnp.where(between(radius - width, radius + width), re, im)
     moved = dot(tripled(in_ref[...], 1), ty_ref[...])
     y0_ref[...] = moved[:, :128]
     y1_ref[...] = moved[:, 128:]
@@ -309,7 +312,7 @@
             near = range(z, min(z + group, last))
             sides = []
             for w in near:
-                line = pl.ds(w, GX, stride=pad)
+                line = slice(w * GX, (w + 1) * GX)
                 sides.append(jnp.concatenate([y0_ref[line, :], y1_ref[line, :]], axis=0))
             field = dot(tx_ref[...], jnp.concatenate(split(jnp.concatenate(sides, axis=1)), axis=0))
             pot = jnp.concatenate([pot_ref[w] for w in near], axis=1)
@@ -412,6 +415,8 @@
                 pltpu.VMEM((pad * GX, 256), F32),
                 pltpu.VMEM((pad * GX, 128), F32),
                 pltpu.VMEM((2 * rows, 128 * packing(size)[1]), BF16),
+                pltpu.VMEM((cols * devices, 128), BF16),
+                pltpu.VMEM((cols * devices, 128), BF16),
             ],
         )
 

time: 76.8 us -> 76.6 us (level)
  no operation moved by 1% of the time
where the time goes in v6:
time: 76.6 us; the launch traced here: 76.3 us
  Pallas kernels  20.7 us (27%)
  waiting for transfers between devices  20.6 us (27%)
  starting transfers between devices  18.1 us (24%)
  blocking collectives  11.5 us (15%)
  between operations  2.09 us (3%)
  other arithmetic  1.93 us (3%)
  local copies, waits for them, and re-layouts  1.44 us (2%)
    pallas_call x6, Pallas kernels, call(): pl.pallas_call(kernel, out_shape=out_shape, in_specs=[SMEM] * len(scalars...  20.7 us
    ppermute x12, starting transfers between devices, exchange(): lax.ppermute(values[k], 'grid', [(d, step(d, k)) for d in range(devices)])  15.1 us
    ppermute x12, waiting for transfers between devices, exchange(): lax.ppermute(values[k], 'grid', [(d, step(d, k)) for d in range(devices)])  14.3 us
    all_to_all x1, blocking collectives, body(): lax.all_to_all(packed, 'band', 0, 0, tiled=True)  11.5 us
    all_to_all x1, waiting for transfers between devices, body(): lax.all_to_all(partial_sum, ('grid', 'band'), 0, 0, tiled=True)  6.39 us
    all_to_all x1, starting transfers between devices, body(): lax.all_to_all(partial_sum, ('grid', 'band'), 0, 0, tiled=True)  2.98 us
  transfers between devices with their start and end apart: 13, of which 13 were waited for; matrix products, arithmetic and copies ran while one was open for 3% of the time, Pallas kernels for 0%

profile of v6, /device:TPU:0, one launch (start us, length us, event | category | flops | bytes accessed | tf_op | source)
XLA Modules:
  0.0 76.3 jit_solution(2190891229775571182)
XLA Ops:
  0.6 1.6 %shard_map.131 = (f32[56,512]{1,0:T(8,128)S(1)}, f32[56,512]{1,0:T(8,128)S(1)}, f32[56,512]{1,0:T(8,128)S(1)}, f32[56,512]{1,0:T(8,128)S(1)}) custom-call(s32[1]{0:T(128)} %bitcast.me_ref, f32[2,96,512]{2,1,0:T(8,128)} %bitcast.12, s32[1,512]{1,0:T(1,128)} %bitcast.15, bf16[4,48,576]{2,1,0:T(8,128)(2,1)} %constant.33.clone.refs_2_.refs_6_), custom_call_target="tpu_custom_call" | custom-call | tf_op jit(solution)/shard_map/pallas_call | solution.py:119
  2.2 3.0 %collective-permute-start = (f32[56,512]{1,0:T(8,128)S(1)}, f32[56,512]{1,0:T(8,128)S(1)}, u32[]{:S(2)}, u32[]{:S(2)}) collective-permute-start(f32[56,512]{1,0:T(8,128)S(1)} %get-tuple-element.22), channel_id=1, source_target_pairs={{0,8},{8,0},{16,24},{24,16},{1,9},{9,1},{17,25},{25,17},{2,10},{10... | collective-permute-start | bytes 344072 | tf_op jit(solution)/shard_map/ppermute | solution.py:367
  5.2 1.5 %collective-permute-start.1 = (f32[56,512]{1,0:T(8,128)S(1)}, f32[56,512]{1,0:T(8,128)S(1)}, u32[]{:S(2)}, u32[]{:S(2)}) collective-permute-start(f32[56,512]{1,0:T(8,128)S(1)} %get-tuple-element.23), channel_id=1, source_target_pairs={{0,16},{8,24},{16,0},{24,8},{1,17},{9,25},{17,1},{25,9},{2,18},{10... | collective-permute-start | bytes 344072 | tf_op jit(solution)/shard_map/ppermute | solution.py:367
  6.8 0.0 collective-permute-start.2
  6.8 1.2 %broadcast_multiply_fusion = f32[24,9216]{1,0:T(8,128)S(1)} fusion(f32[24,9216]{1,0:T(8,128)} %param.14), kind=kLoop, calls=%fused_computation | loop fusion | flops 221184 | bytes 1769472 | tf_op jit(solution)/shard_map/mul | solution.py:380
  8.0 0.5 reshape.27
  8.5 0.0 copy-start.3
  8.5 0.0 copy-start.4
  8.5 0.0 copy-start.5
  8.5 0.0 copy-start.6
  8.6 0.1 pad.4.refs_4_.refs_8_
  8.7 0.0 copy-start
  8.7 0.0 copy-start.1
  8.7 0.0 copy-start.2
  8.7 0.0 copy-start.8
  8.7 0.1 collective-permute-done.refs_1_.refs_5_
  8.8 2.8 %collective-permute-done.1.refs_2_.refs_6_ = f32[56,512]{1,0:T(8,128)S(1)} collective-permute-done((f32[56,512]{1,0:T(8,128)S(1)}, f32[56,512]{1,0:T(8,128)S(1)}, u32[]{:S(2)}, u32[]{:S(2)}) %collective-permute-start.1) | collective-permute-done | bytes 114720 | tf_op jit(solution)/shard_map/ppermute | solution.py:367
  11.6 0.9 %collective-permute-done.2.refs_3_.refs_7_ = f32[56,512]{1,0:T(8,128)S(1)} collective-permute-done((f32[56,512]{1,0:T(8,128)S(1)}, f32[56,512]{1,0:T(8,128)S(1)}, u32[]{:S(2)}, u32[]{:S(2)}) %collective-permute-start.2) | collective-permute-done | bytes 114720 | tf_op jit(solution)/shard_map/ppermute | solution.py:367
  12.5 0.0 copy-done.3
  12.5 0.0 copy-done.4
  12.5 0.0 copy-done.5
  12.5 0.0 copy-done.6
  12.5 8.2 %shard_map.132 = (f32[48,512]{1,0:T(8,128)S(1)}, f32[48,512]{1,0:T(8,128)S(1)}, f32[48,512]{1,0:T(8,128)S(1)}, f32[48,512]{1,0:T(8,128)S(1)}) custom-call(f32[56,512]{1,0:T(8,128)S(1)} %get-tuple-element.21.refs_0_.refs_4_, f32[56,512]{1,0:T(8,128)S(1)} %collective-permute-done.refs_1_.refs_5_, f32[56,512]{1,0:T(8,128)S(1)} %collective-permute-done.1.refs_2_.refs_6_, ...), custom_call_target="tpu_custom_call" | custom-call | tf_op jit(solution)/shard_map/pallas_call | solution.py:119
  20.8 1.1 %collective-permute-start.3 = (f32[48,512]{1,0:T(8,128)S(1)}, f32[48,512]{1,0:T(8,128)S(1)}, u32[]{:S(2)}, u32[]{:S(2)}) collective-permute-start(f32[48,512]{1,0:T(8,128)S(1)} %get-tuple-element.26), channel_id=1, source_target_pairs={{0,8},{8,0},{16,24},{24,16},{1,9},{9,1},{17,25},{25,17},{2,10},{10... | collective-permute-start | bytes 294920 | tf_op jit(solution)/shard_map/ppermute | solution.py:367
  21.8 0.8 %collective-permute-start.4 = (f32[48,512]{1,0:T(8,128)S(1)}, f32[48,512]{1,0:T(8,128)S(1)}, u32[]{:S(2)}, u32[]{:S(2)}) collective-permute-start(f32[48,512]{1,0:T(8,128)S(1)} %get-tuple-element.27), channel_id=1, source_target_pairs={{0,16},{8,24},{16,0},{24,8},{1,17},{9,25},{17,1},{25,9},{2,18},{10... | collective-permute-start | bytes 294920 | tf_op jit(solution)/shard_map/ppermute | solution.py:367
  22.7 1.6 %collective-permute-start.5 = (f32[48,512]{1,0:T(8,128)S(1)}, f32[48,512]{1,0:T(8,128)S(1)}, u32[]{:S(2)}, u32[]{:S(2)}) collective-permute-start(f32[48,512]{1,0:T(8,128)S(1)} %get-tuple-element.28), channel_id=1, source_target_pairs={{0,24},{8,16},{16,8},{24,0},{1,25},{9,17},{17,9},{25,1},{2,26},{10... | collective-permute-start | bytes 294920 | tf_op jit(solution)/shard_map/ppermute | solution.py:367
  25.6 0.8 %collective-permute-done.3.refs_1_ = f32[48,512]{1,0:T(8,128)S(1)} collective-permute-done((f32[48,512]{1,0:T(8,128)S(1)}, f32[48,512]{1,0:T(8,128)S(1)}, u32[]{:S(2)}, u32[]{:S(2)}) %collective-permute-start.3) | collective-permute-done | bytes 98336 | tf_op jit(solution)/shard_map/ppermute | solution.py:367
  26.4 0.1 collective-permute-done.4.refs_2_
  26.5 1.7 %collective-permute-done.5.refs_3_ = f32[48,512]{1,0:T(8,128)S(1)} collective-permute-done((f32[48,512]{1,0:T(8,128)S(1)}, f32[48,512]{1,0:T(8,128)S(1)}, u32[]{:S(2)}, u32[]{:S(2)}) %collective-permute-start.5) | collective-permute-done | bytes 98336 | tf_op jit(solution)/shard_map/ppermute | solution.py:367
  28.2 0.0 copy-done
  28.2 0.0 copy-done.1
  28.2 0.0 copy-done.2
  28.2 0.0 copy-done.8
  28.2 0.7 shard_map.133
  28.9 1.6 %collective-permute-start.6 = (f32[48,512]{1,0:T(8,128)S(1)}, f32[48,512]{1,0:T(8,128)S(1)}, u32[]{:S(2)}, u32[]{:S(2)}) collective-permute-start(f32[48,512]{1,0:T(8,128)S(1)} %get-tuple-element.30), channel_id=1, source_target_pairs={{0,8},{8,0},{16,24},{24,16},{1,9},{9,1},{17,25},{25,17},{2,10},{10... | collective-permute-start | bytes 294920 | tf_op jit(solution)/shard_map/ppermute | solution.py:367
  30.5 0.7 collective-permute-start.7
  31.2 1.3 %collective-permute-start.8 = (f32[48,512]{1,0:T(8,128)S(1)}, f32[48,512]{1,0:T(8,128)S(1)}, u32[]{:S(2)}, u32[]{:S(2)}) collective-permute-start(f32[48,512]{1,0:T(8,128)S(1)} %get-tuple-element.32), channel_id=1, source_target_pairs={{0,24},{8,16},{16,8},{24,0},{1,25},{9,17},{17,9},{25,1},{2,26},{10... | collective-permute-start | bytes 294920 | tf_op jit(solution)/shard_map/ppermute | solution.py:367
  32.5 1.1 %collective-permute-done.6.refs_1_ = f32[48,512]{1,0:T(8,128)S(1)} collective-permute-done((f32[48,512]{1,0:T(8,128)S(1)}, f32[48,512]{1,0:T(8,128)S(1)}, u32[]{:S(2)}, u32[]{:S(2)}) %collective-permute-start.6) | collective-permute-done | bytes 98336 | tf_op jit(solution)/shard_map/ppermute | solution.py:367
  33.6 1.5 %collective-permute-done.7.refs_2_ = f32[48,512]{1,0:T(8,128)S(1)} collective-permute-done((f32[48,512]{1,0:T(8,128)S(1)}, f32[48,512]{1,0:T(8,128)S(1)}, u32[]{:S(2)}, u32[]{:S(2)}) %collective-permute-start.7) | collective-permute-done | bytes 98336 | tf_op jit(solution)/shard_map/ppermute | solution.py:367
  35.1 1.6 %collective-permute-done.8.refs_3_ = f32[48,512]{1,0:T(8,128)S(1)} collective-permute-done((f32[48,512]{1,0:T(8,128)S(1)}, f32[48,512]{1,0:T(8,128)S(1)}, u32[]{:S(2)}, u32[]{:S(2)}) %collective-permute-start.8) | collective-permute-done | bytes 98336 | tf_op jit(solution)/shard_map/ppermute | solution.py:367
  36.7 0.0 copy-start.7
  36.7 8.4 %shard_map.134 = (f32[48,512]{1,0:T(8,128)S(1)}, f32[48,512]{1,0:T(8,128)S(1)}, f32[48,512]{1,0:T(8,128)S(1)}, f32[48,512]{1,0:T(8,128)S(1)}) custom-call(f32[48,512]{1,0:T(8,128)S(1)} %get-tuple-element.29.refs_0_, f32[48,512]{1,0:T(8,128)S(1)} %collective-permute-done.6.refs_1_, f32[48,512]{1,0:T(8,128)S(1)} %collective-permute-done.7.refs_2_, ...), custom_call_target="tpu_custom_call" | custom-call | tf_op jit(solution)/shard_map/pallas_call | solution.py:119
  45.1 1.4 %collective-permute-start.10 = (f32[48,512]{1,0:T(8,128)S(1)}, f32[48,512]{1,0:T(8,128)S(1)}, u32[]{:S(2)}, u32[]{:S(2)}) collective-permute-start(f32[48,512]{1,0:T(8,128)S(1)} %get-tuple-element.35), channel_id=1, source_target_pairs={{0,16},{8,24},{16,0},{24,8},{1,17},{9,25},{17,1},{25,9},{2,18},{10... | collective-permute-start | bytes 294920 | tf_op jit(solution)/shard_map/ppermute | solution.py:367
  46.5 1.2 %collective-permute-start.11 = (f32[48,512]{1,0:T(8,128)S(1)}, f32[48,512]{1,0:T(8,128)S(1)}, u32[]{:S(2)}, u32[]{:S(2)}) collective-permute-start(f32[48,512]{1,0:T(8,128)S(1)} %get-tuple-element.36), channel_id=1, source_target_pairs={{0,24},{8,16},{16,8},{24,0},{1,25},{9,17},{17,9},{25,1},{2,26},{10... | collective-permute-start | bytes 294920 | tf_op jit(solution)/shard_map/ppermute | solution.py:367
  47.6 1.0 %collective-permute-start.9 = (f32[48,512]{1,0:T(8,128)S(1)}, f32[48,512]{1,0:T(8,128)S(1)}, u32[]{:S(2)}, u32[]{:S(2)}) collective-permute-start(f32[48,512]{1,0:T(8,128)S(1)} %get-tuple-element.34), channel_id=1, source_target_pairs={{0,8},{8,0},{16,24},{24,16},{1,9},{9,1},{17,25},{25,17},{2,10},{10... | collective-permute-start | bytes 294920 | tf_op jit(solution)/shard_map/ppermute | solution.py:367
  48.6 1.1 %collective-permute-done.10.refs_2_ = f32[48,512]{1,0:T(8,128)S(1)} collective-permute-done((f32[48,512]{1,0:T(8,128)S(1)}, f32[48,512]{1,0:T(8,128)S(1)}, u32[]{:S(2)}, u32[]{:S(2)}) %collective-permute-start.10) | collective-permute-done | bytes 98336 | tf_op jit(solution)/shard_map/ppermute | solution.py:367
  49.8 2.2 %collective-permute-done.11.refs_3_ = f32[48,512]{1,0:T(8,128)S(1)} collective-permute-done((f32[48,512]{1,0:T(8,128)S(1)}, f32[48,512]{1,0:T(8,128)S(1)}, u32[]{:S(2)}, u32[]{:S(2)}) %collective-permute-start.11) | collective-permute-done | bytes 98336 | tf_op jit(solution)/shard_map/ppermute | solution.py:367
  52.0 0.3 collective-permute-done.9.refs_1_
  52.3 0.0 copy-done.7
  52.3 0.6 shard_map.135
  52.9 11.5 %all_to_all.10.parts_ref = bf16[8,16,512]{2,1,0:T(8,128)(2,1)S(1)} all-to-all(bf16[8,16,512]{2,1,0:T(8,128)(2,1)S(1)} %get-tuple-element.39), channel_id=1, replica_groups=mesh['grid'=4,'band'=8] {'band'}, dimensions={0} | all-to-all | bytes 262144 | tf_op jit(solution)/shard_map/all_to_all | solution.py:445
  64.4 1.1 %shard_map.136 = f32[32,1,128]{2,1,0:T(1,128)} custom-call(bf16[8,16,512]{2,1,0:T(8,128)(2,1)S(1)} %all_to_all.10.parts_ref), custom_call_target="tpu_custom_call" | custom-call | tf_op jit(solution)/shard_map/pallas_call | solution.py:119
  65.4 3.0 %all-to-all-start.1 = ((f32[32,1,128]{2,1,0:T(1,128)}), f32[32,1,128]{2,1,0:T(1,128)S(1)}, u32[]{:S(2)}, u32[]{:S(2)}) async-start(f32[32,1,128]{2,1,0:T(1,128)} %shard_map.136), calls=%async_computation.1 | async-start | bytes 32768 | tf_op jit(solution)/shard_map/all_to_all | solution.py:448
  68.4 0.7 copy.16
  69.2 6.4 %all-to-all-done.1 = f32[32,1,128]{2,1,0:T(1,128)S(1)} async-done(((f32[32,1,128]{2,1,0:T(1,128)}), f32[32,1,128]{2,1,0:T(1,128)S(1)}, u32[]{:S(2)}, u32[]{:S(2)}) %all-to-all-start.1) | async-done | bytes 16416 | tf_op jit(solution)/shard_map/all_to_all | solution.py:448
  75.6 0.1 reduce_sum.9
  75.6 0.1 reshape.29
  75.7 0.6 dynamic-slice_multiply_fusion
Async XLA Ops:
  2.2 6.6 %collective-permute-start = (f32[56,512]{1,0:T(8,128)S(1)}, f32[56,512]{1,0:T(8,128)S(1)}, u32[]{:S(2)}, u32[]{:S(2)}) collective-permute-start(f32[56,512]{1,0:T(8,128)S(1)} %get-tuple-element.22), channel_id=1, source_target_pairs={{0,8},{8,0},{16,24},{24,16},{1,9},{9,1},{17,25},{25,17},{2,10},{10... | collective-permute-start | bytes 344072 | tf_op jit(solution)/shard_map/ppermute | solution.py:367
  5.2 6.4 %collective-permute-start.1 = (f32[56,512]{1,0:T(8,128)S(1)}, f32[56,512]{1,0:T(8,128)S(1)}, u32[]{:S(2)}, u32[]{:S(2)}) collective-permute-start(f32[56,512]{1,0:T(8,128)S(1)} %get-tuple-element.23), channel_id=1, source_target_pairs={{0,16},{8,24},{16,0},{24,8},{1,17},{9,25},{17,1},{25,9},{2,18},{10... | collective-permute-start | bytes 344072 | tf_op jit(solution)/shard_map/ppermute | solution.py:367
  6.8 5.7 %collective-permute-start.2 = (f32[56,512]{1,0:T(8,128)S(1)}, f32[56,512]{1,0:T(8,128)S(1)}, u32[]{:S(2)}, u32[]{:S(2)}) collective-permute-start(f32[56,512]{1,0:T(8,128)S(1)} %get-tuple-element.24), channel_id=1, source_target_pairs={{0,24},{8,16},{16,8},{24,0},{1,25},{9,17},{17,9},{25,1},{2,26},{10... | collective-permute-start | bytes 344072 | tf_op jit(solution)/shard_map/ppermute | solution.py:367
  8.5 4.0 %copy-start.3 = (bf16[384,256]{1,0:T(8,128)(2,1)S(1)}, bf16[384,256]{1,0:T(8,128)(2,1)}, u32[]{:S(2)}) copy-start(bf16[384,256]{1,0:T(8,128)(2,1)} %constant.34.clone.refs_5_.refs_9_) | copy-start | bytes 589828
  8.5 4.0 %copy-start.4 = (bf16[384,224]{1,0:T(8,128)(2,1)S(1)}, bf16[384,224]{1,0:T(8,128)(2,1)}, u32[]{:S(2)}) copy-start(bf16[384,224]{1,0:T(8,128)(2,1)} %constant.35.clone.refs_6_.refs_10_) | copy-start | bytes 516100
  8.5 4.0 %copy-start.5 = (bf16[768,128]{1,0:T(8,128)(2,1)S(1)}, bf16[768,128]{1,0:T(8,128)(2,1)}, u32[]{:S(2)}) copy-start(bf16[768,128]{1,0:T(8,128)(2,1)} %constant.37.clone.refs_8_.refs_12_) | copy-start | bytes 589828
  8.5 4.0 %copy-start.6 = (bf16[224,192]{1,0:T(8,128)(2,1)S(1)}, bf16[224,192]{1,0:T(8,128)(2,1)}, u32[]{:S(2)}) copy-start(bf16[224,192]{1,0:T(8,128)(2,1)} %constant.36.clone.refs_7_.refs_11_) | copy-start | bytes 258052
  8.7 19.5 %copy-start = (f32[2,1,512,96]{2,3,1,0:T(8,128)S(1)}, f32[2,1,512,96]{2,3,1,0:T(8,128)}, u32[]{:S(2)}) copy-start(f32[2,1,512,96]{2,3,1,0:T(8,128)} %param.12) | copy-start | bytes 1179652
  8.7 19.5 %copy-start.1 = (bf16[192,576]{1,0:T(8,128)(2,1)S(1)}, bf16[192,576]{1,0:T(8,128)(2,1)}, u32[]{:S(2)}) copy-start(bf16[192,576]{1,0:T(8,128)(2,1)} %constant.38.clone.refs_7_) | copy-start | bytes 663556
  8.7 19.5 %copy-start.2 = (bf16[4,48,576]{2,1,0:T(8,128)(2,1)S(1)}, bf16[4,48,576]{2,1,0:T(8,128)(2,1)}, u32[]{:S(2)}) copy-start(bf16[4,48,576]{2,1,0:T(8,128)(2,1)} %constant.33.clone.refs_2_.refs_6_) | copy-start | bytes 663556
  8.7 19.5 %copy-start.8 = (s32[512]{0:T(512)S(1)}, s32[512]{0:T(512)}, u32[]{:S(2)}) copy-start(s32[512]{0:T(512)} %param.13) | copy-start | bytes 6148
  20.8 5.6 %collective-permute-start.3 = (f32[48,512]{1,0:T(8,128)S(1)}, f32[48,512]{1,0:T(8,128)S(1)}, u32[]{:S(2)}, u32[]{:S(2)}) collective-permute-start(f32[48,512]{1,0:T(8,128)S(1)} %get-tuple-element.26), channel_id=1, source_target_pairs={{0,8},{8,0},{16,24},{24,16},{1,9},{9,1},{17,25},{25,17},{2,10},{10... | collective-permute-start | bytes 294920 | tf_op jit(solution)/shard_map/ppermute | solution.py:367
  21.8 4.6 %collective-permute-start.4 = (f32[48,512]{1,0:T(8,128)S(1)}, f32[48,512]{1,0:T(8,128)S(1)}, u32[]{:S(2)}, u32[]{:S(2)}) collective-permute-start(f32[48,512]{1,0:T(8,128)S(1)} %get-tuple-element.27), channel_id=1, source_target_pairs={{0,16},{8,24},{16,0},{24,8},{1,17},{9,25},{17,1},{25,9},{2,18},{10... | collective-permute-start | bytes 294920 | tf_op jit(solution)/shard_map/ppermute | solution.py:367
  22.7 5.5 %collective-permute-start.5 = (f32[48,512]{1,0:T(8,128)S(1)}, f32[48,512]{1,0:T(8,128)S(1)}, u32[]{:S(2)}, u32[]{:S(2)}) collective-permute-start(f32[48,512]{1,0:T(8,128)S(1)} %get-tuple-element.28), channel_id=1, source_target_pairs={{0,24},{8,16},{16,8},{24,0},{1,25},{9,17},{17,9},{25,1},{2,26},{10... | collective-permute-start | bytes 294920 | tf_op jit(solution)/shard_map/ppermute | solution.py:367
  28.9 4.7 %collective-permute-start.6 = (f32[48,512]{1,0:T(8,128)S(1)}, f32[48,512]{1,0:T(8,128)S(1)}, u32[]{:S(2)}, u32[]{:S(2)}) collective-permute-start(f32[48,512]{1,0:T(8,128)S(1)} %get-tuple-element.30), channel_id=1, source_target_pairs={{0,8},{8,0},{16,24},{24,16},{1,9},{9,1},{17,25},{25,17},{2,10},{10... | collective-permute-start | bytes 294920 | tf_op jit(solution)/shard_map/ppermute | solution.py:367
  30.5 4.6 %collective-permute-start.7 = (f32[48,512]{1,0:T(8,128)S(1)}, f32[48,512]{1,0:T(8,128)S(1)}, u32[]{:S(2)}, u32[]{:S(2)}) collective-permute-start(f32[48,512]{1,0:T(8,128)S(1)} %get-tuple-element.31), channel_id=1, source_target_pairs={{0,16},{8,24},{16,0},{24,8},{1,17},{9,25},{17,1},{25,9},{2,18},{10... | collective-permute-start | bytes 294920 | tf_op jit(solution)/shard_map/ppermute | solution.py:367
  31.2 5.5 %collective-permute-start.8 = (f32[48,512]{1,0:T(8,128)S(1)}, f32[48,512]{1,0:T(8,128)S(1)}, u32[]{:S(2)}, u32[]{:S(2)}) collective-permute-start(f32[48,512]{1,0:T(8,128)S(1)} %get-tuple-element.32), channel_id=1, source_target_pairs={{0,24},{8,16},{16,8},{24,0},{1,25},{9,17},{17,9},{25,1},{2,26},{10... | collective-permute-start | bytes 294920 | tf_op jit(solution)/shard_map/ppermute | solution.py:367
  36.7 15.6 %copy-start.7 = (bf16[2,128,96]{2,1,0:T(8,128)(2,1)S(1)}, bf16[2,128,96]{2,1,0:T(8,128)(2,1)}, u32[]{:S(2)}) copy-start(bf16[2,128,96]{2,1,0:T(8,128)(2,1)} %constant.39.clone.refs_8_) | copy-start | bytes 147460
  45.1 4.6 %collective-permute-start.10 = (f32[48,512]{1,0:T(8,128)S(1)}, f32[48,512]{1,0:T(8,128)S(1)}, u32[]{:S(2)}, u32[]{:S(2)}) collective-permute-start(f32[48,512]{1,0:T(8,128)S(1)} %get-tuple-element.35), channel_id=1, source_target_pairs={{0,16},{8,24},{16,0},{24,8},{1,17},{9,25},{17,1},{25,9},{2,18},{10... | collective-permute-start | bytes 294920 | tf_op jit(solution)/shard_map/ppermute | solution.py:367
  46.5 5.5 %collective-permute-start.11 = (f32[48,512]{1,0:T(8,128)S(1)}, f32[48,512]{1,0:T(8,128)S(1)}, u32[]{:S(2)}, u32[]{:S(2)}) collective-permute-start(f32[48,512]{1,0:T(8,128)S(1)} %get-tuple-element.36), channel_id=1, source_target_pairs={{0,24},{8,16},{16,8},{24,0},{1,25},{9,17},{17,9},{25,1},{2,26},{10... | collective-permute-start | bytes 294920 | tf_op jit(solution)/shard_map/ppermute | solution.py:367
  47.6 4.6 %collective-permute-start.9 = (f32[48,512]{1,0:T(8,128)S(1)}, f32[48,512]{1,0:T(8,128)S(1)}, u32[]{:S(2)}, u32[]{:S(2)}) collective-permute-start(f32[48,512]{1,0:T(8,128)S(1)} %get-tuple-element.34), channel_id=1, source_target_pairs={{0,8},{8,0},{16,24},{24,16},{1,9},{9,1},{17,25},{25,17},{2,10},{10... | collective-permute-start | bytes 294920 | tf_op jit(solution)/shard_map/ppermute | solution.py:367
  65.4 10.1 %all-to-all-start.1 = ((f32[32,1,128]{2,1,0:T(1,128)}), f32[32,1,128]{2,1,0:T(1,128)S(1)}, u32[]{:S(2)}, u32[]{:S(2)}) async-start(f32[32,1,128]{2,1,0:T(1,128)} %shard_map.136), calls=%async_computation.1 | async-start | bytes 32768 | tf_op jit(solution)/shard_map/all_to_all | solution.py:448

commit v7 on v6

--- a/solution.py
+++ b/solution.py
@@ -74,7 +74,7 @@
     txb[GX : GX + count, :size], txb[GX : GX + count, size:] = -s, c
     high, low = halves(tx)
     tx = np.concatenate([np.concatenate([high, high], 1), np.concatenate([low, 0 * low], 1)], 0)
-    return stacked_table(ty, 0), tx, np.concatenate(halves(txb), 0), stacked_table(tyb, 0)
+    return stacked_table(ty, 0), tx, np.concatenate(halves(txb), 0), np.concatenate(halves(tyb), 1)
 
 
 def packing(size):
@@ -237,60 +237,75 @@
     imag = jnp.concatenate([v for r in range(rows // 2, rows) for v in lines[r]], axis=1)
     left = jnp.concatenate([real, imag], axis=1).astype(BF16)
     right = jnp.concatenate([imag, -real], axis=1).astype(BF16)
-    none = jnp.zeros((GY - bands, left.shape[1]), BF16)
-    tall = jnp.concatenate([left, none, right, none], axis=0)
-    value = dot(left, tall, ((1,), (1,)))
+    none = jnp.zeros((bands, GY - bands), F32)
+    value = jnp.concatenate(
+        [dot(left, left, ((1,), (1,))), none, dot(left, right, ((1,), (1,))), none], axis=1
+    )
     for g in range(sum_ref.shape[0] // bands):
         sum_ref[g * bands : (g + 1) * bands, 0, :] = value
 
 
-def slab_kernel(devices, size, depth, again, *refs):
-    planes, refs = refs[:devices], refs[devices:]
-    marks = planes
-    if again:
-        marks, refs = refs[:devices], refs[devices:]
-    pot_ref, ty_ref, tx_ref, txb_ref, tyb_ref = refs[:5]
-    outs = refs[5 : 5 + devices]
-    in_ref, y0_ref, y1_ref, back_ref, q_ref, box_ref, slot_ref, spot_ref = refs[5 + devices :]
-    pad = round_up(depth, 8)
-    rows = 2 * pad
-    cols = planes[0].shape[1]
-    radius = size // 4
-    places, slots = packing(size)
-    zero = jnp.zeros((), BF16)
-    lane = lax.broadcasted_iota(jnp.int32, (pad, 128), 1)
-
-    def between(first, last):
-        return (lane >= first) & (lane <= last)
-
-    def one_hot(k, at, wide):
-        slot = jnp.broadcast_to(marks[k][rows : rows + 1, at : at + wide], (16, wide)).astype(BF16)
-        spot = jnp.broadcast_to(marks[k][rows + 1 : rows + 2, at : at + wide], (128, wide))
-        down = lax.broadcasted_iota(jnp.int32, (128, wide), 0).astype(F32)
-        hot = jnp.where(spot == down, 1.0, 0.0).astype(BF16)
-        return slot, [hot[16 * i : 16 * i + 16] for i in range(8)]
-
-    def expand(pieces, first, count):
-        slot, hot = pieces
-        tall = []
-        for v in range(first, first + count):
-            here = slot == float(v)
-            tall += [jnp.where(here, piece, zero) for piece in hot]
-        return jnp.concatenate(tall, axis=0)
-
-    lhs = jnp.concatenate(split(jnp.concatenate([ref[:rows] for ref in planes], axis=1)), axis=0)
+def scatter(plane_ref, mark_ref, slots):
+    rows, cols = mark_ref.shape[0] - 8, mark_ref.shape[1]
     row = lax.broadcasted_iota(jnp.int32, (8, 256), 0)
     side = lax.broadcasted_iota(jnp.int32, (8, 256), 1) // 128
     spread = jnp.where(row == side, 1.0, 0.0).astype(BF16)
-    both = dot(jnp.concatenate([ref[rows : rows + 8].astype(BF16) for ref in marks], axis=1), spread, ((0,), (0,)))
-    slot_ref[...] = both[:, :128].astype(BF16)
-    along = lax.broadcasted_iota(jnp.int32, (cols * devices, 128), 1).astype(F32)
-    spot_ref[...] = jnp.where(both[:, 128:] == along, 1.0, 0.0).astype(BF16)
+    both = dot(mark_ref[rows:].astype(BF16), spread, ((0,), (0,)))
+    slot = both[:, :128].astype(BF16)
+    along = lax.broadcasted_iota(jnp.int32, (cols, 128), 1).astype(F32)
+    spot = jnp.where(both[:, 128:] == along, 1.0, 0.0).astype(BF16)
+    lhs = jnp.concatenate(split(plane_ref[:rows]), axis=0)
+    zero = jnp.zeros((), BF16)
+    for t in range(0, slots, 2):
+        hot = [jnp.where(slot == float(v), spot, zero) for v in (t, t + 1)]
+        got = dot(lhs, jnp.concatenate(hot, axis=1))
+        yield t, got[:rows] + got[rows:]
+
+
+def gather(box, mark_ref, out_ref, slots):
+    rows, cols = mark_ref.shape[0] - 8, mark_ref.shape[1]
+    zero = jnp.zeros((), BF16)
+    wide = min(256, cols)
+    for at in range(0, cols, wide):
+        slot = jnp.broadcast_to(mark_ref[rows : rows + 1, at : at + wide], (16, wide)).astype(BF16)
+        spot = jnp.broadcast_to(mark_ref[rows + 1 : rows + 2, at : at + wide], (128, wide))
+        down = lax.broadcasted_iota(jnp.int32, (128, wide), 0).astype(F32)
+        hot = jnp.where(spot == down, 1.0, 0.0).astype(BF16)
+        tall = []
+        for v in range(slots):
+            here = slot == float(v)
+            tall += [jnp.where(here, hot[16 * i : 16 * i + 16], zero) for i in range(8)]
+        got = dot(box, jnp.concatenate(tall, axis=0))
+        out_ref[:, at : at + wide] = got[:rows] + got[rows:]
+
+
+def scatter_kernel(slots, plane_ref, mark_ref, *refs):
+    before, after = refs[:-1], refs[-1]
+    for t, tile in scatter(plane_ref, mark_ref, slots):
+        here = slice(128 * t, 128 * t + 256)
+        after[:, here] = tile + before[0][:, here] if before else tile
+
+
+def gather_kernel(slots, box_ref, mark_ref, out_ref):
+    gather(box_ref[...], mark_ref, out_ref, slots)
+
+
+def slab_kernel(devices, size, depth, plane_ref, before_ref, *refs):
+    marks, refs = refs[: devices - 1], refs[devices - 1 :]
+    pot_ref, ty_ref, tx_ref, txb_ref, tyb_ref = refs[:5]
+    outs, box_ref = refs[5 : 4 + devices], refs[4 + devices]
+    in_ref, y0_ref, y1_ref, back_ref, q_ref = refs[5 + devices :]
+    pad = round_up(depth, 8)
+    radius = size // 4
+    places, slots = packing(size)
+    lane = lax.broadcasted_iota(jnp.int32, (pad, 128), 1)
+
+    def between(first, last):
+        return (lane >= first) & (lane <= last)
+
     in_ref[...] = jnp.zeros(in_ref.shape, F32)
-    for t in range(0, slots, 2):
-        hot = [jnp.where(slot_ref[...] == float(v), spot_ref[...], zero) for v in (t, t + 1)]
-        got = dot(lhs, jnp.concatenate(hot, axis=1))
-        got = got[:rows] + got[rows:]
+    for t, tile in scatter(plane_ref, marks[-1], slots):
+        got = tile + before_ref[:, 128 * t : 128 * t + 256]
         for i, (width, slot, middle) in enumerate(places):
             if slot // 2 * 2 != t:
                 continue
@@ -327,7 +342,9 @@
                         p * GX : (p + 1) * GX, at : at + 128
                     ]
         part = slice(first * GX, last * GX)
-        q_ref[part] = dot(tripled(back_ref[part], 1), tyb_ref[...])
+        high, low = split(back_ref[part])
+        moved = dot(high, tyb_ref[...])
+        q_ref[part] = moved[:, :128] + moved[:, 128:] + dot(low, tyb_ref[:, :128])
 
     for s in range(slots):
         re, im = jnp.zeros((pad, 128), F32), jnp.zeros((pad, 128), F32)
@@ -341,11 +358,8 @@
         box_ref[:, 128 * s : 128 * s + 128] = jnp.concatenate(split(jnp.concatenate([re, im], axis=0)), axis=0)
 
     box = box_ref[...]
-    wide = min(256, cols)
-    for k in range(devices):
-        for at in range(0, cols, wide):
-            got = dot(box, expand(one_hot(k, at, wide), 0, slots))
-            outs[k][:, at : at + wide] = got[:rows] + got[rows:]
+    for k in range(devices - 1):
+        gather(box, marks[k], outs[k], slots)
 
 
 def body(devices, bands, psi, col_map, potential, lower, upper):
@@ -401,11 +415,22 @@
         )
     )
 
-    def slab(values, again):
-        given = values + (marks if again else [])
-        return call(
-            functools.partial(slab_kernel, devices, size, depth, again),
-            [vmem((rows, cols))] * devices,
+    slots_all = packing(size)[1]
+    box_shape = (rows, 128 * slots_all)
+
+    def slab(values):
+        sums = []
+        for k in range(devices - 1):
+            sums = call(
+                functools.partial(scatter_kernel, slots_all),
+                [vmem(box_shape)],
+                [],
+                [(value, True) for value in [values[k], marks[k]] + list(sums)],
+            )
+        given = [values[-1], sums[0]] + marks[1:]
+        *sent, box = call(
+            functools.partial(slab_kernel, devices, size, depth),
+            [vmem((rows, cols))] * (devices - 1) + [vmem((2 * rows, 128 * slots_all), BF16)],
             [],
             [(value, True) for value in given] + [(pot, False)] + [(table, False) for table in tables],
             [
@@ -414,14 +439,18 @@
                 pltpu.VMEM((GX * pad, 128), F32),
                 pltpu.VMEM((pad * GX, 256), F32),
                 pltpu.VMEM((pad * GX, 128), F32),
-                pltpu.VMEM((2 * rows, 128 * packing(size)[1]), BF16),
-                pltpu.VMEM((cols * devices, 128), BF16),
-                pltpu.VMEM((cols * devices, 128), BF16),
             ],
         )
+        own = call(
+            functools.partial(gather_kernel, slots_all),
+            [vmem((rows, cols))],
+            [],
+            [(box, True), (marks[0], True)],
+        )
+        return list(own) + list(sent)
 
     held = pltpu.VMEM((3 * devices * rows, cols), BF16)
-    planes = exchange(slab(marks, False))
+    planes = exchange(slab(marks))
     first, *sent = call(
         functools.partial(middle_kernel, devices, step, size),
         [vmem((2, size, cols))] + [vmem((rows, cols))] * devices,
@@ -429,7 +458,7 @@
         [(value, True) for value in planes] + [(psi_t, False), (col_row, False), (ahead, False), (back, False)],
         [held],
     )
-    planes = exchange(slab(exchange(sent), True))
+    planes = exchange(slab(exchange(sent)))
     filtered, packed = call(
         functools.partial(last_kernel, devices, bands, step, size),
         [vmem((2, size, cols)), vmem((bands, 2 * slots, cols), BF16)],

time: 76.6 us -> 72.2 us (0.943)
  waiting for transfers between devices: 20.6 us -> 15.4 us
    ppermute x12, waiting for transfers between devices: 14.3 us -> 9.03 us  [exchange(): lax.ppermute(values[k], 'grid', [(d, step(d, k)) for d in range(devices)])]
    pallas_call x6 -> x14, Pallas kernels: 20.7 us -> 20.9 us  [call(): pl.pallas_call(kernel, out_shape=out_shape, in_specs=[SMEM] * len(scalars...]
  transfers between devices with their start and end apart: 13 -> 13, of which waited for: 13 -> 11; matrix products, arithmetic and copies ran while one was open for 3% -> 4% of each run, Pallas kernels for 0% -> 8%
where the time goes in v7:
time: 72.2 us; the launch traced here: 72 us
  Pallas kernels  20.9 us (29%)
  starting transfers between devices  18.6 us (26%)
  waiting for transfers between devices  15.4 us (21%)
  blocking collectives  11.4 us (16%)
  between operations  2.19 us (3%)
  other arithmetic  1.93 us (3%)
  local copies, waits for them, and re-layouts  1.44 us (2%)
    pallas_call x14, Pallas kernels, call(): pl.pallas_call(kernel, out_shape=out_shape, in_specs=[SMEM] * len(scalars...  20.9 us
    ppermute x12, starting transfers between devices, exchange(): lax.ppermute(values[k], 'grid', [(d, step(d, k)) for d in range(devices)])  15.4 us
    all_to_all x1, blocking collectives, body(): lax.all_to_all(packed, 'band', 0, 0, tiled=True)  11.4 us
    ppermute x12, waiting for transfers between devices, exchange(): lax.ppermute(values[k], 'grid', [(d, step(d, k)) for d in range(devices)])  9.03 us
    all_to_all x1, waiting for transfers between devices, body(): lax.all_to_all(partial_sum, ('grid', 'band'), 0, 0, tiled=True)  6.39 us
    all_to_all x1, starting transfers between devices, body(): lax.all_to_all(partial_sum, ('grid', 'band'), 0, 0, tiled=True)  3.23 us
  transfers between devices with their start and end apart: 13, of which 11 were waited for; matrix products, arithmetic and copies ran while one was open for 4% of the time, Pallas kernels for 8%

profile of v7, /device:TPU:0, one launch (start us, length us, event | category | flops | bytes accessed | tf_op | source)
XLA Modules:
  0.0 72.0 jit_solution(14016787292706126193)
XLA Ops:
  0.6 1.6 %shard_map.131 = (f32[56,512]{1,0:T(8,128)S(1)}, f32[56,512]{1,0:T(8,128)S(1)}, f32[56,512]{1,0:T(8,128)S(1)}, f32[56,512]{1,0:T(8,128)S(1)}) custom-call(s32[1]{0:T(128)} %bitcast.me_ref, f32[2,96,512]{2,1,0:T(8,128)} %bitcast.12, s32[1,512]{1,0:T(1,128)} %bitcast.15, bf16[4,48,576]{2,1,0:T(8,128)(2,1)} %constant.33.clone.refs_2_.refs_6_), custom_call_target="tpu_custom_call" | custom-call | tf_op jit(solution)/shard_map/pallas_call | solution.py:119
  2.2 3.0 %collective-permute-start.2 = (f32[56,512]{1,0:T(8,128)S(1)}, f32[56,512]{1,0:T(8,128)S(1)}, u32[]{:S(2)}, u32[]{:S(2)}) collective-permute-start(f32[56,512]{1,0:T(8,128)S(1)} %get-tuple-element.23), channel_id=1, source_target_pairs={{0,8},{8,0},{16,24},{24,16},{1,9},{9,1},{17,25},{25,17},{2,10},{10... | collective-permute-start | bytes 344072 | tf_op jit(solution)/shard_map/ppermute | solution.py:381
  5.2 1.5 %collective-permute-start.1 = (f32[56,512]{1,0:T(8,128)S(1)}, f32[56,512]{1,0:T(8,128)S(1)}, u32[]{:S(2)}, u32[]{:S(2)}) collective-permute-start(f32[56,512]{1,0:T(8,128)S(1)} %get-tuple-element.22), channel_id=1, source_target_pairs={{0,16},{8,24},{16,0},{24,8},{1,17},{9,25},{17,1},{25,9},{2,18},{10... | collective-permute-start | bytes 344072 | tf_op jit(solution)/shard_map/ppermute | solution.py:381
  6.8 0.0 collective-permute-start
  6.8 1.2 %broadcast_multiply_fusion = f32[24,9216]{1,0:T(8,128)S(1)} fusion(f32[24,9216]{1,0:T(8,128)} %param.14), kind=kLoop, calls=%fused_computation | loop fusion | flops 221184 | bytes 1769472 | tf_op jit(solution)/shard_map/mul | solution.py:394
  8.0 0.8 %shard_map.132.refs_0_ = f32[48,2048]{1,0:T(8,128)S(1)} custom-call(f32[56,512]{1,0:T(8,128)S(1)} %get-tuple-element.24.plane_ref.mark_ref, f32[56,512]{1,0:T(8,128)S(1)} %get-tuple-element.24.plane_ref.mark_ref), custom_call_target="tpu_custom_call" | custom-call | tf_op jit(solution)/shard_map/pallas_call | solution.py:119
  8.8 0.5 reshape.27
  9.3 0.1 pad.4.refs_3_
  9.4 0.0 copy-start.3
  9.4 0.0 copy-start.4
  9.4 0.0 copy-start.5
  9.4 0.0 copy-start.6
  9.4 0.0 collective-permute-done.2.plane_ref.mark_ref.refs_0_
  9.4 0.8 %shard_map.133.refs_0_ = f32[48,2048]{1,0:T(8,128)S(1)} custom-call(f32[56,512]{1,0:T(8,128)S(1)} %collective-permute-done.2.plane_ref.mark_ref.refs_0_, f32[56,512]{1,0:T(8,128)S(1)} %collective-permute-done.2.plane_ref.mark_ref.refs_0_, f32[48,2048]{1,0:T(8,128)S(1)} %shard_map.132.refs_0_), custom_call_target="tpu_custom_call" | custom-call | tf_op jit(solution)/shard_map/pallas_call | solution.py:119
  10.2 1.4 %collective-permute-done.1.plane_ref.mark_ref.refs_1_ = f32[56,512]{1,0:T(8,128)S(1)} collective-permute-done((f32[56,512]{1,0:T(8,128)S(1)}, f32[56,512]{1,0:T(8,128)S(1)}, u32[]{:S(2)}, u32[]{:S(2)}) %collective-permute-start.1) | collective-permute-done | bytes 114720 | tf_op jit(solution)/shard_map/ppermute | solution.py:381
  11.6 0.8 %shard_map.134.before_ref = f32[48,2048]{1,0:T(8,128)S(1)} custom-call(f32[56,512]{1,0:T(8,128)S(1)} %collective-permute-done.1.plane_ref.mark_ref.refs_1_, f32[56,512]{1,0:T(8,128)S(1)} %collective-permute-done.1.plane_ref.mark_ref.refs_1_, f32[48,2048]{1,0:T(8,128)S(1)} %shard_map.133.refs_0_), custom_call_target="tpu_custom_call" | custom-call | tf_op jit(solution)/shard_map/pallas_call | solution.py:119
  12.4 0.0 copy-start
  12.4 0.0 copy-start.1
  12.4 0.0 copy-start.2
  12.4 0.0 copy-start.8
  12.4 0.1 collective-permute-done.plane_ref.refs_2_
  12.5 0.0 copy-done.3
  12.5 0.0 copy-done.4
  12.5 0.0 copy-done.5
  12.5 0.0 copy-done.6
  12.5 5.6 %shard_map.135 = (f32[48,512]{1,0:T(8,128)S(1)}, f32[48,512]{1,0:T(8,128)S(1)}, f32[48,512]{1,0:T(8,128)S(1)}, bf16[96,2048]{1,0:T(8,128)(2,1)S(1)}) custom-call(f32[56,512]{1,0:T(8,128)S(1)} %collective-permute-done.plane_ref.refs_2_, f32[48,2048]{1,0:T(8,128)S(1)} %shard_map.134.before_ref, ...), custom_call_target="tpu_custom_call" | custom-call | tf_op jit(solution)/shard_map/pallas_call | solution.py:119
  18.2 1.1 %collective-permute-start.3 = (f32[48,512]{1,0:T(8,128)S(1)}, f32[48,512]{1,0:T(8,128)S(1)}, u32[]{:S(2)}, u32[]{:S(2)}) collective-permute-start(f32[48,512]{1,0:T(8,128)S(1)} %get-tuple-element.26), channel_id=1, source_target_pairs={{0,8},{8,0},{16,24},{24,16},{1,9},{9,1},{17,25},{25,17},{2,10},{10... | collective-permute-start | bytes 294920 | tf_op jit(solution)/shard_map/ppermute | solution.py:381
  19.3 1.7 %collective-permute-start.4 = (f32[48,512]{1,0:T(8,128)S(1)}, f32[48,512]{1,0:T(8,128)S(1)}, u32[]{:S(2)}, u32[]{:S(2)}) collective-permute-start(f32[48,512]{1,0:T(8,128)S(1)} %get-tuple-element.27), channel_id=1, source_target_pairs={{0,16},{8,24},{16,0},{24,8},{1,17},{9,25},{17,1},{25,9},{2,18},{10... | collective-permute-start | bytes 294920 | tf_op jit(solution)/shard_map/ppermute | solution.py:381
  21.0 0.9 %collective-permute-start.5 = (f32[48,512]{1,0:T(8,128)S(1)}, f32[48,512]{1,0:T(8,128)S(1)}, u32[]{:S(2)}, u32[]{:S(2)}) collective-permute-start(f32[48,512]{1,0:T(8,128)S(1)} %get-tuple-element.28), channel_id=1, source_target_pairs={{0,24},{8,16},{16,8},{24,0},{1,25},{9,17},{17,9},{25,1},{2,26},{10... | collective-permute-start | bytes 294920 | tf_op jit(solution)/shard_map/ppermute | solution.py:381
  23.2 0.5 shard_map.136.refs_0_
  23.7 0.2 collective-permute-done.3.refs_1_
  23.8 0.8 %collective-permute-done.4.refs_2_ = f32[48,512]{1,0:T(8,128)S(1)} collective-permute-done((f32[48,512]{1,0:T(8,128)S(1)}, f32[48,512]{1,0:T(8,128)S(1)}, u32[]{:S(2)}, u32[]{:S(2)}) %collective-permute-start.4) | collective-permute-done | bytes 98336 | tf_op jit(solution)/shard_map/ppermute | solution.py:381
  24.6 1.8 %collective-permute-done.5.refs_3_ = f32[48,512]{1,0:T(8,128)S(1)} collective-permute-done((f32[48,512]{1,0:T(8,128)S(1)}, f32[48,512]{1,0:T(8,128)S(1)}, u32[]{:S(2)}, u32[]{:S(2)}) %collective-permute-start.5) | collective-permute-done | bytes 98336 | tf_op jit(solution)/shard_map/ppermute | solution.py:381
  26.5 0.0 copy-done
  26.5 0.0 copy-done.1
  26.5 0.0 copy-done.2
  26.5 0.7 %shard_map.137 = (f32[2,96,512]{2,1,0:T(8,128)S(1)}, f32[48,512]{1,0:T(8,128)S(1)}, f32[48,512]{1,0:T(8,128)S(1)}, f32[48,512]{1,0:T(8,128)S(1)}, f32[48,512]{1,0:T(8,128)S(1)}) custom-call(s32[1]{0:T(128)} %bitcast.me_ref, f32[1]{0:T(128)S(6)} %copy.17.low_ref, f32[1]{0:T(128)S(6)} %copy.18.up_ref, f32[48,512]{1,0:T(8,128)S(1)} %shard_map.136.refs_0_, ...), custom_call_target="tpu_custom_call" | custom-call | tf_op jit(solution)/shard_map/pallas_call | solution.py:119
  27.2 1.5 %collective-permute-start.8 = (f32[48,512]{1,0:T(8,128)S(1)}, f32[48,512]{1,0:T(8,128)S(1)}, u32[]{:S(2)}, u32[]{:S(2)}) collective-permute-start(f32[48,512]{1,0:T(8,128)S(1)} %get-tuple-element.31), channel_id=1, source_target_pairs={{0,8},{8,0},{16,24},{24,16},{1,9},{9,1},{17,25},{25,17},{2,10},{10... | collective-permute-start | bytes 294920 | tf_op jit(solution)/shard_map/ppermute | solution.py:381
  28.8 0.2 collective-permute-start.7
  28.9 1.8 %collective-permute-start.6 = (f32[48,512]{1,0:T(8,128)S(1)}, f32[48,512]{1,0:T(8,128)S(1)}, u32[]{:S(2)}, u32[]{:S(2)}) collective-permute-start(f32[48,512]{1,0:T(8,128)S(1)} %get-tuple-element.29), channel_id=1, source_target_pairs={{0,24},{8,16},{16,8},{24,0},{1,25},{9,17},{17,9},{25,1},{2,26},{10... | collective-permute-start | bytes 294920 | tf_op jit(solution)/shard_map/ppermute | solution.py:381
  30.8 0.8 %shard_map.138.refs_0_ = f32[48,2048]{1,0:T(8,128)S(1)} custom-call(f32[48,512]{1,0:T(8,128)S(1)} %get-tuple-element.32.plane_ref, f32[56,512]{1,0:T(8,128)S(1)} %get-tuple-element.24.plane_ref.mark_ref), custom_call_target="tpu_custom_call" | custom-call | tf_op jit(solution)/shard_map/pallas_call | solution.py:119
  31.5 0.4 collective-permute-done.8.plane_ref
  31.9 0.8 %shard_map.139.refs_0_ = f32[48,2048]{1,0:T(8,128)S(1)} custom-call(f32[48,512]{1,0:T(8,128)S(1)} %collective-permute-done.8.plane_ref, f32[56,512]{1,0:T(8,128)S(1)} %collective-permute-done.2.plane_ref.mark_ref.refs_0_, f32[48,2048]{1,0:T(8,128)S(1)} %shard_map.138.refs_0_), custom_call_target="tpu_custom_call" | custom-call | tf_op jit(solution)/shard_map/pallas_call | solution.py:119
  32.7 0.7 collective-permute-done.7.plane_ref
  33.4 0.8 %shard_map.140.before_ref = f32[48,2048]{1,0:T(8,128)S(1)} custom-call(f32[48,512]{1,0:T(8,128)S(1)} %collective-permute-done.7.plane_ref, f32[56,512]{1,0:T(8,128)S(1)} %collective-permute-done.1.plane_ref.mark_ref.refs_1_, f32[48,2048]{1,0:T(8,128)S(1)} %shard_map.139.refs_0_), custom_call_target="tpu_custom_call" | custom-call | tf_op jit(solution)/shard_map/pallas_call | solution.py:119
  34.2 0.0 copy-start.7
  34.2 0.3 collective-permute-done.6.plane_ref
  34.5 5.8 %shard_map.141 = (f32[48,512]{1,0:T(8,128)S(1)}, f32[48,512]{1,0:T(8,128)S(1)}, f32[48,512]{1,0:T(8,128)S(1)}, bf16[96,2048]{1,0:T(8,128)(2,1)S(1)}) custom-call(f32[48,512]{1,0:T(8,128)S(1)} %collective-permute-done.6.plane_ref, f32[48,2048]{1,0:T(8,128)S(1)} %shard_map.140.before_ref, f32[56,512]{1,0:T(8,128)S(1)} %collective-permute-done.2.plane_ref.mark_ref.refs_0_, ...), custom_call_target="tpu_custom_call" | custom-call | tf_op jit(solution)/shard_map/pallas_call | solution.py:119
  40.3 1.9 %collective-permute-start.10 = (f32[48,512]{1,0:T(8,128)S(1)}, f32[48,512]{1,0:T(8,128)S(1)}, u32[]{:S(2)}, u32[]{:S(2)}) collective-permute-start(f32[48,512]{1,0:T(8,128)S(1)} %get-tuple-element.35), channel_id=1, source_target_pairs={{0,16},{8,24},{16,0},{24,8},{1,17},{9,25},{17,1},{25,9},{2,18},{10... | collective-permute-start | bytes 294920 | tf_op jit(solution)/shard_map/ppermute | solution.py:381
  42.2 0.6 collective-permute-start.11
  42.8 1.0 %collective-permute-start.9 = (f32[48,512]{1,0:T(8,128)S(1)}, f32[48,512]{1,0:T(8,128)S(1)}, u32[]{:S(2)}, u32[]{:S(2)}) collective-permute-start(f32[48,512]{1,0:T(8,128)S(1)} %get-tuple-element.34), channel_id=1, source_target_pairs={{0,8},{8,0},{16,24},{24,16},{1,9},{9,1},{17,25},{25,17},{2,10},{10... | collective-permute-start | bytes 294920 | tf_op jit(solution)/shard_map/ppermute | solution.py:381
  43.8 0.5 shard_map.142.refs_0_
  44.3 0.7 collective-permute-done.10.refs_2_
  44.9 2.8 %collective-permute-done.11.refs_3_ = f32[48,512]{1,0:T(8,128)S(1)} collective-permute-done((f32[48,512]{1,0:T(8,128)S(1)}, f32[48,512]{1,0:T(8,128)S(1)}, u32[]{:S(2)}, u32[]{:S(2)}) %collective-permute-start.11) | collective-permute-done | bytes 98336 | tf_op jit(solution)/shard_map/ppermute | solution.py:381
  47.7 0.0 collective-permute-done.9.refs_1_
  47.7 0.6 shard_map.143
  48.3 11.4 %all_to_all.10.parts_ref = bf16[8,16,512]{2,1,0:T(8,128)(2,1)S(1)} all-to-all(bf16[8,16,512]{2,1,0:T(8,128)(2,1)S(1)} %get-tuple-element.39), channel_id=1, replica_groups=mesh['grid'=4,'band'=8] {'band'}, dimensions={0} | all-to-all | bytes 262144 | tf_op jit(solution)/shard_map/all_to_all | solution.py:474
  59.8 1.0 %shard_map.144 = f32[32,1,128]{2,1,0:T(1,128)} custom-call(bf16[8,16,512]{2,1,0:T(8,128)(2,1)S(1)} %all_to_all.10.parts_ref), custom_call_target="tpu_custom_call" | custom-call | tf_op jit(solution)/shard_map/pallas_call | solution.py:119
  60.8 3.2 %all-to-all-start.1 = ((f32[32,1,128]{2,1,0:T(1,128)}), f32[32,1,128]{2,1,0:T(1,128)S(1)}, u32[]{:S(2)}, u32[]{:S(2)}) async-start(f32[32,1,128]{2,1,0:T(1,128)} %shard_map.144), calls=%async_computation.1 | async-start | bytes 32768 | tf_op jit(solution)/shard_map/all_to_all | solution.py:477
  64.1 0.7 %copy.16 = f32[2,1,512,96]{2,3,1,0:T(8,128)} copy(f32[2,1,512,96]{2,3,1,0:T(8,128)S(1)} %bitcast.11) | data formatting | bytes 786432
  64.8 6.4 %all-to-all-done.1 = f32[32,1,128]{2,1,0:T(1,128)S(1)} async-done(((f32[32,1,128]{2,1,0:T(1,128)}), f32[32,1,128]{2,1,0:T(1,128)S(1)}, u32[]{:S(2)}, u32[]{:S(2)}) %all-to-all-start.1) | async-done | bytes 16416 | tf_op jit(solution)/shard_map/all_to_all | solution.py:477
  71.2 0.1 reduce_sum.9
  71.2 0.1 reshape.29
  71.3 0.6 dynamic-slice_multiply_fusion
  (2 shorter events, 0.0 us)
Async XLA Ops:
  2.2 7.2 %collective-permute-start.2 = (f32[56,512]{1,0:T(8,128)S(1)}, f32[56,512]{1,0:T(8,128)S(1)}, u32[]{:S(2)}, u32[]{:S(2)}) collective-permute-start(f32[56,512]{1,0:T(8,128)S(1)} %get-tuple-element.23), channel_id=1, source_target_pairs={{0,8},{8,0},{16,24},{24,16},{1,9},{9,1},{17,25},{25,17},{2,10},{10... | collective-permute-start | bytes 344072 | tf_op jit(solution)/shard_map/ppermute | solution.py:381
  5.2 6.4 %collective-permute-start.1 = (f32[56,512]{1,0:T(8,128)S(1)}, f32[56,512]{1,0:T(8,128)S(1)}, u32[]{:S(2)}, u32[]{:S(2)}) collective-permute-start(f32[56,512]{1,0:T(8,128)S(1)} %get-tuple-element.22), channel_id=1, source_target_pairs={{0,16},{8,24},{16,0},{24,8},{1,17},{9,25},{17,1},{25,9},{2,18},{10... | collective-permute-start | bytes 344072 | tf_op jit(solution)/shard_map/ppermute | solution.py:381
  6.8 5.7 %collective-permute-start = (f32[56,512]{1,0:T(8,128)S(1)}, f32[56,512]{1,0:T(8,128)S(1)}, u32[]{:S(2)}, u32[]{:S(2)}) collective-permute-start(f32[56,512]{1,0:T(8,128)S(1)} %get-tuple-element.21), channel_id=1, source_target_pairs={{0,24},{8,16},{16,8},{24,0},{1,25},{9,17},{17,9},{25,1},{2,26},{10... | collective-permute-start | bytes 344072 | tf_op jit(solution)/shard_map/ppermute | solution.py:381
  9.4 3.1 %copy-start.3 = (bf16[384,256]{1,0:T(8,128)(2,1)S(1)}, bf16[384,256]{1,0:T(8,128)(2,1)}, u32[]{:S(2)}) copy-start(bf16[384,256]{1,0:T(8,128)(2,1)} %constant.34.clone.refs_4_) | copy-start | bytes 589828
  9.4 3.1 %copy-start.4 = (bf16[384,224]{1,0:T(8,128)(2,1)S(1)}, bf16[384,224]{1,0:T(8,128)(2,1)}, u32[]{:S(2)}) copy-start(bf16[384,224]{1,0:T(8,128)(2,1)} %constant.35.clone.refs_5_) | copy-start | bytes 516100
  9.4 3.1 %copy-start.5 = (bf16[256,256]{1,0:T(8,128)(2,1)S(1)}, bf16[256,256]{1,0:T(8,128)(2,1)}, u32[]{:S(2)}) copy-start(bf16[256,256]{1,0:T(8,128)(2,1)} %constant.37.clone.refs_7_) | copy-start | bytes 393220
  9.4 3.1 %copy-start.6 = (bf16[224,192]{1,0:T(8,128)(2,1)S(1)}, bf16[224,192]{1,0:T(8,128)(2,1)}, u32[]{:S(2)}) copy-start(bf16[224,192]{1,0:T(8,128)(2,1)} %constant.36.clone.refs_6_) | copy-start | bytes 258052
  12.4 14.1 %copy-start = (f32[2,1,512,96]{2,3,1,0:T(8,128)S(1)}, f32[2,1,512,96]{2,3,1,0:T(8,128)}, u32[]{:S(2)}) copy-start(f32[2,1,512,96]{2,3,1,0:T(8,128)} %param.12) | copy-start | bytes 1179652
  12.4 14.1 %copy-start.1 = (bf16[192,576]{1,0:T(8,128)(2,1)S(1)}, bf16[192,576]{1,0:T(8,128)(2,1)}, u32[]{:S(2)}) copy-start(bf16[192,576]{1,0:T(8,128)(2,1)} %constant.38.clone.refs_7_) | copy-start | bytes 663556
  12.4 14.1 %copy-start.2 = (bf16[4,48,576]{2,1,0:T(8,128)(2,1)S(1)}, bf16[4,48,576]{2,1,0:T(8,128)(2,1)}, u32[]{:S(2)}) copy-start(bf16[4,48,576]{2,1,0:T(8,128)(2,1)} %constant.33.clone.refs_2_.refs_6_) | copy-start | bytes 663556
  12.4 14.1 %copy-start.8 = (s32[512]{0:T(512)S(1)}, s32[512]{0:T(512)}, u32[]{:S(2)}) copy-start(s32[512]{0:T(512)} %param.13) | copy-start | bytes 6148
  18.2 5.7 %collective-permute-start.3 = (f32[48,512]{1,0:T(8,128)S(1)}, f32[48,512]{1,0:T(8,128)S(1)}, u32[]{:S(2)}, u32[]{:S(2)}) collective-permute-start(f32[48,512]{1,0:T(8,128)S(1)} %get-tuple-element.26), channel_id=1, source_target_pairs={{0,8},{8,0},{16,24},{24,16},{1,9},{9,1},{17,25},{25,17},{2,10},{10... | collective-permute-start | bytes 294920 | tf_op jit(solution)/shard_map/ppermute | solution.py:381
  19.3 5.4 %collective-permute-start.4 = (f32[48,512]{1,0:T(8,128)S(1)}, f32[48,512]{1,0:T(8,128)S(1)}, u32[]{:S(2)}, u32[]{:S(2)}) collective-permute-start(f32[48,512]{1,0:T(8,128)S(1)} %get-tuple-element.27), channel_id=1, source_target_pairs={{0,16},{8,24},{16,0},{24,8},{1,17},{9,25},{17,1},{25,9},{2,18},{10... | collective-permute-start | bytes 294920 | tf_op jit(solution)/shard_map/ppermute | solution.py:381
  21.0 5.5 %collective-permute-start.5 = (f32[48,512]{1,0:T(8,128)S(1)}, f32[48,512]{1,0:T(8,128)S(1)}, u32[]{:S(2)}, u32[]{:S(2)}) collective-permute-start(f32[48,512]{1,0:T(8,128)S(1)} %get-tuple-element.28), channel_id=1, source_target_pairs={{0,24},{8,16},{16,8},{24,0},{1,25},{9,17},{17,9},{25,1},{2,26},{10... | collective-permute-start | bytes 294920 | tf_op jit(solution)/shard_map/ppermute | solution.py:381
  27.2 4.7 %collective-permute-start.8 = (f32[48,512]{1,0:T(8,128)S(1)}, f32[48,512]{1,0:T(8,128)S(1)}, u32[]{:S(2)}, u32[]{:S(2)}) collective-permute-start(f32[48,512]{1,0:T(8,128)S(1)} %get-tuple-element.31), channel_id=1, source_target_pairs={{0,8},{8,0},{16,24},{24,16},{1,9},{9,1},{17,25},{25,17},{2,10},{10... | collective-permute-start | bytes 294920 | tf_op jit(solution)/shard_map/ppermute | solution.py:381
  28.8 4.6 %collective-permute-start.7 = (f32[48,512]{1,0:T(8,128)S(1)}, f32[48,512]{1,0:T(8,128)S(1)}, u32[]{:S(2)}, u32[]{:S(2)}) collective-permute-start(f32[48,512]{1,0:T(8,128)S(1)} %get-tuple-element.30), channel_id=1, source_target_pairs={{0,16},{8,24},{16,0},{24,8},{1,17},{9,25},{17,1},{25,9},{2,18},{10... | collective-permute-start | bytes 294920 | tf_op jit(solution)/shard_map/ppermute | solution.py:381
  28.9 5.5 %collective-permute-start.6 = (f32[48,512]{1,0:T(8,128)S(1)}, f32[48,512]{1,0:T(8,128)S(1)}, u32[]{:S(2)}, u32[]{:S(2)}) collective-permute-start(f32[48,512]{1,0:T(8,128)S(1)} %get-tuple-element.29), channel_id=1, source_target_pairs={{0,24},{8,16},{16,8},{24,0},{1,25},{9,17},{17,9},{25,1},{2,26},{10... | collective-permute-start | bytes 294920 | tf_op jit(solution)/shard_map/ppermute | solution.py:381
  34.2 13.5 %copy-start.7 = (bf16[2,128,96]{2,1,0:T(8,128)(2,1)S(1)}, bf16[2,128,96]{2,1,0:T(8,128)(2,1)}, u32[]{:S(2)}) copy-start(bf16[2,128,96]{2,1,0:T(8,128)(2,1)} %constant.39.clone.refs_8_) | copy-start | bytes 147460
  40.3 4.7 %collective-permute-start.10 = (f32[48,512]{1,0:T(8,128)S(1)}, f32[48,512]{1,0:T(8,128)S(1)}, u32[]{:S(2)}, u32[]{:S(2)}) collective-permute-start(f32[48,512]{1,0:T(8,128)S(1)} %get-tuple-element.35), channel_id=1, source_target_pairs={{0,16},{8,24},{16,0},{24,8},{1,17},{9,25},{17,1},{25,9},{2,18},{10... | collective-permute-start | bytes 294920 | tf_op jit(solution)/shard_map/ppermute | solution.py:381
  42.2 5.5 %collective-permute-start.11 = (f32[48,512]{1,0:T(8,128)S(1)}, f32[48,512]{1,0:T(8,128)S(1)}, u32[]{:S(2)}, u32[]{:S(2)}) collective-permute-start(f32[48,512]{1,0:T(8,128)S(1)} %get-tuple-element.36), channel_id=1, source_target_pairs={{0,24},{8,16},{16,8},{24,0},{1,25},{9,17},{17,9},{25,1},{2,26},{10... | collective-permute-start | bytes 294920 | tf_op jit(solution)/shard_map/ppermute | solution.py:381
  42.8 4.9 %collective-permute-start.9 = (f32[48,512]{1,0:T(8,128)S(1)}, f32[48,512]{1,0:T(8,128)S(1)}, u32[]{:S(2)}, u32[]{:S(2)}) collective-permute-start(f32[48,512]{1,0:T(8,128)S(1)} %get-tuple-element.34), channel_id=1, source_target_pairs={{0,8},{8,0},{16,24},{24,16},{1,9},{9,1},{17,25},{25,17},{2,10},{10... | collective-permute-start | bytes 294920 | tf_op jit(solution)/shard_map/ppermute | solution.py:381
  60.8 10.4 %all-to-all-start.1 = ((f32[32,1,128]{2,1,0:T(1,128)}), f32[32,1,128]{2,1,0:T(1,128)S(1)}, u32[]{:S(2)}, u32[]{:S(2)}) async-start(f32[32,1,128]{2,1,0:T(1,128)} %shard_map.144), calls=%async_computation.1 | async-start | bytes 32768 | tf_op jit(solution)/shard_map/all_to_all | solution.py:477

commit v8 on v7

--- a/solution.py
+++ b/solution.py
@@ -36,21 +36,28 @@
     return np.where(index < size // 2, index, index - size)
 
 
+def kept(size):
+    radius = size // 4
+    return round_up(radius + 1, 8), radius
+
+
 def z_tables(size, devices, pad):
     depth = size // devices
     rows = 2 * pad
-    freq = np.arange(size)
-    ahead = np.zeros((devices, rows, 2 * size))
-    back = np.zeros((2 * size, devices * rows))
+    first, last = kept(size)
+    count = first + last
+    freq = np.concatenate([np.arange(first), np.arange(size - last, size)])
+    ahead = np.zeros((devices, rows, 2 * count))
+    back = np.zeros((2 * count, devices * rows))
     for d in range(devices):
         plane = d * depth + np.arange(depth)
         angle = 2 * np.pi * ((plane[:, None] * freq[None, :]) % size) / size
         c, s = np.cos(angle), np.sin(angle)
-        ahead[d, :depth, :size], ahead[d, :depth, size:] = c, -s
-        ahead[d, pad : pad + depth, :size], ahead[d, pad : pad + depth, size:] = s, c
+        ahead[d, :depth, :count], ahead[d, :depth, count:] = c, -s
+        ahead[d, pad : pad + depth, :count], ahead[d, pad : pad + depth, count:] = s, c
         at = d * rows
-        back[:size, at : at + depth], back[:size, at + pad : at + pad + depth] = c.T, s.T
-        back[size:, at : at + depth], back[size:, at + pad : at + pad + depth] = -s.T, c.T
+        back[:count, at : at + depth], back[:count, at + pad : at + pad + depth] = c.T, s.T
+        back[count:, at : at + depth], back[count:, at + pad : at + pad + depth] = -s.T, c.T
     return stacked_table(ahead, 2), stacked_table(back, 1)
 
 
@@ -138,10 +145,16 @@
     cols = col_row.shape[1]
     radius = size // 4
     gx, gy = position(col_row, size)
-    index = lax.broadcasted_iota(jnp.int32, (size, cols), 0)
-    freq = jnp.where(index < size // 2, index, index - size).astype(F32)
+    first, last = kept(size)
+    index = lax.broadcasted_iota(jnp.int32, (first + last, cols), 0)
+    freq = jnp.where(index < first, index, index - (first + last)).astype(F32)
     radius2 = (gx * gx + gy * gy) + freq * freq
     return radius2 <= float(radius * radius), radius2 * (2.0 / (radius * radius))
+
+
+def kept_rows(ref, p, size):
+    first, last = kept(size)
+    return jnp.concatenate([ref[p, :first], ref[p, size - last :]], axis=0)
 
 
 def to_planes(me, parts, table_ref, outs, step):
@@ -162,13 +175,18 @@
         for j, value in enumerate((high, low, high)):
             held[pl.ds(pl.multiple_of(j * third + at, 16), rows), :] = value
     total = dot(table_ref[...], held[...])
-    return total[:size], total[size:]
+    return total[: sum(kept(size))], total[sum(kept(size)) :]
 
 
 def first_kernel(devices, step, size, me_ref, *refs):
     far, refs = refs[:3], refs[3:]
     outs, (psi_ref, col_ref, ahead_ref, sems) = refs[:devices], refs[devices:]
-    copies = [pltpu.make_async_copy(far[i], refs[devices + i], sems.at[i]) for i in range(3)]
+    first, last = kept(size)
+    pairs = [(far[1], col_ref), (far[2], ahead_ref)]
+    for p in range(2):
+        pairs.append((far[0].at[p, :first], psi_ref.at[p, :first]))
+        pairs.append((far[0].at[p, size - last :], psi_ref.at[p, first:]))
+    copies = [pltpu.make_async_copy(source, target, sems.at[i]) for i, (source, target) in enumerate(pairs)]
     for copy in copies:
         copy.start()
     for copy in copies:
@@ -200,7 +218,7 @@
     back = from_planes(me_ref[0], planes, back_ref, held, step, size)
     parts = []
     for p in range(2):
-        value = jnp.where(inside, ((kinetic - center) * psi_ref[p] + back[p]) / half, 0.0)
+        value = jnp.where(inside, ((kinetic - center) * kept_rows(psi_ref, p, size) + back[p]) / half, 0.0)
         first_ref[p] = value
         parts.append(value)
     to_planes(me_ref[0], parts, ahead_ref, outs, step)
@@ -213,11 +231,14 @@
     half = (up_ref[0] - low_ref[0]) / 2.0
     inside, kinetic = sphere(col_ref[...], size)
     back = from_planes(me_ref[0], planes, back_ref, held, step, size)
+    first, last = kept(size)
     total = None
     for p in range(2):
-        value = 2.0 * ((kinetic - center) * first_ref[p] + back[p]) / half - psi_ref[p]
+        value = 2.0 * ((kinetic - center) * first_ref[p] + back[p]) / half - kept_rows(psi_ref, p, size)
         value = jnp.where(inside, value, 0.0)
-        filtered_ref[p] = value
+        filtered_ref[p, :first] = value[:first]
+        filtered_ref[p, first : size - last] = jnp.zeros((size - last - first, value.shape[1]), F32)
+        filtered_ref[p, size - last :] = value[first:]
         piece = dot(pick_ref[p], value.astype(BF16))
         total = piece if total is None else total + piece
     rows = packed_ref.shape[1]
@@ -225,24 +246,35 @@
         packed_ref[k] = total[k * rows : (k + 1) * rows].astype(BF16)
 
 
-def gram_kernel(bands, parts_ref, sum_ref, held):
+def gram_kernel(bands, parts_ref, sum_ref):
     rows, cols = parts_ref.shape[1:]
-    blocks = cols // 128
-    for k in range(bands):
-        value = parts_ref[k].astype(F32)
-        for j in range(blocks):
-            held[j, k * rows : (k + 1) * rows, :] = value[:, 128 * j : 128 * j + 128]
-    lines = [[held[j, pl.ds(r, bands, stride=rows), :] for j in range(blocks)] for r in range(rows)]
-    real = jnp.concatenate([v for r in range(rows // 2) for v in lines[r]], axis=1)
-    imag = jnp.concatenate([v for r in range(rows // 2, rows) for v in lines[r]], axis=1)
-    left = jnp.concatenate([real, imag], axis=1).astype(BF16)
-    right = jnp.concatenate([imag, -real], axis=1).astype(BF16)
-    none = jnp.zeros((bands, GY - bands), F32)
-    value = jnp.concatenate(
-        [dot(left, left, ((1,), (1,))), none, dot(left, right, ((1,), (1,))), none], axis=1
-    )
+    count = bands * rows
+    stacked = parts_ref[...].reshape(count, cols)
+    product = dot(stacked, stacked, ((1,), (1,)))
+    down = lax.broadcasted_iota(jnp.int32, (count, count), 0) % rows
+    along = lax.broadcasted_iota(jnp.int32, (count, count), 1) % rows
+    real = jnp.where(down == along, product, 0.0)
+    imag = jnp.where(along == down + rows // 2, product, jnp.where(down == along + rows // 2, -product, 0.0))
+    place = lax.broadcasted_iota(jnp.int32, (count, 128), 0) // rows
+    spot = lax.broadcasted_iota(jnp.int32, (count, 128), 1)
+    pieces, places = [], []
+    for p, value in enumerate((real, imag)):
+        value = jnp.sum(value.reshape(bands, rows, count), axis=1)
+        hot = jnp.where(place + p * GY == spot, 1.0, 0.0).astype(BF16)
+        for _ in range(3):
+            pieces.append(value.astype(BF16))
+            value = value - pieces[-1].astype(F32)
+            places.append(hot)
+    value = dot(jnp.concatenate(pieces, axis=1), jnp.concatenate(places, axis=0))
     for g in range(sum_ref.shape[0] // bands):
         sum_ref[g * bands : (g + 1) * bands, 0, :] = value
+
+
+def total_kernel(own, scale, me_ref, parts_ref, out_ref):
+    value = jnp.sum(parts_ref[...], axis=0) * scale
+    value = pltpu.roll(value, lax.rem(128 - me_ref[0] * own, 128), 1)
+    out_ref[0] = value[:, :own]
+    out_ref[1] = value[:, GY : GY + own]
 
 
 def scatter(plane_ref, mark_ref, slots):
@@ -385,11 +417,11 @@
     tables = plane_tables(size)
     count = 2 * radius + 1
     slots = round_up(-(-count // bands), 8)
-    pick = np.zeros((2, bands * 2 * slots, size), ml_dtypes.bfloat16)
+    pick = np.zeros((2, bands * 2 * slots, sum(kept(size))), ml_dtypes.bfloat16)
     for j in range(count):
         at = (j % bands) * 2 * slots + j // bands
-        pick[0, at, (j - radius) % size] = 1
-        pick[1, at + slots, (j - radius) % size] = 1
+        pick[0, at, (j - radius) % sum(kept(size))] = 1
+        pick[1, at + slots, (j - radius) % sum(kept(size))] = 1
 
     pot = (potential * (1.0 / float(size**3))).reshape(depth, size, size)
     pot = jnp.pad(pot, ((0, 0), (0, 0), (0, 128 - size)))
@@ -406,10 +438,10 @@
             [me_arg],
             [(psi_t, True), (col_row, True), (ahead, True)],
             [
-                pltpu.VMEM(psi_t.shape, F32),
+                pltpu.VMEM((2, sum(kept(size)), cols), F32),
                 pltpu.VMEM(col_row.shape, jnp.int32),
                 pltpu.VMEM(ahead.shape, BF16),
-                pltpu.SemaphoreType.DMA((3,)),
+                pltpu.SemaphoreType.DMA((6,)),
             ],
             far=True,
         )
@@ -453,7 +485,7 @@
     planes = exchange(slab(marks))
     first, *sent = call(
         functools.partial(middle_kernel, devices, step, size),
-        [vmem((2, size, cols))] + [vmem((rows, cols))] * devices,
+        [vmem((2, sum(kept(size)), cols))] + [vmem((rows, cols))] * devices,
         [me_arg, lower, upper],
         [(value, True) for value in planes] + [(psi_t, False), (col_row, False), (ahead, False), (back, False)],
         [held],
@@ -472,12 +504,14 @@
         [vmem((devices * bands, 1, 128))],
         [],
         [(lax.all_to_all(packed, "band", 0, 0, tiled=True), True)],
-        [pltpu.VMEM((cols // 128, bands * 2 * slots, 128), F32)],
     )
-    sums = jnp.sum(lax.all_to_all(partial_sum, ("grid", "band"), 0, 0, tiled=True), axis=0)
     own = bands // devices
-    sums = sums.reshape(2, 1, GY)
-    gram = lax.dynamic_slice(sums, (0, 0, me * own), (2, 1, own)) / (4.0 * radius**3)
+    (gram,) = call(
+        functools.partial(total_kernel, own, 1.0 / (4.0 * radius**3)),
+        [jax.ShapeDtypeStruct((2, 1, own), F32)],
+        [me_arg],
+        [(lax.all_to_all(partial_sum, ("grid", "band"), 0, 0, tiled=True), True)],
+    )
     return jnp.transpose(filtered, (0, 2, 1)).reshape(psi.shape), gram
 
 

time: 72.2 us -> 71.9 us (level)
    pallas_call x14 -> x15, Pallas kernels: 20.9 us -> 21.3 us  [call(): pl.pallas_call(kernel, out_shape=out_shape, in_specs=[SMEM] * len(scalars...]
where the time goes in v8:
time: 71.9 us; the launch traced here: 71.6 us
  Pallas kernels  21.3 us (30%)
  starting transfers between devices  18.6 us (26%)
  waiting for transfers between devices  15.4 us (21%)
  blocking collectives  11.5 us (16%)
  between operations  2.19 us (3%)
  local copies, waits for them, and re-layouts  1.36 us (2%)
  other arithmetic  1.24 us (2%)
    pallas_call x15, Pallas kernels, call(): pl.pallas_call(kernel, out_shape=out_shape, in_specs=[SMEM] * len(scalars...  21.3 us
    ppermute x12, starting transfers between devices, exchange(): lax.ppermute(values[k], 'grid', [(d, step(d, k)) for d in range(devices)])  15.4 us
    all_to_all x1, blocking collectives, body(): lax.all_to_all(packed, 'band', 0, 0, tiled=True)  11.5 us
    ppermute x12, waiting for transfers between devices, exchange(): lax.ppermute(values[k], 'grid', [(d, step(d, k)) for d in range(devices)])  9.04 us
    all_to_all x1, waiting for transfers between devices, body(): lax.all_to_all(partial_sum, ('grid', 'band'), 0, 0, tiled=True)  6.4 us
    all_to_all x1, starting transfers between devices, body(): lax.all_to_all(partial_sum, ('grid', 'band'), 0, 0, tiled=True)  3.24 us
  transfers between devices with their start and end apart: 13, of which 11 were waited for; matrix products, arithmetic and copies ran while one was open for 4% of the time, Pallas kernels for 8%

profile of v8, /device:TPU:0, one launch (start us, length us, event | category | flops | bytes accessed | tf_op | source)
XLA Modules:
  0.0 71.6 jit_solution(4537381601365200893)
XLA Ops:
  0.6 1.5 %shard_map.131 = (f32[56,512]{1,0:T(8,128)S(1)}, f32[56,512]{1,0:T(8,128)S(1)}, f32[56,512]{1,0:T(8,128)S(1)}, f32[56,512]{1,0:T(8,128)S(1)}) custom-call(s32[1]{0:T(128)} %bitcast.me_ref, f32[2,96,512]{2,1,0:T(8,128)} %bitcast.11, s32[1,512]{1,0:T(1,128)} %bitcast.14, bf16[4,48,336]{2,1,0:T(8,128)(2,1)} %constant.24.clone.refs_2_.refs_6_), custom_call_target="tpu_custom_call" | custom-call | tf_op jit(solution)/shard_map/pallas_call | solution.py:126
  2.1 3.0 %collective-permute-start.2 = (f32[56,512]{1,0:T(8,128)S(1)}, f32[56,512]{1,0:T(8,128)S(1)}, u32[]{:S(2)}, u32[]{:S(2)}) collective-permute-start(f32[56,512]{1,0:T(8,128)S(1)} %get-tuple-element.23), channel_id=1, source_target_pairs={{0,8},{8,0},{16,24},{24,16},{1,9},{9,1},{17,25},{25,17},{2,10},{10... | collective-permute-start | bytes 344072 | tf_op jit(solution)/shard_map/ppermute | solution.py:413
  5.1 1.5 %collective-permute-start.1 = (f32[56,512]{1,0:T(8,128)S(1)}, f32[56,512]{1,0:T(8,128)S(1)}, u32[]{:S(2)}, u32[]{:S(2)}) collective-permute-start(f32[56,512]{1,0:T(8,128)S(1)} %get-tuple-element.22), channel_id=1, source_target_pairs={{0,16},{8,24},{16,0},{24,8},{1,17},{9,25},{17,1},{25,9},{2,18},{10... | collective-permute-start | bytes 344072 | tf_op jit(solution)/shard_map/ppermute | solution.py:413
  6.6 0.0 collective-permute-start
  6.7 1.2 %broadcast_multiply_fusion = f32[24,9216]{1,0:T(8,128)S(1)} fusion(f32[24,9216]{1,0:T(8,128)} %param.14), kind=kLoop, calls=%fused_computation | loop fusion | flops 221184 | bytes 1769472 | tf_op jit(solution)/shard_map/mul | solution.py:426
  7.9 0.8 %shard_map.132.refs_0_ = f32[48,2048]{1,0:T(8,128)S(1)} custom-call(f32[56,512]{1,0:T(8,128)S(1)} %get-tuple-element.24.plane_ref.mark_ref, f32[56,512]{1,0:T(8,128)S(1)} %get-tuple-element.24.plane_ref.mark_ref), custom_call_target="tpu_custom_call" | custom-call | tf_op jit(solution)/shard_map/pallas_call | solution.py:126
  8.7 0.5 reshape.22
  9.1 0.1 pad.4.refs_3_
  9.2 0.0 copy-start.1
  9.3 0.0 copy-start.2
  9.3 0.0 copy-start.5
  9.3 0.0 copy-start.6
  9.3 0.0 collective-permute-done.2.plane_ref.mark_ref.refs_0_
  9.3 0.8 %shard_map.133.refs_0_ = f32[48,2048]{1,0:T(8,128)S(1)} custom-call(f32[56,512]{1,0:T(8,128)S(1)} %collective-permute-done.2.plane_ref.mark_ref.refs_0_, f32[56,512]{1,0:T(8,128)S(1)} %collective-permute-done.2.plane_ref.mark_ref.refs_0_, f32[48,2048]{1,0:T(8,128)S(1)} %shard_map.132.refs_0_), custom_call_target="tpu_custom_call" | custom-call | tf_op jit(solution)/shard_map/pallas_call | solution.py:126
  10.1 1.4 %collective-permute-done.1.plane_ref.mark_ref.refs_1_ = f32[56,512]{1,0:T(8,128)S(1)} collective-permute-done((f32[56,512]{1,0:T(8,128)S(1)}, f32[56,512]{1,0:T(8,128)S(1)}, u32[]{:S(2)}, u32[]{:S(2)}) %collective-permute-start.1) | collective-permute-done | bytes 114720 | tf_op jit(solution)/shard_map/ppermute | solution.py:413
  11.5 0.8 %shard_map.134.before_ref = f32[48,2048]{1,0:T(8,128)S(1)} custom-call(f32[56,512]{1,0:T(8,128)S(1)} %collective-permute-done.1.plane_ref.mark_ref.refs_1_, f32[56,512]{1,0:T(8,128)S(1)} %collective-permute-done.1.plane_ref.mark_ref.refs_1_, f32[48,2048]{1,0:T(8,128)S(1)} %shard_map.133.refs_0_), custom_call_target="tpu_custom_call" | custom-call | tf_op jit(solution)/shard_map/pallas_call | solution.py:126
  12.3 0.0 copy-start
  12.3 0.0 copy-start.3
  12.3 0.0 copy-start.4
  12.3 0.0 copy-start.8
  12.3 0.1 collective-permute-done.plane_ref.refs_2_
  12.4 0.0 copy-done.1
  12.4 0.0 copy-done.2
  12.4 0.0 copy-done.5
  12.4 0.0 copy-done.6
  12.4 5.6 %shard_map.135 = (f32[48,512]{1,0:T(8,128)S(1)}, f32[48,512]{1,0:T(8,128)S(1)}, f32[48,512]{1,0:T(8,128)S(1)}, bf16[96,2048]{1,0:T(8,128)(2,1)S(1)}) custom-call(f32[56,512]{1,0:T(8,128)S(1)} %collective-permute-done.plane_ref.refs_2_, f32[48,2048]{1,0:T(8,128)S(1)} %shard_map.134.before_ref, ...), custom_call_target="tpu_custom_call" | custom-call | tf_op jit(solution)/shard_map/pallas_call | solution.py:126
  18.0 1.1 %collective-permute-start.3 = (f32[48,512]{1,0:T(8,128)S(1)}, f32[48,512]{1,0:T(8,128)S(1)}, u32[]{:S(2)}, u32[]{:S(2)}) collective-permute-start(f32[48,512]{1,0:T(8,128)S(1)} %get-tuple-element.26), channel_id=1, source_target_pairs={{0,8},{8,0},{16,24},{24,16},{1,9},{9,1},{17,25},{25,17},{2,10},{10... | collective-permute-start | bytes 294920 | tf_op jit(solution)/shard_map/ppermute | solution.py:413
  19.1 1.7 %collective-permute-start.4 = (f32[48,512]{1,0:T(8,128)S(1)}, f32[48,512]{1,0:T(8,128)S(1)}, u32[]{:S(2)}, u32[]{:S(2)}) collective-permute-start(f32[48,512]{1,0:T(8,128)S(1)} %get-tuple-element.27), channel_id=1, source_target_pairs={{0,16},{8,24},{16,0},{24,8},{1,17},{9,25},{17,1},{25,9},{2,18},{10... | collective-permute-start | bytes 294920 | tf_op jit(solution)/shard_map/ppermute | solution.py:413
  20.8 0.9 %collective-permute-start.5 = (f32[48,512]{1,0:T(8,128)S(1)}, f32[48,512]{1,0:T(8,128)S(1)}, u32[]{:S(2)}, u32[]{:S(2)}) collective-permute-start(f32[48,512]{1,0:T(8,128)S(1)} %get-tuple-element.28), channel_id=1, source_target_pairs={{0,24},{8,16},{16,8},{24,0},{1,25},{9,17},{17,9},{25,1},{2,26},{10... | collective-permute-start | bytes 294920 | tf_op jit(solution)/shard_map/ppermute | solution.py:413
  23.0 0.5 shard_map.136.refs_0_
  23.5 0.2 collective-permute-done.3.refs_1_
  23.7 0.8 %collective-permute-done.4.refs_2_ = f32[48,512]{1,0:T(8,128)S(1)} collective-permute-done((f32[48,512]{1,0:T(8,128)S(1)}, f32[48,512]{1,0:T(8,128)S(1)}, u32[]{:S(2)}, u32[]{:S(2)}) %collective-permute-start.4) | collective-permute-done | bytes 98336 | tf_op jit(solution)/shard_map/ppermute | solution.py:413
  24.5 1.8 %collective-permute-done.5.refs_3_ = f32[48,512]{1,0:T(8,128)S(1)} collective-permute-done((f32[48,512]{1,0:T(8,128)S(1)}, f32[48,512]{1,0:T(8,128)S(1)}, u32[]{:S(2)}, u32[]{:S(2)}) %collective-permute-start.5) | collective-permute-done | bytes 98336 | tf_op jit(solution)/shard_map/ppermute | solution.py:413
  26.3 0.0 copy-done
  26.3 0.0 copy-done.3
  26.3 0.0 copy-done.4
  26.3 0.0 copy-done.8
  26.4 0.6 shard_map.137
  27.0 1.6 %collective-permute-start.8 = (f32[48,512]{1,0:T(8,128)S(1)}, f32[48,512]{1,0:T(8,128)S(1)}, u32[]{:S(2)}, u32[]{:S(2)}) collective-permute-start(f32[48,512]{1,0:T(8,128)S(1)} %get-tuple-element.31), channel_id=1, source_target_pairs={{0,8},{8,0},{16,24},{24,16},{1,9},{9,1},{17,25},{25,17},{2,10},{10... | collective-permute-start | bytes 294920 | tf_op jit(solution)/shard_map/ppermute | solution.py:413
  28.5 0.2 collective-permute-start.7
  28.7 1.8 %collective-permute-start.6 = (f32[48,512]{1,0:T(8,128)S(1)}, f32[48,512]{1,0:T(8,128)S(1)}, u32[]{:S(2)}, u32[]{:S(2)}) collective-permute-start(f32[48,512]{1,0:T(8,128)S(1)} %get-tuple-element.29), channel_id=1, source_target_pairs={{0,24},{8,16},{16,8},{24,0},{1,25},{9,17},{17,9},{25,1},{2,26},{10... | collective-permute-start | bytes 294920 | tf_op jit(solution)/shard_map/ppermute | solution.py:413
  30.5 0.8 %shard_map.138.refs_0_ = f32[48,2048]{1,0:T(8,128)S(1)} custom-call(f32[48,512]{1,0:T(8,128)S(1)} %get-tuple-element.32.plane_ref, f32[56,512]{1,0:T(8,128)S(1)} %get-tuple-element.24.plane_ref.mark_ref), custom_call_target="tpu_custom_call" | custom-call | tf_op jit(solution)/shard_map/pallas_call | solution.py:126
  31.3 0.4 collective-permute-done.8.plane_ref
  31.7 0.8 %shard_map.139.refs_0_ = f32[48,2048]{1,0:T(8,128)S(1)} custom-call(f32[48,512]{1,0:T(8,128)S(1)} %collective-permute-done.8.plane_ref, f32[56,512]{1,0:T(8,128)S(1)} %collective-permute-done.2.plane_ref.mark_ref.refs_0_, f32[48,2048]{1,0:T(8,128)S(1)} %shard_map.138.refs_0_), custom_call_target="tpu_custom_call" | custom-call | tf_op jit(solution)/shard_map/pallas_call | solution.py:126
  32.4 0.7 collective-permute-done.7.plane_ref
  33.1 0.8 %shard_map.140.before_ref = f32[48,2048]{1,0:T(8,128)S(1)} custom-call(f32[48,512]{1,0:T(8,128)S(1)} %collective-permute-done.7.plane_ref, f32[56,512]{1,0:T(8,128)S(1)} %collective-permute-done.1.plane_ref.mark_ref.refs_1_, f32[48,2048]{1,0:T(8,128)S(1)} %shard_map.139.refs_0_), custom_call_target="tpu_custom_call" | custom-call | tf_op jit(solution)/shard_map/pallas_call | solution.py:126
  33.9 0.0 copy-start.7
  33.9 0.3 collective-permute-done.6.plane_ref
  34.2 5.8 %shard_map.141 = (f32[48,512]{1,0:T(8,128)S(1)}, f32[48,512]{1,0:T(8,128)S(1)}, f32[48,512]{1,0:T(8,128)S(1)}, bf16[96,2048]{1,0:T(8,128)(2,1)S(1)}) custom-call(f32[48,512]{1,0:T(8,128)S(1)} %collective-permute-done.6.plane_ref, f32[48,2048]{1,0:T(8,128)S(1)} %shard_map.140.before_ref, f32[56,512]{1,0:T(8,128)S(1)} %collective-permute-done.2.plane_ref.mark_ref.refs_0_, ...), custom_call_target="tpu_custom_call" | custom-call | tf_op jit(solution)/shard_map/pallas_call | solution.py:126
  40.0 1.9 %collective-permute-start.10 = (f32[48,512]{1,0:T(8,128)S(1)}, f32[48,512]{1,0:T(8,128)S(1)}, u32[]{:S(2)}, u32[]{:S(2)}) collective-permute-start(f32[48,512]{1,0:T(8,128)S(1)} %get-tuple-element.35), channel_id=1, source_target_pairs={{0,16},{8,24},{16,0},{24,8},{1,17},{9,25},{17,1},{25,9},{2,18},{10... | collective-permute-start | bytes 294920 | tf_op jit(solution)/shard_map/ppermute | solution.py:413
  41.9 0.6 collective-permute-start.11
  42.5 1.0 %collective-permute-start.9 = (f32[48,512]{1,0:T(8,128)S(1)}, f32[48,512]{1,0:T(8,128)S(1)}, u32[]{:S(2)}, u32[]{:S(2)}) collective-permute-start(f32[48,512]{1,0:T(8,128)S(1)} %get-tuple-element.34), channel_id=1, source_target_pairs={{0,8},{8,0},{16,24},{24,16},{1,9},{9,1},{17,25},{25,17},{2,10},{10... | collective-permute-start | bytes 294920 | tf_op jit(solution)/shard_map/ppermute | solution.py:413
  43.6 0.5 shard_map.142.refs_0_
  44.1 0.7 collective-permute-done.10.refs_2_
  44.7 2.8 %collective-permute-done.11.refs_3_ = f32[48,512]{1,0:T(8,128)S(1)} collective-permute-done((f32[48,512]{1,0:T(8,128)S(1)}, f32[48,512]{1,0:T(8,128)S(1)}, u32[]{:S(2)}, u32[]{:S(2)}) %collective-permute-start.11) | collective-permute-done | bytes 98336 | tf_op jit(solution)/shard_map/ppermute | solution.py:413
  47.5 0.0 collective-permute-done.9.refs_1_
  47.5 0.0 copy-done.7
  47.5 0.5 shard_map.143
  48.0 11.5 %all_to_all.10.parts_ref = bf16[8,16,512]{2,1,0:T(8,128)(2,1)S(1)} all-to-all(bf16[8,16,512]{2,1,0:T(8,128)(2,1)S(1)} %get-tuple-element.39), channel_id=1, replica_groups=mesh['grid'=4,'band'=8] {'band'}, dimensions={0} | all-to-all | bytes 262144 | tf_op jit(solution)/shard_map/all_to_all | solution.py:506
  59.5 1.0 %shard_map.144 = f32[32,1,128]{2,1,0:T(1,128)} custom-call(bf16[8,16,512]{2,1,0:T(8,128)(2,1)S(1)} %all_to_all.10.parts_ref), custom_call_target="tpu_custom_call" | custom-call | tf_op jit(solution)/shard_map/pallas_call | solution.py:126
  60.5 3.2 %all-to-all-start.1 = ((f32[32,1,128]{2,1,0:T(1,128)}), f32[32,1,128]{2,1,0:T(1,128)S(1)}, u32[]{:S(2)}, u32[]{:S(2)}) async-start(f32[32,1,128]{2,1,0:T(1,128)} %shard_map.144), calls=%async_computation.1 | async-start | bytes 32768 | tf_op jit(solution)/shard_map/all_to_all | solution.py:513
  63.7 0.7 %copy.15 = f32[2,1,512,96]{2,3,1,0:T(8,128)} copy(f32[2,1,512,96]{2,3,1,0:T(8,128)S(1)} %bitcast.10) | data formatting | bytes 786432
  64.5 6.4 %all-to-all-done.1.parts_ref = f32[32,1,128]{2,1,0:T(1,128)S(1)} async-done(((f32[32,1,128]{2,1,0:T(1,128)}), f32[32,1,128]{2,1,0:T(1,128)S(1)}, u32[]{:S(2)}, u32[]{:S(2)}) %all-to-all-start.1) | async-done | bytes 16416 | tf_op jit(solution)/shard_map/all_to_all | solution.py:513
  70.9 0.7 %shard_map.145 = f32[2,1,2]{2,1,0:T(1,128)} custom-call(s32[1]{0:T(128)} %bitcast.me_ref, f32[32,1,128]{2,1,0:T(1,128)S(1)} %all-to-all-done.1.parts_ref), custom_call_target="tpu_custom_call" | custom-call | tf_op jit(solution)/shard_map/pallas_call | solution.py:126
Async XLA Ops:
  2.1 7.2 %collective-permute-start.2 = (f32[56,512]{1,0:T(8,128)S(1)}, f32[56,512]{1,0:T(8,128)S(1)}, u32[]{:S(2)}, u32[]{:S(2)}) collective-permute-start(f32[56,512]{1,0:T(8,128)S(1)} %get-tuple-element.23), channel_id=1, source_target_pairs={{0,8},{8,0},{16,24},{24,16},{1,9},{9,1},{17,25},{25,17},{2,10},{10... | collective-permute-start | bytes 344072 | tf_op jit(solution)/shard_map/ppermute | solution.py:413
  5.1 6.4 %collective-permute-start.1 = (f32[56,512]{1,0:T(8,128)S(1)}, f32[56,512]{1,0:T(8,128)S(1)}, u32[]{:S(2)}, u32[]{:S(2)}) collective-permute-start(f32[56,512]{1,0:T(8,128)S(1)} %get-tuple-element.22), channel_id=1, source_target_pairs={{0,16},{8,24},{16,0},{24,8},{1,17},{9,25},{17,1},{25,9},{2,18},{10... | collective-permute-start | bytes 344072 | tf_op jit(solution)/shard_map/ppermute | solution.py:413
  6.6 5.7 %collective-permute-start = (f32[56,512]{1,0:T(8,128)S(1)}, f32[56,512]{1,0:T(8,128)S(1)}, u32[]{:S(2)}, u32[]{:S(2)}) collective-permute-start(f32[56,512]{1,0:T(8,128)S(1)} %get-tuple-element.21), channel_id=1, source_target_pairs={{0,24},{8,16},{16,8},{24,0},{1,25},{9,17},{17,9},{25,1},{2,26},{10... | collective-permute-start | bytes 344072 | tf_op jit(solution)/shard_map/ppermute | solution.py:413
  9.2 3.1 %copy-start.1 = (bf16[384,256]{1,0:T(8,128)(2,1)S(1)}, bf16[384,256]{1,0:T(8,128)(2,1)}, u32[]{:S(2)}) copy-start(bf16[384,256]{1,0:T(8,128)(2,1)} %constant.25.clone.refs_4_) | copy-start | bytes 589828
  9.3 3.1 %copy-start.2 = (bf16[384,224]{1,0:T(8,128)(2,1)S(1)}, bf16[384,224]{1,0:T(8,128)(2,1)}, u32[]{:S(2)}) copy-start(bf16[384,224]{1,0:T(8,128)(2,1)} %constant.26.clone.refs_5_) | copy-start | bytes 516100
  9.3 3.1 %copy-start.5 = (bf16[256,256]{1,0:T(8,128)(2,1)S(1)}, bf16[256,256]{1,0:T(8,128)(2,1)}, u32[]{:S(2)}) copy-start(bf16[256,256]{1,0:T(8,128)(2,1)} %constant.28.clone.refs_7_) | copy-start | bytes 393220
  9.3 3.1 %copy-start.6 = (bf16[224,192]{1,0:T(8,128)(2,1)S(1)}, bf16[224,192]{1,0:T(8,128)(2,1)}, u32[]{:S(2)}) copy-start(bf16[224,192]{1,0:T(8,128)(2,1)} %constant.27.clone.refs_6_) | copy-start | bytes 258052
  12.3 14.1 %copy-start = (f32[2,1,512,96]{2,3,1,0:T(8,128)S(1)}, f32[2,1,512,96]{2,3,1,0:T(8,128)}, u32[]{:S(2)}) copy-start(f32[2,1,512,96]{2,3,1,0:T(8,128)} %param.12) | copy-start | bytes 1179652
  12.3 14.1 %copy-start.3 = (bf16[4,48,336]{2,1,0:T(8,128)(2,1)S(1)}, bf16[4,48,336]{2,1,0:T(8,128)(2,1)}, u32[]{:S(2)}) copy-start(bf16[4,48,336]{2,1,0:T(8,128)(2,1)} %constant.24.clone.refs_2_.refs_6_) | copy-start | bytes 387076
  12.3 14.1 %copy-start.4 = (bf16[112,576]{1,0:T(8,128)(2,1)S(1)}, bf16[112,576]{1,0:T(8,128)(2,1)}, u32[]{:S(2)}) copy-start(bf16[112,576]{1,0:T(8,128)(2,1)} %constant.29.clone.refs_7_) | copy-start | bytes 387076
  12.3 14.1 %copy-start.8 = (s32[512]{0:T(512)S(1)}, s32[512]{0:T(512)}, u32[]{:S(2)}) copy-start(s32[512]{0:T(512)} %param.13) | copy-start | bytes 6148
  18.0 5.7 %collective-permute-start.3 = (f32[48,512]{1,0:T(8,128)S(1)}, f32[48,512]{1,0:T(8,128)S(1)}, u32[]{:S(2)}, u32[]{:S(2)}) collective-permute-start(f32[48,512]{1,0:T(8,128)S(1)} %get-tuple-element.26), channel_id=1, source_target_pairs={{0,8},{8,0},{16,24},{24,16},{1,9},{9,1},{17,25},{25,17},{2,10},{10... | collective-permute-start | bytes 294920 | tf_op jit(solution)/shard_map/ppermute | solution.py:413
  19.1 5.4 %collective-permute-start.4 = (f32[48,512]{1,0:T(8,128)S(1)}, f32[48,512]{1,0:T(8,128)S(1)}, u32[]{:S(2)}, u32[]{:S(2)}) collective-permute-start(f32[48,512]{1,0:T(8,128)S(1)} %get-tuple-element.27), channel_id=1, source_target_pairs={{0,16},{8,24},{16,0},{24,8},{1,17},{9,25},{17,1},{25,9},{2,18},{10... | collective-permute-start | bytes 294920 | tf_op jit(solution)/shard_map/ppermute | solution.py:413
  20.8 5.5 %collective-permute-start.5 = (f32[48,512]{1,0:T(8,128)S(1)}, f32[48,512]{1,0:T(8,128)S(1)}, u32[]{:S(2)}, u32[]{:S(2)}) collective-permute-start(f32[48,512]{1,0:T(8,128)S(1)} %get-tuple-element.28), channel_id=1, source_target_pairs={{0,24},{8,16},{16,8},{24,0},{1,25},{9,17},{17,9},{25,1},{2,26},{10... | collective-permute-start | bytes 294920 | tf_op jit(solution)/shard_map/ppermute | solution.py:413
  27.0 4.7 %collective-permute-start.8 = (f32[48,512]{1,0:T(8,128)S(1)}, f32[48,512]{1,0:T(8,128)S(1)}, u32[]{:S(2)}, u32[]{:S(2)}) collective-permute-start(f32[48,512]{1,0:T(8,128)S(1)} %get-tuple-element.31), channel_id=1, source_target_pairs={{0,8},{8,0},{16,24},{24,16},{1,9},{9,1},{17,25},{25,17},{2,10},{10... | collective-permute-start | bytes 294920 | tf_op jit(solution)/shard_map/ppermute | solution.py:413
  28.5 4.6 %collective-permute-start.7 = (f32[48,512]{1,0:T(8,128)S(1)}, f32[48,512]{1,0:T(8,128)S(1)}, u32[]{:S(2)}, u32[]{:S(2)}) collective-permute-start(f32[48,512]{1,0:T(8,128)S(1)} %get-tuple-element.30), channel_id=1, source_target_pairs={{0,16},{8,24},{16,0},{24,8},{1,17},{9,25},{17,1},{25,9},{2,18},{10... | collective-permute-start | bytes 294920 | tf_op jit(solution)/shard_map/ppermute | solution.py:413
  28.7 5.5 %collective-permute-start.6 = (f32[48,512]{1,0:T(8,128)S(1)}, f32[48,512]{1,0:T(8,128)S(1)}, u32[]{:S(2)}, u32[]{:S(2)}) collective-permute-start(f32[48,512]{1,0:T(8,128)S(1)} %get-tuple-element.29), channel_id=1, source_target_pairs={{0,24},{8,16},{16,8},{24,0},{1,25},{9,17},{17,9},{25,1},{2,26},{10... | collective-permute-start | bytes 294920 | tf_op jit(solution)/shard_map/ppermute | solution.py:413
  33.9 13.5 %copy-start.7 = (bf16[2,128,56]{2,1,0:T(8,128)(2,1)S(1)}, bf16[2,128,56]{2,1,0:T(8,128)(2,1)}, u32[]{:S(2)}) copy-start(bf16[2,128,56]{2,1,0:T(8,128)(2,1)} %constant.30.clone.refs_8_) | copy-start | bytes 86020
  40.0 4.7 %collective-permute-start.10 = (f32[48,512]{1,0:T(8,128)S(1)}, f32[48,512]{1,0:T(8,128)S(1)}, u32[]{:S(2)}, u32[]{:S(2)}) collective-permute-start(f32[48,512]{1,0:T(8,128)S(1)} %get-tuple-element.35), channel_id=1, source_target_pairs={{0,16},{8,24},{16,0},{24,8},{1,17},{9,25},{17,1},{25,9},{2,18},{10... | collective-permute-start | bytes 294920 | tf_op jit(solution)/shard_map/ppermute | solution.py:413
  41.9 5.5 %collective-permute-start.11 = (f32[48,512]{1,0:T(8,128)S(1)}, f32[48,512]{1,0:T(8,128)S(1)}, u32[]{:S(2)}, u32[]{:S(2)}) collective-permute-start(f32[48,512]{1,0:T(8,128)S(1)} %get-tuple-element.36), channel_id=1, source_target_pairs={{0,24},{8,16},{16,8},{24,0},{1,25},{9,17},{17,9},{25,1},{2,26},{10... | collective-permute-start | bytes 294920 | tf_op jit(solution)/shard_map/ppermute | solution.py:413
  42.5 4.9 %collective-permute-start.9 = (f32[48,512]{1,0:T(8,128)S(1)}, f32[48,512]{1,0:T(8,128)S(1)}, u32[]{:S(2)}, u32[]{:S(2)}) collective-permute-start(f32[48,512]{1,0:T(8,128)S(1)} %get-tuple-element.34), channel_id=1, source_target_pairs={{0,8},{8,0},{16,24},{24,16},{1,9},{9,1},{17,25},{25,17},{2,10},{10... | collective-permute-start | bytes 294920 | tf_op jit(solution)/shard_map/ppermute | solution.py:413
  60.5 10.4 %all-to-all-start.1 = ((f32[32,1,128]{2,1,0:T(1,128)}), f32[32,1,128]{2,1,0:T(1,128)S(1)}, u32[]{:S(2)}, u32[]{:S(2)}) async-start(f32[32,1,128]{2,1,0:T(1,128)} %shard_map.144), calls=%async_computation.1 | async-start | bytes 32768 | tf_op jit(solution)/shard_map/all_to_all | solution.py:513

commit v9 on v8

--- a/solution.py
+++ b/solution.py
@@ -157,28 +157,40 @@
     return jnp.concatenate([ref[p, :first], ref[p, size - last :]], axis=0)
 
 
-def to_planes(me, parts, table_ref, outs, step):
+def swapped(k, devices):
+    bits = devices.bit_length() - 1
+    if bits % 2:
+        return k
+    half = bits // 2
+    return (k >> half) | ((k & ((1 << half) - 1)) << half)
+
+
+def peers_of(devices, me_ref, odd_ref):
+    return [me_ref[0] ^ (k + odd_ref[0] * (swapped(k, devices) - k)) for k in range(devices)]
+
+
+def to_planes(peers, parts, table_ref, outs):
     value = tripled(jnp.concatenate(parts, axis=0), 0)
-    table = jnp.concatenate([table_ref[step(me, k)] for k in range(len(outs))], axis=0)
+    table = jnp.concatenate([table_ref[peers[k]] for k in range(len(outs))], axis=0)
     total = dot(table, value)
     rows = table_ref.shape[1]
     for k in range(len(outs)):
         outs[k][:rows] = total[k * rows : (k + 1) * rows]
 
 
-def from_planes(me, planes, table_ref, held, step, size):
+def from_planes(peers, planes, table_ref, held, size):
     rows = planes[0].shape[0]
     third = rows * len(planes)
     for k in range(len(planes)):
         high, low = split(planes[k][...])
-        at = step(me, k) * rows
+        at = peers[k] * rows
         for j, value in enumerate((high, low, high)):
             held[pl.ds(pl.multiple_of(j * third + at, 16), rows), :] = value
     total = dot(table_ref[...], held[...])
     return total[: sum(kept(size))], total[sum(kept(size)) :]
 
 
-def first_kernel(devices, step, size, me_ref, *refs):
+def first_kernel(devices, size, me_ref, odd_ref, *refs):
     far, refs = refs[:3], refs[3:]
     outs, (psi_ref, col_ref, ahead_ref, sems) = refs[:devices], refs[devices:]
     first, last = kept(size)
@@ -193,7 +205,7 @@
         copy.wait()
     inside, _ = sphere(col_ref[...], size)
     parts = [jnp.where(inside, psi_ref[p], 0.0) for p in range(2)]
-    to_planes(me_ref[0], parts, ahead_ref, outs, step)
+    to_planes(peers_of(devices, me_ref, odd_ref), parts, ahead_ref, outs)
     radius = size // 4
     gx, gy = position(col_ref[...], size)
     used = gx * gx + gy * gy <= float(radius * radius)
@@ -208,29 +220,30 @@
         outs[k][rows:] = place
 
 
-def middle_kernel(devices, step, size, me_ref, low_ref, up_ref, *refs):
+def middle_kernel(devices, size, me_ref, odd_ref, low_ref, up_ref, *refs):
     planes, refs = refs[:devices], refs[devices:]
     psi_ref, col_ref, ahead_ref, back_ref, first_ref = refs[:5]
     outs, held = refs[5 : 5 + devices], refs[5 + devices]
     center = (up_ref[0] + low_ref[0]) / 2.0
     half = (up_ref[0] - low_ref[0]) / 2.0
     inside, kinetic = sphere(col_ref[...], size)
-    back = from_planes(me_ref[0], planes, back_ref, held, step, size)
+    peers = peers_of(devices, me_ref, odd_ref)
+    back = from_planes(peers, planes, back_ref, held, size)
     parts = []
     for p in range(2):
         value = jnp.where(inside, ((kinetic - center) * kept_rows(psi_ref, p, size) + back[p]) / half, 0.0)
         first_ref[p] = value
         parts.append(value)
-    to_planes(me_ref[0], parts, ahead_ref, outs, step)
-
-
-def last_kernel(devices, bands, step, size, me_ref, low_ref, up_ref, *refs):
+    to_planes(peers, parts, ahead_ref, outs)
+
+
+def last_kernel(devices, bands, size, me_ref, odd_ref, low_ref, up_ref, *refs):
     planes, refs = refs[:devices], refs[devices:]
     psi_ref, first_ref, col_ref, back_ref, pick_ref, filtered_ref, packed_ref, held = refs
     center = (up_ref[0] + low_ref[0]) / 2.0
     half = (up_ref[0] - low_ref[0]) / 2.0
     inside, kinetic = sphere(col_ref[...], size)
-    back = from_planes(me_ref[0], planes, back_ref, held, step, size)
+    back = from_planes(peers_of(devices, me_ref, odd_ref), planes, back_ref, held, size)
     first, last = kept(size)
     total = None
     for p in range(2):
@@ -246,7 +259,7 @@
         packed_ref[k] = total[k * rows : (k + 1) * rows].astype(BF16)
 
 
-def gram_kernel(bands, parts_ref, sum_ref):
+def gram_kernel(bands, parts_ref, sum_ref, spare_ref):
     rows, cols = parts_ref.shape[1:]
     count = bands * rows
     stacked = parts_ref[...].reshape(count, cols)
@@ -268,6 +281,7 @@
     value = dot(jnp.concatenate(pieces, axis=1), jnp.concatenate(places, axis=0))
     for g in range(sum_ref.shape[0] // bands):
         sum_ref[g * bands : (g + 1) * bands, 0, :] = value
+    spare_ref[...] = value
 
 
 def total_kernel(own, scale, me_ref, parts_ref, out_ref):
@@ -402,15 +416,17 @@
     rows = 2 * pad
     me = lax.axis_index("grid")
     me_arg = me.astype(jnp.int32).reshape(1)
+    odd_arg = (lax.axis_index("band") & 1).astype(jnp.int32).reshape(1)
     if devices & (devices - 1):
         raise ValueError("mesh size")
 
-    def step(at, k):
-        return at ^ k
+    def pairs(k):
+        steps = [swapped(k, devices) if band % 2 else k for band in range(bands)]
+        return [(d * bands + b, (d ^ steps[b]) * bands + b) for d in range(devices) for b in range(bands)]
 
     def exchange(values):
         return [values[0]] + [
-            lax.ppermute(values[k], "grid", [(d, step(d, k)) for d in range(devices)]) for k in range(1, devices)
+            lax.ppermute(values[k], ("grid", "band"), pairs(k)) for k in range(1, devices)
         ]
 
     ahead, back = z_tables(size, devices, pad)
@@ -433,9 +449,9 @@
 
     marks = exchange(
         call(
-            functools.partial(first_kernel, devices, step, size),
+            functools.partial(first_kernel, devices, size),
             [vmem((rows + 8, cols))] * devices,
-            [me_arg],
+            [me_arg, odd_arg],
             [(psi_t, True), (col_row, True), (ahead, True)],
             [
                 pltpu.VMEM((2, sum(kept(size)), cols), F32),
@@ -484,24 +500,24 @@
     held = pltpu.VMEM((3 * devices * rows, cols), BF16)
     planes = exchange(slab(marks))
     first, *sent = call(
-        functools.partial(middle_kernel, devices, step, size),
+        functools.partial(middle_kernel, devices, size),
         [vmem((2, sum(kept(size)), cols))] + [vmem((rows, cols))] * devices,
-        [me_arg, lower, upper],
+        [me_arg, odd_arg, lower, upper],
         [(value, True) for value in planes] + [(psi_t, False), (col_row, False), (ahead, False), (back, False)],
         [held],
     )
     planes = exchange(slab(exchange(sent)))
     filtered, packed = call(
-        functools.partial(last_kernel, devices, bands, step, size),
+        functools.partial(last_kernel, devices, bands, size),
         [vmem((2, size, cols)), vmem((bands, 2 * slots, cols), BF16)],
-        [me_arg, lower, upper],
+        [me_arg, odd_arg, lower, upper],
         [(value, True) for value in planes]
         + [(psi_t, False), (first, True), (col_row, False), (back, False), (pick, False)],
         [held],
     )
-    (partial_sum,) = call(
+    partial_sum, _ = call(
         functools.partial(gram_kernel, bands),
-        [vmem((devices * bands, 1, 128))],
+        [vmem((devices * bands, 1, 128)), vmem((bands, 128))],
         [],
         [(lax.all_to_all(packed, "band", 0, 0, tiled=True), True)],
     )

time: 71.9 us -> 72.2 us (level)
  waiting for transfers between devices: 15.4 us -> 16.3 us
    ppermute x12, waiting for transfers between devices: 9.04 us -> 9.9 us  [exchange(): lax.ppermute(values[k], ('grid', 'band'), pairs(k))]
  transfers between devices with their start and end apart: 13 -> 13, of which waited for: 11 -> 12; matrix products, arithmetic and copies ran while one was open for 4% -> 4% of each run, Pallas kernels for 8% -> 8%
where the time goes in v9:
time: 72.2 us; the launch traced here: 72 us
  Pallas kernels  21.3 us (30%)
  starting transfers between devices  18.1 us (25%)
  waiting for transfers between devices  16.3 us (23%)
  blocking collectives  11.5 us (16%)
  between operations  2.19 us (3%)
  local copies, waits for them, and re-layouts  1.36 us (2%)
  other arithmetic  1.24 us (2%)
    pallas_call x15, Pallas kernels, call(): pl.pallas_call(kernel, out_shape=out_shape, in_specs=[SMEM] * len(scalars...  21.3 us
    ppermute x12, starting transfers between devices, exchange(): lax.ppermute(values[k], ('grid', 'band'), pairs(k))  15.6 us
    all_to_all x1, blocking collectives, body(): lax.all_to_all(packed, 'band', 0, 0, tiled=True)  11.5 us
    ppermute x12, waiting for transfers between devices, exchange(): lax.ppermute(values[k], ('grid', 'band'), pairs(k))  9.9 us
    all_to_all x1, waiting for transfers between devices, body(): lax.all_to_all(partial_sum, ('grid', 'band'), 0, 0, tiled=True)  6.39 us
    all_to_all x1, starting transfers between devices, body(): lax.all_to_all(partial_sum, ('grid', 'band'), 0, 0, tiled=True)  2.57 us
  transfers between devices with their start and end apart: 13, of which 12 were waited for; matrix products, arithmetic and copies ran while one was open for 4% of the time, Pallas kernels for 8%

profile of v9, /device:TPU:0, one launch (start us, length us, event | category | flops | bytes accessed | tf_op | source)
XLA Modules:
  0.0 72.0 jit_solution(2970812076631464178)
XLA Ops:
  0.6 1.5 %shard_map.131 = (f32[56,512]{1,0:T(8,128)S(1)}, f32[56,512]{1,0:T(8,128)S(1)}, f32[56,512]{1,0:T(8,128)S(1)}, f32[56,512]{1,0:T(8,128)S(1)}) custom-call(s32[1]{0:T(128)} %bitcast.me_ref, s32[1]{0:T(128)} %bitcast.1.odd_ref, f32[2,96,512]{2,1,0:T(8,128)} %bitcast.12, s32[1,512]{1,0:T(1,128)} %bitcast.15, bf16[4,48,336]{2,1,0:T(8,128)(2,1)} %constant.29.clone.refs_2_.refs_6_), custom_call_target="tpu_custom_call" | custom-call | tf_op jit(solution)/shard_map/pallas_call | solution.py:126
  2.1 3.0 %collective-permute-start.2 = (f32[56,512]{1,0:T(8,128)S(1)}, f32[56,512]{1,0:T(8,128)S(1)}, u32[]{:S(2)}, u32[]{:S(2)}) collective-permute-start(f32[56,512]{1,0:T(8,128)S(1)} %get-tuple-element.24), channel_id=1, source_target_pairs={{0,8},{1,17},{2,10},{3,19},{4,12},{5,21},{6,14},{7,23},{8,0},{9,25... | collective-permute-start | bytes 344072 | tf_op jit(solution)/shard_map/ppermute | solution.py:429
  5.1 1.5 %collective-permute-start.1 = (f32[56,512]{1,0:T(8,128)S(1)}, f32[56,512]{1,0:T(8,128)S(1)}, u32[]{:S(2)}, u32[]{:S(2)}) collective-permute-start(f32[56,512]{1,0:T(8,128)S(1)} %get-tuple-element.23), channel_id=1, source_target_pairs={{0,16},{1,9},{2,18},{3,11},{4,20},{5,13},{6,22},{7,15},{8,24},{9,1... | collective-permute-start | bytes 344072 | tf_op jit(solution)/shard_map/ppermute | solution.py:429
  6.6 0.0 collective-permute-start
  6.7 1.2 %broadcast_multiply_fusion = f32[24,9216]{1,0:T(8,128)S(1)} fusion(f32[24,9216]{1,0:T(8,128)} %param.14), kind=kLoop, calls=%fused_computation | loop fusion | flops 221184 | bytes 1769472 | tf_op jit(solution)/shard_map/mul | solution.py:442
  7.9 0.8 %shard_map.132.refs_0_ = f32[48,2048]{1,0:T(8,128)S(1)} custom-call(f32[56,512]{1,0:T(8,128)S(1)} %get-tuple-element.25.plane_ref.mark_ref, f32[56,512]{1,0:T(8,128)S(1)} %get-tuple-element.25.plane_ref.mark_ref), custom_call_target="tpu_custom_call" | custom-call | tf_op jit(solution)/shard_map/pallas_call | solution.py:126
  8.7 0.5 reshape.26
  9.1 0.1 pad.4.refs_3_
  9.2 0.0 copy-start.1
  9.3 0.0 copy-start.2
  9.3 0.0 copy-start.5
  9.3 0.0 copy-start.6
  9.3 0.0 collective-permute-done.2.plane_ref.mark_ref.refs_0_
  9.3 0.8 %shard_map.133.refs_0_ = f32[48,2048]{1,0:T(8,128)S(1)} custom-call(f32[56,512]{1,0:T(8,128)S(1)} %collective-permute-done.2.plane_ref.mark_ref.refs_0_, f32[56,512]{1,0:T(8,128)S(1)} %collective-permute-done.2.plane_ref.mark_ref.refs_0_, f32[48,2048]{1,0:T(8,128)S(1)} %shard_map.132.refs_0_), custom_call_target="tpu_custom_call" | custom-call | tf_op jit(solution)/shard_map/pallas_call | solution.py:126
  10.1 1.4 %collective-permute-done.1.plane_ref.mark_ref.refs_1_ = f32[56,512]{1,0:T(8,128)S(1)} collective-permute-done((f32[56,512]{1,0:T(8,128)S(1)}, f32[56,512]{1,0:T(8,128)S(1)}, u32[]{:S(2)}, u32[]{:S(2)}) %collective-permute-start.1) | collective-permute-done | bytes 114720 | tf_op jit(solution)/shard_map/ppermute | solution.py:429
  11.5 0.8 %shard_map.134.before_ref = f32[48,2048]{1,0:T(8,128)S(1)} custom-call(f32[56,512]{1,0:T(8,128)S(1)} %collective-permute-done.1.plane_ref.mark_ref.refs_1_, f32[56,512]{1,0:T(8,128)S(1)} %collective-permute-done.1.plane_ref.mark_ref.refs_1_, f32[48,2048]{1,0:T(8,128)S(1)} %shard_map.133.refs_0_), custom_call_target="tpu_custom_call" | custom-call | tf_op jit(solution)/shard_map/pallas_call | solution.py:126
  12.3 0.0 copy-start
  12.3 0.0 copy-start.3
  12.3 0.0 copy-start.4
  12.3 0.0 copy-start.8
  12.3 0.1 collective-permute-done.plane_ref.refs_2_
  12.4 0.0 copy-done.1
  12.4 0.0 copy-done.2
  12.4 0.0 copy-done.5
  12.4 0.0 copy-done.6
  12.4 5.6 %shard_map.135 = (f32[48,512]{1,0:T(8,128)S(1)}, f32[48,512]{1,0:T(8,128)S(1)}, f32[48,512]{1,0:T(8,128)S(1)}, bf16[96,2048]{1,0:T(8,128)(2,1)S(1)}) custom-call(f32[56,512]{1,0:T(8,128)S(1)} %collective-permute-done.plane_ref.refs_2_, f32[48,2048]{1,0:T(8,128)S(1)} %shard_map.134.before_ref, ...), custom_call_target="tpu_custom_call" | custom-call | tf_op jit(solution)/shard_map/pallas_call | solution.py:126
  18.0 1.3 %collective-permute-start.3 = (f32[48,512]{1,0:T(8,128)S(1)}, f32[48,512]{1,0:T(8,128)S(1)}, u32[]{:S(2)}, u32[]{:S(2)}) collective-permute-start(f32[48,512]{1,0:T(8,128)S(1)} %get-tuple-element.27), channel_id=1, source_target_pairs={{0,8},{1,17},{2,10},{3,19},{4,12},{5,21},{6,14},{7,23},{8,0},{9,25... | collective-permute-start | bytes 294920 | tf_op jit(solution)/shard_map/ppermute | solution.py:429
  19.4 1.3 %collective-permute-start.4 = (f32[48,512]{1,0:T(8,128)S(1)}, f32[48,512]{1,0:T(8,128)S(1)}, u32[]{:S(2)}, u32[]{:S(2)}) collective-permute-start(f32[48,512]{1,0:T(8,128)S(1)} %get-tuple-element.28), channel_id=1, source_target_pairs={{0,16},{1,9},{2,18},{3,11},{4,20},{5,13},{6,22},{7,15},{8,24},{9,1... | collective-permute-start | bytes 294920 | tf_op jit(solution)/shard_map/ppermute | solution.py:429
  20.7 1.2 %collective-permute-start.5 = (f32[48,512]{1,0:T(8,128)S(1)}, f32[48,512]{1,0:T(8,128)S(1)}, u32[]{:S(2)}, u32[]{:S(2)}) collective-permute-start(f32[48,512]{1,0:T(8,128)S(1)} %get-tuple-element.29), channel_id=1, source_target_pairs={{0,24},{1,25},{2,26},{3,27},{4,28},{5,29},{6,30},{7,31},{8,16},{9,... | collective-permute-start | bytes 294920 | tf_op jit(solution)/shard_map/ppermute | solution.py:429
  23.2 0.5 shard_map.136.refs_0_
  23.7 0.1 collective-permute-done.3.refs_1_
  23.8 1.2 %collective-permute-done.4.refs_2_ = f32[48,512]{1,0:T(8,128)S(1)} collective-permute-done((f32[48,512]{1,0:T(8,128)S(1)}, f32[48,512]{1,0:T(8,128)S(1)}, u32[]{:S(2)}, u32[]{:S(2)}) %collective-permute-start.4) | collective-permute-done | bytes 98336 | tf_op jit(solution)/shard_map/ppermute | solution.py:429
  25.0 1.7 %collective-permute-done.5.refs_3_ = f32[48,512]{1,0:T(8,128)S(1)} collective-permute-done((f32[48,512]{1,0:T(8,128)S(1)}, f32[48,512]{1,0:T(8,128)S(1)}, u32[]{:S(2)}, u32[]{:S(2)}) %collective-permute-start.5) | collective-permute-done | bytes 98336 | tf_op jit(solution)/shard_map/ppermute | solution.py:429
  26.6 0.0 copy-done
  26.6 0.0 copy-done.3
  26.6 0.0 copy-done.4
  26.6 0.0 copy-done.8
  26.6 0.6 shard_map.137
  27.3 1.5 %collective-permute-start.8 = (f32[48,512]{1,0:T(8,128)S(1)}, f32[48,512]{1,0:T(8,128)S(1)}, u32[]{:S(2)}, u32[]{:S(2)}) collective-permute-start(f32[48,512]{1,0:T(8,128)S(1)} %get-tuple-element.32), channel_id=1, source_target_pairs={{0,8},{1,17},{2,10},{3,19},{4,12},{5,21},{6,14},{7,23},{8,0},{9,25... | collective-permute-start | bytes 294920 | tf_op jit(solution)/shard_map/ppermute | solution.py:429
  28.7 1.2 %collective-permute-start.7 = (f32[48,512]{1,0:T(8,128)S(1)}, f32[48,512]{1,0:T(8,128)S(1)}, u32[]{:S(2)}, u32[]{:S(2)}) collective-permute-start(f32[48,512]{1,0:T(8,128)S(1)} %get-tuple-element.31), channel_id=1, source_target_pairs={{0,16},{1,9},{2,18},{3,11},{4,20},{5,13},{6,22},{7,15},{8,24},{9,1... | collective-permute-start | bytes 294920 | tf_op jit(solution)/shard_map/ppermute | solution.py:429
  29.9 0.9 %collective-permute-start.6 = (f32[48,512]{1,0:T(8,128)S(1)}, f32[48,512]{1,0:T(8,128)S(1)}, u32[]{:S(2)}, u32[]{:S(2)}) collective-permute-start(f32[48,512]{1,0:T(8,128)S(1)} %get-tuple-element.30), channel_id=1, source_target_pairs={{0,24},{1,25},{2,26},{3,27},{4,28},{5,29},{6,30},{7,31},{8,16},{9,... | collective-permute-start | bytes 294920 | tf_op jit(solution)/shard_map/ppermute | solution.py:429
  30.8 0.8 %shard_map.138.refs_0_ = f32[48,2048]{1,0:T(8,128)S(1)} custom-call(f32[48,512]{1,0:T(8,128)S(1)} %get-tuple-element.33.plane_ref, f32[56,512]{1,0:T(8,128)S(1)} %get-tuple-element.25.plane_ref.mark_ref), custom_call_target="tpu_custom_call" | custom-call | tf_op jit(solution)/shard_map/pallas_call | solution.py:126
  31.6 1.3 %collective-permute-done.8.plane_ref = f32[48,512]{1,0:T(8,128)S(1)} collective-permute-done((f32[48,512]{1,0:T(8,128)S(1)}, f32[48,512]{1,0:T(8,128)S(1)}, u32[]{:S(2)}, u32[]{:S(2)}) %collective-permute-start.8) | collective-permute-done | bytes 98336 | tf_op jit(solution)/shard_map/ppermute | solution.py:429
  32.9 0.8 %shard_map.139.refs_0_ = f32[48,2048]{1,0:T(8,128)S(1)} custom-call(f32[48,512]{1,0:T(8,128)S(1)} %collective-permute-done.8.plane_ref, f32[56,512]{1,0:T(8,128)S(1)} %collective-permute-done.2.plane_ref.mark_ref.refs_0_, f32[48,2048]{1,0:T(8,128)S(1)} %shard_map.138.refs_0_), custom_call_target="tpu_custom_call" | custom-call | tf_op jit(solution)/shard_map/pallas_call | solution.py:126
  33.7 0.5 collective-permute-done.7.plane_ref
  34.2 0.8 %shard_map.140.before_ref = f32[48,2048]{1,0:T(8,128)S(1)} custom-call(f32[48,512]{1,0:T(8,128)S(1)} %collective-permute-done.7.plane_ref, f32[56,512]{1,0:T(8,128)S(1)} %collective-permute-done.1.plane_ref.mark_ref.refs_1_, f32[48,2048]{1,0:T(8,128)S(1)} %shard_map.139.refs_0_), custom_call_target="tpu_custom_call" | custom-call | tf_op jit(solution)/shard_map/pallas_call | solution.py:126
  35.0 0.0 copy-start.7
  35.0 0.5 collective-permute-done.6.plane_ref
  35.4 5.8 %shard_map.141 = (f32[48,512]{1,0:T(8,128)S(1)}, f32[48,512]{1,0:T(8,128)S(1)}, f32[48,512]{1,0:T(8,128)S(1)}, bf16[96,2048]{1,0:T(8,128)(2,1)S(1)}) custom-call(f32[48,512]{1,0:T(8,128)S(1)} %collective-permute-done.6.plane_ref, f32[48,2048]{1,0:T(8,128)S(1)} %shard_map.140.before_ref, f32[56,512]{1,0:T(8,128)S(1)} %collective-permute-done.2.plane_ref.mark_ref.refs_0_, ...), custom_call_target="tpu_custom_call" | custom-call | tf_op jit(solution)/shard_map/pallas_call | solution.py:126
  41.3 0.9 %collective-permute-start.10 = (f32[48,512]{1,0:T(8,128)S(1)}, f32[48,512]{1,0:T(8,128)S(1)}, u32[]{:S(2)}, u32[]{:S(2)}) collective-permute-start(f32[48,512]{1,0:T(8,128)S(1)} %get-tuple-element.36), channel_id=1, source_target_pairs={{0,16},{1,9},{2,18},{3,11},{4,20},{5,13},{6,22},{7,15},{8,24},{9,1... | collective-permute-start | bytes 294920 | tf_op jit(solution)/shard_map/ppermute | solution.py:429
  42.1 1.2 %collective-permute-start.11 = (f32[48,512]{1,0:T(8,128)S(1)}, f32[48,512]{1,0:T(8,128)S(1)}, u32[]{:S(2)}, u32[]{:S(2)}) collective-permute-start(f32[48,512]{1,0:T(8,128)S(1)} %get-tuple-element.37), channel_id=1, source_target_pairs={{0,24},{1,25},{2,26},{3,27},{4,28},{5,29},{6,30},{7,31},{8,16},{9,... | collective-permute-start | bytes 294920 | tf_op jit(solution)/shard_map/ppermute | solution.py:429
  43.3 1.5 %collective-permute-start.9 = (f32[48,512]{1,0:T(8,128)S(1)}, f32[48,512]{1,0:T(8,128)S(1)}, u32[]{:S(2)}, u32[]{:S(2)}) collective-permute-start(f32[48,512]{1,0:T(8,128)S(1)} %get-tuple-element.35), channel_id=1, source_target_pairs={{0,8},{1,17},{2,10},{3,19},{4,12},{5,21},{6,14},{7,23},{8,0},{9,25... | collective-permute-start | bytes 294920 | tf_op jit(solution)/shard_map/ppermute | solution.py:429
  44.8 0.5 shard_map.142.refs_0_
  45.3 0.9 %collective-permute-done.10.refs_2_ = f32[48,512]{1,0:T(8,128)S(1)} collective-permute-done((f32[48,512]{1,0:T(8,128)S(1)}, f32[48,512]{1,0:T(8,128)S(1)}, u32[]{:S(2)}, u32[]{:S(2)}) %collective-permute-start.10) | collective-permute-done | bytes 98336 | tf_op jit(solution)/shard_map/ppermute | solution.py:429
  46.2 1.5 %collective-permute-done.11.refs_3_ = f32[48,512]{1,0:T(8,128)S(1)} collective-permute-done((f32[48,512]{1,0:T(8,128)S(1)}, f32[48,512]{1,0:T(8,128)S(1)}, u32[]{:S(2)}, u32[]{:S(2)}) %collective-permute-start.11) | collective-permute-done | bytes 98336 | tf_op jit(solution)/shard_map/ppermute | solution.py:429
  47.7 0.9 %collective-permute-done.9.refs_1_ = f32[48,512]{1,0:T(8,128)S(1)} collective-permute-done((f32[48,512]{1,0:T(8,128)S(1)}, f32[48,512]{1,0:T(8,128)S(1)}, u32[]{:S(2)}, u32[]{:S(2)}) %collective-permute-start.9) | collective-permute-done | bytes 98336 | tf_op jit(solution)/shard_map/ppermute | solution.py:429
  48.5 0.0 copy-done.7
  48.5 0.5 shard_map.143
  49.1 11.5 %all_to_all.10.parts_ref = bf16[8,16,512]{2,1,0:T(8,128)(2,1)S(1)} all-to-all(bf16[8,16,512]{2,1,0:T(8,128)(2,1)S(1)} %get-tuple-element.40), channel_id=1, replica_groups=mesh['grid'=4,'band'=8] {'band'}, dimensions={0} | all-to-all | bytes 262144 | tf_op jit(solution)/shard_map/all_to_all | solution.py:522
  60.5 1.0 %shard_map.144 = (f32[32,1,128]{2,1,0:T(1,128)}, f32[8,128]{1,0:T(8,128)}) custom-call(bf16[8,16,512]{2,1,0:T(8,128)(2,1)S(1)} %all_to_all.10.parts_ref), custom_call_target="tpu_custom_call" | custom-call | tf_op jit(solution)/shard_map/pallas_call | solution.py:126
  61.5 2.6 %all-to-all-start.1 = ((f32[32,1,128]{2,1,0:T(1,128)}), f32[32,1,128]{2,1,0:T(1,128)S(1)}, u32[]{:S(2)}, u32[]{:S(2)}) async-start(f32[32,1,128]{2,1,0:T(1,128)} %get-tuple-element.41), calls=%async_computation.1 | async-start | bytes 32768 | tf_op jit(solution)/shard_map/all_to_all | solution.py:529
  64.1 0.7 %copy.15 = f32[2,1,512,96]{2,3,1,0:T(8,128)} copy(f32[2,1,512,96]{2,3,1,0:T(8,128)S(1)} %bitcast.11) | data formatting | bytes 786432
  64.8 6.4 %all-to-all-done.1.parts_ref = f32[32,1,128]{2,1,0:T(1,128)S(1)} async-done(((f32[32,1,128]{2,1,0:T(1,128)}), f32[32,1,128]{2,1,0:T(1,128)S(1)}, u32[]{:S(2)}, u32[]{:S(2)}) %all-to-all-start.1) | async-done | bytes 16416 | tf_op jit(solution)/shard_map/all_to_all | solution.py:529
  71.2 0.7 %shard_map.145 = f32[2,1,2]{2,1,0:T(1,128)} custom-call(s32[1]{0:T(128)} %bitcast.me_ref, f32[32,1,128]{2,1,0:T(1,128)S(1)} %all-to-all-done.1.parts_ref), custom_call_target="tpu_custom_call" | custom-call | tf_op jit(solution)/shard_map/pallas_call | solution.py:126
Async XLA Ops:
  2.1 7.2 %collective-permute-start.2 = (f32[56,512]{1,0:T(8,128)S(1)}, f32[56,512]{1,0:T(8,128)S(1)}, u32[]{:S(2)}, u32[]{:S(2)}) collective-permute-start(f32[56,512]{1,0:T(8,128)S(1)} %get-tuple-element.24), channel_id=1, source_target_pairs={{0,8},{1,17},{2,10},{3,19},{4,12},{5,21},{6,14},{7,23},{8,0},{9,25... | collective-permute-start | bytes 344072 | tf_op jit(solution)/shard_map/ppermute | solution.py:429
  5.1 6.4 %collective-permute-start.1 = (f32[56,512]{1,0:T(8,128)S(1)}, f32[56,512]{1,0:T(8,128)S(1)}, u32[]{:S(2)}, u32[]{:S(2)}) collective-permute-start(f32[56,512]{1,0:T(8,128)S(1)} %get-tuple-element.23), channel_id=1, source_target_pairs={{0,16},{1,9},{2,18},{3,11},{4,20},{5,13},{6,22},{7,15},{8,24},{9,1... | collective-permute-start | bytes 344072 | tf_op jit(solution)/shard_map/ppermute | solution.py:429
  6.6 5.7 %collective-permute-start = (f32[56,512]{1,0:T(8,128)S(1)}, f32[56,512]{1,0:T(8,128)S(1)}, u32[]{:S(2)}, u32[]{:S(2)}) collective-permute-start(f32[56,512]{1,0:T(8,128)S(1)} %get-tuple-element.22), channel_id=1, source_target_pairs={{0,24},{1,25},{2,26},{3,27},{4,28},{5,29},{6,30},{7,31},{8,16},{9,... | collective-permute-start | bytes 344072 | tf_op jit(solution)/shard_map/ppermute | solution.py:429
  9.2 3.1 %copy-start.1 = (bf16[384,256]{1,0:T(8,128)(2,1)S(1)}, bf16[384,256]{1,0:T(8,128)(2,1)}, u32[]{:S(2)}) copy-start(bf16[384,256]{1,0:T(8,128)(2,1)} %constant.30.clone.refs_4_) | copy-start | bytes 589828
  9.3 3.1 %copy-start.2 = (bf16[384,224]{1,0:T(8,128)(2,1)S(1)}, bf16[384,224]{1,0:T(8,128)(2,1)}, u32[]{:S(2)}) copy-start(bf16[384,224]{1,0:T(8,128)(2,1)} %constant.31.clone.refs_5_) | copy-start | bytes 516100
  9.3 3.1 %copy-start.5 = (bf16[256,256]{1,0:T(8,128)(2,1)S(1)}, bf16[256,256]{1,0:T(8,128)(2,1)}, u32[]{:S(2)}) copy-start(bf16[256,256]{1,0:T(8,128)(2,1)} %constant.33.clone.refs_7_) | copy-start | bytes 393220
  9.3 3.1 %copy-start.6 = (bf16[224,192]{1,0:T(8,128)(2,1)S(1)}, bf16[224,192]{1,0:T(8,128)(2,1)}, u32[]{:S(2)}) copy-start(bf16[224,192]{1,0:T(8,128)(2,1)} %constant.32.clone.refs_6_) | copy-start | bytes 258052
  12.3 14.4 %copy-start = (f32[2,1,512,96]{2,3,1,0:T(8,128)S(1)}, f32[2,1,512,96]{2,3,1,0:T(8,128)}, u32[]{:S(2)}) copy-start(f32[2,1,512,96]{2,3,1,0:T(8,128)} %param.12) | copy-start | bytes 1179652
  12.3 14.4 %copy-start.3 = (bf16[4,48,336]{2,1,0:T(8,128)(2,1)S(1)}, bf16[4,48,336]{2,1,0:T(8,128)(2,1)}, u32[]{:S(2)}) copy-start(bf16[4,48,336]{2,1,0:T(8,128)(2,1)} %constant.29.clone.refs_2_.refs_6_) | copy-start | bytes 387076
  12.3 14.4 %copy-start.4 = (bf16[112,576]{1,0:T(8,128)(2,1)S(1)}, bf16[112,576]{1,0:T(8,128)(2,1)}, u32[]{:S(2)}) copy-start(bf16[112,576]{1,0:T(8,128)(2,1)} %constant.34.clone.refs_7_) | copy-start | bytes 387076
  12.3 14.3 %copy-start.8 = (s32[512]{0:T(512)S(1)}, s32[512]{0:T(512)}, u32[]{:S(2)}) copy-start(s32[512]{0:T(512)} %param.13) | copy-start | bytes 6148
  18.0 5.7 %collective-permute-start.3 = (f32[48,512]{1,0:T(8,128)S(1)}, f32[48,512]{1,0:T(8,128)S(1)}, u32[]{:S(2)}, u32[]{:S(2)}) collective-permute-start(f32[48,512]{1,0:T(8,128)S(1)} %get-tuple-element.27), channel_id=1, source_target_pairs={{0,8},{1,17},{2,10},{3,19},{4,12},{5,21},{6,14},{7,23},{8,0},{9,25... | collective-permute-start | bytes 294920 | tf_op jit(solution)/shard_map/ppermute | solution.py:429
  19.4 5.6 %collective-permute-start.4 = (f32[48,512]{1,0:T(8,128)S(1)}, f32[48,512]{1,0:T(8,128)S(1)}, u32[]{:S(2)}, u32[]{:S(2)}) collective-permute-start(f32[48,512]{1,0:T(8,128)S(1)} %get-tuple-element.28), channel_id=1, source_target_pairs={{0,16},{1,9},{2,18},{3,11},{4,20},{5,13},{6,22},{7,15},{8,24},{9,1... | collective-permute-start | bytes 294920 | tf_op jit(solution)/shard_map/ppermute | solution.py:429
  20.7 5.9 %collective-permute-start.5 = (f32[48,512]{1,0:T(8,128)S(1)}, f32[48,512]{1,0:T(8,128)S(1)}, u32[]{:S(2)}, u32[]{:S(2)}) collective-permute-start(f32[48,512]{1,0:T(8,128)S(1)} %get-tuple-element.29), channel_id=1, source_target_pairs={{0,24},{1,25},{2,26},{3,27},{4,28},{5,29},{6,30},{7,31},{8,16},{9,... | collective-permute-start | bytes 294920 | tf_op jit(solution)/shard_map/ppermute | solution.py:429
  27.3 5.6 %collective-permute-start.8 = (f32[48,512]{1,0:T(8,128)S(1)}, f32[48,512]{1,0:T(8,128)S(1)}, u32[]{:S(2)}, u32[]{:S(2)}) collective-permute-start(f32[48,512]{1,0:T(8,128)S(1)} %get-tuple-element.32), channel_id=1, source_target_pairs={{0,8},{1,17},{2,10},{3,19},{4,12},{5,21},{6,14},{7,23},{8,0},{9,25... | collective-permute-start | bytes 294920 | tf_op jit(solution)/shard_map/ppermute | solution.py:429
  28.7 5.5 %collective-permute-start.7 = (f32[48,512]{1,0:T(8,128)S(1)}, f32[48,512]{1,0:T(8,128)S(1)}, u32[]{:S(2)}, u32[]{:S(2)}) collective-permute-start(f32[48,512]{1,0:T(8,128)S(1)} %get-tuple-element.31), channel_id=1, source_target_pairs={{0,16},{1,9},{2,18},{3,11},{4,20},{5,13},{6,22},{7,15},{8,24},{9,1... | collective-permute-start | bytes 294920 | tf_op jit(solution)/shard_map/ppermute | solution.py:429
  29.9 5.5 %collective-permute-start.6 = (f32[48,512]{1,0:T(8,128)S(1)}, f32[48,512]{1,0:T(8,128)S(1)}, u32[]{:S(2)}, u32[]{:S(2)}) collective-permute-start(f32[48,512]{1,0:T(8,128)S(1)} %get-tuple-element.30), channel_id=1, source_target_pairs={{0,24},{1,25},{2,26},{3,27},{4,28},{5,29},{6,30},{7,31},{8,16},{9,... | collective-permute-start | bytes 294920 | tf_op jit(solution)/shard_map/ppermute | solution.py:429
  35.0 13.6 %copy-start.7 = (bf16[2,128,56]{2,1,0:T(8,128)(2,1)S(1)}, bf16[2,128,56]{2,1,0:T(8,128)(2,1)}, u32[]{:S(2)}) copy-start(bf16[2,128,56]{2,1,0:T(8,128)(2,1)} %constant.35.clone.refs_8_) | copy-start | bytes 86020
  41.3 4.9 %collective-permute-start.10 = (f32[48,512]{1,0:T(8,128)S(1)}, f32[48,512]{1,0:T(8,128)S(1)}, u32[]{:S(2)}, u32[]{:S(2)}) collective-permute-start(f32[48,512]{1,0:T(8,128)S(1)} %get-tuple-element.36), channel_id=1, source_target_pairs={{0,16},{1,9},{2,18},{3,11},{4,20},{5,13},{6,22},{7,15},{8,24},{9,1... | collective-permute-start | bytes 294920 | tf_op jit(solution)/shard_map/ppermute | solution.py:429
  42.1 5.5 %collective-permute-start.11 = (f32[48,512]{1,0:T(8,128)S(1)}, f32[48,512]{1,0:T(8,128)S(1)}, u32[]{:S(2)}, u32[]{:S(2)}) collective-permute-start(f32[48,512]{1,0:T(8,128)S(1)} %get-tuple-element.37), channel_id=1, source_target_pairs={{0,24},{1,25},{2,26},{3,27},{4,28},{5,29},{6,30},{7,31},{8,16},{9,... | collective-permute-start | bytes 294920 | tf_op jit(solution)/shard_map/ppermute | solution.py:429
  43.3 5.2 %collective-permute-start.9 = (f32[48,512]{1,0:T(8,128)S(1)}, f32[48,512]{1,0:T(8,128)S(1)}, u32[]{:S(2)}, u32[]{:S(2)}) collective-permute-start(f32[48,512]{1,0:T(8,128)S(1)} %get-tuple-element.35), channel_id=1, source_target_pairs={{0,8},{1,17},{2,10},{3,19},{4,12},{5,21},{6,14},{7,23},{8,0},{9,25... | collective-permute-start | bytes 294920 | tf_op jit(solution)/shard_map/ppermute | solution.py:429
  61.5 9.7 %all-to-all-start.1 = ((f32[32,1,128]{2,1,0:T(1,128)}), f32[32,1,128]{2,1,0:T(1,128)S(1)}, u32[]{:S(2)}, u32[]{:S(2)}) async-start(f32[32,1,128]{2,1,0:T(1,128)} %get-tuple-element.41), calls=%async_computation.1 | async-start | bytes 32768 | tf_op jit(solution)/shard_map/all_to_all | solution.py:529

commit v10 on v8

--- a/solution.py
+++ b/solution.py
@@ -451,15 +451,16 @@
     box_shape = (rows, 128 * slots_all)
 
     def slab(values):
+        order = [0] + list(range(devices - 1, 0, -1))
         sums = []
-        for k in range(devices - 1):
+        for k in order[:-1]:
             sums = call(
                 functools.partial(scatter_kernel, slots_all),
                 [vmem(box_shape)],
                 [],
                 [(value, True) for value in [values[k], marks[k]] + list(sums)],
             )
-        given = [values[-1], sums[0]] + marks[1:]
+        given = [values[order[-1]], sums[0]] + [marks[k] for k in order[1:]]
         *sent, box = call(
             functools.partial(slab_kernel, devices, size, depth),
             [vmem((rows, cols))] * (devices - 1) + [vmem((2 * rows, 128 * slots_all), BF16)],
@@ -479,7 +480,7 @@
             [],
             [(box, True), (marks[0], True)],
         )
-        return list(own) + list(sent)
+        return list(own) + [sent[order.index(k) - 1] for k in range(1, devices)]
 
     held = pltpu.VMEM((3 * devices * rows, cols), BF16)
     planes = exchange(slab(marks))

time: 71.9 us -> 71.6 us (level)
  starting transfers between devices: 18.6 us -> 17.8 us
  transfers between devices with their start and end apart: 13 -> 13, of which waited for: 11 -> 8; matrix products, arithmetic and copies ran while one was open for 4% -> 4% of each run, Pallas kernels for 8% -> 8%
where the time goes in v10:
time: 71.6 us; the launch traced here: 71.4 us
  Pallas kernels  21.3 us (30%)
  starting transfers between devices  17.8 us (25%)
  waiting for transfers between devices  15.9 us (22%)
  blocking collectives  11.4 us (16%)
  between operations  2.24 us (3%)
  local copies, waits for them, and re-layouts  1.36 us (2%)
  other arithmetic  1.24 us (2%)
    pallas_call x15, Pallas kernels, call(): pl.pallas_call(kernel, out_shape=out_shape, in_specs=[SMEM] * len(scalars...  21.3 us
    ppermute x12, starting transfers between devices, exchange(): lax.ppermute(values[k], 'grid', [(d, step(d, k)) for d in range(devices)])  15.3 us
    all_to_all x1, blocking collectives, body(): lax.all_to_all(packed, 'band', 0, 0, tiled=True)  11.4 us
    ppermute x12, waiting for transfers between devices, exchange(): lax.ppermute(values[k], 'grid', [(d, step(d, k)) for d in range(devices)])  9.55 us
    all_to_all x1, waiting for transfers between devices, body(): lax.all_to_all(partial_sum, ('grid', 'band'), 0, 0, tiled=True)  6.4 us
    all_to_all x1, starting transfers between devices, body(): lax.all_to_all(partial_sum, ('grid', 'band'), 0, 0, tiled=True)  2.55 us
  transfers between devices with their start and end apart: 13, of which 8 were waited for; matrix products, arithmetic and copies ran while one was open for 4% of the time, Pallas kernels for 8%

profile of v10, /device:TPU:0, one launch (start us, length us, event | category | flops | bytes accessed | tf_op | source)
XLA Modules:
  0.0 71.4 jit_solution(14332136254066284048)
XLA Ops:
  0.6 1.5 %shard_map.131 = (f32[56,512]{1,0:T(8,128)S(1)}, f32[56,512]{1,0:T(8,128)S(1)}, f32[56,512]{1,0:T(8,128)S(1)}, f32[56,512]{1,0:T(8,128)S(1)}) custom-call(s32[1]{0:T(128)} %bitcast.me_ref, f32[2,96,512]{2,1,0:T(8,128)} %bitcast.11, s32[1,512]{1,0:T(1,128)} %bitcast.14, bf16[4,48,336]{2,1,0:T(8,128)(2,1)} %constant.24.clone.refs_2_.refs_6_), custom_call_target="tpu_custom_call" | custom-call | tf_op jit(solution)/shard_map/pallas_call | solution.py:126
  2.1 4.0 %collective-permute-start.2 = (f32[56,512]{1,0:T(8,128)S(1)}, f32[56,512]{1,0:T(8,128)S(1)}, u32[]{:S(2)}, u32[]{:S(2)}) collective-permute-start(f32[56,512]{1,0:T(8,128)S(1)} %get-tuple-element.23), channel_id=1, source_target_pairs={{0,24},{8,16},{16,8},{24,0},{1,25},{9,17},{17,9},{25,1},{2,26},{10... | collective-permute-start | bytes 344072 | tf_op jit(solution)/shard_map/ppermute | solution.py:413
  6.1 0.5 collective-permute-start.1
  6.6 0.1 collective-permute-start
  6.7 1.2 %broadcast_multiply_fusion = f32[24,9216]{1,0:T(8,128)S(1)} fusion(f32[24,9216]{1,0:T(8,128)} %param.14), kind=kLoop, calls=%fused_computation | loop fusion | flops 221184 | bytes 1769472 | tf_op jit(solution)/shard_map/mul | solution.py:426
  8.0 0.8 %shard_map.132.refs_0_ = f32[48,2048]{1,0:T(8,128)S(1)} custom-call(f32[56,512]{1,0:T(8,128)S(1)} %get-tuple-element.24.plane_ref.mark_ref, f32[56,512]{1,0:T(8,128)S(1)} %get-tuple-element.24.plane_ref.mark_ref), custom_call_target="tpu_custom_call" | custom-call | tf_op jit(solution)/shard_map/pallas_call | solution.py:126
  8.7 0.5 reshape.22
  9.2 0.1 pad.4.refs_3_
  9.3 0.0 copy-start.1
  9.3 0.0 copy-start.2
  9.3 0.0 copy-start.5
  9.3 0.0 copy-start.6
  9.3 0.3 collective-permute-done.2.plane_ref.mark_ref.refs_0_
  9.6 0.8 %shard_map.133.refs_0_ = f32[48,2048]{1,0:T(8,128)S(1)} custom-call(f32[56,512]{1,0:T(8,128)S(1)} %collective-permute-done.2.plane_ref.mark_ref.refs_0_, f32[56,512]{1,0:T(8,128)S(1)} %collective-permute-done.2.plane_ref.mark_ref.refs_0_, f32[48,2048]{1,0:T(8,128)S(1)} %shard_map.132.refs_0_), custom_call_target="tpu_custom_call" | custom-call | tf_op jit(solution)/shard_map/pallas_call | solution.py:126
  10.4 1.3 %collective-permute-done.1.plane_ref.mark_ref.refs_1_ = f32[56,512]{1,0:T(8,128)S(1)} collective-permute-done((f32[56,512]{1,0:T(8,128)S(1)}, f32[56,512]{1,0:T(8,128)S(1)}, u32[]{:S(2)}, u32[]{:S(2)}) %collective-permute-start.1) | collective-permute-done | bytes 114720 | tf_op jit(solution)/shard_map/ppermute | solution.py:413
  11.7 0.8 %shard_map.134.before_ref = f32[48,2048]{1,0:T(8,128)S(1)} custom-call(f32[56,512]{1,0:T(8,128)S(1)} %collective-permute-done.1.plane_ref.mark_ref.refs_1_, f32[56,512]{1,0:T(8,128)S(1)} %collective-permute-done.1.plane_ref.mark_ref.refs_1_, f32[48,2048]{1,0:T(8,128)S(1)} %shard_map.133.refs_0_), custom_call_target="tpu_custom_call" | custom-call | tf_op jit(solution)/shard_map/pallas_call | solution.py:126
  12.4 0.0 copy-start
  12.5 0.0 copy-start.3
  12.5 0.0 copy-start.4
  12.5 0.0 copy-start.8
  12.5 0.0 collective-permute-done.plane_ref.refs_2_
  12.5 0.0 copy-done.1
  12.5 0.0 copy-done.2
  12.5 0.0 copy-done.5
  12.5 0.0 copy-done.6
  12.5 5.6 %shard_map.135 = (f32[48,512]{1,0:T(8,128)S(1)}, f32[48,512]{1,0:T(8,128)S(1)}, f32[48,512]{1,0:T(8,128)S(1)}, bf16[96,2048]{1,0:T(8,128)(2,1)S(1)}) custom-call(f32[56,512]{1,0:T(8,128)S(1)} %collective-permute-done.plane_ref.refs_2_, f32[48,2048]{1,0:T(8,128)S(1)} %shard_map.134.before_ref, ...), custom_call_target="tpu_custom_call" | custom-call | tf_op jit(solution)/shard_map/pallas_call | solution.py:126
  18.2 1.8 %collective-permute-start.3 = (f32[48,512]{1,0:T(8,128)S(1)}, f32[48,512]{1,0:T(8,128)S(1)}, u32[]{:S(2)}, u32[]{:S(2)}) collective-permute-start(f32[48,512]{1,0:T(8,128)S(1)} %get-tuple-element.26), channel_id=1, source_target_pairs={{0,8},{8,0},{16,24},{24,16},{1,9},{9,1},{17,25},{25,17},{2,10},{10... | collective-permute-start | bytes 294920 | tf_op jit(solution)/shard_map/ppermute | solution.py:413
  19.9 1.0 %collective-permute-start.4 = (f32[48,512]{1,0:T(8,128)S(1)}, f32[48,512]{1,0:T(8,128)S(1)}, u32[]{:S(2)}, u32[]{:S(2)}) collective-permute-start(f32[48,512]{1,0:T(8,128)S(1)} %get-tuple-element.27), channel_id=1, source_target_pairs={{0,16},{8,24},{16,0},{24,8},{1,17},{9,25},{17,1},{25,9},{2,18},{10... | collective-permute-start | bytes 294920 | tf_op jit(solution)/shard_map/ppermute | solution.py:413
  20.9 0.8 %collective-permute-start.5 = (f32[48,512]{1,0:T(8,128)S(1)}, f32[48,512]{1,0:T(8,128)S(1)}, u32[]{:S(2)}, u32[]{:S(2)}) collective-permute-start(f32[48,512]{1,0:T(8,128)S(1)} %get-tuple-element.28), channel_id=1, source_target_pairs={{0,24},{8,16},{16,8},{24,0},{1,25},{9,17},{17,9},{25,1},{2,26},{10... | collective-permute-start | bytes 294920 | tf_op jit(solution)/shard_map/ppermute | solution.py:413
  23.0 0.5 shard_map.136.refs_0_
  23.5 0.0 collective-permute-done.3.refs_1_
  23.5 3.0 %collective-permute-done.4.refs_2_ = f32[48,512]{1,0:T(8,128)S(1)} collective-permute-done((f32[48,512]{1,0:T(8,128)S(1)}, f32[48,512]{1,0:T(8,128)S(1)}, u32[]{:S(2)}, u32[]{:S(2)}) %collective-permute-start.4) | collective-permute-done | bytes 98336 | tf_op jit(solution)/shard_map/ppermute | solution.py:413
  26.5 0.0 collective-permute-done.5.refs_3_
  26.6 0.0 copy-done
  26.6 0.0 copy-done.3
  26.6 0.0 copy-done.4
  26.6 0.0 copy-done.8
  26.6 0.6 shard_map.137
  27.2 1.5 %collective-permute-start.8 = (f32[48,512]{1,0:T(8,128)S(1)}, f32[48,512]{1,0:T(8,128)S(1)}, u32[]{:S(2)}, u32[]{:S(2)}) collective-permute-start(f32[48,512]{1,0:T(8,128)S(1)} %get-tuple-element.31), channel_id=1, source_target_pairs={{0,24},{8,16},{16,8},{24,0},{1,25},{9,17},{17,9},{25,1},{2,26},{10... | collective-permute-start | bytes 294920 | tf_op jit(solution)/shard_map/ppermute | solution.py:413
  28.7 1.0 %collective-permute-start.7 = (f32[48,512]{1,0:T(8,128)S(1)}, f32[48,512]{1,0:T(8,128)S(1)}, u32[]{:S(2)}, u32[]{:S(2)}) collective-permute-start(f32[48,512]{1,0:T(8,128)S(1)} %get-tuple-element.30), channel_id=1, source_target_pairs={{0,16},{8,24},{16,0},{24,8},{1,17},{9,25},{17,1},{25,9},{2,18},{10... | collective-permute-start | bytes 294920 | tf_op jit(solution)/shard_map/ppermute | solution.py:413
  29.7 1.1 %collective-permute-start.6 = (f32[48,512]{1,0:T(8,128)S(1)}, f32[48,512]{1,0:T(8,128)S(1)}, u32[]{:S(2)}, u32[]{:S(2)}) collective-permute-start(f32[48,512]{1,0:T(8,128)S(1)} %get-tuple-element.29), channel_id=1, source_target_pairs={{0,8},{8,0},{16,24},{24,16},{1,9},{9,1},{17,25},{25,17},{2,10},{10... | collective-permute-start | bytes 294920 | tf_op jit(solution)/shard_map/ppermute | solution.py:413
  30.8 0.8 %shard_map.138.refs_0_ = f32[48,2048]{1,0:T(8,128)S(1)} custom-call(f32[48,512]{1,0:T(8,128)S(1)} %get-tuple-element.32.plane_ref, f32[56,512]{1,0:T(8,128)S(1)} %get-tuple-element.24.plane_ref.mark_ref), custom_call_target="tpu_custom_call" | custom-call | tf_op jit(solution)/shard_map/pallas_call | solution.py:126
  31.5 1.8 %collective-permute-done.8.plane_ref = f32[48,512]{1,0:T(8,128)S(1)} collective-permute-done((f32[48,512]{1,0:T(8,128)S(1)}, f32[48,512]{1,0:T(8,128)S(1)}, u32[]{:S(2)}, u32[]{:S(2)}) %collective-permute-start.8) | collective-permute-done | bytes 98336 | tf_op jit(solution)/shard_map/ppermute | solution.py:413
  33.3 0.8 %shard_map.139.refs_0_ = f32[48,2048]{1,0:T(8,128)S(1)} custom-call(f32[48,512]{1,0:T(8,128)S(1)} %collective-permute-done.8.plane_ref, f32[56,512]{1,0:T(8,128)S(1)} %collective-permute-done.2.plane_ref.mark_ref.refs_0_, f32[48,2048]{1,0:T(8,128)S(1)} %shard_map.138.refs_0_), custom_call_target="tpu_custom_call" | custom-call | tf_op jit(solution)/shard_map/pallas_call | solution.py:126
  34.1 0.0 collective-permute-done.7.plane_ref
  34.1 0.8 %shard_map.140.before_ref = f32[48,2048]{1,0:T(8,128)S(1)} custom-call(f32[48,512]{1,0:T(8,128)S(1)} %collective-permute-done.7.plane_ref, f32[56,512]{1,0:T(8,128)S(1)} %collective-permute-done.1.plane_ref.mark_ref.refs_1_, f32[48,2048]{1,0:T(8,128)S(1)} %shard_map.139.refs_0_), custom_call_target="tpu_custom_call" | custom-call | tf_op jit(solution)/shard_map/pallas_call | solution.py:126
  34.9 0.0 copy-start.7
  34.9 0.0 collective-permute-done.6.plane_ref
  34.9 5.8 %shard_map.141 = (f32[48,512]{1,0:T(8,128)S(1)}, f32[48,512]{1,0:T(8,128)S(1)}, f32[48,512]{1,0:T(8,128)S(1)}, bf16[96,2048]{1,0:T(8,128)(2,1)S(1)}) custom-call(f32[48,512]{1,0:T(8,128)S(1)} %collective-permute-done.6.plane_ref, f32[48,2048]{1,0:T(8,128)S(1)} %shard_map.140.before_ref, f32[56,512]{1,0:T(8,128)S(1)} %collective-permute-done.2.plane_ref.mark_ref.refs_0_, ...), custom_call_target="tpu_custom_call" | custom-call | tf_op jit(solution)/shard_map/pallas_call | solution.py:126
  40.7 0.9 %collective-permute-start.10 = (f32[48,512]{1,0:T(8,128)S(1)}, f32[48,512]{1,0:T(8,128)S(1)}, u32[]{:S(2)}, u32[]{:S(2)}) collective-permute-start(f32[48,512]{1,0:T(8,128)S(1)} %get-tuple-element.35), channel_id=1, source_target_pairs={{0,16},{8,24},{16,0},{24,8},{1,17},{9,25},{17,1},{25,9},{2,18},{10... | collective-permute-start | bytes 294920 | tf_op jit(solution)/shard_map/ppermute | solution.py:413
  41.6 1.3 %collective-permute-start.11 = (f32[48,512]{1,0:T(8,128)S(1)}, f32[48,512]{1,0:T(8,128)S(1)}, u32[]{:S(2)}, u32[]{:S(2)}) collective-permute-start(f32[48,512]{1,0:T(8,128)S(1)} %get-tuple-element.36), channel_id=1, source_target_pairs={{0,24},{8,16},{16,8},{24,0},{1,25},{9,17},{17,9},{25,1},{2,26},{10... | collective-permute-start | bytes 294920 | tf_op jit(solution)/shard_map/ppermute | solution.py:413
  42.9 1.4 %collective-permute-start.9 = (f32[48,512]{1,0:T(8,128)S(1)}, f32[48,512]{1,0:T(8,128)S(1)}, u32[]{:S(2)}, u32[]{:S(2)}) collective-permute-start(f32[48,512]{1,0:T(8,128)S(1)} %get-tuple-element.34), channel_id=1, source_target_pairs={{0,8},{8,0},{16,24},{24,16},{1,9},{9,1},{17,25},{25,17},{2,10},{10... | collective-permute-start | bytes 294920 | tf_op jit(solution)/shard_map/ppermute | solution.py:413
  44.3 0.5 shard_map.142.refs_0_
  44.8 0.7 collective-permute-done.10.refs_2_
  45.4 1.7 %collective-permute-done.11.refs_3_ = f32[48,512]{1,0:T(8,128)S(1)} collective-permute-done((f32[48,512]{1,0:T(8,128)S(1)}, f32[48,512]{1,0:T(8,128)S(1)}, u32[]{:S(2)}, u32[]{:S(2)}) %collective-permute-start.11) | collective-permute-done | bytes 98336 | tf_op jit(solution)/shard_map/ppermute | solution.py:413
  47.1 0.8 %collective-permute-done.9.refs_1_ = f32[48,512]{1,0:T(8,128)S(1)} collective-permute-done((f32[48,512]{1,0:T(8,128)S(1)}, f32[48,512]{1,0:T(8,128)S(1)}, u32[]{:S(2)}, u32[]{:S(2)}) %collective-permute-start.9) | collective-permute-done | bytes 98336 | tf_op jit(solution)/shard_map/ppermute | solution.py:413
  47.9 0.0 copy-done.7
  47.9 0.5 shard_map.143
  48.5 11.4 %all_to_all.10.parts_ref = bf16[8,16,512]{2,1,0:T(8,128)(2,1)S(1)} all-to-all(bf16[8,16,512]{2,1,0:T(8,128)(2,1)S(1)} %get-tuple-element.39), channel_id=1, replica_groups=mesh['grid'=4,'band'=8] {'band'}, dimensions={0} | all-to-all | bytes 262144 | tf_op jit(solution)/shard_map/all_to_all | solution.py:507
  59.9 1.0 %shard_map.144 = f32[32,1,128]{2,1,0:T(1,128)} custom-call(bf16[8,16,512]{2,1,0:T(8,128)(2,1)S(1)} %all_to_all.10.parts_ref), custom_call_target="tpu_custom_call" | custom-call | tf_op jit(solution)/shard_map/pallas_call | solution.py:126
  60.9 2.5 %all-to-all-start.1 = ((f32[32,1,128]{2,1,0:T(1,128)}), f32[32,1,128]{2,1,0:T(1,128)S(1)}, u32[]{:S(2)}, u32[]{:S(2)}) async-start(f32[32,1,128]{2,1,0:T(1,128)} %shard_map.144), calls=%async_computation.1 | async-start | bytes 32768 | tf_op jit(solution)/shard_map/all_to_all | solution.py:514
  63.5 0.7 %copy.15 = f32[2,1,512,96]{2,3,1,0:T(8,128)} copy(f32[2,1,512,96]{2,3,1,0:T(8,128)S(1)} %bitcast.10) | data formatting | bytes 786432
  64.2 6.4 %all-to-all-done.1.parts_ref = f32[32,1,128]{2,1,0:T(1,128)S(1)} async-done(((f32[32,1,128]{2,1,0:T(1,128)}), f32[32,1,128]{2,1,0:T(1,128)S(1)}, u32[]{:S(2)}, u32[]{:S(2)}) %all-to-all-start.1) | async-done | bytes 16416 | tf_op jit(solution)/shard_map/all_to_all | solution.py:514
  70.6 0.7 %shard_map.145 = f32[2,1,2]{2,1,0:T(1,128)} custom-call(s32[1]{0:T(128)} %bitcast.me_ref, f32[32,1,128]{2,1,0:T(1,128)S(1)} %all-to-all-done.1.parts_ref), custom_call_target="tpu_custom_call" | custom-call | tf_op jit(solution)/shard_map/pallas_call | solution.py:126
Async XLA Ops:
  2.1 7.5 %collective-permute-start.2 = (f32[56,512]{1,0:T(8,128)S(1)}, f32[56,512]{1,0:T(8,128)S(1)}, u32[]{:S(2)}, u32[]{:S(2)}) collective-permute-start(f32[56,512]{1,0:T(8,128)S(1)} %get-tuple-element.23), channel_id=1, source_target_pairs={{0,24},{8,16},{16,8},{24,0},{1,25},{9,17},{17,9},{25,1},{2,26},{10... | collective-permute-start | bytes 344072 | tf_op jit(solution)/shard_map/ppermute | solution.py:413
  6.1 5.6 %collective-permute-start.1 = (f32[56,512]{1,0:T(8,128)S(1)}, f32[56,512]{1,0:T(8,128)S(1)}, u32[]{:S(2)}, u32[]{:S(2)}) collective-permute-start(f32[56,512]{1,0:T(8,128)S(1)} %get-tuple-element.22), channel_id=1, source_target_pairs={{0,16},{8,24},{16,0},{24,8},{1,17},{9,25},{17,1},{25,9},{2,18},{10... | collective-permute-start | bytes 344072 | tf_op jit(solution)/shard_map/ppermute | solution.py:413
  6.6 5.9 %collective-permute-start = (f32[56,512]{1,0:T(8,128)S(1)}, f32[56,512]{1,0:T(8,128)S(1)}, u32[]{:S(2)}, u32[]{:S(2)}) collective-permute-start(f32[56,512]{1,0:T(8,128)S(1)} %get-tuple-element.21), channel_id=1, source_target_pairs={{0,8},{8,0},{16,24},{24,16},{1,9},{9,1},{17,25},{25,17},{2,10},{10... | collective-permute-start | bytes 344072 | tf_op jit(solution)/shard_map/ppermute | solution.py:413
  9.3 3.2 %copy-start.1 = (bf16[384,256]{1,0:T(8,128)(2,1)S(1)}, bf16[384,256]{1,0:T(8,128)(2,1)}, u32[]{:S(2)}) copy-start(bf16[384,256]{1,0:T(8,128)(2,1)} %constant.25.clone.refs_4_) | copy-start | bytes 589828
  9.3 3.2 %copy-start.2 = (bf16[384,224]{1,0:T(8,128)(2,1)S(1)}, bf16[384,224]{1,0:T(8,128)(2,1)}, u32[]{:S(2)}) copy-start(bf16[384,224]{1,0:T(8,128)(2,1)} %constant.26.clone.refs_5_) | copy-start | bytes 516100
  9.3 3.2 %copy-start.5 = (bf16[256,256]{1,0:T(8,128)(2,1)S(1)}, bf16[256,256]{1,0:T(8,128)(2,1)}, u32[]{:S(2)}) copy-start(bf16[256,256]{1,0:T(8,128)(2,1)} %constant.28.clone.refs_7_) | copy-start | bytes 393220
  9.3 3.2 %copy-start.6 = (bf16[224,192]{1,0:T(8,128)(2,1)S(1)}, bf16[224,192]{1,0:T(8,128)(2,1)}, u32[]{:S(2)}) copy-start(bf16[224,192]{1,0:T(8,128)(2,1)} %constant.27.clone.refs_6_) | copy-start | bytes 258052
  12.4 14.1 %copy-start = (f32[2,1,512,96]{2,3,1,0:T(8,128)S(1)}, f32[2,1,512,96]{2,3,1,0:T(8,128)}, u32[]{:S(2)}) copy-start(f32[2,1,512,96]{2,3,1,0:T(8,128)} %param.12) | copy-start | bytes 1179652
  12.5 14.1 %copy-start.3 = (bf16[4,48,336]{2,1,0:T(8,128)(2,1)S(1)}, bf16[4,48,336]{2,1,0:T(8,128)(2,1)}, u32[]{:S(2)}) copy-start(bf16[4,48,336]{2,1,0:T(8,128)(2,1)} %constant.24.clone.refs_2_.refs_6_) | copy-start | bytes 387076
  12.5 14.1 %copy-start.4 = (bf16[112,576]{1,0:T(8,128)(2,1)S(1)}, bf16[112,576]{1,0:T(8,128)(2,1)}, u32[]{:S(2)}) copy-start(bf16[112,576]{1,0:T(8,128)(2,1)} %constant.29.clone.refs_7_) | copy-start | bytes 387076
  12.5 14.1 %copy-start.8 = (s32[512]{0:T(512)S(1)}, s32[512]{0:T(512)}, u32[]{:S(2)}) copy-start(s32[512]{0:T(512)} %param.13) | copy-start | bytes 6148
  18.2 5.3 %collective-permute-start.3 = (f32[48,512]{1,0:T(8,128)S(1)}, f32[48,512]{1,0:T(8,128)S(1)}, u32[]{:S(2)}, u32[]{:S(2)}) collective-permute-start(f32[48,512]{1,0:T(8,128)S(1)} %get-tuple-element.26), channel_id=1, source_target_pairs={{0,8},{8,0},{16,24},{24,16},{1,9},{9,1},{17,25},{25,17},{2,10},{10... | collective-permute-start | bytes 294920 | tf_op jit(solution)/shard_map/ppermute | solution.py:413
  19.9 6.6 %collective-permute-start.4 = (f32[48,512]{1,0:T(8,128)S(1)}, f32[48,512]{1,0:T(8,128)S(1)}, u32[]{:S(2)}, u32[]{:S(2)}) collective-permute-start(f32[48,512]{1,0:T(8,128)S(1)} %get-tuple-element.27), channel_id=1, source_target_pairs={{0,16},{8,24},{16,0},{24,8},{1,17},{9,25},{17,1},{25,9},{2,18},{10... | collective-permute-start | bytes 294920 | tf_op jit(solution)/shard_map/ppermute | solution.py:413
  20.9 5.6 %collective-permute-start.5 = (f32[48,512]{1,0:T(8,128)S(1)}, f32[48,512]{1,0:T(8,128)S(1)}, u32[]{:S(2)}, u32[]{:S(2)}) collective-permute-start(f32[48,512]{1,0:T(8,128)S(1)} %get-tuple-element.28), channel_id=1, source_target_pairs={{0,24},{8,16},{16,8},{24,0},{1,25},{9,17},{17,9},{25,1},{2,26},{10... | collective-permute-start | bytes 294920 | tf_op jit(solution)/shard_map/ppermute | solution.py:413
  27.2 6.1 %collective-permute-start.8 = (f32[48,512]{1,0:T(8,128)S(1)}, f32[48,512]{1,0:T(8,128)S(1)}, u32[]{:S(2)}, u32[]{:S(2)}) collective-permute-start(f32[48,512]{1,0:T(8,128)S(1)} %get-tuple-element.31), channel_id=1, source_target_pairs={{0,24},{8,16},{16,8},{24,0},{1,25},{9,17},{17,9},{25,1},{2,26},{10... | collective-permute-start | bytes 294920 | tf_op jit(solution)/shard_map/ppermute | solution.py:413
  28.7 5.4 %collective-permute-start.7 = (f32[48,512]{1,0:T(8,128)S(1)}, f32[48,512]{1,0:T(8,128)S(1)}, u32[]{:S(2)}, u32[]{:S(2)}) collective-permute-start(f32[48,512]{1,0:T(8,128)S(1)} %get-tuple-element.30), channel_id=1, source_target_pairs={{0,16},{8,24},{16,0},{24,8},{1,17},{9,25},{17,1},{25,9},{2,18},{10... | collective-permute-start | bytes 294920 | tf_op jit(solution)/shard_map/ppermute | solution.py:413
  29.7 5.2 %collective-permute-start.6 = (f32[48,512]{1,0:T(8,128)S(1)}, f32[48,512]{1,0:T(8,128)S(1)}, u32[]{:S(2)}, u32[]{:S(2)}) collective-permute-start(f32[48,512]{1,0:T(8,128)S(1)} %get-tuple-element.29), channel_id=1, source_target_pairs={{0,8},{8,0},{16,24},{24,16},{1,9},{9,1},{17,25},{25,17},{2,10},{10... | collective-permute-start | bytes 294920 | tf_op jit(solution)/shard_map/ppermute | solution.py:413
  34.9 13.0 %copy-start.7 = (bf16[2,128,56]{2,1,0:T(8,128)(2,1)S(1)}, bf16[2,128,56]{2,1,0:T(8,128)(2,1)}, u32[]{:S(2)}) copy-start(bf16[2,128,56]{2,1,0:T(8,128)(2,1)} %constant.30.clone.refs_8_) | copy-start | bytes 86020
  40.7 4.7 %collective-permute-start.10 = (f32[48,512]{1,0:T(8,128)S(1)}, f32[48,512]{1,0:T(8,128)S(1)}, u32[]{:S(2)}, u32[]{:S(2)}) collective-permute-start(f32[48,512]{1,0:T(8,128)S(1)} %get-tuple-element.35), channel_id=1, source_target_pairs={{0,16},{8,24},{16,0},{24,8},{1,17},{9,25},{17,1},{25,9},{2,18},{10... | collective-permute-start | bytes 294920 | tf_op jit(solution)/shard_map/ppermute | solution.py:413
  41.6 5.5 %collective-permute-start.11 = (f32[48,512]{1,0:T(8,128)S(1)}, f32[48,512]{1,0:T(8,128)S(1)}, u32[]{:S(2)}, u32[]{:S(2)}) collective-permute-start(f32[48,512]{1,0:T(8,128)S(1)} %get-tuple-element.36), channel_id=1, source_target_pairs={{0,24},{8,16},{16,8},{24,0},{1,25},{9,17},{17,9},{25,1},{2,26},{10... | collective-permute-start | bytes 294920 | tf_op jit(solution)/shard_map/ppermute | solution.py:413
  42.9 5.0 %collective-permute-start.9 = (f32[48,512]{1,0:T(8,128)S(1)}, f32[48,512]{1,0:T(8,128)S(1)}, u32[]{:S(2)}, u32[]{:S(2)}) collective-permute-start(f32[48,512]{1,0:T(8,128)S(1)} %get-tuple-element.34), channel_id=1, source_target_pairs={{0,8},{8,0},{16,24},{24,16},{1,9},{9,1},{17,25},{25,17},{2,10},{10... | collective-permute-start | bytes 294920 | tf_op jit(solution)/shard_map/ppermute | solution.py:413
  60.9 9.7 %all-to-all-start.1 = ((f32[32,1,128]{2,1,0:T(1,128)}), f32[32,1,128]{2,1,0:T(1,128)S(1)}, u32[]{:S(2)}, u32[]{:S(2)}) async-start(f32[32,1,128]{2,1,0:T(1,128)} %shard_map.144), calls=%async_computation.1 | async-start | bytes 32768 | tf_op jit(solution)/shard_map/all_to_all | solution.py:514

commit v11 on v10

--- a/solution.py
+++ b/solution.py
@@ -189,11 +189,7 @@
     copies = [pltpu.make_async_copy(source, target, sems.at[i]) for i, (source, target) in enumerate(pairs)]
     for copy in copies:
         copy.start()
-    for copy in copies:
-        copy.wait()
-    inside, _ = sphere(col_ref[...], size)
-    parts = [jnp.where(inside, psi_ref[p], 0.0) for p in range(2)]
-    to_planes(me_ref[0], parts, ahead_ref, outs, step)
+    copies[0].wait()
     radius = size // 4
     gx, gy = position(col_ref[...], size)
     used = gx * gx + gy * gy <= float(radius * radius)
@@ -206,6 +202,11 @@
     place = jnp.where(used, jnp.where(row == 0, slot, lane + gy), -9.0)
     for k in range(devices):
         outs[k][rows:] = place
+    inside, _ = sphere(col_ref[...], size)
+    for copy in copies[1:]:
+        copy.wait()
+    parts = [jnp.where(inside, psi_ref[p], 0.0) for p in range(2)]
+    to_planes(me_ref[0], parts, ahead_ref, outs, step)
 
 
 def middle_kernel(devices, step, size, me_ref, low_ref, up_ref, *refs):
@@ -246,21 +247,27 @@
         packed_ref[k] = total[k * rows : (k + 1) * rows].astype(BF16)
 
 
-def gram_kernel(bands, parts_ref, sum_ref):
+def rest(value, unit):
+    return value & (unit - 1) if unit & (unit - 1) == 0 else value % unit
+
+
+def gram_kernel(bands, parts_ref, sum_ref, spare_ref):
     rows, cols = parts_ref.shape[1:]
     count = bands * rows
     stacked = parts_ref[...].reshape(count, cols)
     product = dot(stacked, stacked, ((1,), (1,)))
-    down = lax.broadcasted_iota(jnp.int32, (count, count), 0) % rows
-    along = lax.broadcasted_iota(jnp.int32, (count, count), 1) % rows
+    down = lax.broadcasted_iota(jnp.int32, (count, count), 0)
+    along = lax.broadcasted_iota(jnp.int32, (count, count), 1)
+    down, along = rest(down, rows), rest(along, rows)
     real = jnp.where(down == along, product, 0.0)
     imag = jnp.where(along == down + rows // 2, product, jnp.where(down == along + rows // 2, -product, 0.0))
-    place = lax.broadcasted_iota(jnp.int32, (count, 128), 0) // rows
-    spot = lax.broadcasted_iota(jnp.int32, (count, 128), 1)
+    place = lax.broadcasted_iota(jnp.int32, (count, 128), 0)
+    spot = lax.broadcasted_iota(jnp.int32, (count, 128), 1) * rows
     pieces, places = [], []
     for p, value in enumerate((real, imag)):
         value = jnp.sum(value.reshape(bands, rows, count), axis=1)
-        hot = jnp.where(place + p * GY == spot, 1.0, 0.0).astype(BF16)
+        gap = place + p * GY * rows - spot
+        hot = jnp.where((gap >= 0) & (gap < rows), 1.0, 0.0).astype(BF16)
         for _ in range(3):
             pieces.append(value.astype(BF16))
             value = value - pieces[-1].astype(F32)
@@ -268,6 +275,7 @@
     value = dot(jnp.concatenate(pieces, axis=1), jnp.concatenate(places, axis=0))
     for g in range(sum_ref.shape[0] // bands):
         sum_ref[g * bands : (g + 1) * bands, 0, :] = value
+    spare_ref[...] = value
 
 
 def total_kernel(own, scale, me_ref, parts_ref, out_ref):
@@ -297,7 +305,7 @@
 def gather(box, mark_ref, out_ref, slots):
     rows, cols = mark_ref.shape[0] - 8, mark_ref.shape[1]
     zero = jnp.zeros((), BF16)
-    wide = min(256, cols)
+    wide = min(512, cols)
     for at in range(0, cols, wide):
         slot = jnp.broadcast_to(mark_ref[rows : rows + 1, at : at + wide], (16, wide)).astype(BF16)
         spot = jnp.broadcast_to(mark_ref[rows + 1 : rows + 2, at : at + wide], (128, wide))
@@ -500,9 +508,9 @@
         + [(psi_t, False), (first, True), (col_row, False), (back, False), (pick, False)],
         [held],
     )
-    (partial_sum,) = call(
+    partial_sum, _ = call(
         functools.partial(gram_kernel, bands),
-        [vmem((devices * bands, 1, 128))],
+        [vmem((devices * bands, 1, 128)), vmem((bands, 128))],
         [],
         [(lax.all_to_all(packed, "band", 0, 0, tiled=True), True)],
     )

time: 71.6 us -> 71.5 us (level)
  no operation moved by 1% of the time
where the time goes in v11:
time: 71.5 us; the launch traced here: 71.2 us
  Pallas kernels  21.2 us (30%)
  starting transfers between devices  17.8 us (25%)
  waiting for transfers between devices  15.9 us (22%)
  blocking collectives  11.5 us (16%)
  between operations  2.24 us (3%)
  local copies, waits for them, and re-layouts  1.36 us (2%)
  other arithmetic  1.24 us (2%)
    pallas_call x15, Pallas kernels, call(): pl.pallas_call(kernel, out_shape=out_shape, in_specs=[SMEM] * len(scalars...  21.2 us
    ppermute x12, starting transfers between devices, exchange(): lax.ppermute(values[k], 'grid', [(d, step(d, k)) for d in range(devices)])  15.3 us
    all_to_all x1, blocking collectives, body(): lax.all_to_all(packed, 'band', 0, 0, tiled=True)  11.5 us
    ppermute x12, waiting for transfers between devices, exchange(): lax.ppermute(values[k], 'grid', [(d, step(d, k)) for d in range(devices)])  9.54 us
    all_to_all x1, waiting for transfers between devices, body(): lax.all_to_all(partial_sum, ('grid', 'band'), 0, 0, tiled=True)  6.39 us
    all_to_all x1, starting transfers between devices, body(): lax.all_to_all(partial_sum, ('grid', 'band'), 0, 0, tiled=True)  2.57 us
  transfers between devices with their start and end apart: 13, of which 8 were waited for; matrix products, arithmetic and copies ran while one was open for 4% of the time, Pallas kernels for 8%

profile of v11, /device:TPU:0, one launch (start us, length us, event | category | flops | bytes accessed | tf_op | source)
XLA Modules:
  0.0 71.2 jit_solution(4436477332671157281)
XLA Ops:
  0.6 1.3 %shard_map.131 = (f32[56,512]{1,0:T(8,128)S(1)}, f32[56,512]{1,0:T(8,128)S(1)}, f32[56,512]{1,0:T(8,128)S(1)}, f32[56,512]{1,0:T(8,128)S(1)}) custom-call(s32[1]{0:T(128)} %bitcast.me_ref, f32[2,96,512]{2,1,0:T(8,128)} %bitcast.11, s32[1,512]{1,0:T(1,128)} %bitcast.14, bf16[4,48,336]{2,1,0:T(8,128)(2,1)} %constant.24.clone.refs_2_.refs_6_), custom_call_target="tpu_custom_call" | custom-call | tf_op jit(solution)/shard_map/pallas_call | solution.py:126
  2.0 4.0 %collective-permute-start.2 = (f32[56,512]{1,0:T(8,128)S(1)}, f32[56,512]{1,0:T(8,128)S(1)}, u32[]{:S(2)}, u32[]{:S(2)}) collective-permute-start(f32[56,512]{1,0:T(8,128)S(1)} %get-tuple-element.24), channel_id=1, source_target_pairs={{0,24},{8,16},{16,8},{24,0},{1,25},{9,17},{17,9},{25,1},{2,26},{10... | collective-permute-start | bytes 344072 | tf_op jit(solution)/shard_map/ppermute | solution.py:421
  5.9 0.5 collective-permute-start.1
  6.4 0.1 collective-permute-start
  6.6 1.2 %broadcast_multiply_fusion = f32[24,9216]{1,0:T(8,128)S(1)} fusion(f32[24,9216]{1,0:T(8,128)} %param.14), kind=kLoop, calls=%fused_computation | loop fusion | flops 221184 | bytes 1769472 | tf_op jit(solution)/shard_map/mul | solution.py:434
  7.8 0.8 %shard_map.132.refs_0_ = f32[48,2048]{1,0:T(8,128)S(1)} custom-call(f32[56,512]{1,0:T(8,128)S(1)} %get-tuple-element.25.plane_ref.mark_ref, f32[56,512]{1,0:T(8,128)S(1)} %get-tuple-element.25.plane_ref.mark_ref), custom_call_target="tpu_custom_call" | custom-call | tf_op jit(solution)/shard_map/pallas_call | solution.py:126
  8.6 0.5 reshape.22
  9.1 0.1 pad.4.refs_3_
  9.2 0.0 copy-start.1
  9.2 0.0 copy-start.2
  9.2 0.0 copy-start.5
  9.2 0.0 copy-start.6
  9.2 0.3 collective-permute-done.2.plane_ref.mark_ref.refs_0_
  9.5 0.8 %shard_map.133.refs_0_ = f32[48,2048]{1,0:T(8,128)S(1)} custom-call(f32[56,512]{1,0:T(8,128)S(1)} %collective-permute-done.2.plane_ref.mark_ref.refs_0_, f32[56,512]{1,0:T(8,128)S(1)} %collective-permute-done.2.plane_ref.mark_ref.refs_0_, f32[48,2048]{1,0:T(8,128)S(1)} %shard_map.132.refs_0_), custom_call_target="tpu_custom_call" | custom-call | tf_op jit(solution)/shard_map/pallas_call | solution.py:126
  10.3 1.3 %collective-permute-done.1.plane_ref.mark_ref.refs_1_ = f32[56,512]{1,0:T(8,128)S(1)} collective-permute-done((f32[56,512]{1,0:T(8,128)S(1)}, f32[56,512]{1,0:T(8,128)S(1)}, u32[]{:S(2)}, u32[]{:S(2)}) %collective-permute-start.1) | collective-permute-done | bytes 114720 | tf_op jit(solution)/shard_map/ppermute | solution.py:421
  11.5 0.8 %shard_map.134.before_ref = f32[48,2048]{1,0:T(8,128)S(1)} custom-call(f32[56,512]{1,0:T(8,128)S(1)} %collective-permute-done.1.plane_ref.mark_ref.refs_1_, f32[56,512]{1,0:T(8,128)S(1)} %collective-permute-done.1.plane_ref.mark_ref.refs_1_, f32[48,2048]{1,0:T(8,128)S(1)} %shard_map.133.refs_0_), custom_call_target="tpu_custom_call" | custom-call | tf_op jit(solution)/shard_map/pallas_call | solution.py:126
  12.3 0.0 copy-start
  12.3 0.0 copy-start.3
  12.3 0.0 copy-start.4
  12.4 0.0 copy-start.8
  12.4 0.0 collective-permute-done.plane_ref.refs_2_
  12.4 0.0 copy-done.1
  12.4 0.0 copy-done.2
  12.4 0.0 copy-done.5
  12.4 0.0 copy-done.6
  12.4 5.6 %shard_map.135 = (f32[48,512]{1,0:T(8,128)S(1)}, f32[48,512]{1,0:T(8,128)S(1)}, f32[48,512]{1,0:T(8,128)S(1)}, bf16[96,2048]{1,0:T(8,128)(2,1)S(1)}) custom-call(f32[56,512]{1,0:T(8,128)S(1)} %collective-permute-done.plane_ref.refs_2_, f32[48,2048]{1,0:T(8,128)S(1)} %shard_map.134.before_ref, ...), custom_call_target="tpu_custom_call" | custom-call | tf_op jit(solution)/shard_map/pallas_call | solution.py:126
  18.1 1.7 %collective-permute-start.3 = (f32[48,512]{1,0:T(8,128)S(1)}, f32[48,512]{1,0:T(8,128)S(1)}, u32[]{:S(2)}, u32[]{:S(2)}) collective-permute-start(f32[48,512]{1,0:T(8,128)S(1)} %get-tuple-element.27), channel_id=1, source_target_pairs={{0,8},{8,0},{16,24},{24,16},{1,9},{9,1},{17,25},{25,17},{2,10},{10... | collective-permute-start | bytes 294920 | tf_op jit(solution)/shard_map/ppermute | solution.py:421
  19.8 1.0 %collective-permute-start.4 = (f32[48,512]{1,0:T(8,128)S(1)}, f32[48,512]{1,0:T(8,128)S(1)}, u32[]{:S(2)}, u32[]{:S(2)}) collective-permute-start(f32[48,512]{1,0:T(8,128)S(1)} %get-tuple-element.28), channel_id=1, source_target_pairs={{0,16},{8,24},{16,0},{24,8},{1,17},{9,25},{17,1},{25,9},{2,18},{10... | collective-permute-start | bytes 294920 | tf_op jit(solution)/shard_map/ppermute | solution.py:421
  20.8 0.8 %collective-permute-start.5 = (f32[48,512]{1,0:T(8,128)S(1)}, f32[48,512]{1,0:T(8,128)S(1)}, u32[]{:S(2)}, u32[]{:S(2)}) collective-permute-start(f32[48,512]{1,0:T(8,128)S(1)} %get-tuple-element.29), channel_id=1, source_target_pairs={{0,24},{8,16},{16,8},{24,0},{1,25},{9,17},{17,9},{25,1},{2,26},{10... | collective-permute-start | bytes 294920 | tf_op jit(solution)/shard_map/ppermute | solution.py:421
  22.9 0.5 shard_map.136.refs_0_
  23.4 0.0 collective-permute-done.3.refs_1_
  23.4 3.0 %collective-permute-done.4.refs_2_ = f32[48,512]{1,0:T(8,128)S(1)} collective-permute-done((f32[48,512]{1,0:T(8,128)S(1)}, f32[48,512]{1,0:T(8,128)S(1)}, u32[]{:S(2)}, u32[]{:S(2)}) %collective-permute-start.4) | collective-permute-done | bytes 98336 | tf_op jit(solution)/shard_map/ppermute | solution.py:421
  26.4 0.0 collective-permute-done.5.refs_3_
  26.4 0.0 copy-done
  26.4 0.0 copy-done.3
  26.4 0.0 copy-done.4
  26.4 0.0 copy-done.8
  26.4 0.6 shard_map.137
  27.1 1.5 %collective-permute-start.8 = (f32[48,512]{1,0:T(8,128)S(1)}, f32[48,512]{1,0:T(8,128)S(1)}, u32[]{:S(2)}, u32[]{:S(2)}) collective-permute-start(f32[48,512]{1,0:T(8,128)S(1)} %get-tuple-element.32), channel_id=1, source_target_pairs={{0,24},{8,16},{16,8},{24,0},{1,25},{9,17},{17,9},{25,1},{2,26},{10... | collective-permute-start | bytes 294920 | tf_op jit(solution)/shard_map/ppermute | solution.py:421
  28.6 1.0 %collective-permute-start.7 = (f32[48,512]{1,0:T(8,128)S(1)}, f32[48,512]{1,0:T(8,128)S(1)}, u32[]{:S(2)}, u32[]{:S(2)}) collective-permute-start(f32[48,512]{1,0:T(8,128)S(1)} %get-tuple-element.31), channel_id=1, source_target_pairs={{0,16},{8,24},{16,0},{24,8},{1,17},{9,25},{17,1},{25,9},{2,18},{10... | collective-permute-start | bytes 294920 | tf_op jit(solution)/shard_map/ppermute | solution.py:421
  29.5 1.1 %collective-permute-start.6 = (f32[48,512]{1,0:T(8,128)S(1)}, f32[48,512]{1,0:T(8,128)S(1)}, u32[]{:S(2)}, u32[]{:S(2)}) collective-permute-start(f32[48,512]{1,0:T(8,128)S(1)} %get-tuple-element.30), channel_id=1, source_target_pairs={{0,8},{8,0},{16,24},{24,16},{1,9},{9,1},{17,25},{25,17},{2,10},{10... | collective-permute-start | bytes 294920 | tf_op jit(solution)/shard_map/ppermute | solution.py:421
  30.6 0.8 %shard_map.138.refs_0_ = f32[48,2048]{1,0:T(8,128)S(1)} custom-call(f32[48,512]{1,0:T(8,128)S(1)} %get-tuple-element.33.plane_ref, f32[56,512]{1,0:T(8,128)S(1)} %get-tuple-element.25.plane_ref.mark_ref), custom_call_target="tpu_custom_call" | custom-call | tf_op jit(solution)/shard_map/pallas_call | solution.py:126
  31.4 1.8 %collective-permute-done.8.plane_ref = f32[48,512]{1,0:T(8,128)S(1)} collective-permute-done((f32[48,512]{1,0:T(8,128)S(1)}, f32[48,512]{1,0:T(8,128)S(1)}, u32[]{:S(2)}, u32[]{:S(2)}) %collective-permute-start.8) | collective-permute-done | bytes 98336 | tf_op jit(solution)/shard_map/ppermute | solution.py:421
  33.2 0.8 %shard_map.139.refs_0_ = f32[48,2048]{1,0:T(8,128)S(1)} custom-call(f32[48,512]{1,0:T(8,128)S(1)} %collective-permute-done.8.plane_ref, f32[56,512]{1,0:T(8,128)S(1)} %collective-permute-done.2.plane_ref.mark_ref.refs_0_, f32[48,2048]{1,0:T(8,128)S(1)} %shard_map.138.refs_0_), custom_call_target="tpu_custom_call" | custom-call | tf_op jit(solution)/shard_map/pallas_call | solution.py:126
  34.0 0.0 collective-permute-done.7.plane_ref
  34.0 0.8 %shard_map.140.before_ref = f32[48,2048]{1,0:T(8,128)S(1)} custom-call(f32[48,512]{1,0:T(8,128)S(1)} %collective-permute-done.7.plane_ref, f32[56,512]{1,0:T(8,128)S(1)} %collective-permute-done.1.plane_ref.mark_ref.refs_1_, f32[48,2048]{1,0:T(8,128)S(1)} %shard_map.139.refs_0_), custom_call_target="tpu_custom_call" | custom-call | tf_op jit(solution)/shard_map/pallas_call | solution.py:126
  34.7 0.0 copy-start.7
  34.8 0.0 collective-permute-done.6.plane_ref
  34.8 5.8 %shard_map.141 = (f32[48,512]{1,0:T(8,128)S(1)}, f32[48,512]{1,0:T(8,128)S(1)}, f32[48,512]{1,0:T(8,128)S(1)}, bf16[96,2048]{1,0:T(8,128)(2,1)S(1)}) custom-call(f32[48,512]{1,0:T(8,128)S(1)} %collective-permute-done.6.plane_ref, f32[48,2048]{1,0:T(8,128)S(1)} %shard_map.140.before_ref, f32[56,512]{1,0:T(8,128)S(1)} %collective-permute-done.2.plane_ref.mark_ref.refs_0_, ...), custom_call_target="tpu_custom_call" | custom-call | tf_op jit(solution)/shard_map/pallas_call | solution.py:126
  40.6 0.9 %collective-permute-start.10 = (f32[48,512]{1,0:T(8,128)S(1)}, f32[48,512]{1,0:T(8,128)S(1)}, u32[]{:S(2)}, u32[]{:S(2)}) collective-permute-start(f32[48,512]{1,0:T(8,128)S(1)} %get-tuple-element.36), channel_id=1, source_target_pairs={{0,16},{8,24},{16,0},{24,8},{1,17},{9,25},{17,1},{25,9},{2,18},{10... | collective-permute-start | bytes 294920 | tf_op jit(solution)/shard_map/ppermute | solution.py:421
  41.5 1.3 %collective-permute-start.11 = (f32[48,512]{1,0:T(8,128)S(1)}, f32[48,512]{1,0:T(8,128)S(1)}, u32[]{:S(2)}, u32[]{:S(2)}) collective-permute-start(f32[48,512]{1,0:T(8,128)S(1)} %get-tuple-element.37), channel_id=1, source_target_pairs={{0,24},{8,16},{16,8},{24,0},{1,25},{9,17},{17,9},{25,1},{2,26},{10... | collective-permute-start | bytes 294920 | tf_op jit(solution)/shard_map/ppermute | solution.py:421
  42.8 1.4 %collective-permute-start.9 = (f32[48,512]{1,0:T(8,128)S(1)}, f32[48,512]{1,0:T(8,128)S(1)}, u32[]{:S(2)}, u32[]{:S(2)}) collective-permute-start(f32[48,512]{1,0:T(8,128)S(1)} %get-tuple-element.35), channel_id=1, source_target_pairs={{0,8},{8,0},{16,24},{24,16},{1,9},{9,1},{17,25},{25,17},{2,10},{10... | collective-permute-start | bytes 294920 | tf_op jit(solution)/shard_map/ppermute | solution.py:421
  44.2 0.5 shard_map.142.refs_0_
  44.6 0.7 collective-permute-done.10.refs_2_
  45.3 1.7 %collective-permute-done.11.refs_3_ = f32[48,512]{1,0:T(8,128)S(1)} collective-permute-done((f32[48,512]{1,0:T(8,128)S(1)}, f32[48,512]{1,0:T(8,128)S(1)}, u32[]{:S(2)}, u32[]{:S(2)}) %collective-permute-start.11) | collective-permute-done | bytes 98336 | tf_op jit(solution)/shard_map/ppermute | solution.py:421
  47.0 0.8 %collective-permute-done.9.refs_1_ = f32[48,512]{1,0:T(8,128)S(1)} collective-permute-done((f32[48,512]{1,0:T(8,128)S(1)}, f32[48,512]{1,0:T(8,128)S(1)}, u32[]{:S(2)}, u32[]{:S(2)}) %collective-permute-start.9) | collective-permute-done | bytes 98336 | tf_op jit(solution)/shard_map/ppermute | solution.py:421
  47.8 0.0 copy-done.7
  47.8 0.5 shard_map.143
  48.3 11.5 %all_to_all.10.parts_ref = bf16[8,16,512]{2,1,0:T(8,128)(2,1)S(1)} all-to-all(bf16[8,16,512]{2,1,0:T(8,128)(2,1)S(1)} %get-tuple-element.40), channel_id=1, replica_groups=mesh['grid'=4,'band'=8] {'band'}, dimensions={0} | all-to-all | bytes 262144 | tf_op jit(solution)/shard_map/all_to_all | solution.py:515
  59.8 1.0 %shard_map.144 = (f32[32,1,128]{2,1,0:T(1,128)}, f32[8,128]{1,0:T(8,128)}) custom-call(bf16[8,16,512]{2,1,0:T(8,128)(2,1)S(1)} %all_to_all.10.parts_ref), custom_call_target="tpu_custom_call" | custom-call | tf_op jit(solution)/shard_map/pallas_call | solution.py:126
  60.8 2.6 %all-to-all-start.1 = ((f32[32,1,128]{2,1,0:T(1,128)}), f32[32,1,128]{2,1,0:T(1,128)S(1)}, u32[]{:S(2)}, u32[]{:S(2)}) async-start(f32[32,1,128]{2,1,0:T(1,128)} %get-tuple-element.41), calls=%async_computation.1 | async-start | bytes 32768 | tf_op jit(solution)/shard_map/all_to_all | solution.py:522
  63.4 0.7 %copy.15 = f32[2,1,512,96]{2,3,1,0:T(8,128)} copy(f32[2,1,512,96]{2,3,1,0:T(8,128)S(1)} %bitcast.10) | data formatting | bytes 786432
  64.1 6.4 %all-to-all-done.1.parts_ref = f32[32,1,128]{2,1,0:T(1,128)S(1)} async-done(((f32[32,1,128]{2,1,0:T(1,128)}), f32[32,1,128]{2,1,0:T(1,128)S(1)}, u32[]{:S(2)}, u32[]{:S(2)}) %all-to-all-start.1) | async-done | bytes 16416 | tf_op jit(solution)/shard_map/all_to_all | solution.py:522
  70.5 0.7 %shard_map.145 = f32[2,1,2]{2,1,0:T(1,128)} custom-call(s32[1]{0:T(128)} %bitcast.me_ref, f32[32,1,128]{2,1,0:T(1,128)S(1)} %all-to-all-done.1.parts_ref), custom_call_target="tpu_custom_call" | custom-call | tf_op jit(solution)/shard_map/pallas_call | solution.py:126
Async XLA Ops:
  2.0 7.5 %collective-permute-start.2 = (f32[56,512]{1,0:T(8,128)S(1)}, f32[56,512]{1,0:T(8,128)S(1)}, u32[]{:S(2)}, u32[]{:S(2)}) collective-permute-start(f32[56,512]{1,0:T(8,128)S(1)} %get-tuple-element.24), channel_id=1, source_target_pairs={{0,24},{8,16},{16,8},{24,0},{1,25},{9,17},{17,9},{25,1},{2,26},{10... | collective-permute-start | bytes 344072 | tf_op jit(solution)/shard_map/ppermute | solution.py:421
  5.9 5.6 %collective-permute-start.1 = (f32[56,512]{1,0:T(8,128)S(1)}, f32[56,512]{1,0:T(8,128)S(1)}, u32[]{:S(2)}, u32[]{:S(2)}) collective-permute-start(f32[56,512]{1,0:T(8,128)S(1)} %get-tuple-element.23), channel_id=1, source_target_pairs={{0,16},{8,24},{16,0},{24,8},{1,17},{9,25},{17,1},{25,9},{2,18},{10... | collective-permute-start | bytes 344072 | tf_op jit(solution)/shard_map/ppermute | solution.py:421
  6.4 5.9 %collective-permute-start = (f32[56,512]{1,0:T(8,128)S(1)}, f32[56,512]{1,0:T(8,128)S(1)}, u32[]{:S(2)}, u32[]{:S(2)}) collective-permute-start(f32[56,512]{1,0:T(8,128)S(1)} %get-tuple-element.22), channel_id=1, source_target_pairs={{0,8},{8,0},{16,24},{24,16},{1,9},{9,1},{17,25},{25,17},{2,10},{10... | collective-permute-start | bytes 344072 | tf_op jit(solution)/shard_map/ppermute | solution.py:421
  9.2 3.2 %copy-start.1 = (bf16[384,256]{1,0:T(8,128)(2,1)S(1)}, bf16[384,256]{1,0:T(8,128)(2,1)}, u32[]{:S(2)}) copy-start(bf16[384,256]{1,0:T(8,128)(2,1)} %constant.25.clone.refs_4_) | copy-start | bytes 589828
  9.2 3.2 %copy-start.2 = (bf16[384,224]{1,0:T(8,128)(2,1)S(1)}, bf16[384,224]{1,0:T(8,128)(2,1)}, u32[]{:S(2)}) copy-start(bf16[384,224]{1,0:T(8,128)(2,1)} %constant.26.clone.refs_5_) | copy-start | bytes 516100
  9.2 3.2 %copy-start.5 = (bf16[256,256]{1,0:T(8,128)(2,1)S(1)}, bf16[256,256]{1,0:T(8,128)(2,1)}, u32[]{:S(2)}) copy-start(bf16[256,256]{1,0:T(8,128)(2,1)} %constant.28.clone.refs_7_) | copy-start | bytes 393220
  9.2 3.2 %copy-start.6 = (bf16[224,192]{1,0:T(8,128)(2,1)S(1)}, bf16[224,192]{1,0:T(8,128)(2,1)}, u32[]{:S(2)}) copy-start(bf16[224,192]{1,0:T(8,128)(2,1)} %constant.27.clone.refs_6_) | copy-start | bytes 258052
  12.3 14.1 %copy-start = (f32[2,1,512,96]{2,3,1,0:T(8,128)S(1)}, f32[2,1,512,96]{2,3,1,0:T(8,128)}, u32[]{:S(2)}) copy-start(f32[2,1,512,96]{2,3,1,0:T(8,128)} %param.12) | copy-start | bytes 1179652
  12.3 14.1 %copy-start.3 = (bf16[4,48,336]{2,1,0:T(8,128)(2,1)S(1)}, bf16[4,48,336]{2,1,0:T(8,128)(2,1)}, u32[]{:S(2)}) copy-start(bf16[4,48,336]{2,1,0:T(8,128)(2,1)} %constant.24.clone.refs_2_.refs_6_) | copy-start | bytes 387076
  12.3 14.1 %copy-start.4 = (bf16[112,576]{1,0:T(8,128)(2,1)S(1)}, bf16[112,576]{1,0:T(8,128)(2,1)}, u32[]{:S(2)}) copy-start(bf16[112,576]{1,0:T(8,128)(2,1)} %constant.29.clone.refs_7_) | copy-start | bytes 387076
  12.4 14.1 %copy-start.8 = (s32[512]{0:T(512)S(1)}, s32[512]{0:T(512)}, u32[]{:S(2)}) copy-start(s32[512]{0:T(512)} %param.13) | copy-start | bytes 6148
  18.1 5.3 %collective-permute-start.3 = (f32[48,512]{1,0:T(8,128)S(1)}, f32[48,512]{1,0:T(8,128)S(1)}, u32[]{:S(2)}, u32[]{:S(2)}) collective-permute-start(f32[48,512]{1,0:T(8,128)S(1)} %get-tuple-element.27), channel_id=1, source_target_pairs={{0,8},{8,0},{16,24},{24,16},{1,9},{9,1},{17,25},{25,17},{2,10},{10... | collective-permute-start | bytes 294920 | tf_op jit(solution)/shard_map/ppermute | solution.py:421
  19.8 6.6 %collective-permute-start.4 = (f32[48,512]{1,0:T(8,128)S(1)}, f32[48,512]{1,0:T(8,128)S(1)}, u32[]{:S(2)}, u32[]{:S(2)}) collective-permute-start(f32[48,512]{1,0:T(8,128)S(1)} %get-tuple-element.28), channel_id=1, source_target_pairs={{0,16},{8,24},{16,0},{24,8},{1,17},{9,25},{17,1},{25,9},{2,18},{10... | collective-permute-start | bytes 294920 | tf_op jit(solution)/shard_map/ppermute | solution.py:421
  20.8 5.6 %collective-permute-start.5 = (f32[48,512]{1,0:T(8,128)S(1)}, f32[48,512]{1,0:T(8,128)S(1)}, u32[]{:S(2)}, u32[]{:S(2)}) collective-permute-start(f32[48,512]{1,0:T(8,128)S(1)} %get-tuple-element.29), channel_id=1, source_target_pairs={{0,24},{8,16},{16,8},{24,0},{1,25},{9,17},{17,9},{25,1},{2,26},{10... | collective-permute-start | bytes 294920 | tf_op jit(solution)/shard_map/ppermute | solution.py:421
  27.1 6.1 %collective-permute-start.8 = (f32[48,512]{1,0:T(8,128)S(1)}, f32[48,512]{1,0:T(8,128)S(1)}, u32[]{:S(2)}, u32[]{:S(2)}) collective-permute-start(f32[48,512]{1,0:T(8,128)S(1)} %get-tuple-element.32), channel_id=1, source_target_pairs={{0,24},{8,16},{16,8},{24,0},{1,25},{9,17},{17,9},{25,1},{2,26},{10... | collective-permute-start | bytes 294920 | tf_op jit(solution)/shard_map/ppermute | solution.py:421
  28.6 5.4 %collective-permute-start.7 = (f32[48,512]{1,0:T(8,128)S(1)}, f32[48,512]{1,0:T(8,128)S(1)}, u32[]{:S(2)}, u32[]{:S(2)}) collective-permute-start(f32[48,512]{1,0:T(8,128)S(1)} %get-tuple-element.31), channel_id=1, source_target_pairs={{0,16},{8,24},{16,0},{24,8},{1,17},{9,25},{17,1},{25,9},{2,18},{10... | collective-permute-start | bytes 294920 | tf_op jit(solution)/shard_map/ppermute | solution.py:421
  29.5 5.2 %collective-permute-start.6 = (f32[48,512]{1,0:T(8,128)S(1)}, f32[48,512]{1,0:T(8,128)S(1)}, u32[]{:S(2)}, u32[]{:S(2)}) collective-permute-start(f32[48,512]{1,0:T(8,128)S(1)} %get-tuple-element.30), channel_id=1, source_target_pairs={{0,8},{8,0},{16,24},{24,16},{1,9},{9,1},{17,25},{25,17},{2,10},{10... | collective-permute-start | bytes 294920 | tf_op jit(solution)/shard_map/ppermute | solution.py:421
  34.7 13.1 %copy-start.7 = (bf16[2,128,56]{2,1,0:T(8,128)(2,1)S(1)}, bf16[2,128,56]{2,1,0:T(8,128)(2,1)}, u32[]{:S(2)}) copy-start(bf16[2,128,56]{2,1,0:T(8,128)(2,1)} %constant.30.clone.refs_8_) | copy-start | bytes 86020
  40.6 4.7 %collective-permute-start.10 = (f32[48,512]{1,0:T(8,128)S(1)}, f32[48,512]{1,0:T(8,128)S(1)}, u32[]{:S(2)}, u32[]{:S(2)}) collective-permute-start(f32[48,512]{1,0:T(8,128)S(1)} %get-tuple-element.36), channel_id=1, source_target_pairs={{0,16},{8,24},{16,0},{24,8},{1,17},{9,25},{17,1},{25,9},{2,18},{10... | collective-permute-start | bytes 294920 | tf_op jit(solution)/shard_map/ppermute | solution.py:421
  41.5 5.5 %collective-permute-start.11 = (f32[48,512]{1,0:T(8,128)S(1)}, f32[48,512]{1,0:T(8,128)S(1)}, u32[]{:S(2)}, u32[]{:S(2)}) collective-permute-start(f32[48,512]{1,0:T(8,128)S(1)} %get-tuple-element.37), channel_id=1, source_target_pairs={{0,24},{8,16},{16,8},{24,0},{1,25},{9,17},{17,9},{25,1},{2,26},{10... | collective-permute-start | bytes 294920 | tf_op jit(solution)/shard_map/ppermute | solution.py:421
  42.8 5.0 %collective-permute-start.9 = (f32[48,512]{1,0:T(8,128)S(1)}, f32[48,512]{1,0:T(8,128)S(1)}, u32[]{:S(2)}, u32[]{:S(2)}) collective-permute-start(f32[48,512]{1,0:T(8,128)S(1)} %get-tuple-element.35), channel_id=1, source_target_pairs={{0,8},{8,0},{16,24},{24,16},{1,9},{9,1},{17,25},{25,17},{2,10},{10... | collective-permute-start | bytes 294920 | tf_op jit(solution)/shard_map/ppermute | solution.py:421
  60.8 9.7 %all-to-all-start.1 = ((f32[32,1,128]{2,1,0:T(1,128)}), f32[32,1,128]{2,1,0:T(1,128)S(1)}, u32[]{:S(2)}, u32[]{:S(2)}) async-start(f32[32,1,128]{2,1,0:T(1,128)} %get-tuple-element.41), calls=%async_computation.1 | async-start | bytes 32768 | tf_op jit(solution)/shard_map/all_to_all | solution.py:522

commit v12 on v11

--- a/solution.py
+++ b/solution.py
@@ -344,7 +344,7 @@
         return (lane >= first) & (lane <= last)
 
     in_ref[...] = jnp.zeros(in_ref.shape, F32)
-    for t, tile in scatter(plane_ref, marks[-1], slots):
+    for t, tile in scatter(plane_ref, marks[0], slots):
         got = tile + before_ref[:, 128 * t : 128 * t + 256]
         for i, (width, slot, middle) in enumerate(places):
             if slot // 2 * 2 != t:
@@ -468,7 +468,7 @@
                 [],
                 [(value, True) for value in [values[k], marks[k]] + list(sums)],
             )
-        given = [values[order[-1]], sums[0]] + [marks[k] for k in order[1:]]
+        given = [values[1], sums[0]] + marks[1:]
         *sent, box = call(
             functools.partial(slab_kernel, devices, size, depth),
             [vmem((rows, cols))] * (devices - 1) + [vmem((2 * rows, 128 * slots_all), BF16)],
@@ -488,7 +488,7 @@
             [],
             [(box, True), (marks[0], True)],
         )
-        return list(own) + [sent[order.index(k) - 1] for k in range(1, devices)]
+        return list(own) + list(sent)
 
     held = pltpu.VMEM((3 * devices * rows, cols), BF16)
     planes = exchange(slab(marks))

time: 71.5 us -> 71.5 us (level)
  no operation moved by 1% of the time
where the time goes in v12:
time: 71.5 us; the launch traced here: 71.2 us
  Pallas kernels  21.2 us (30%)
  starting transfers between devices  17.8 us (25%)
  waiting for transfers between devices  15.9 us (22%)
  blocking collectives  11.5 us (16%)
  between operations  2.24 us (3%)
  local copies, waits for them, and re-layouts  1.36 us (2%)
  other arithmetic  1.24 us (2%)
    pallas_call x15, Pallas kernels, call(): pl.pallas_call(kernel, out_shape=out_shape, in_specs=[SMEM] * len(scalars...  21.2 us
    ppermute x12, starting transfers between devices, exchange(): lax.ppermute(values[k], 'grid', [(d, step(d, k)) for d in range(devices)])  15.3 us
    all_to_all x1, blocking collectives, body(): lax.all_to_all(packed, 'band', 0, 0, tiled=True)  11.5 us
    ppermute x12, waiting for transfers between devices, exchange(): lax.ppermute(values[k], 'grid', [(d, step(d, k)) for d in range(devices)])  9.54 us
    all_to_all x1, waiting for transfers between devices, body(): lax.all_to_all(partial_sum, ('grid', 'band'), 0, 0, tiled=True)  6.39 us
    all_to_all x1, starting transfers between devices, body(): lax.all_to_all(partial_sum, ('grid', 'band'), 0, 0, tiled=True)  2.57 us
  transfers between devices with their start and end apart: 13, of which 8 were waited for; matrix products, arithmetic and copies ran while one was open for 4% of the time, Pallas kernels for 8%

profile of v12, /device:TPU:0, one launch (start us, length us, event | category | flops | bytes accessed | tf_op | source)
XLA Modules:
  0.0 71.2 jit_solution(483409305149837226)
XLA Ops:
  0.6 1.3 %shard_map.131 = (f32[56,512]{1,0:T(8,128)S(1)}, f32[56,512]{1,0:T(8,128)S(1)}, f32[56,512]{1,0:T(8,128)S(1)}, f32[56,512]{1,0:T(8,128)S(1)}) custom-call(s32[1]{0:T(128)} %bitcast.me_ref, f32[2,96,512]{2,1,0:T(8,128)} %bitcast.11, s32[1,512]{1,0:T(1,128)} %bitcast.14, bf16[4,48,336]{2,1,0:T(8,128)(2,1)} %constant.24.clone.refs_2_.refs_6_), custom_call_target="tpu_custom_call" | custom-call | tf_op jit(solution)/shard_map/pallas_call | solution.py:126
  2.0 4.0 %collective-permute-start.2 = (f32[56,512]{1,0:T(8,128)S(1)}, f32[56,512]{1,0:T(8,128)S(1)}, u32[]{:S(2)}, u32[]{:S(2)}) collective-permute-start(f32[56,512]{1,0:T(8,128)S(1)} %get-tuple-element.24), channel_id=1, source_target_pairs={{0,24},{8,16},{16,8},{24,0},{1,25},{9,17},{17,9},{25,1},{2,26},{10... | collective-permute-start | bytes 344072 | tf_op jit(solution)/shard_map/ppermute | solution.py:421
  5.9 0.5 collective-permute-start.1
  6.4 0.1 collective-permute-start
  6.6 1.2 %broadcast_multiply_fusion = f32[24,9216]{1,0:T(8,128)S(1)} fusion(f32[24,9216]{1,0:T(8,128)} %param.14), kind=kLoop, calls=%fused_computation | loop fusion | flops 221184 | bytes 1769472 | tf_op jit(solution)/shard_map/mul | solution.py:434
  7.8 0.8 %shard_map.132.refs_0_ = f32[48,2048]{1,0:T(8,128)S(1)} custom-call(f32[56,512]{1,0:T(8,128)S(1)} %get-tuple-element.25.plane_ref.mark_ref, f32[56,512]{1,0:T(8,128)S(1)} %get-tuple-element.25.plane_ref.mark_ref), custom_call_target="tpu_custom_call" | custom-call | tf_op jit(solution)/shard_map/pallas_call | solution.py:126
  8.6 0.5 reshape.22
  9.1 0.1 pad.4.refs_3_
  9.2 0.0 copy-start.1
  9.2 0.0 copy-start.2
  9.2 0.0 copy-start.5
  9.2 0.0 copy-start.6
  9.2 0.3 collective-permute-done.2.plane_ref.mark_ref.refs_2_
  9.5 0.8 %shard_map.133.refs_0_ = f32[48,2048]{1,0:T(8,128)S(1)} custom-call(f32[56,512]{1,0:T(8,128)S(1)} %collective-permute-done.2.plane_ref.mark_ref.refs_2_, f32[56,512]{1,0:T(8,128)S(1)} %collective-permute-done.2.plane_ref.mark_ref.refs_2_, f32[48,2048]{1,0:T(8,128)S(1)} %shard_map.132.refs_0_), custom_call_target="tpu_custom_call" | custom-call | tf_op jit(solution)/shard_map/pallas_call | solution.py:126
  10.3 1.3 %collective-permute-done.1.plane_ref.mark_ref.refs_1_ = f32[56,512]{1,0:T(8,128)S(1)} collective-permute-done((f32[56,512]{1,0:T(8,128)S(1)}, f32[56,512]{1,0:T(8,128)S(1)}, u32[]{:S(2)}, u32[]{:S(2)}) %collective-permute-start.1) | collective-permute-done | bytes 114720 | tf_op jit(solution)/shard_map/ppermute | solution.py:421
  11.5 0.8 %shard_map.134.before_ref = f32[48,2048]{1,0:T(8,128)S(1)} custom-call(f32[56,512]{1,0:T(8,128)S(1)} %collective-permute-done.1.plane_ref.mark_ref.refs_1_, f32[56,512]{1,0:T(8,128)S(1)} %collective-permute-done.1.plane_ref.mark_ref.refs_1_, f32[48,2048]{1,0:T(8,128)S(1)} %shard_map.133.refs_0_), custom_call_target="tpu_custom_call" | custom-call | tf_op jit(solution)/shard_map/pallas_call | solution.py:126
  12.3 0.0 copy-start
  12.3 0.0 copy-start.3
  12.3 0.0 copy-start.4
  12.4 0.0 copy-start.8
  12.4 0.0 collective-permute-done.plane_ref.refs_0_
  12.4 0.0 copy-done.1
  12.4 0.0 copy-done.2
  12.4 0.0 copy-done.5
  12.4 0.0 copy-done.6
  12.4 5.6 %shard_map.135 = (f32[48,512]{1,0:T(8,128)S(1)}, f32[48,512]{1,0:T(8,128)S(1)}, f32[48,512]{1,0:T(8,128)S(1)}, bf16[96,2048]{1,0:T(8,128)(2,1)S(1)}) custom-call(f32[56,512]{1,0:T(8,128)S(1)} %collective-permute-done.plane_ref.refs_0_, f32[48,2048]{1,0:T(8,128)S(1)} %shard_map.134.before_ref, f32[56,512]{1,0:T(8,128)S(1)} %collective-permute-done.plane_ref.refs_0_, ...), custom_call_target="tpu_custom_call" | custom-call | tf_op jit(solution)/shard_map/pallas_call | solution.py:126
  18.1 1.7 %collective-permute-start.3 = (f32[48,512]{1,0:T(8,128)S(1)}, f32[48,512]{1,0:T(8,128)S(1)}, u32[]{:S(2)}, u32[]{:S(2)}) collective-permute-start(f32[48,512]{1,0:T(8,128)S(1)} %get-tuple-element.27), channel_id=1, source_target_pairs={{0,8},{8,0},{16,24},{24,16},{1,9},{9,1},{17,25},{25,17},{2,10},{10... | collective-permute-start | bytes 294920 | tf_op jit(solution)/shard_map/ppermute | solution.py:421
  19.8 1.0 %collective-permute-start.4 = (f32[48,512]{1,0:T(8,128)S(1)}, f32[48,512]{1,0:T(8,128)S(1)}, u32[]{:S(2)}, u32[]{:S(2)}) collective-permute-start(f32[48,512]{1,0:T(8,128)S(1)} %get-tuple-element.28), channel_id=1, source_target_pairs={{0,16},{8,24},{16,0},{24,8},{1,17},{9,25},{17,1},{25,9},{2,18},{10... | collective-permute-start | bytes 294920 | tf_op jit(solution)/shard_map/ppermute | solution.py:421
  20.8 0.8 %collective-permute-start.5 = (f32[48,512]{1,0:T(8,128)S(1)}, f32[48,512]{1,0:T(8,128)S(1)}, u32[]{:S(2)}, u32[]{:S(2)}) collective-permute-start(f32[48,512]{1,0:T(8,128)S(1)} %get-tuple-element.29), channel_id=1, source_target_pairs={{0,24},{8,16},{16,8},{24,0},{1,25},{9,17},{17,9},{25,1},{2,26},{10... | collective-permute-start | bytes 294920 | tf_op jit(solution)/shard_map/ppermute | solution.py:421
  22.9 0.5 shard_map.136.refs_0_
  23.4 0.0 collective-permute-done.3.refs_1_
  23.4 3.0 %collective-permute-done.4.refs_2_ = f32[48,512]{1,0:T(8,128)S(1)} collective-permute-done((f32[48,512]{1,0:T(8,128)S(1)}, f32[48,512]{1,0:T(8,128)S(1)}, u32[]{:S(2)}, u32[]{:S(2)}) %collective-permute-start.4) | collective-permute-done | bytes 98336 | tf_op jit(solution)/shard_map/ppermute | solution.py:421
  26.4 0.0 collective-permute-done.5.refs_3_
  26.4 0.0 copy-done
  26.4 0.0 copy-done.3
  26.4 0.0 copy-done.4
  26.4 0.0 copy-done.8
  26.4 0.6 shard_map.137
  27.1 1.5 %collective-permute-start.8 = (f32[48,512]{1,0:T(8,128)S(1)}, f32[48,512]{1,0:T(8,128)S(1)}, u32[]{:S(2)}, u32[]{:S(2)}) collective-permute-start(f32[48,512]{1,0:T(8,128)S(1)} %get-tuple-element.32), channel_id=1, source_target_pairs={{0,24},{8,16},{16,8},{24,0},{1,25},{9,17},{17,9},{25,1},{2,26},{10... | collective-permute-start | bytes 294920 | tf_op jit(solution)/shard_map/ppermute | solution.py:421
  28.6 1.0 %collective-permute-start.7 = (f32[48,512]{1,0:T(8,128)S(1)}, f32[48,512]{1,0:T(8,128)S(1)}, u32[]{:S(2)}, u32[]{:S(2)}) collective-permute-start(f32[48,512]{1,0:T(8,128)S(1)} %get-tuple-element.31), channel_id=1, source_target_pairs={{0,16},{8,24},{16,0},{24,8},{1,17},{9,25},{17,1},{25,9},{2,18},{10... | collective-permute-start | bytes 294920 | tf_op jit(solution)/shard_map/ppermute | solution.py:421
  29.5 1.1 %collective-permute-start.6 = (f32[48,512]{1,0:T(8,128)S(1)}, f32[48,512]{1,0:T(8,128)S(1)}, u32[]{:S(2)}, u32[]{:S(2)}) collective-permute-start(f32[48,512]{1,0:T(8,128)S(1)} %get-tuple-element.30), channel_id=1, source_target_pairs={{0,8},{8,0},{16,24},{24,16},{1,9},{9,1},{17,25},{25,17},{2,10},{10... | collective-permute-start | bytes 294920 | tf_op jit(solution)/shard_map/ppermute | solution.py:421
  30.6 0.8 %shard_map.138.refs_0_ = f32[48,2048]{1,0:T(8,128)S(1)} custom-call(f32[48,512]{1,0:T(8,128)S(1)} %get-tuple-element.33.plane_ref, f32[56,512]{1,0:T(8,128)S(1)} %get-tuple-element.25.plane_ref.mark_ref), custom_call_target="tpu_custom_call" | custom-call | tf_op jit(solution)/shard_map/pallas_call | solution.py:126
  31.4 1.8 %collective-permute-done.8.plane_ref = f32[48,512]{1,0:T(8,128)S(1)} collective-permute-done((f32[48,512]{1,0:T(8,128)S(1)}, f32[48,512]{1,0:T(8,128)S(1)}, u32[]{:S(2)}, u32[]{:S(2)}) %collective-permute-start.8) | collective-permute-done | bytes 98336 | tf_op jit(solution)/shard_map/ppermute | solution.py:421
  33.2 0.8 %shard_map.139.refs_0_ = f32[48,2048]{1,0:T(8,128)S(1)} custom-call(f32[48,512]{1,0:T(8,128)S(1)} %collective-permute-done.8.plane_ref, f32[56,512]{1,0:T(8,128)S(1)} %collective-permute-done.2.plane_ref.mark_ref.refs_2_, f32[48,2048]{1,0:T(8,128)S(1)} %shard_map.138.refs_0_), custom_call_target="tpu_custom_call" | custom-call | tf_op jit(solution)/shard_map/pallas_call | solution.py:126
  34.0 0.0 collective-permute-done.7.plane_ref
  34.0 0.8 %shard_map.140.before_ref = f32[48,2048]{1,0:T(8,128)S(1)} custom-call(f32[48,512]{1,0:T(8,128)S(1)} %collective-permute-done.7.plane_ref, f32[56,512]{1,0:T(8,128)S(1)} %collective-permute-done.1.plane_ref.mark_ref.refs_1_, f32[48,2048]{1,0:T(8,128)S(1)} %shard_map.139.refs_0_), custom_call_target="tpu_custom_call" | custom-call | tf_op jit(solution)/shard_map/pallas_call | solution.py:126
  34.7 0.0 copy-start.7
  34.8 0.0 collective-permute-done.6.plane_ref
  34.8 5.8 %shard_map.141 = (f32[48,512]{1,0:T(8,128)S(1)}, f32[48,512]{1,0:T(8,128)S(1)}, f32[48,512]{1,0:T(8,128)S(1)}, bf16[96,2048]{1,0:T(8,128)(2,1)S(1)}) custom-call(f32[48,512]{1,0:T(8,128)S(1)} %collective-permute-done.6.plane_ref, f32[48,2048]{1,0:T(8,128)S(1)} %shard_map.140.before_ref, f32[56,512]{1,0:T(8,128)S(1)} %collective-permute-done.plane_ref.refs_0_, ...), custom_call_target="tpu_custom_call" | custom-call | tf_op jit(solution)/shard_map/pallas_call | solution.py:126
  40.6 0.9 %collective-permute-start.10 = (f32[48,512]{1,0:T(8,128)S(1)}, f32[48,512]{1,0:T(8,128)S(1)}, u32[]{:S(2)}, u32[]{:S(2)}) collective-permute-start(f32[48,512]{1,0:T(8,128)S(1)} %get-tuple-element.36), channel_id=1, source_target_pairs={{0,16},{8,24},{16,0},{24,8},{1,17},{9,25},{17,1},{25,9},{2,18},{10... | collective-permute-start | bytes 294920 | tf_op jit(solution)/shard_map/ppermute | solution.py:421
  41.5 1.3 %collective-permute-start.11 = (f32[48,512]{1,0:T(8,128)S(1)}, f32[48,512]{1,0:T(8,128)S(1)}, u32[]{:S(2)}, u32[]{:S(2)}) collective-permute-start(f32[48,512]{1,0:T(8,128)S(1)} %get-tuple-element.37), channel_id=1, source_target_pairs={{0,24},{8,16},{16,8},{24,0},{1,25},{9,17},{17,9},{25,1},{2,26},{10... | collective-permute-start | bytes 294920 | tf_op jit(solution)/shard_map/ppermute | solution.py:421
  42.8 1.3 %collective-permute-start.9 = (f32[48,512]{1,0:T(8,128)S(1)}, f32[48,512]{1,0:T(8,128)S(1)}, u32[]{:S(2)}, u32[]{:S(2)}) collective-permute-start(f32[48,512]{1,0:T(8,128)S(1)} %get-tuple-element.35), channel_id=1, source_target_pairs={{0,8},{8,0},{16,24},{24,16},{1,9},{9,1},{17,25},{25,17},{2,10},{10... | collective-permute-start | bytes 294920 | tf_op jit(solution)/shard_map/ppermute | solution.py:421
  44.1 0.5 shard_map.142.refs_0_
  44.6 0.7 collective-permute-done.10.refs_2_
  45.3 1.8 %collective-permute-done.11.refs_3_ = f32[48,512]{1,0:T(8,128)S(1)} collective-permute-done((f32[48,512]{1,0:T(8,128)S(1)}, f32[48,512]{1,0:T(8,128)S(1)}, u32[]{:S(2)}, u32[]{:S(2)}) %collective-permute-start.11) | collective-permute-done | bytes 98336 | tf_op jit(solution)/shard_map/ppermute | solution.py:421
  47.0 0.8 %collective-permute-done.9.refs_1_ = f32[48,512]{1,0:T(8,128)S(1)} collective-permute-done((f32[48,512]{1,0:T(8,128)S(1)}, f32[48,512]{1,0:T(8,128)S(1)}, u32[]{:S(2)}, u32[]{:S(2)}) %collective-permute-start.9) | collective-permute-done | bytes 98336 | tf_op jit(solution)/shard_map/ppermute | solution.py:421
  47.8 0.0 copy-done.7
  47.8 0.5 shard_map.143
  48.3 11.5 %all_to_all.10.parts_ref = bf16[8,16,512]{2,1,0:T(8,128)(2,1)S(1)} all-to-all(bf16[8,16,512]{2,1,0:T(8,128)(2,1)S(1)} %get-tuple-element.40), channel_id=1, replica_groups=mesh['grid'=4,'band'=8] {'band'}, dimensions={0} | all-to-all | bytes 262144 | tf_op jit(solution)/shard_map/all_to_all | solution.py:515
  59.8 1.0 %shard_map.144 = (f32[32,1,128]{2,1,0:T(1,128)}, f32[8,128]{1,0:T(8,128)}) custom-call(bf16[8,16,512]{2,1,0:T(8,128)(2,1)S(1)} %all_to_all.10.parts_ref), custom_call_target="tpu_custom_call" | custom-call | tf_op jit(solution)/shard_map/pallas_call | solution.py:126
  60.8 2.6 %all-to-all-start.1 = ((f32[32,1,128]{2,1,0:T(1,128)}), f32[32,1,128]{2,1,0:T(1,128)S(1)}, u32[]{:S(2)}, u32[]{:S(2)}) async-start(f32[32,1,128]{2,1,0:T(1,128)} %get-tuple-element.41), calls=%async_computation.1 | async-start | bytes 32768 | tf_op jit(solution)/shard_map/all_to_all | solution.py:522
  63.4 0.7 %copy.15 = f32[2,1,512,96]{2,3,1,0:T(8,128)} copy(f32[2,1,512,96]{2,3,1,0:T(8,128)S(1)} %bitcast.10) | data formatting | bytes 786432
  64.1 6.4 %all-to-all-done.1.parts_ref = f32[32,1,128]{2,1,0:T(1,128)S(1)} async-done(((f32[32,1,128]{2,1,0:T(1,128)}), f32[32,1,128]{2,1,0:T(1,128)S(1)}, u32[]{:S(2)}, u32[]{:S(2)}) %all-to-all-start.1) | async-done | bytes 16416 | tf_op jit(solution)/shard_map/all_to_all | solution.py:522
  70.5 0.7 %shard_map.145 = f32[2,1,2]{2,1,0:T(1,128)} custom-call(s32[1]{0:T(128)} %bitcast.me_ref, f32[32,1,128]{2,1,0:T(1,128)S(1)} %all-to-all-done.1.parts_ref), custom_call_target="tpu_custom_call" | custom-call | tf_op jit(solution)/shard_map/pallas_call | solution.py:126
Async XLA Ops:
  2.0 7.5 %collective-permute-start.2 = (f32[56,512]{1,0:T(8,128)S(1)}, f32[56,512]{1,0:T(8,128)S(1)}, u32[]{:S(2)}, u32[]{:S(2)}) collective-permute-start(f32[56,512]{1,0:T(8,128)S(1)} %get-tuple-element.24), channel_id=1, source_target_pairs={{0,24},{8,16},{16,8},{24,0},{1,25},{9,17},{17,9},{25,1},{2,26},{10... | collective-permute-start | bytes 344072 | tf_op jit(solution)/shard_map/ppermute | solution.py:421
  5.9 5.6 %collective-permute-start.1 = (f32[56,512]{1,0:T(8,128)S(1)}, f32[56,512]{1,0:T(8,128)S(1)}, u32[]{:S(2)}, u32[]{:S(2)}) collective-permute-start(f32[56,512]{1,0:T(8,128)S(1)} %get-tuple-element.23), channel_id=1, source_target_pairs={{0,16},{8,24},{16,0},{24,8},{1,17},{9,25},{17,1},{25,9},{2,18},{10... | collective-permute-start | bytes 344072 | tf_op jit(solution)/shard_map/ppermute | solution.py:421
  6.4 5.9 %collective-permute-start = (f32[56,512]{1,0:T(8,128)S(1)}, f32[56,512]{1,0:T(8,128)S(1)}, u32[]{:S(2)}, u32[]{:S(2)}) collective-permute-start(f32[56,512]{1,0:T(8,128)S(1)} %get-tuple-element.22), channel_id=1, source_target_pairs={{0,8},{8,0},{16,24},{24,16},{1,9},{9,1},{17,25},{25,17},{2,10},{10... | collective-permute-start | bytes 344072 | tf_op jit(solution)/shard_map/ppermute | solution.py:421
  9.2 3.2 %copy-start.1 = (bf16[384,256]{1,0:T(8,128)(2,1)S(1)}, bf16[384,256]{1,0:T(8,128)(2,1)}, u32[]{:S(2)}) copy-start(bf16[384,256]{1,0:T(8,128)(2,1)} %constant.25.clone.refs_4_) | copy-start | bytes 589828
  9.2 3.2 %copy-start.2 = (bf16[384,224]{1,0:T(8,128)(2,1)S(1)}, bf16[384,224]{1,0:T(8,128)(2,1)}, u32[]{:S(2)}) copy-start(bf16[384,224]{1,0:T(8,128)(2,1)} %constant.26.clone.refs_5_) | copy-start | bytes 516100
  9.2 3.2 %copy-start.5 = (bf16[256,256]{1,0:T(8,128)(2,1)S(1)}, bf16[256,256]{1,0:T(8,128)(2,1)}, u32[]{:S(2)}) copy-start(bf16[256,256]{1,0:T(8,128)(2,1)} %constant.28.clone.refs_7_) | copy-start | bytes 393220
  9.2 3.2 %copy-start.6 = (bf16[224,192]{1,0:T(8,128)(2,1)S(1)}, bf16[224,192]{1,0:T(8,128)(2,1)}, u32[]{:S(2)}) copy-start(bf16[224,192]{1,0:T(8,128)(2,1)} %constant.27.clone.refs_6_) | copy-start | bytes 258052
  12.3 14.1 %copy-start = (f32[2,1,512,96]{2,3,1,0:T(8,128)S(1)}, f32[2,1,512,96]{2,3,1,0:T(8,128)}, u32[]{:S(2)}) copy-start(f32[2,1,512,96]{2,3,1,0:T(8,128)} %param.12) | copy-start | bytes 1179652
  12.3 14.1 %copy-start.3 = (bf16[4,48,336]{2,1,0:T(8,128)(2,1)S(1)}, bf16[4,48,336]{2,1,0:T(8,128)(2,1)}, u32[]{:S(2)}) copy-start(bf16[4,48,336]{2,1,0:T(8,128)(2,1)} %constant.24.clone.refs_2_.refs_6_) | copy-start | bytes 387076
  12.3 14.1 %copy-start.4 = (bf16[112,576]{1,0:T(8,128)(2,1)S(1)}, bf16[112,576]{1,0:T(8,128)(2,1)}, u32[]{:S(2)}) copy-start(bf16[112,576]{1,0:T(8,128)(2,1)} %constant.29.clone.refs_7_) | copy-start | bytes 387076
  12.4 14.1 %copy-start.8 = (s32[512]{0:T(512)S(1)}, s32[512]{0:T(512)}, u32[]{:S(2)}) copy-start(s32[512]{0:T(512)} %param.13) | copy-start | bytes 6148
  18.1 5.3 %collective-permute-start.3 = (f32[48,512]{1,0:T(8,128)S(1)}, f32[48,512]{1,0:T(8,128)S(1)}, u32[]{:S(2)}, u32[]{:S(2)}) collective-permute-start(f32[48,512]{1,0:T(8,128)S(1)} %get-tuple-element.27), channel_id=1, source_target_pairs={{0,8},{8,0},{16,24},{24,16},{1,9},{9,1},{17,25},{25,17},{2,10},{10... | collective-permute-start | bytes 294920 | tf_op jit(solution)/shard_map/ppermute | solution.py:421
  19.8 6.6 %collective-permute-start.4 = (f32[48,512]{1,0:T(8,128)S(1)}, f32[48,512]{1,0:T(8,128)S(1)}, u32[]{:S(2)}, u32[]{:S(2)}) collective-permute-start(f32[48,512]{1,0:T(8,128)S(1)} %get-tuple-element.28), channel_id=1, source_target_pairs={{0,16},{8,24},{16,0},{24,8},{1,17},{9,25},{17,1},{25,9},{2,18},{10... | collective-permute-start | bytes 294920 | tf_op jit(solution)/shard_map/ppermute | solution.py:421
  20.8 5.6 %collective-permute-start.5 = (f32[48,512]{1,0:T(8,128)S(1)}, f32[48,512]{1,0:T(8,128)S(1)}, u32[]{:S(2)}, u32[]{:S(2)}) collective-permute-start(f32[48,512]{1,0:T(8,128)S(1)} %get-tuple-element.29), channel_id=1, source_target_pairs={{0,24},{8,16},{16,8},{24,0},{1,25},{9,17},{17,9},{25,1},{2,26},{10... | collective-permute-start | bytes 294920 | tf_op jit(solution)/shard_map/ppermute | solution.py:421
  27.1 6.1 %collective-permute-start.8 = (f32[48,512]{1,0:T(8,128)S(1)}, f32[48,512]{1,0:T(8,128)S(1)}, u32[]{:S(2)}, u32[]{:S(2)}) collective-permute-start(f32[48,512]{1,0:T(8,128)S(1)} %get-tuple-element.32), channel_id=1, source_target_pairs={{0,24},{8,16},{16,8},{24,0},{1,25},{9,17},{17,9},{25,1},{2,26},{10... | collective-permute-start | bytes 294920 | tf_op jit(solution)/shard_map/ppermute | solution.py:421
  28.6 5.4 %collective-permute-start.7 = (f32[48,512]{1,0:T(8,128)S(1)}, f32[48,512]{1,0:T(8,128)S(1)}, u32[]{:S(2)}, u32[]{:S(2)}) collective-permute-start(f32[48,512]{1,0:T(8,128)S(1)} %get-tuple-element.31), channel_id=1, source_target_pairs={{0,16},{8,24},{16,0},{24,8},{1,17},{9,25},{17,1},{25,9},{2,18},{10... | collective-permute-start | bytes 294920 | tf_op jit(solution)/shard_map/ppermute | solution.py:421
  29.5 5.2 %collective-permute-start.6 = (f32[48,512]{1,0:T(8,128)S(1)}, f32[48,512]{1,0:T(8,128)S(1)}, u32[]{:S(2)}, u32[]{:S(2)}) collective-permute-start(f32[48,512]{1,0:T(8,128)S(1)} %get-tuple-element.30), channel_id=1, source_target_pairs={{0,8},{8,0},{16,24},{24,16},{1,9},{9,1},{17,25},{25,17},{2,10},{10... | collective-permute-start | bytes 294920 | tf_op jit(solution)/shard_map/ppermute | solution.py:421
  34.7 13.1 %copy-start.7 = (bf16[2,128,56]{2,1,0:T(8,128)(2,1)S(1)}, bf16[2,128,56]{2,1,0:T(8,128)(2,1)}, u32[]{:S(2)}) copy-start(bf16[2,128,56]{2,1,0:T(8,128)(2,1)} %constant.30.clone.refs_8_) | copy-start | bytes 86020
  40.6 4.7 %collective-permute-start.10 = (f32[48,512]{1,0:T(8,128)S(1)}, f32[48,512]{1,0:T(8,128)S(1)}, u32[]{:S(2)}, u32[]{:S(2)}) collective-permute-start(f32[48,512]{1,0:T(8,128)S(1)} %get-tuple-element.36), channel_id=1, source_target_pairs={{0,16},{8,24},{16,0},{24,8},{1,17},{9,25},{17,1},{25,9},{2,18},{10... | collective-permute-start | bytes 294920 | tf_op jit(solution)/shard_map/ppermute | solution.py:421
  41.5 5.5 %collective-permute-start.11 = (f32[48,512]{1,0:T(8,128)S(1)}, f32[48,512]{1,0:T(8,128)S(1)}, u32[]{:S(2)}, u32[]{:S(2)}) collective-permute-start(f32[48,512]{1,0:T(8,128)S(1)} %get-tuple-element.37), channel_id=1, source_target_pairs={{0,24},{8,16},{16,8},{24,0},{1,25},{9,17},{17,9},{25,1},{2,26},{10... | collective-permute-start | bytes 294920 | tf_op jit(solution)/shard_map/ppermute | solution.py:421
  42.8 5.0 %collective-permute-start.9 = (f32[48,512]{1,0:T(8,128)S(1)}, f32[48,512]{1,0:T(8,128)S(1)}, u32[]{:S(2)}, u32[]{:S(2)}) collective-permute-start(f32[48,512]{1,0:T(8,128)S(1)} %get-tuple-element.35), channel_id=1, source_target_pairs={{0,8},{8,0},{16,24},{24,16},{1,9},{9,1},{17,25},{25,17},{2,10},{10... | collective-permute-start | bytes 294920 | tf_op jit(solution)/shard_map/ppermute | solution.py:421
  60.8 9.7 %all-to-all-start.1 = ((f32[32,1,128]{2,1,0:T(1,128)}), f32[32,1,128]{2,1,0:T(1,128)S(1)}, u32[]{:S(2)}, u32[]{:S(2)}) async-start(f32[32,1,128]{2,1,0:T(1,128)} %get-tuple-element.41), calls=%async_computation.1 | async-start | bytes 32768 | tf_op jit(solution)/shard_map/all_to_all | solution.py:522

commit v13 on v11

--- a/solution.py
+++ b/solution.py
@@ -417,9 +417,11 @@
         return at ^ k
 
     def exchange(values):
-        return [values[0]] + [
-            lax.ppermute(values[k], "grid", [(d, step(d, k)) for d in range(devices)]) for k in range(1, devices)
+        moved = [
+            lax.ppermute(values[k], "grid", [(d, step(d, k)) for d in range(devices)])
+            for k in range(devices - 1, 0, -1)
         ]
+        return [values[0]] + moved[::-1]
 
     ahead, back = z_tables(size, devices, pad)
     tables = plane_tables(size)

time: 71.5 us -> 71.5 us (level)
  no operation moved by 1% of the time
where the time goes in v13:
time: 71.5 us; the launch traced here: 71.2 us
  Pallas kernels  21.2 us (30%)
  starting transfers between devices  17.8 us (25%)
  waiting for transfers between devices  15.9 us (22%)
  blocking collectives  11.5 us (16%)
  between operations  2.24 us (3%)
  local copies, waits for them, and re-layouts  1.36 us (2%)
  other arithmetic  1.24 us (2%)
    pallas_call x15, Pallas kernels, call(): pl.pallas_call(kernel, out_shape=out_shape, in_specs=[SMEM] * len(scalars...  21.2 us
    ppermute x12, starting transfers between devices, exchange(): lax.ppermute(values[k], 'grid', [(d, step(d, k)) for d in range(devices)])  15.3 us
    all_to_all x1, blocking collectives, body(): lax.all_to_all(packed, 'band', 0, 0, tiled=True)  11.5 us
    ppermute x12, waiting for transfers between devices, exchange(): lax.ppermute(values[k], 'grid', [(d, step(d, k)) for d in range(devices)])  9.54 us
    all_to_all x1, waiting for transfers between devices, body(): lax.all_to_all(partial_sum, ('grid', 'band'), 0, 0, tiled=True)  6.39 us
    all_to_all x1, starting transfers between devices, body(): lax.all_to_all(partial_sum, ('grid', 'band'), 0, 0, tiled=True)  2.57 us
  transfers between devices with their start and end apart: 13, of which 8 were waited for; matrix products, arithmetic and copies ran while one was open for 4% of the time, Pallas kernels for 8%

profile of v13, /device:TPU:0, one launch (start us, length us, event | category | flops | bytes accessed | tf_op | source)
XLA Modules:
  0.0 71.2 jit_solution(4436477332671157281)
XLA Ops:
  0.6 1.3 %shard_map.131 = (f32[56,512]{1,0:T(8,128)S(1)}, f32[56,512]{1,0:T(8,128)S(1)}, f32[56,512]{1,0:T(8,128)S(1)}, f32[56,512]{1,0:T(8,128)S(1)}) custom-call(s32[1]{0:T(128)} %bitcast.me_ref, f32[2,96,512]{2,1,0:T(8,128)} %bitcast.11, s32[1,512]{1,0:T(1,128)} %bitcast.14, bf16[4,48,336]{2,1,0:T(8,128)(2,1)} %constant.24.clone.refs_2_.refs_6_), custom_call_target="tpu_custom_call" | custom-call | tf_op jit(solution)/shard_map/pallas_call | solution.py:126
  2.0 4.0 %collective-permute-start.2 = (f32[56,512]{1,0:T(8,128)S(1)}, f32[56,512]{1,0:T(8,128)S(1)}, u32[]{:S(2)}, u32[]{:S(2)}) collective-permute-start(f32[56,512]{1,0:T(8,128)S(1)} %get-tuple-element.24), channel_id=1, source_target_pairs={{0,24},{8,16},{16,8},{24,0},{1,25},{9,17},{17,9},{25,1},{2,26},{10... | collective-permute-start | bytes 344072 | tf_op jit(solution)/shard_map/ppermute | solution.py:421
  5.9 0.5 collective-permute-start.1
  6.4 0.1 collective-permute-start
  6.6 1.2 %broadcast_multiply_fusion = f32[24,9216]{1,0:T(8,128)S(1)} fusion(f32[24,9216]{1,0:T(8,128)} %param.14), kind=kLoop, calls=%fused_computation | loop fusion | flops 221184 | bytes 1769472 | tf_op jit(solution)/shard_map/mul | solution.py:436
  7.8 0.8 %shard_map.132.refs_0_ = f32[48,2048]{1,0:T(8,128)S(1)} custom-call(f32[56,512]{1,0:T(8,128)S(1)} %get-tuple-element.25.plane_ref.mark_ref, f32[56,512]{1,0:T(8,128)S(1)} %get-tuple-element.25.plane_ref.mark_ref), custom_call_target="tpu_custom_call" | custom-call | tf_op jit(solution)/shard_map/pallas_call | solution.py:126
  8.6 0.5 reshape.22
  9.1 0.1 pad.4.refs_3_
  9.2 0.0 copy-start.1
  9.2 0.0 copy-start.2
  9.2 0.0 copy-start.5
  9.2 0.0 copy-start.6
  9.2 0.3 collective-permute-done.2.plane_ref.mark_ref.refs_0_
  9.5 0.8 %shard_map.133.refs_0_ = f32[48,2048]{1,0:T(8,128)S(1)} custom-call(f32[56,512]{1,0:T(8,128)S(1)} %collective-permute-done.2.plane_ref.mark_ref.refs_0_, f32[56,512]{1,0:T(8,128)S(1)} %collective-permute-done.2.plane_ref.mark_ref.refs_0_, f32[48,2048]{1,0:T(8,128)S(1)} %shard_map.132.refs_0_), custom_call_target="tpu_custom_call" | custom-call | tf_op jit(solution)/shard_map/pallas_call | solution.py:126
  10.3 1.3 %collective-permute-done.1.plane_ref.mark_ref.refs_1_ = f32[56,512]{1,0:T(8,128)S(1)} collective-permute-done((f32[56,512]{1,0:T(8,128)S(1)}, f32[56,512]{1,0:T(8,128)S(1)}, u32[]{:S(2)}, u32[]{:S(2)}) %collective-permute-start.1) | collective-permute-done | bytes 114720 | tf_op jit(solution)/shard_map/ppermute | solution.py:421
  11.5 0.8 %shard_map.134.before_ref = f32[48,2048]{1,0:T(8,128)S(1)} custom-call(f32[56,512]{1,0:T(8,128)S(1)} %collective-permute-done.1.plane_ref.mark_ref.refs_1_, f32[56,512]{1,0:T(8,128)S(1)} %collective-permute-done.1.plane_ref.mark_ref.refs_1_, f32[48,2048]{1,0:T(8,128)S(1)} %shard_map.133.refs_0_), custom_call_target="tpu_custom_call" | custom-call | tf_op jit(solution)/shard_map/pallas_call | solution.py:126
  12.3 0.0 copy-start
  12.3 0.0 copy-start.3
  12.3 0.0 copy-start.4
  12.4 0.0 copy-start.8
  12.4 0.0 collective-permute-done.plane_ref.refs_2_
  12.4 0.0 copy-done.1
  12.4 0.0 copy-done.2
  12.4 0.0 copy-done.5
  12.4 0.0 copy-done.6
  12.4 5.6 %shard_map.135 = (f32[48,512]{1,0:T(8,128)S(1)}, f32[48,512]{1,0:T(8,128)S(1)}, f32[48,512]{1,0:T(8,128)S(1)}, bf16[96,2048]{1,0:T(8,128)(2,1)S(1)}) custom-call(f32[56,512]{1,0:T(8,128)S(1)} %collective-permute-done.plane_ref.refs_2_, f32[48,2048]{1,0:T(8,128)S(1)} %shard_map.134.before_ref, ...), custom_call_target="tpu_custom_call" | custom-call | tf_op jit(solution)/shard_map/pallas_call | solution.py:126
  18.1 1.7 %collective-permute-start.3 = (f32[48,512]{1,0:T(8,128)S(1)}, f32[48,512]{1,0:T(8,128)S(1)}, u32[]{:S(2)}, u32[]{:S(2)}) collective-permute-start(f32[48,512]{1,0:T(8,128)S(1)} %get-tuple-element.27), channel_id=1, source_target_pairs={{0,8},{8,0},{16,24},{24,16},{1,9},{9,1},{17,25},{25,17},{2,10},{10... | collective-permute-start | bytes 294920 | tf_op jit(solution)/shard_map/ppermute | solution.py:421
  19.8 1.0 %collective-permute-start.4 = (f32[48,512]{1,0:T(8,128)S(1)}, f32[48,512]{1,0:T(8,128)S(1)}, u32[]{:S(2)}, u32[]{:S(2)}) collective-permute-start(f32[48,512]{1,0:T(8,128)S(1)} %get-tuple-element.28), channel_id=1, source_target_pairs={{0,16},{8,24},{16,0},{24,8},{1,17},{9,25},{17,1},{25,9},{2,18},{10... | collective-permute-start | bytes 294920 | tf_op jit(solution)/shard_map/ppermute | solution.py:421
  20.8 0.8 %collective-permute-start.5 = (f32[48,512]{1,0:T(8,128)S(1)}, f32[48,512]{1,0:T(8,128)S(1)}, u32[]{:S(2)}, u32[]{:S(2)}) collective-permute-start(f32[48,512]{1,0:T(8,128)S(1)} %get-tuple-element.29), channel_id=1, source_target_pairs={{0,24},{8,16},{16,8},{24,0},{1,25},{9,17},{17,9},{25,1},{2,26},{10... | collective-permute-start | bytes 294920 | tf_op jit(solution)/shard_map/ppermute | solution.py:421
  22.9 0.5 shard_map.136.refs_0_
  23.4 0.0 collective-permute-done.3.refs_1_
  23.4 3.0 %collective-permute-done.4.refs_2_ = f32[48,512]{1,0:T(8,128)S(1)} collective-permute-done((f32[48,512]{1,0:T(8,128)S(1)}, f32[48,512]{1,0:T(8,128)S(1)}, u32[]{:S(2)}, u32[]{:S(2)}) %collective-permute-start.4) | collective-permute-done | bytes 98336 | tf_op jit(solution)/shard_map/ppermute | solution.py:421
  26.4 0.0 collective-permute-done.5.refs_3_
  26.4 0.0 copy-done
  26.4 0.0 copy-done.3
  26.4 0.0 copy-done.4
  26.4 0.0 copy-done.8
  26.4 0.6 shard_map.137
  27.1 1.5 %collective-permute-start.8 = (f32[48,512]{1,0:T(8,128)S(1)}, f32[48,512]{1,0:T(8,128)S(1)}, u32[]{:S(2)}, u32[]{:S(2)}) collective-permute-start(f32[48,512]{1,0:T(8,128)S(1)} %get-tuple-element.32), channel_id=1, source_target_pairs={{0,24},{8,16},{16,8},{24,0},{1,25},{9,17},{17,9},{25,1},{2,26},{10... | collective-permute-start | bytes 294920 | tf_op jit(solution)/shard_map/ppermute | solution.py:421
  28.6 1.0 %collective-permute-start.7 = (f32[48,512]{1,0:T(8,128)S(1)}, f32[48,512]{1,0:T(8,128)S(1)}, u32[]{:S(2)}, u32[]{:S(2)}) collective-permute-start(f32[48,512]{1,0:T(8,128)S(1)} %get-tuple-element.31), channel_id=1, source_target_pairs={{0,16},{8,24},{16,0},{24,8},{1,17},{9,25},{17,1},{25,9},{2,18},{10... | collective-permute-start | bytes 294920 | tf_op jit(solution)/shard_map/ppermute | solution.py:421
  29.5 1.1 %collective-permute-start.6 = (f32[48,512]{1,0:T(8,128)S(1)}, f32[48,512]{1,0:T(8,128)S(1)}, u32[]{:S(2)}, u32[]{:S(2)}) collective-permute-start(f32[48,512]{1,0:T(8,128)S(1)} %get-tuple-element.30), channel_id=1, source_target_pairs={{0,8},{8,0},{16,24},{24,16},{1,9},{9,1},{17,25},{25,17},{2,10},{10... | collective-permute-start | bytes 294920 | tf_op jit(solution)/shard_map/ppermute | solution.py:421
  30.6 0.8 %shard_map.138.refs_0_ = f32[48,2048]{1,0:T(8,128)S(1)} custom-call(f32[48,512]{1,0:T(8,128)S(1)} %get-tuple-element.33.plane_ref, f32[56,512]{1,0:T(8,128)S(1)} %get-tuple-element.25.plane_ref.mark_ref), custom_call_target="tpu_custom_call" | custom-call | tf_op jit(solution)/shard_map/pallas_call | solution.py:126
  31.4 1.8 %collective-permute-done.8.plane_ref = f32[48,512]{1,0:T(8,128)S(1)} collective-permute-done((f32[48,512]{1,0:T(8,128)S(1)}, f32[48,512]{1,0:T(8,128)S(1)}, u32[]{:S(2)}, u32[]{:S(2)}) %collective-permute-start.8) | collective-permute-done | bytes 98336 | tf_op jit(solution)/shard_map/ppermute | solution.py:421
  33.2 0.8 %shard_map.139.refs_0_ = f32[48,2048]{1,0:T(8,128)S(1)} custom-call(f32[48,512]{1,0:T(8,128)S(1)} %collective-permute-done.8.plane_ref, f32[56,512]{1,0:T(8,128)S(1)} %collective-permute-done.2.plane_ref.mark_ref.refs_0_, f32[48,2048]{1,0:T(8,128)S(1)} %shard_map.138.refs_0_), custom_call_target="tpu_custom_call" | custom-call | tf_op jit(solution)/shard_map/pallas_call | solution.py:126
  34.0 0.0 collective-permute-done.7.plane_ref
  34.0 0.8 %shard_map.140.before_ref = f32[48,2048]{1,0:T(8,128)S(1)} custom-call(f32[48,512]{1,0:T(8,128)S(1)} %collective-permute-done.7.plane_ref, f32[56,512]{1,0:T(8,128)S(1)} %collective-permute-done.1.plane_ref.mark_ref.refs_1_, f32[48,2048]{1,0:T(8,128)S(1)} %shard_map.139.refs_0_), custom_call_target="tpu_custom_call" | custom-call | tf_op jit(solution)/shard_map/pallas_call | solution.py:126
  34.7 0.0 copy-start.7
  34.8 0.0 collective-permute-done.6.plane_ref
  34.8 5.8 %shard_map.141 = (f32[48,512]{1,0:T(8,128)S(1)}, f32[48,512]{1,0:T(8,128)S(1)}, f32[48,512]{1,0:T(8,128)S(1)}, bf16[96,2048]{1,0:T(8,128)(2,1)S(1)}) custom-call(f32[48,512]{1,0:T(8,128)S(1)} %collective-permute-done.6.plane_ref, f32[48,2048]{1,0:T(8,128)S(1)} %shard_map.140.before_ref, f32[56,512]{1,0:T(8,128)S(1)} %collective-permute-done.2.plane_ref.mark_ref.refs_0_, ...), custom_call_target="tpu_custom_call" | custom-call | tf_op jit(solution)/shard_map/pallas_call | solution.py:126
  40.6 0.9 %collective-permute-start.10 = (f32[48,512]{1,0:T(8,128)S(1)}, f32[48,512]{1,0:T(8,128)S(1)}, u32[]{:S(2)}, u32[]{:S(2)}) collective-permute-start(f32[48,512]{1,0:T(8,128)S(1)} %get-tuple-element.36), channel_id=1, source_target_pairs={{0,16},{8,24},{16,0},{24,8},{1,17},{9,25},{17,1},{25,9},{2,18},{10... | collective-permute-start | bytes 294920 | tf_op jit(solution)/shard_map/ppermute | solution.py:421
  41.5 1.3 %collective-permute-start.11 = (f32[48,512]{1,0:T(8,128)S(1)}, f32[48,512]{1,0:T(8,128)S(1)}, u32[]{:S(2)}, u32[]{:S(2)}) collective-permute-start(f32[48,512]{1,0:T(8,128)S(1)} %get-tuple-element.37), channel_id=1, source_target_pairs={{0,24},{8,16},{16,8},{24,0},{1,25},{9,17},{17,9},{25,1},{2,26},{10... | collective-permute-start | bytes 294920 | tf_op jit(solution)/shard_map/ppermute | solution.py:421
  42.8 1.4 %collective-permute-start.9 = (f32[48,512]{1,0:T(8,128)S(1)}, f32[48,512]{1,0:T(8,128)S(1)}, u32[]{:S(2)}, u32[]{:S(2)}) collective-permute-start(f32[48,512]{1,0:T(8,128)S(1)} %get-tuple-element.35), channel_id=1, source_target_pairs={{0,8},{8,0},{16,24},{24,16},{1,9},{9,1},{17,25},{25,17},{2,10},{10... | collective-permute-start | bytes 294920 | tf_op jit(solution)/shard_map/ppermute | solution.py:421
  44.2 0.5 shard_map.142.refs_0_
  44.6 0.7 collective-permute-done.10.refs_2_
  45.3 1.7 %collective-permute-done.11.refs_3_ = f32[48,512]{1,0:T(8,128)S(1)} collective-permute-done((f32[48,512]{1,0:T(8,128)S(1)}, f32[48,512]{1,0:T(8,128)S(1)}, u32[]{:S(2)}, u32[]{:S(2)}) %collective-permute-start.11) | collective-permute-done | bytes 98336 | tf_op jit(solution)/shard_map/ppermute | solution.py:421
  47.0 0.8 %collective-permute-done.9.refs_1_ = f32[48,512]{1,0:T(8,128)S(1)} collective-permute-done((f32[48,512]{1,0:T(8,128)S(1)}, f32[48,512]{1,0:T(8,128)S(1)}, u32[]{:S(2)}, u32[]{:S(2)}) %collective-permute-start.9) | collective-permute-done | bytes 98336 | tf_op jit(solution)/shard_map/ppermute | solution.py:421
  47.8 0.0 copy-done.7
  47.8 0.5 shard_map.143
  48.3 11.5 %all_to_all.10.parts_ref = bf16[8,16,512]{2,1,0:T(8,128)(2,1)S(1)} all-to-all(bf16[8,16,512]{2,1,0:T(8,128)(2,1)S(1)} %get-tuple-element.40), channel_id=1, replica_groups=mesh['grid'=4,'band'=8] {'band'}, dimensions={0} | all-to-all | bytes 262144 | tf_op jit(solution)/shard_map/all_to_all | solution.py:517
  59.8 1.0 %shard_map.144 = (f32[32,1,128]{2,1,0:T(1,128)}, f32[8,128]{1,0:T(8,128)}) custom-call(bf16[8,16,512]{2,1,0:T(8,128)(2,1)S(1)} %all_to_all.10.parts_ref), custom_call_target="tpu_custom_call" | custom-call | tf_op jit(solution)/shard_map/pallas_call | solution.py:126
  60.8 2.6 %all-to-all-start.1 = ((f32[32,1,128]{2,1,0:T(1,128)}), f32[32,1,128]{2,1,0:T(1,128)S(1)}, u32[]{:S(2)}, u32[]{:S(2)}) async-start(f32[32,1,128]{2,1,0:T(1,128)} %get-tuple-element.41), calls=%async_computation.1 | async-start | bytes 32768 | tf_op jit(solution)/shard_map/all_to_all | solution.py:524
  63.4 0.7 %copy.15 = f32[2,1,512,96]{2,3,1,0:T(8,128)} copy(f32[2,1,512,96]{2,3,1,0:T(8,128)S(1)} %bitcast.10) | data formatting | bytes 786432
  64.1 6.4 %all-to-all-done.1.parts_ref = f32[32,1,128]{2,1,0:T(1,128)S(1)} async-done(((f32[32,1,128]{2,1,0:T(1,128)}), f32[32,1,128]{2,1,0:T(1,128)S(1)}, u32[]{:S(2)}, u32[]{:S(2)}) %all-to-all-start.1) | async-done | bytes 16416 | tf_op jit(solution)/shard_map/all_to_all | solution.py:524
  70.5 0.7 %shard_map.145 = f32[2,1,2]{2,1,0:T(1,128)} custom-call(s32[1]{0:T(128)} %bitcast.me_ref, f32[32,1,128]{2,1,0:T(1,128)S(1)} %all-to-all-done.1.parts_ref), custom_call_target="tpu_custom_call" | custom-call | tf_op jit(solution)/shard_map/pallas_call | solution.py:126
Async XLA Ops:
  2.0 7.5 %collective-permute-start.2 = (f32[56,512]{1,0:T(8,128)S(1)}, f32[56,512]{1,0:T(8,128)S(1)}, u32[]{:S(2)}, u32[]{:S(2)}) collective-permute-start(f32[56,512]{1,0:T(8,128)S(1)} %get-tuple-element.24), channel_id=1, source_target_pairs={{0,24},{8,16},{16,8},{24,0},{1,25},{9,17},{17,9},{25,1},{2,26},{10... | collective-permute-start | bytes 344072 | tf_op jit(solution)/shard_map/ppermute | solution.py:421
  5.9 5.6 %collective-permute-start.1 = (f32[56,512]{1,0:T(8,128)S(1)}, f32[56,512]{1,0:T(8,128)S(1)}, u32[]{:S(2)}, u32[]{:S(2)}) collective-permute-start(f32[56,512]{1,0:T(8,128)S(1)} %get-tuple-element.23), channel_id=1, source_target_pairs={{0,16},{8,24},{16,0},{24,8},{1,17},{9,25},{17,1},{25,9},{2,18},{10... | collective-permute-start | bytes 344072 | tf_op jit(solution)/shard_map/ppermute | solution.py:421
  6.4 5.9 %collective-permute-start = (f32[56,512]{1,0:T(8,128)S(1)}, f32[56,512]{1,0:T(8,128)S(1)}, u32[]{:S(2)}, u32[]{:S(2)}) collective-permute-start(f32[56,512]{1,0:T(8,128)S(1)} %get-tuple-element.22), channel_id=1, source_target_pairs={{0,8},{8,0},{16,24},{24,16},{1,9},{9,1},{17,25},{25,17},{2,10},{10... | collective-permute-start | bytes 344072 | tf_op jit(solution)/shard_map/ppermute | solution.py:421
  9.2 3.2 %copy-start.1 = (bf16[384,256]{1,0:T(8,128)(2,1)S(1)}, bf16[384,256]{1,0:T(8,128)(2,1)}, u32[]{:S(2)}) copy-start(bf16[384,256]{1,0:T(8,128)(2,1)} %constant.25.clone.refs_4_) | copy-start | bytes 589828
  9.2 3.2 %copy-start.2 = (bf16[384,224]{1,0:T(8,128)(2,1)S(1)}, bf16[384,224]{1,0:T(8,128)(2,1)}, u32[]{:S(2)}) copy-start(bf16[384,224]{1,0:T(8,128)(2,1)} %constant.26.clone.refs_5_) | copy-start | bytes 516100
  9.2 3.2 %copy-start.5 = (bf16[256,256]{1,0:T(8,128)(2,1)S(1)}, bf16[256,256]{1,0:T(8,128)(2,1)}, u32[]{:S(2)}) copy-start(bf16[256,256]{1,0:T(8,128)(2,1)} %constant.28.clone.refs_7_) | copy-start | bytes 393220
  9.2 3.2 %copy-start.6 = (bf16[224,192]{1,0:T(8,128)(2,1)S(1)}, bf16[224,192]{1,0:T(8,128)(2,1)}, u32[]{:S(2)}) copy-start(bf16[224,192]{1,0:T(8,128)(2,1)} %constant.27.clone.refs_6_) | copy-start | bytes 258052
  12.3 14.1 %copy-start = (f32[2,1,512,96]{2,3,1,0:T(8,128)S(1)}, f32[2,1,512,96]{2,3,1,0:T(8,128)}, u32[]{:S(2)}) copy-start(f32[2,1,512,96]{2,3,1,0:T(8,128)} %param.12) | copy-start | bytes 1179652
  12.3 14.1 %copy-start.3 = (bf16[4,48,336]{2,1,0:T(8,128)(2,1)S(1)}, bf16[4,48,336]{2,1,0:T(8,128)(2,1)}, u32[]{:S(2)}) copy-start(bf16[4,48,336]{2,1,0:T(8,128)(2,1)} %constant.24.clone.refs_2_.refs_6_) | copy-start | bytes 387076
  12.3 14.1 %copy-start.4 = (bf16[112,576]{1,0:T(8,128)(2,1)S(1)}, bf16[112,576]{1,0:T(8,128)(2,1)}, u32[]{:S(2)}) copy-start(bf16[112,576]{1,0:T(8,128)(2,1)} %constant.29.clone.refs_7_) | copy-start | bytes 387076
  12.4 14.1 %copy-start.8 = (s32[512]{0:T(512)S(1)}, s32[512]{0:T(512)}, u32[]{:S(2)}) copy-start(s32[512]{0:T(512)} %param.13) | copy-start | bytes 6148
  18.1 5.3 %collective-permute-start.3 = (f32[48,512]{1,0:T(8,128)S(1)}, f32[48,512]{1,0:T(8,128)S(1)}, u32[]{:S(2)}, u32[]{:S(2)}) collective-permute-start(f32[48,512]{1,0:T(8,128)S(1)} %get-tuple-element.27), channel_id=1, source_target_pairs={{0,8},{8,0},{16,24},{24,16},{1,9},{9,1},{17,25},{25,17},{2,10},{10... | collective-permute-start | bytes 294920 | tf_op jit(solution)/shard_map/ppermute | solution.py:421
  19.8 6.6 %collective-permute-start.4 = (f32[48,512]{1,0:T(8,128)S(1)}, f32[48,512]{1,0:T(8,128)S(1)}, u32[]{:S(2)}, u32[]{:S(2)}) collective-permute-start(f32[48,512]{1,0:T(8,128)S(1)} %get-tuple-element.28), channel_id=1, source_target_pairs={{0,16},{8,24},{16,0},{24,8},{1,17},{9,25},{17,1},{25,9},{2,18},{10... | collective-permute-start | bytes 294920 | tf_op jit(solution)/shard_map/ppermute | solution.py:421
  20.8 5.6 %collective-permute-start.5 = (f32[48,512]{1,0:T(8,128)S(1)}, f32[48,512]{1,0:T(8,128)S(1)}, u32[]{:S(2)}, u32[]{:S(2)}) collective-permute-start(f32[48,512]{1,0:T(8,128)S(1)} %get-tuple-element.29), channel_id=1, source_target_pairs={{0,24},{8,16},{16,8},{24,0},{1,25},{9,17},{17,9},{25,1},{2,26},{10... | collective-permute-start | bytes 294920 | tf_op jit(solution)/shard_map/ppermute | solution.py:421
  27.1 6.1 %collective-permute-start.8 = (f32[48,512]{1,0:T(8,128)S(1)}, f32[48,512]{1,0:T(8,128)S(1)}, u32[]{:S(2)}, u32[]{:S(2)}) collective-permute-start(f32[48,512]{1,0:T(8,128)S(1)} %get-tuple-element.32), channel_id=1, source_target_pairs={{0,24},{8,16},{16,8},{24,0},{1,25},{9,17},{17,9},{25,1},{2,26},{10... | collective-permute-start | bytes 294920 | tf_op jit(solution)/shard_map/ppermute | solution.py:421
  28.6 5.4 %collective-permute-start.7 = (f32[48,512]{1,0:T(8,128)S(1)}, f32[48,512]{1,0:T(8,128)S(1)}, u32[]{:S(2)}, u32[]{:S(2)}) collective-permute-start(f32[48,512]{1,0:T(8,128)S(1)} %get-tuple-element.31), channel_id=1, source_target_pairs={{0,16},{8,24},{16,0},{24,8},{1,17},{9,25},{17,1},{25,9},{2,18},{10... | collective-permute-start | bytes 294920 | tf_op jit(solution)/shard_map/ppermute | solution.py:421
  29.5 5.2 %collective-permute-start.6 = (f32[48,512]{1,0:T(8,128)S(1)}, f32[48,512]{1,0:T(8,128)S(1)}, u32[]{:S(2)}, u32[]{:S(2)}) collective-permute-start(f32[48,512]{1,0:T(8,128)S(1)} %get-tuple-element.30), channel_id=1, source_target_pairs={{0,8},{8,0},{16,24},{24,16},{1,9},{9,1},{17,25},{25,17},{2,10},{10... | collective-permute-start | bytes 294920 | tf_op jit(solution)/shard_map/ppermute | solution.py:421
  34.7 13.1 %copy-start.7 = (bf16[2,128,56]{2,1,0:T(8,128)(2,1)S(1)}, bf16[2,128,56]{2,1,0:T(8,128)(2,1)}, u32[]{:S(2)}) copy-start(bf16[2,128,56]{2,1,0:T(8,128)(2,1)} %constant.30.clone.refs_8_) | copy-start | bytes 86020
  40.6 4.7 %collective-permute-start.10 = (f32[48,512]{1,0:T(8,128)S(1)}, f32[48,512]{1,0:T(8,128)S(1)}, u32[]{:S(2)}, u32[]{:S(2)}) collective-permute-start(f32[48,512]{1,0:T(8,128)S(1)} %get-tuple-element.36), channel_id=1, source_target_pairs={{0,16},{8,24},{16,0},{24,8},{1,17},{9,25},{17,1},{25,9},{2,18},{10... | collective-permute-start | bytes 294920 | tf_op jit(solution)/shard_map/ppermute | solution.py:421
  41.5 5.5 %collective-permute-start.11 = (f32[48,512]{1,0:T(8,128)S(1)}, f32[48,512]{1,0:T(8,128)S(1)}, u32[]{:S(2)}, u32[]{:S(2)}) collective-permute-start(f32[48,512]{1,0:T(8,128)S(1)} %get-tuple-element.37), channel_id=1, source_target_pairs={{0,24},{8,16},{16,8},{24,0},{1,25},{9,17},{17,9},{25,1},{2,26},{10... | collective-permute-start | bytes 294920 | tf_op jit(solution)/shard_map/ppermute | solution.py:421
  42.8 5.0 %collective-permute-start.9 = (f32[48,512]{1,0:T(8,128)S(1)}, f32[48,512]{1,0:T(8,128)S(1)}, u32[]{:S(2)}, u32[]{:S(2)}) collective-permute-start(f32[48,512]{1,0:T(8,128)S(1)} %get-tuple-element.35), channel_id=1, source_target_pairs={{0,8},{8,0},{16,24},{24,16},{1,9},{9,1},{17,25},{25,17},{2,10},{10... | collective-permute-start | bytes 294920 | tf_op jit(solution)/shard_map/ppermute | solution.py:421
  60.8 9.7 %all-to-all-start.1 = ((f32[32,1,128]{2,1,0:T(1,128)}), f32[32,1,128]{2,1,0:T(1,128)S(1)}, u32[]{:S(2)}, u32[]{:S(2)}) async-start(f32[32,1,128]{2,1,0:T(1,128)} %get-tuple-element.41), calls=%async_computation.1 | async-start | bytes 32768 | tf_op jit(solution)/shard_map/all_to_all | solution.py:524

commit v14 on v11

--- a/solution.py
+++ b/solution.py
@@ -416,10 +416,10 @@
     def step(at, k):
         return at ^ k
 
-    def exchange(values):
-        return [values[0]] + [
-            lax.ppermute(values[k], "grid", [(d, step(d, k)) for d in range(devices)]) for k in range(1, devices)
-        ]
+    def exchange(values, late=0):
+        order = list(range(1, late + 1)) + list(range(devices - 1, late, -1))
+        moved = {k: lax.ppermute(values[k], "grid", [(d, step(d, k)) for d in range(devices)]) for k in order}
+        return [values[0]] + [moved[k] for k in range(1, devices)]
 
     ahead, back = z_tables(size, devices, pad)
     tables = plane_tables(size)
@@ -499,7 +499,7 @@
         [(value, True) for value in planes] + [(psi_t, False), (col_row, False), (ahead, False), (back, False)],
         [held],
     )
-    planes = exchange(slab(exchange(sent)))
+    planes = exchange(slab(exchange(sent)), late=1)
     filtered, packed = call(
         functools.partial(last_kernel, devices, bands, step, size),
         [vmem((2, size, cols)), vmem((bands, 2 * slots, cols), BF16)],

time: 71.5 us -> 71.5 us (level)
  no operation moved by 1% of the time
where the time goes in v14:
time: 71.5 us; the launch traced here: 71.2 us
  Pallas kernels  21.2 us (30%)
  starting transfers between devices  17.8 us (25%)
  waiting for transfers between devices  15.9 us (22%)
  blocking collectives  11.5 us (16%)
  between operations  2.24 us (3%)
  local copies, waits for them, and re-layouts  1.36 us (2%)
  other arithmetic  1.24 us (2%)
    pallas_call x15, Pallas kernels, call(): pl.pallas_call(kernel, out_shape=out_shape, in_specs=[SMEM] * len(scalars...  21.2 us
    ppermute x12, starting transfers between devices, exchange(): lax.ppermute(values[k], 'grid', [(d, step(d, k)) for d in range(devices)])  15.3 us
    all_to_all x1, blocking collectives, body(): lax.all_to_all(packed, 'band', 0, 0, tiled=True)  11.5 us
    ppermute x12, waiting for transfers between devices, exchange(): lax.ppermute(values[k], 'grid', [(d, step(d, k)) for d in range(devices)])  9.54 us
    all_to_all x1, waiting for transfers between devices, body(): lax.all_to_all(partial_sum, ('grid', 'band'), 0, 0, tiled=True)  6.39 us
    all_to_all x1, starting transfers between devices, body(): lax.all_to_all(partial_sum, ('grid', 'band'), 0, 0, tiled=True)  2.57 us
  transfers between devices with their start and end apart: 13, of which 8 were waited for; matrix products, arithmetic and copies ran while one was open for 4% of the time, Pallas kernels for 8%

profile of v14, /device:TPU:0, one launch (start us, length us, event | category | flops | bytes accessed | tf_op | source)
XLA Modules:
  0.0 71.2 jit_solution(4436477332671157281)
XLA Ops:
  0.6 1.3 %shard_map.131 = (f32[56,512]{1,0:T(8,128)S(1)}, f32[56,512]{1,0:T(8,128)S(1)}, f32[56,512]{1,0:T(8,128)S(1)}, f32[56,512]{1,0:T(8,128)S(1)}) custom-call(s32[1]{0:T(128)} %bitcast.me_ref, f32[2,96,512]{2,1,0:T(8,128)} %bitcast.11, s32[1,512]{1,0:T(1,128)} %bitcast.14, bf16[4,48,336]{2,1,0:T(8,128)(2,1)} %constant.24.clone.refs_2_.refs_6_), custom_call_target="tpu_custom_call" | custom-call | tf_op jit(solution)/shard_map/pallas_call | solution.py:126
  2.0 4.0 %collective-permute-start.2 = (f32[56,512]{1,0:T(8,128)S(1)}, f32[56,512]{1,0:T(8,128)S(1)}, u32[]{:S(2)}, u32[]{:S(2)}) collective-permute-start(f32[56,512]{1,0:T(8,128)S(1)} %get-tuple-element.24), channel_id=1, source_target_pairs={{0,24},{8,16},{16,8},{24,0},{1,25},{9,17},{17,9},{25,1},{2,26},{10... | collective-permute-start | bytes 344072 | tf_op jit(solution)/shard_map/ppermute | solution.py:421
  5.9 0.5 collective-permute-start.1
  6.4 0.1 collective-permute-start
  6.6 1.2 %broadcast_multiply_fusion = f32[24,9216]{1,0:T(8,128)S(1)} fusion(f32[24,9216]{1,0:T(8,128)} %param.14), kind=kLoop, calls=%fused_computation | loop fusion | flops 221184 | bytes 1769472 | tf_op jit(solution)/shard_map/mul | solution.py:434
  7.8 0.8 %shard_map.132.refs_0_ = f32[48,2048]{1,0:T(8,128)S(1)} custom-call(f32[56,512]{1,0:T(8,128)S(1)} %get-tuple-element.25.plane_ref.mark_ref, f32[56,512]{1,0:T(8,128)S(1)} %get-tuple-element.25.plane_ref.mark_ref), custom_call_target="tpu_custom_call" | custom-call | tf_op jit(solution)/shard_map/pallas_call | solution.py:126
  8.6 0.5 reshape.22
  9.1 0.1 pad.4.refs_3_
  9.2 0.0 copy-start.1
  9.2 0.0 copy-start.2
  9.2 0.0 copy-start.5
  9.2 0.0 copy-start.6
  9.2 0.3 collective-permute-done.2.plane_ref.mark_ref.refs_0_
  9.5 0.8 %shard_map.133.refs_0_ = f32[48,2048]{1,0:T(8,128)S(1)} custom-call(f32[56,512]{1,0:T(8,128)S(1)} %collective-permute-done.2.plane_ref.mark_ref.refs_0_, f32[56,512]{1,0:T(8,128)S(1)} %collective-permute-done.2.plane_ref.mark_ref.refs_0_, f32[48,2048]{1,0:T(8,128)S(1)} %shard_map.132.refs_0_), custom_call_target="tpu_custom_call" | custom-call | tf_op jit(solution)/shard_map/pallas_call | solution.py:126
  10.3 1.3 %collective-permute-done.1.plane_ref.mark_ref.refs_1_ = f32[56,512]{1,0:T(8,128)S(1)} collective-permute-done((f32[56,512]{1,0:T(8,128)S(1)}, f32[56,512]{1,0:T(8,128)S(1)}, u32[]{:S(2)}, u32[]{:S(2)}) %collective-permute-start.1) | collective-permute-done | bytes 114720 | tf_op jit(solution)/shard_map/ppermute | solution.py:421
  11.5 0.8 %shard_map.134.before_ref = f32[48,2048]{1,0:T(8,128)S(1)} custom-call(f32[56,512]{1,0:T(8,128)S(1)} %collective-permute-done.1.plane_ref.mark_ref.refs_1_, f32[56,512]{1,0:T(8,128)S(1)} %collective-permute-done.1.plane_ref.mark_ref.refs_1_, f32[48,2048]{1,0:T(8,128)S(1)} %shard_map.133.refs_0_), custom_call_target="tpu_custom_call" | custom-call | tf_op jit(solution)/shard_map/pallas_call | solution.py:126
  12.3 0.0 copy-start
  12.3 0.0 copy-start.3
  12.3 0.0 copy-start.4
  12.4 0.0 copy-start.8
  12.4 0.0 collective-permute-done.plane_ref.refs_2_
  12.4 0.0 copy-done.1
  12.4 0.0 copy-done.2
  12.4 0.0 copy-done.5
  12.4 0.0 copy-done.6
  12.4 5.6 %shard_map.135 = (f32[48,512]{1,0:T(8,128)S(1)}, f32[48,512]{1,0:T(8,128)S(1)}, f32[48,512]{1,0:T(8,128)S(1)}, bf16[96,2048]{1,0:T(8,128)(2,1)S(1)}) custom-call(f32[56,512]{1,0:T(8,128)S(1)} %collective-permute-done.plane_ref.refs_2_, f32[48,2048]{1,0:T(8,128)S(1)} %shard_map.134.before_ref, ...), custom_call_target="tpu_custom_call" | custom-call | tf_op jit(solution)/shard_map/pallas_call | solution.py:126
  18.1 1.7 %collective-permute-start.3 = (f32[48,512]{1,0:T(8,128)S(1)}, f32[48,512]{1,0:T(8,128)S(1)}, u32[]{:S(2)}, u32[]{:S(2)}) collective-permute-start(f32[48,512]{1,0:T(8,128)S(1)} %get-tuple-element.27), channel_id=1, source_target_pairs={{0,8},{8,0},{16,24},{24,16},{1,9},{9,1},{17,25},{25,17},{2,10},{10... | collective-permute-start | bytes 294920 | tf_op jit(solution)/shard_map/ppermute | solution.py:421
  19.8 1.0 %collective-permute-start.4 = (f32[48,512]{1,0:T(8,128)S(1)}, f32[48,512]{1,0:T(8,128)S(1)}, u32[]{:S(2)}, u32[]{:S(2)}) collective-permute-start(f32[48,512]{1,0:T(8,128)S(1)} %get-tuple-element.28), channel_id=1, source_target_pairs={{0,16},{8,24},{16,0},{24,8},{1,17},{9,25},{17,1},{25,9},{2,18},{10... | collective-permute-start | bytes 294920 | tf_op jit(solution)/shard_map/ppermute | solution.py:421
  20.8 0.8 %collective-permute-start.5 = (f32[48,512]{1,0:T(8,128)S(1)}, f32[48,512]{1,0:T(8,128)S(1)}, u32[]{:S(2)}, u32[]{:S(2)}) collective-permute-start(f32[48,512]{1,0:T(8,128)S(1)} %get-tuple-element.29), channel_id=1, source_target_pairs={{0,24},{8,16},{16,8},{24,0},{1,25},{9,17},{17,9},{25,1},{2,26},{10... | collective-permute-start | bytes 294920 | tf_op jit(solution)/shard_map/ppermute | solution.py:421
  22.9 0.5 shard_map.136.refs_0_
  23.4 0.0 collective-permute-done.3.refs_1_
  23.4 3.0 %collective-permute-done.4.refs_2_ = f32[48,512]{1,0:T(8,128)S(1)} collective-permute-done((f32[48,512]{1,0:T(8,128)S(1)}, f32[48,512]{1,0:T(8,128)S(1)}, u32[]{:S(2)}, u32[]{:S(2)}) %collective-permute-start.4) | collective-permute-done | bytes 98336 | tf_op jit(solution)/shard_map/ppermute | solution.py:421
  26.4 0.0 collective-permute-done.5.refs_3_
  26.4 0.0 copy-done
  26.4 0.0 copy-done.3
  26.4 0.0 copy-done.4
  26.4 0.0 copy-done.8
  26.4 0.6 shard_map.137
  27.1 1.5 %collective-permute-start.8 = (f32[48,512]{1,0:T(8,128)S(1)}, f32[48,512]{1,0:T(8,128)S(1)}, u32[]{:S(2)}, u32[]{:S(2)}) collective-permute-start(f32[48,512]{1,0:T(8,128)S(1)} %get-tuple-element.32), channel_id=1, source_target_pairs={{0,24},{8,16},{16,8},{24,0},{1,25},{9,17},{17,9},{25,1},{2,26},{10... | collective-permute-start | bytes 294920 | tf_op jit(solution)/shard_map/ppermute | solution.py:421
  28.6 1.0 %collective-permute-start.7 = (f32[48,512]{1,0:T(8,128)S(1)}, f32[48,512]{1,0:T(8,128)S(1)}, u32[]{:S(2)}, u32[]{:S(2)}) collective-permute-start(f32[48,512]{1,0:T(8,128)S(1)} %get-tuple-element.31), channel_id=1, source_target_pairs={{0,16},{8,24},{16,0},{24,8},{1,17},{9,25},{17,1},{25,9},{2,18},{10... | collective-permute-start | bytes 294920 | tf_op jit(solution)/shard_map/ppermute | solution.py:421
  29.5 1.1 %collective-permute-start.6 = (f32[48,512]{1,0:T(8,128)S(1)}, f32[48,512]{1,0:T(8,128)S(1)}, u32[]{:S(2)}, u32[]{:S(2)}) collective-permute-start(f32[48,512]{1,0:T(8,128)S(1)} %get-tuple-element.30), channel_id=1, source_target_pairs={{0,8},{8,0},{16,24},{24,16},{1,9},{9,1},{17,25},{25,17},{2,10},{10... | collective-permute-start | bytes 294920 | tf_op jit(solution)/shard_map/ppermute | solution.py:421
  30.6 0.8 %shard_map.138.refs_0_ = f32[48,2048]{1,0:T(8,128)S(1)} custom-call(f32[48,512]{1,0:T(8,128)S(1)} %get-tuple-element.33.plane_ref, f32[56,512]{1,0:T(8,128)S(1)} %get-tuple-element.25.plane_ref.mark_ref), custom_call_target="tpu_custom_call" | custom-call | tf_op jit(solution)/shard_map/pallas_call | solution.py:126
  31.4 1.8 %collective-permute-done.8.plane_ref = f32[48,512]{1,0:T(8,128)S(1)} collective-permute-done((f32[48,512]{1,0:T(8,128)S(1)}, f32[48,512]{1,0:T(8,128)S(1)}, u32[]{:S(2)}, u32[]{:S(2)}) %collective-permute-start.8) | collective-permute-done | bytes 98336 | tf_op jit(solution)/shard_map/ppermute | solution.py:421
  33.2 0.8 %shard_map.139.refs_0_ = f32[48,2048]{1,0:T(8,128)S(1)} custom-call(f32[48,512]{1,0:T(8,128)S(1)} %collective-permute-done.8.plane_ref, f32[56,512]{1,0:T(8,128)S(1)} %collective-permute-done.2.plane_ref.mark_ref.refs_0_, f32[48,2048]{1,0:T(8,128)S(1)} %shard_map.138.refs_0_), custom_call_target="tpu_custom_call" | custom-call | tf_op jit(solution)/shard_map/pallas_call | solution.py:126
  34.0 0.0 collective-permute-done.7.plane_ref
  34.0 0.8 %shard_map.140.before_ref = f32[48,2048]{1,0:T(8,128)S(1)} custom-call(f32[48,512]{1,0:T(8,128)S(1)} %collective-permute-done.7.plane_ref, f32[56,512]{1,0:T(8,128)S(1)} %collective-permute-done.1.plane_ref.mark_ref.refs_1_, f32[48,2048]{1,0:T(8,128)S(1)} %shard_map.139.refs_0_), custom_call_target="tpu_custom_call" | custom-call | tf_op jit(solution)/shard_map/pallas_call | solution.py:126
  34.7 0.0 copy-start.7
  34.8 0.0 collective-permute-done.6.plane_ref
  34.8 5.8 %shard_map.141 = (f32[48,512]{1,0:T(8,128)S(1)}, f32[48,512]{1,0:T(8,128)S(1)}, f32[48,512]{1,0:T(8,128)S(1)}, bf16[96,2048]{1,0:T(8,128)(2,1)S(1)}) custom-call(f32[48,512]{1,0:T(8,128)S(1)} %collective-permute-done.6.plane_ref, f32[48,2048]{1,0:T(8,128)S(1)} %shard_map.140.before_ref, f32[56,512]{1,0:T(8,128)S(1)} %collective-permute-done.2.plane_ref.mark_ref.refs_0_, ...), custom_call_target="tpu_custom_call" | custom-call | tf_op jit(solution)/shard_map/pallas_call | solution.py:126
  40.6 0.9 %collective-permute-start.10 = (f32[48,512]{1,0:T(8,128)S(1)}, f32[48,512]{1,0:T(8,128)S(1)}, u32[]{:S(2)}, u32[]{:S(2)}) collective-permute-start(f32[48,512]{1,0:T(8,128)S(1)} %get-tuple-element.36), channel_id=1, source_target_pairs={{0,16},{8,24},{16,0},{24,8},{1,17},{9,25},{17,1},{25,9},{2,18},{10... | collective-permute-start | bytes 294920 | tf_op jit(solution)/shard_map/ppermute | solution.py:421
  41.5 1.3 %collective-permute-start.11 = (f32[48,512]{1,0:T(8,128)S(1)}, f32[48,512]{1,0:T(8,128)S(1)}, u32[]{:S(2)}, u32[]{:S(2)}) collective-permute-start(f32[48,512]{1,0:T(8,128)S(1)} %get-tuple-element.37), channel_id=1, source_target_pairs={{0,24},{8,16},{16,8},{24,0},{1,25},{9,17},{17,9},{25,1},{2,26},{10... | collective-permute-start | bytes 294920 | tf_op jit(solution)/shard_map/ppermute | solution.py:421
  42.8 1.4 %collective-permute-start.9 = (f32[48,512]{1,0:T(8,128)S(1)}, f32[48,512]{1,0:T(8,128)S(1)}, u32[]{:S(2)}, u32[]{:S(2)}) collective-permute-start(f32[48,512]{1,0:T(8,128)S(1)} %get-tuple-element.35), channel_id=1, source_target_pairs={{0,8},{8,0},{16,24},{24,16},{1,9},{9,1},{17,25},{25,17},{2,10},{10... | collective-permute-start | bytes 294920 | tf_op jit(solution)/shard_map/ppermute | solution.py:421
  44.2 0.5 shard_map.142.refs_0_
  44.6 0.7 collective-permute-done.10.refs_2_
  45.3 1.7 %collective-permute-done.11.refs_3_ = f32[48,512]{1,0:T(8,128)S(1)} collective-permute-done((f32[48,512]{1,0:T(8,128)S(1)}, f32[48,512]{1,0:T(8,128)S(1)}, u32[]{:S(2)}, u32[]{:S(2)}) %collective-permute-start.11) | collective-permute-done | bytes 98336 | tf_op jit(solution)/shard_map/ppermute | solution.py:421
  47.0 0.8 %collective-permute-done.9.refs_1_ = f32[48,512]{1,0:T(8,128)S(1)} collective-permute-done((f32[48,512]{1,0:T(8,128)S(1)}, f32[48,512]{1,0:T(8,128)S(1)}, u32[]{:S(2)}, u32[]{:S(2)}) %collective-permute-start.9) | collective-permute-done | bytes 98336 | tf_op jit(solution)/shard_map/ppermute | solution.py:421
  47.8 0.0 copy-done.7
  47.8 0.5 shard_map.143
  48.3 11.5 %all_to_all.10.parts_ref = bf16[8,16,512]{2,1,0:T(8,128)(2,1)S(1)} all-to-all(bf16[8,16,512]{2,1,0:T(8,128)(2,1)S(1)} %get-tuple-element.40), channel_id=1, replica_groups=mesh['grid'=4,'band'=8] {'band'}, dimensions={0} | all-to-all | bytes 262144 | tf_op jit(solution)/shard_map/all_to_all | solution.py:515
  59.8 1.0 %shard_map.144 = (f32[32,1,128]{2,1,0:T(1,128)}, f32[8,128]{1,0:T(8,128)}) custom-call(bf16[8,16,512]{2,1,0:T(8,128)(2,1)S(1)} %all_to_all.10.parts_ref), custom_call_target="tpu_custom_call" | custom-call | tf_op jit(solution)/shard_map/pallas_call | solution.py:126
  60.8 2.6 %all-to-all-start.1 = ((f32[32,1,128]{2,1,0:T(1,128)}), f32[32,1,128]{2,1,0:T(1,128)S(1)}, u32[]{:S(2)}, u32[]{:S(2)}) async-start(f32[32,1,128]{2,1,0:T(1,128)} %get-tuple-element.41), calls=%async_computation.1 | async-start | bytes 32768 | tf_op jit(solution)/shard_map/all_to_all | solution.py:522
  63.4 0.7 %copy.15 = f32[2,1,512,96]{2,3,1,0:T(8,128)} copy(f32[2,1,512,96]{2,3,1,0:T(8,128)S(1)} %bitcast.10) | data formatting | bytes 786432
  64.1 6.4 %all-to-all-done.1.parts_ref = f32[32,1,128]{2,1,0:T(1,128)S(1)} async-done(((f32[32,1,128]{2,1,0:T(1,128)}), f32[32,1,128]{2,1,0:T(1,128)S(1)}, u32[]{:S(2)}, u32[]{:S(2)}) %all-to-all-start.1) | async-done | bytes 16416 | tf_op jit(solution)/shard_map/all_to_all | solution.py:522
  70.5 0.7 %shard_map.145 = f32[2,1,2]{2,1,0:T(1,128)} custom-call(s32[1]{0:T(128)} %bitcast.me_ref, f32[32,1,128]{2,1,0:T(1,128)S(1)} %all-to-all-done.1.parts_ref), custom_call_target="tpu_custom_call" | custom-call | tf_op jit(solution)/shard_map/pallas_call | solution.py:126
Async XLA Ops:
  2.0 7.5 %collective-permute-start.2 = (f32[56,512]{1,0:T(8,128)S(1)}, f32[56,512]{1,0:T(8,128)S(1)}, u32[]{:S(2)}, u32[]{:S(2)}) collective-permute-start(f32[56,512]{1,0:T(8,128)S(1)} %get-tuple-element.24), channel_id=1, source_target_pairs={{0,24},{8,16},{16,8},{24,0},{1,25},{9,17},{17,9},{25,1},{2,26},{10... | collective-permute-start | bytes 344072 | tf_op jit(solution)/shard_map/ppermute | solution.py:421
  5.9 5.6 %collective-permute-start.1 = (f32[56,512]{1,0:T(8,128)S(1)}, f32[56,512]{1,0:T(8,128)S(1)}, u32[]{:S(2)}, u32[]{:S(2)}) collective-permute-start(f32[56,512]{1,0:T(8,128)S(1)} %get-tuple-element.23), channel_id=1, source_target_pairs={{0,16},{8,24},{16,0},{24,8},{1,17},{9,25},{17,1},{25,9},{2,18},{10... | collective-permute-start | bytes 344072 | tf_op jit(solution)/shard_map/ppermute | solution.py:421
  6.4 5.9 %collective-permute-start = (f32[56,512]{1,0:T(8,128)S(1)}, f32[56,512]{1,0:T(8,128)S(1)}, u32[]{:S(2)}, u32[]{:S(2)}) collective-permute-start(f32[56,512]{1,0:T(8,128)S(1)} %get-tuple-element.22), channel_id=1, source_target_pairs={{0,8},{8,0},{16,24},{24,16},{1,9},{9,1},{17,25},{25,17},{2,10},{10... | collective-permute-start | bytes 344072 | tf_op jit(solution)/shard_map/ppermute | solution.py:421
  9.2 3.2 %copy-start.1 = (bf16[384,256]{1,0:T(8,128)(2,1)S(1)}, bf16[384,256]{1,0:T(8,128)(2,1)}, u32[]{:S(2)}) copy-start(bf16[384,256]{1,0:T(8,128)(2,1)} %constant.25.clone.refs_4_) | copy-start | bytes 589828
  9.2 3.2 %copy-start.2 = (bf16[384,224]{1,0:T(8,128)(2,1)S(1)}, bf16[384,224]{1,0:T(8,128)(2,1)}, u32[]{:S(2)}) copy-start(bf16[384,224]{1,0:T(8,128)(2,1)} %constant.26.clone.refs_5_) | copy-start | bytes 516100
  9.2 3.2 %copy-start.5 = (bf16[256,256]{1,0:T(8,128)(2,1)S(1)}, bf16[256,256]{1,0:T(8,128)(2,1)}, u32[]{:S(2)}) copy-start(bf16[256,256]{1,0:T(8,128)(2,1)} %constant.28.clone.refs_7_) | copy-start | bytes 393220
  9.2 3.2 %copy-start.6 = (bf16[224,192]{1,0:T(8,128)(2,1)S(1)}, bf16[224,192]{1,0:T(8,128)(2,1)}, u32[]{:S(2)}) copy-start(bf16[224,192]{1,0:T(8,128)(2,1)} %constant.27.clone.refs_6_) | copy-start | bytes 258052
  12.3 14.1 %copy-start = (f32[2,1,512,96]{2,3,1,0:T(8,128)S(1)}, f32[2,1,512,96]{2,3,1,0:T(8,128)}, u32[]{:S(2)}) copy-start(f32[2,1,512,96]{2,3,1,0:T(8,128)} %param.12) | copy-start | bytes 1179652
  12.3 14.1 %copy-start.3 = (bf16[4,48,336]{2,1,0:T(8,128)(2,1)S(1)}, bf16[4,48,336]{2,1,0:T(8,128)(2,1)}, u32[]{:S(2)}) copy-start(bf16[4,48,336]{2,1,0:T(8,128)(2,1)} %constant.24.clone.refs_2_.refs_6_) | copy-start | bytes 387076
  12.3 14.1 %copy-start.4 = (bf16[112,576]{1,0:T(8,128)(2,1)S(1)}, bf16[112,576]{1,0:T(8,128)(2,1)}, u32[]{:S(2)}) copy-start(bf16[112,576]{1,0:T(8,128)(2,1)} %constant.29.clone.refs_7_) | copy-start | bytes 387076
  12.4 14.1 %copy-start.8 = (s32[512]{0:T(512)S(1)}, s32[512]{0:T(512)}, u32[]{:S(2)}) copy-start(s32[512]{0:T(512)} %param.13) | copy-start | bytes 6148
  18.1 5.3 %collective-permute-start.3 = (f32[48,512]{1,0:T(8,128)S(1)}, f32[48,512]{1,0:T(8,128)S(1)}, u32[]{:S(2)}, u32[]{:S(2)}) collective-permute-start(f32[48,512]{1,0:T(8,128)S(1)} %get-tuple-element.27), channel_id=1, source_target_pairs={{0,8},{8,0},{16,24},{24,16},{1,9},{9,1},{17,25},{25,17},{2,10},{10... | collective-permute-start | bytes 294920 | tf_op jit(solution)/shard_map/ppermute | solution.py:421
  19.8 6.6 %collective-permute-start.4 = (f32[48,512]{1,0:T(8,128)S(1)}, f32[48,512]{1,0:T(8,128)S(1)}, u32[]{:S(2)}, u32[]{:S(2)}) collective-permute-start(f32[48,512]{1,0:T(8,128)S(1)} %get-tuple-element.28), channel_id=1, source_target_pairs={{0,16},{8,24},{16,0},{24,8},{1,17},{9,25},{17,1},{25,9},{2,18},{10... | collective-permute-start | bytes 294920 | tf_op jit(solution)/shard_map/ppermute | solution.py:421
  20.8 5.6 %collective-permute-start.5 = (f32[48,512]{1,0:T(8,128)S(1)}, f32[48,512]{1,0:T(8,128)S(1)}, u32[]{:S(2)}, u32[]{:S(2)}) collective-permute-start(f32[48,512]{1,0:T(8,128)S(1)} %get-tuple-element.29), channel_id=1, source_target_pairs={{0,24},{8,16},{16,8},{24,0},{1,25},{9,17},{17,9},{25,1},{2,26},{10... | collective-permute-start | bytes 294920 | tf_op jit(solution)/shard_map/ppermute | solution.py:421
  27.1 6.1 %collective-permute-start.8 = (f32[48,512]{1,0:T(8,128)S(1)}, f32[48,512]{1,0:T(8,128)S(1)}, u32[]{:S(2)}, u32[]{:S(2)}) collective-permute-start(f32[48,512]{1,0:T(8,128)S(1)} %get-tuple-element.32), channel_id=1, source_target_pairs={{0,24},{8,16},{16,8},{24,0},{1,25},{9,17},{17,9},{25,1},{2,26},{10... | collective-permute-start | bytes 294920 | tf_op jit(solution)/shard_map/ppermute | solution.py:421
  28.6 5.4 %collective-permute-start.7 = (f32[48,512]{1,0:T(8,128)S(1)}, f32[48,512]{1,0:T(8,128)S(1)}, u32[]{:S(2)}, u32[]{:S(2)}) collective-permute-start(f32[48,512]{1,0:T(8,128)S(1)} %get-tuple-element.31), channel_id=1, source_target_pairs={{0,16},{8,24},{16,0},{24,8},{1,17},{9,25},{17,1},{25,9},{2,18},{10... | collective-permute-start | bytes 294920 | tf_op jit(solution)/shard_map/ppermute | solution.py:421
  29.5 5.2 %collective-permute-start.6 = (f32[48,512]{1,0:T(8,128)S(1)}, f32[48,512]{1,0:T(8,128)S(1)}, u32[]{:S(2)}, u32[]{:S(2)}) collective-permute-start(f32[48,512]{1,0:T(8,128)S(1)} %get-tuple-element.30), channel_id=1, source_target_pairs={{0,8},{8,0},{16,24},{24,16},{1,9},{9,1},{17,25},{25,17},{2,10},{10... | collective-permute-start | bytes 294920 | tf_op jit(solution)/shard_map/ppermute | solution.py:421
  34.7 13.1 %copy-start.7 = (bf16[2,128,56]{2,1,0:T(8,128)(2,1)S(1)}, bf16[2,128,56]{2,1,0:T(8,128)(2,1)}, u32[]{:S(2)}) copy-start(bf16[2,128,56]{2,1,0:T(8,128)(2,1)} %constant.30.clone.refs_8_) | copy-start | bytes 86020
  40.6 4.7 %collective-permute-start.10 = (f32[48,512]{1,0:T(8,128)S(1)}, f32[48,512]{1,0:T(8,128)S(1)}, u32[]{:S(2)}, u32[]{:S(2)}) collective-permute-start(f32[48,512]{1,0:T(8,128)S(1)} %get-tuple-element.36), channel_id=1, source_target_pairs={{0,16},{8,24},{16,0},{24,8},{1,17},{9,25},{17,1},{25,9},{2,18},{10... | collective-permute-start | bytes 294920 | tf_op jit(solution)/shard_map/ppermute | solution.py:421
  41.5 5.5 %collective-permute-start.11 = (f32[48,512]{1,0:T(8,128)S(1)}, f32[48,512]{1,0:T(8,128)S(1)}, u32[]{:S(2)}, u32[]{:S(2)}) collective-permute-start(f32[48,512]{1,0:T(8,128)S(1)} %get-tuple-element.37), channel_id=1, source_target_pairs={{0,24},{8,16},{16,8},{24,0},{1,25},{9,17},{17,9},{25,1},{2,26},{10... | collective-permute-start | bytes 294920 | tf_op jit(solution)/shard_map/ppermute | solution.py:421
  42.8 5.0 %collective-permute-start.9 = (f32[48,512]{1,0:T(8,128)S(1)}, f32[48,512]{1,0:T(8,128)S(1)}, u32[]{:S(2)}, u32[]{:S(2)}) collective-permute-start(f32[48,512]{1,0:T(8,128)S(1)} %get-tuple-element.35), channel_id=1, source_target_pairs={{0,8},{8,0},{16,24},{24,16},{1,9},{9,1},{17,25},{25,17},{2,10},{10... | collective-permute-start | bytes 294920 | tf_op jit(solution)/shard_map/ppermute | solution.py:421
  60.8 9.7 %all-to-all-start.1 = ((f32[32,1,128]{2,1,0:T(1,128)}), f32[32,1,128]{2,1,0:T(1,128)S(1)}, u32[]{:S(2)}, u32[]{:S(2)}) async-start(f32[32,1,128]{2,1,0:T(1,128)} %get-tuple-element.41), calls=%async_computation.1 | async-start | bytes 32768 | tf_op jit(solution)/shard_map/all_to_all | solution.py:522

commit v15 on v13

--- a/solution.py
+++ b/solution.py
@@ -360,7 +360,7 @@
     if depth < pad:
         q_ref[depth * GX :] = jnp.zeros(((pad - depth) * GX, 128), F32)
 
-    chunk, group = 8, 4
+    chunk, group = 8, 8
     for first in range(0, depth, chunk):
         last = min(depth, first + chunk)
         for z in range(first, last, group):

time: 71.5 us -> 70 us (0.979)
  Pallas kernels: 21.2 us -> 19.6 us
    pallas_call x15, Pallas kernels: 21.2 us -> 19.6 us  [call(): pl.pallas_call(kernel, out_shape=out_shape, in_specs=[SMEM] * len(scalars...]
where the time goes in v15:
time: 70 us; the launch traced here: 69.7 us
  Pallas kernels  19.6 us (28%)
  starting transfers between devices  17.8 us (25%)
  waiting for transfers between devices  15.9 us (23%)
  blocking collectives  11.5 us (16%)
  between operations  2.24 us (3%)
  local copies, waits for them, and re-layouts  1.36 us (2%)
  other arithmetic  1.24 us (2%)
    pallas_call x15, Pallas kernels, call(): pl.pallas_call(kernel, out_shape=out_shape, in_specs=[SMEM] * len(scalars...  19.6 us
    ppermute x12, starting transfers between devices, exchange(): lax.ppermute(values[k], 'grid', [(d, step(d, k)) for d in range(devices)])  15.3 us
    all_to_all x1, blocking collectives, body(): lax.all_to_all(packed, 'band', 0, 0, tiled=True)  11.5 us
    ppermute x12, waiting for transfers between devices, exchange(): lax.ppermute(values[k], 'grid', [(d, step(d, k)) for d in range(devices)])  9.53 us
    all_to_all x1, waiting for transfers between devices, body(): lax.all_to_all(partial_sum, ('grid', 'band'), 0, 0, tiled=True)  6.39 us
    all_to_all x1, starting transfers between devices, body(): lax.all_to_all(partial_sum, ('grid', 'band'), 0, 0, tiled=True)  2.57 us
  transfers between devices with their start and end apart: 13, of which 8 were waited for; matrix products, arithmetic and copies ran while one was open for 4% of the time, Pallas kernels for 8%

profile of v15, /device:TPU:0, one launch (start us, length us, event | category | flops | bytes accessed | tf_op | source)
XLA Modules:
  0.0 69.7 jit_solution(16228773631024464230)
XLA Ops:
  0.6 1.3 %shard_map.131 = (f32[56,512]{1,0:T(8,128)S(1)}, f32[56,512]{1,0:T(8,128)S(1)}, f32[56,512]{1,0:T(8,128)S(1)}, f32[56,512]{1,0:T(8,128)S(1)}) custom-call(s32[1]{0:T(128)} %bitcast.me_ref, f32[2,96,512]{2,1,0:T(8,128)} %bitcast.11, s32[1,512]{1,0:T(1,128)} %bitcast.14, bf16[4,48,336]{2,1,0:T(8,128)(2,1)} %constant.24.clone.refs_2_.refs_6_), custom_call_target="tpu_custom_call" | custom-call | tf_op jit(solution)/shard_map/pallas_call | solution.py:126
  2.0 4.0 %collective-permute-start.2 = (f32[56,512]{1,0:T(8,128)S(1)}, f32[56,512]{1,0:T(8,128)S(1)}, u32[]{:S(2)}, u32[]{:S(2)}) collective-permute-start(f32[56,512]{1,0:T(8,128)S(1)} %get-tuple-element.24), channel_id=1, source_target_pairs={{0,24},{8,16},{16,8},{24,0},{1,25},{9,17},{17,9},{25,1},{2,26},{10... | collective-permute-start | bytes 344072 | tf_op jit(solution)/shard_map/ppermute | solution.py:421
  5.9 0.5 collective-permute-start.1
  6.4 0.1 collective-permute-start
  6.6 1.2 %broadcast_multiply_fusion = f32[24,9216]{1,0:T(8,128)S(1)} fusion(f32[24,9216]{1,0:T(8,128)} %param.14), kind=kLoop, calls=%fused_computation | loop fusion | flops 221184 | bytes 1769472 | tf_op jit(solution)/shard_map/mul | solution.py:436
  7.8 0.8 %shard_map.132.refs_0_ = f32[48,2048]{1,0:T(8,128)S(1)} custom-call(f32[56,512]{1,0:T(8,128)S(1)} %get-tuple-element.25.plane_ref.mark_ref, f32[56,512]{1,0:T(8,128)S(1)} %get-tuple-element.25.plane_ref.mark_ref), custom_call_target="tpu_custom_call" | custom-call | tf_op jit(solution)/shard_map/pallas_call | solution.py:126
  8.6 0.5 reshape.22
  9.1 0.1 pad.4.refs_3_
  9.2 0.0 copy-start.1
  9.2 0.0 copy-start.2
  9.2 0.0 copy-start.5
  9.2 0.0 copy-start.6
  9.2 0.3 collective-permute-done.2.plane_ref.mark_ref.refs_0_
  9.5 0.8 %shard_map.133.refs_0_ = f32[48,2048]{1,0:T(8,128)S(1)} custom-call(f32[56,512]{1,0:T(8,128)S(1)} %collective-permute-done.2.plane_ref.mark_ref.refs_0_, f32[56,512]{1,0:T(8,128)S(1)} %collective-permute-done.2.plane_ref.mark_ref.refs_0_, f32[48,2048]{1,0:T(8,128)S(1)} %shard_map.132.refs_0_), custom_call_target="tpu_custom_call" | custom-call | tf_op jit(solution)/shard_map/pallas_call | solution.py:126
  10.3 1.3 %collective-permute-done.1.plane_ref.mark_ref.refs_1_ = f32[56,512]{1,0:T(8,128)S(1)} collective-permute-done((f32[56,512]{1,0:T(8,128)S(1)}, f32[56,512]{1,0:T(8,128)S(1)}, u32[]{:S(2)}, u32[]{:S(2)}) %collective-permute-start.1) | collective-permute-done | bytes 114720 | tf_op jit(solution)/shard_map/ppermute | solution.py:421
  11.5 0.8 %shard_map.134.before_ref = f32[48,2048]{1,0:T(8,128)S(1)} custom-call(f32[56,512]{1,0:T(8,128)S(1)} %collective-permute-done.1.plane_ref.mark_ref.refs_1_, f32[56,512]{1,0:T(8,128)S(1)} %collective-permute-done.1.plane_ref.mark_ref.refs_1_, f32[48,2048]{1,0:T(8,128)S(1)} %shard_map.133.refs_0_), custom_call_target="tpu_custom_call" | custom-call | tf_op jit(solution)/shard_map/pallas_call | solution.py:126
  12.3 0.0 copy-start
  12.3 0.0 copy-start.3
  12.3 0.0 copy-start.4
  12.3 0.0 copy-start.8
  12.4 0.0 collective-permute-done.plane_ref.refs_2_
  12.4 0.0 copy-done.1
  12.4 0.0 copy-done.2
  12.4 0.0 copy-done.5
  12.4 0.0 copy-done.6
  12.4 4.9 %shard_map.135 = (f32[48,512]{1,0:T(8,128)S(1)}, f32[48,512]{1,0:T(8,128)S(1)}, f32[48,512]{1,0:T(8,128)S(1)}, bf16[96,2048]{1,0:T(8,128)(2,1)S(1)}) custom-call(f32[56,512]{1,0:T(8,128)S(1)} %collective-permute-done.plane_ref.refs_2_, f32[48,2048]{1,0:T(8,128)S(1)} %shard_map.134.before_ref, ...), custom_call_target="tpu_custom_call" | custom-call | tf_op jit(solution)/shard_map/pallas_call | solution.py:126
  17.4 1.7 %collective-permute-start.3 = (f32[48,512]{1,0:T(8,128)S(1)}, f32[48,512]{1,0:T(8,128)S(1)}, u32[]{:S(2)}, u32[]{:S(2)}) collective-permute-start(f32[48,512]{1,0:T(8,128)S(1)} %get-tuple-element.27), channel_id=1, source_target_pairs={{0,8},{8,0},{16,24},{24,16},{1,9},{9,1},{17,25},{25,17},{2,10},{10... | collective-permute-start | bytes 294920 | tf_op jit(solution)/shard_map/ppermute | solution.py:421
  19.1 1.0 %collective-permute-start.4 = (f32[48,512]{1,0:T(8,128)S(1)}, f32[48,512]{1,0:T(8,128)S(1)}, u32[]{:S(2)}, u32[]{:S(2)}) collective-permute-start(f32[48,512]{1,0:T(8,128)S(1)} %get-tuple-element.28), channel_id=1, source_target_pairs={{0,16},{8,24},{16,0},{24,8},{1,17},{9,25},{17,1},{25,9},{2,18},{10... | collective-permute-start | bytes 294920 | tf_op jit(solution)/shard_map/ppermute | solution.py:421
  20.1 0.8 %collective-permute-start.5 = (f32[48,512]{1,0:T(8,128)S(1)}, f32[48,512]{1,0:T(8,128)S(1)}, u32[]{:S(2)}, u32[]{:S(2)}) collective-permute-start(f32[48,512]{1,0:T(8,128)S(1)} %get-tuple-element.29), channel_id=1, source_target_pairs={{0,24},{8,16},{16,8},{24,0},{1,25},{9,17},{17,9},{25,1},{2,26},{10... | collective-permute-start | bytes 294920 | tf_op jit(solution)/shard_map/ppermute | solution.py:421
  22.2 0.5 shard_map.136.refs_0_
  22.7 0.0 collective-permute-done.3.refs_1_
  22.7 3.0 %collective-permute-done.4.refs_2_ = f32[48,512]{1,0:T(8,128)S(1)} collective-permute-done((f32[48,512]{1,0:T(8,128)S(1)}, f32[48,512]{1,0:T(8,128)S(1)}, u32[]{:S(2)}, u32[]{:S(2)}) %collective-permute-start.4) | collective-permute-done | bytes 98336 | tf_op jit(solution)/shard_map/ppermute | solution.py:421
  25.7 0.0 collective-permute-done.5.refs_3_
  25.7 0.0 copy-done
  25.7 0.0 copy-done.3
  25.7 0.0 copy-done.4
  25.7 0.0 copy-done.8
  25.7 0.6 shard_map.137
  26.4 1.5 %collective-permute-start.8 = (f32[48,512]{1,0:T(8,128)S(1)}, f32[48,512]{1,0:T(8,128)S(1)}, u32[]{:S(2)}, u32[]{:S(2)}) collective-permute-start(f32[48,512]{1,0:T(8,128)S(1)} %get-tuple-element.32), channel_id=1, source_target_pairs={{0,24},{8,16},{16,8},{24,0},{1,25},{9,17},{17,9},{25,1},{2,26},{10... | collective-permute-start | bytes 294920 | tf_op jit(solution)/shard_map/ppermute | solution.py:421
  27.9 1.0 %collective-permute-start.7 = (f32[48,512]{1,0:T(8,128)S(1)}, f32[48,512]{1,0:T(8,128)S(1)}, u32[]{:S(2)}, u32[]{:S(2)}) collective-permute-start(f32[48,512]{1,0:T(8,128)S(1)} %get-tuple-element.31), channel_id=1, source_target_pairs={{0,16},{8,24},{16,0},{24,8},{1,17},{9,25},{17,1},{25,9},{2,18},{10... | collective-permute-start | bytes 294920 | tf_op jit(solution)/shard_map/ppermute | solution.py:421
  28.8 1.1 %collective-permute-start.6 = (f32[48,512]{1,0:T(8,128)S(1)}, f32[48,512]{1,0:T(8,128)S(1)}, u32[]{:S(2)}, u32[]{:S(2)}) collective-permute-start(f32[48,512]{1,0:T(8,128)S(1)} %get-tuple-element.30), channel_id=1, source_target_pairs={{0,8},{8,0},{16,24},{24,16},{1,9},{9,1},{17,25},{25,17},{2,10},{10... | collective-permute-start | bytes 294920 | tf_op jit(solution)/shard_map/ppermute | solution.py:421
  29.9 0.8 %shard_map.138.refs_0_ = f32[48,2048]{1,0:T(8,128)S(1)} custom-call(f32[48,512]{1,0:T(8,128)S(1)} %get-tuple-element.33.plane_ref, f32[56,512]{1,0:T(8,128)S(1)} %get-tuple-element.25.plane_ref.mark_ref), custom_call_target="tpu_custom_call" | custom-call | tf_op jit(solution)/shard_map/pallas_call | solution.py:126
  30.7 1.8 %collective-permute-done.8.plane_ref = f32[48,512]{1,0:T(8,128)S(1)} collective-permute-done((f32[48,512]{1,0:T(8,128)S(1)}, f32[48,512]{1,0:T(8,128)S(1)}, u32[]{:S(2)}, u32[]{:S(2)}) %collective-permute-start.8) | collective-permute-done | bytes 98336 | tf_op jit(solution)/shard_map/ppermute | solution.py:421
  32.5 0.8 %shard_map.139.refs_0_ = f32[48,2048]{1,0:T(8,128)S(1)} custom-call(f32[48,512]{1,0:T(8,128)S(1)} %collective-permute-done.8.plane_ref, f32[56,512]{1,0:T(8,128)S(1)} %collective-permute-done.2.plane_ref.mark_ref.refs_0_, f32[48,2048]{1,0:T(8,128)S(1)} %shard_map.138.refs_0_), custom_call_target="tpu_custom_call" | custom-call | tf_op jit(solution)/shard_map/pallas_call | solution.py:126
  33.3 0.0 collective-permute-done.7.plane_ref
  33.3 0.8 %shard_map.140.before_ref = f32[48,2048]{1,0:T(8,128)S(1)} custom-call(f32[48,512]{1,0:T(8,128)S(1)} %collective-permute-done.7.plane_ref, f32[56,512]{1,0:T(8,128)S(1)} %collective-permute-done.1.plane_ref.mark_ref.refs_1_, f32[48,2048]{1,0:T(8,128)S(1)} %shard_map.139.refs_0_), custom_call_target="tpu_custom_call" | custom-call | tf_op jit(solution)/shard_map/pallas_call | solution.py:126
  34.0 0.0 copy-start.7
  34.1 0.0 collective-permute-done.6.plane_ref
  34.1 4.9 %shard_map.141 = (f32[48,512]{1,0:T(8,128)S(1)}, f32[48,512]{1,0:T(8,128)S(1)}, f32[48,512]{1,0:T(8,128)S(1)}, bf16[96,2048]{1,0:T(8,128)(2,1)S(1)}) custom-call(f32[48,512]{1,0:T(8,128)S(1)} %collective-permute-done.6.plane_ref, f32[48,2048]{1,0:T(8,128)S(1)} %shard_map.140.before_ref, f32[56,512]{1,0:T(8,128)S(1)} %collective-permute-done.2.plane_ref.mark_ref.refs_0_, ...), custom_call_target="tpu_custom_call" | custom-call | tf_op jit(solution)/shard_map/pallas_call | solution.py:126
  39.0 0.9 %collective-permute-start.10 = (f32[48,512]{1,0:T(8,128)S(1)}, f32[48,512]{1,0:T(8,128)S(1)}, u32[]{:S(2)}, u32[]{:S(2)}) collective-permute-start(f32[48,512]{1,0:T(8,128)S(1)} %get-tuple-element.36), channel_id=1, source_target_pairs={{0,16},{8,24},{16,0},{24,8},{1,17},{9,25},{17,1},{25,9},{2,18},{10... | collective-permute-start | bytes 294920 | tf_op jit(solution)/shard_map/ppermute | solution.py:421
  39.9 1.3 %collective-permute-start.11 = (f32[48,512]{1,0:T(8,128)S(1)}, f32[48,512]{1,0:T(8,128)S(1)}, u32[]{:S(2)}, u32[]{:S(2)}) collective-permute-start(f32[48,512]{1,0:T(8,128)S(1)} %get-tuple-element.37), channel_id=1, source_target_pairs={{0,24},{8,16},{16,8},{24,0},{1,25},{9,17},{17,9},{25,1},{2,26},{10... | collective-permute-start | bytes 294920 | tf_op jit(solution)/shard_map/ppermute | solution.py:421
  41.2 1.3 %collective-permute-start.9 = (f32[48,512]{1,0:T(8,128)S(1)}, f32[48,512]{1,0:T(8,128)S(1)}, u32[]{:S(2)}, u32[]{:S(2)}) collective-permute-start(f32[48,512]{1,0:T(8,128)S(1)} %get-tuple-element.35), channel_id=1, source_target_pairs={{0,8},{8,0},{16,24},{24,16},{1,9},{9,1},{17,25},{25,17},{2,10},{10... | collective-permute-start | bytes 294920 | tf_op jit(solution)/shard_map/ppermute | solution.py:421
  42.6 0.5 shard_map.142.refs_0_
  43.1 0.7 collective-permute-done.10.refs_2_
  43.7 1.8 %collective-permute-done.11.refs_3_ = f32[48,512]{1,0:T(8,128)S(1)} collective-permute-done((f32[48,512]{1,0:T(8,128)S(1)}, f32[48,512]{1,0:T(8,128)S(1)}, u32[]{:S(2)}, u32[]{:S(2)}) %collective-permute-start.11) | collective-permute-done | bytes 98336 | tf_op jit(solution)/shard_map/ppermute | solution.py:421
  45.5 0.8 %collective-permute-done.9.refs_1_ = f32[48,512]{1,0:T(8,128)S(1)} collective-permute-done((f32[48,512]{1,0:T(8,128)S(1)}, f32[48,512]{1,0:T(8,128)S(1)}, u32[]{:S(2)}, u32[]{:S(2)}) %collective-permute-start.9) | collective-permute-done | bytes 98336 | tf_op jit(solution)/shard_map/ppermute | solution.py:421
  46.2 0.0 copy-done.7
  46.2 0.5 shard_map.143
  46.8 11.5 %all_to_all.10.parts_ref = bf16[8,16,512]{2,1,0:T(8,128)(2,1)S(1)} all-to-all(bf16[8,16,512]{2,1,0:T(8,128)(2,1)S(1)} %get-tuple-element.40), channel_id=1, replica_groups=mesh['grid'=4,'band'=8] {'band'}, dimensions={0} | all-to-all | bytes 262144 | tf_op jit(solution)/shard_map/all_to_all | solution.py:517
  58.2 1.0 %shard_map.144 = (f32[32,1,128]{2,1,0:T(1,128)}, f32[8,128]{1,0:T(8,128)}) custom-call(bf16[8,16,512]{2,1,0:T(8,128)(2,1)S(1)} %all_to_all.10.parts_ref), custom_call_target="tpu_custom_call" | custom-call | tf_op jit(solution)/shard_map/pallas_call | solution.py:126
  59.2 2.6 %all-to-all-start.1 = ((f32[32,1,128]{2,1,0:T(1,128)}), f32[32,1,128]{2,1,0:T(1,128)S(1)}, u32[]{:S(2)}, u32[]{:S(2)}) async-start(f32[32,1,128]{2,1,0:T(1,128)} %get-tuple-element.41), calls=%async_computation.1 | async-start | bytes 32768 | tf_op jit(solution)/shard_map/all_to_all | solution.py:524
  61.8 0.7 %copy.15 = f32[2,1,512,96]{2,3,1,0:T(8,128)} copy(f32[2,1,512,96]{2,3,1,0:T(8,128)S(1)} %bitcast.10) | data formatting | bytes 786432
  62.6 6.4 %all-to-all-done.1.parts_ref = f32[32,1,128]{2,1,0:T(1,128)S(1)} async-done(((f32[32,1,128]{2,1,0:T(1,128)}), f32[32,1,128]{2,1,0:T(1,128)S(1)}, u32[]{:S(2)}, u32[]{:S(2)}) %all-to-all-start.1) | async-done | bytes 16416 | tf_op jit(solution)/shard_map/all_to_all | solution.py:524
  69.0 0.7 %shard_map.145 = f32[2,1,2]{2,1,0:T(1,128)} custom-call(s32[1]{0:T(128)} %bitcast.me_ref, f32[32,1,128]{2,1,0:T(1,128)S(1)} %all-to-all-done.1.parts_ref), custom_call_target="tpu_custom_call" | custom-call | tf_op jit(solution)/shard_map/pallas_call | solution.py:126
Async XLA Ops:
  2.0 7.5 %collective-permute-start.2 = (f32[56,512]{1,0:T(8,128)S(1)}, f32[56,512]{1,0:T(8,128)S(1)}, u32[]{:S(2)}, u32[]{:S(2)}) collective-permute-start(f32[56,512]{1,0:T(8,128)S(1)} %get-tuple-element.24), channel_id=1, source_target_pairs={{0,24},{8,16},{16,8},{24,0},{1,25},{9,17},{17,9},{25,1},{2,26},{10... | collective-permute-start | bytes 344072 | tf_op jit(solution)/shard_map/ppermute | solution.py:421
  5.9 5.6 %collective-permute-start.1 = (f32[56,512]{1,0:T(8,128)S(1)}, f32[56,512]{1,0:T(8,128)S(1)}, u32[]{:S(2)}, u32[]{:S(2)}) collective-permute-start(f32[56,512]{1,0:T(8,128)S(1)} %get-tuple-element.23), channel_id=1, source_target_pairs={{0,16},{8,24},{16,0},{24,8},{1,17},{9,25},{17,1},{25,9},{2,18},{10... | collective-permute-start | bytes 344072 | tf_op jit(solution)/shard_map/ppermute | solution.py:421
  6.4 5.9 %collective-permute-start = (f32[56,512]{1,0:T(8,128)S(1)}, f32[56,512]{1,0:T(8,128)S(1)}, u32[]{:S(2)}, u32[]{:S(2)}) collective-permute-start(f32[56,512]{1,0:T(8,128)S(1)} %get-tuple-element.22), channel_id=1, source_target_pairs={{0,8},{8,0},{16,24},{24,16},{1,9},{9,1},{17,25},{25,17},{2,10},{10... | collective-permute-start | bytes 344072 | tf_op jit(solution)/shard_map/ppermute | solution.py:421
  9.2 3.2 %copy-start.1 = (bf16[384,256]{1,0:T(8,128)(2,1)S(1)}, bf16[384,256]{1,0:T(8,128)(2,1)}, u32[]{:S(2)}) copy-start(bf16[384,256]{1,0:T(8,128)(2,1)} %constant.25.clone.refs_4_) | copy-start | bytes 589828
  9.2 3.2 %copy-start.2 = (bf16[384,224]{1,0:T(8,128)(2,1)S(1)}, bf16[384,224]{1,0:T(8,128)(2,1)}, u32[]{:S(2)}) copy-start(bf16[384,224]{1,0:T(8,128)(2,1)} %constant.26.clone.refs_5_) | copy-start | bytes 516100
  9.2 3.2 %copy-start.5 = (bf16[256,256]{1,0:T(8,128)(2,1)S(1)}, bf16[256,256]{1,0:T(8,128)(2,1)}, u32[]{:S(2)}) copy-start(bf16[256,256]{1,0:T(8,128)(2,1)} %constant.28.clone.refs_7_) | copy-start | bytes 393220
  9.2 3.2 %copy-start.6 = (bf16[224,192]{1,0:T(8,128)(2,1)S(1)}, bf16[224,192]{1,0:T(8,128)(2,1)}, u32[]{:S(2)}) copy-start(bf16[224,192]{1,0:T(8,128)(2,1)} %constant.27.clone.refs_6_) | copy-start | bytes 258052
  12.3 13.4 %copy-start = (f32[2,1,512,96]{2,3,1,0:T(8,128)S(1)}, f32[2,1,512,96]{2,3,1,0:T(8,128)}, u32[]{:S(2)}) copy-start(f32[2,1,512,96]{2,3,1,0:T(8,128)} %param.12) | copy-start | bytes 1179652
  12.3 13.4 %copy-start.3 = (bf16[4,48,336]{2,1,0:T(8,128)(2,1)S(1)}, bf16[4,48,336]{2,1,0:T(8,128)(2,1)}, u32[]{:S(2)}) copy-start(bf16[4,48,336]{2,1,0:T(8,128)(2,1)} %constant.24.clone.refs_2_.refs_6_) | copy-start | bytes 387076
  12.3 13.4 %copy-start.4 = (bf16[112,576]{1,0:T(8,128)(2,1)S(1)}, bf16[112,576]{1,0:T(8,128)(2,1)}, u32[]{:S(2)}) copy-start(bf16[112,576]{1,0:T(8,128)(2,1)} %constant.29.clone.refs_7_) | copy-start | bytes 387076
  12.3 13.4 %copy-start.8 = (s32[512]{0:T(512)S(1)}, s32[512]{0:T(512)}, u32[]{:S(2)}) copy-start(s32[512]{0:T(512)} %param.13) | copy-start | bytes 6148
  17.4 5.3 %collective-permute-start.3 = (f32[48,512]{1,0:T(8,128)S(1)}, f32[48,512]{1,0:T(8,128)S(1)}, u32[]{:S(2)}, u32[]{:S(2)}) collective-permute-start(f32[48,512]{1,0:T(8,128)S(1)} %get-tuple-element.27), channel_id=1, source_target_pairs={{0,8},{8,0},{16,24},{24,16},{1,9},{9,1},{17,25},{25,17},{2,10},{10... | collective-permute-start | bytes 294920 | tf_op jit(solution)/shard_map/ppermute | solution.py:421
  19.1 6.6 %collective-permute-start.4 = (f32[48,512]{1,0:T(8,128)S(1)}, f32[48,512]{1,0:T(8,128)S(1)}, u32[]{:S(2)}, u32[]{:S(2)}) collective-permute-start(f32[48,512]{1,0:T(8,128)S(1)} %get-tuple-element.28), channel_id=1, source_target_pairs={{0,16},{8,24},{16,0},{24,8},{1,17},{9,25},{17,1},{25,9},{2,18},{10... | collective-permute-start | bytes 294920 | tf_op jit(solution)/shard_map/ppermute | solution.py:421
  20.1 5.6 %collective-permute-start.5 = (f32[48,512]{1,0:T(8,128)S(1)}, f32[48,512]{1,0:T(8,128)S(1)}, u32[]{:S(2)}, u32[]{:S(2)}) collective-permute-start(f32[48,512]{1,0:T(8,128)S(1)} %get-tuple-element.29), channel_id=1, source_target_pairs={{0,24},{8,16},{16,8},{24,0},{1,25},{9,17},{17,9},{25,1},{2,26},{10... | collective-permute-start | bytes 294920 | tf_op jit(solution)/shard_map/ppermute | solution.py:421
  26.4 6.1 %collective-permute-start.8 = (f32[48,512]{1,0:T(8,128)S(1)}, f32[48,512]{1,0:T(8,128)S(1)}, u32[]{:S(2)}, u32[]{:S(2)}) collective-permute-start(f32[48,512]{1,0:T(8,128)S(1)} %get-tuple-element.32), channel_id=1, source_target_pairs={{0,24},{8,16},{16,8},{24,0},{1,25},{9,17},{17,9},{25,1},{2,26},{10... | collective-permute-start | bytes 294920 | tf_op jit(solution)/shard_map/ppermute | solution.py:421
  27.9 5.4 %collective-permute-start.7 = (f32[48,512]{1,0:T(8,128)S(1)}, f32[48,512]{1,0:T(8,128)S(1)}, u32[]{:S(2)}, u32[]{:S(2)}) collective-permute-start(f32[48,512]{1,0:T(8,128)S(1)} %get-tuple-element.31), channel_id=1, source_target_pairs={{0,16},{8,24},{16,0},{24,8},{1,17},{9,25},{17,1},{25,9},{2,18},{10... | collective-permute-start | bytes 294920 | tf_op jit(solution)/shard_map/ppermute | solution.py:421
  28.8 5.2 %collective-permute-start.6 = (f32[48,512]{1,0:T(8,128)S(1)}, f32[48,512]{1,0:T(8,128)S(1)}, u32[]{:S(2)}, u32[]{:S(2)}) collective-permute-start(f32[48,512]{1,0:T(8,128)S(1)} %get-tuple-element.30), channel_id=1, source_target_pairs={{0,8},{8,0},{16,24},{24,16},{1,9},{9,1},{17,25},{25,17},{2,10},{10... | collective-permute-start | bytes 294920 | tf_op jit(solution)/shard_map/ppermute | solution.py:421
  34.0 12.2 %copy-start.7 = (bf16[2,128,56]{2,1,0:T(8,128)(2,1)S(1)}, bf16[2,128,56]{2,1,0:T(8,128)(2,1)}, u32[]{:S(2)}) copy-start(bf16[2,128,56]{2,1,0:T(8,128)(2,1)} %constant.30.clone.refs_8_) | copy-start | bytes 86020
  39.0 4.7 %collective-permute-start.10 = (f32[48,512]{1,0:T(8,128)S(1)}, f32[48,512]{1,0:T(8,128)S(1)}, u32[]{:S(2)}, u32[]{:S(2)}) collective-permute-start(f32[48,512]{1,0:T(8,128)S(1)} %get-tuple-element.36), channel_id=1, source_target_pairs={{0,16},{8,24},{16,0},{24,8},{1,17},{9,25},{17,1},{25,9},{2,18},{10... | collective-permute-start | bytes 294920 | tf_op jit(solution)/shard_map/ppermute | solution.py:421
  39.9 5.5 %collective-permute-start.11 = (f32[48,512]{1,0:T(8,128)S(1)}, f32[48,512]{1,0:T(8,128)S(1)}, u32[]{:S(2)}, u32[]{:S(2)}) collective-permute-start(f32[48,512]{1,0:T(8,128)S(1)} %get-tuple-element.37), channel_id=1, source_target_pairs={{0,24},{8,16},{16,8},{24,0},{1,25},{9,17},{17,9},{25,1},{2,26},{10... | collective-permute-start | bytes 294920 | tf_op jit(solution)/shard_map/ppermute | solution.py:421
  41.2 5.0 %collective-permute-start.9 = (f32[48,512]{1,0:T(8,128)S(1)}, f32[48,512]{1,0:T(8,128)S(1)}, u32[]{:S(2)}, u32[]{:S(2)}) collective-permute-start(f32[48,512]{1,0:T(8,128)S(1)} %get-tuple-element.35), channel_id=1, source_target_pairs={{0,8},{8,0},{16,24},{24,16},{1,9},{9,1},{17,25},{25,17},{2,10},{10... | collective-permute-start | bytes 294920 | tf_op jit(solution)/shard_map/ppermute | solution.py:421
  59.2 9.7 %all-to-all-start.1 = ((f32[32,1,128]{2,1,0:T(1,128)}), f32[32,1,128]{2,1,0:T(1,128)S(1)}, u32[]{:S(2)}, u32[]{:S(2)}) async-start(f32[32,1,128]{2,1,0:T(1,128)} %get-tuple-element.41), calls=%async_computation.1 | async-start | bytes 32768 | tf_op jit(solution)/shard_map/all_to_all | solution.py:524

commit v16 on v15

--- a/solution.py
+++ b/solution.py
@@ -360,7 +360,7 @@
     if depth < pad:
         q_ref[depth * GX :] = jnp.zeros(((pad - depth) * GX, 128), F32)
 
-    chunk, group = 8, 8
+    chunk, group = 24, 8
     for first in range(0, depth, chunk):
         last = min(depth, first + chunk)
         for z in range(first, last, group):

time: 70 us -> 69.6 us (level)
  no operation moved by 1% of the time
where the time goes in v16:
time: 69.6 us; the launch traced here: 69.3 us
  Pallas kernels  19.3 us (28%)
  starting transfers between devices  17.8 us (26%)
  waiting for transfers between devices  15.9 us (23%)
  blocking collectives  11.5 us (17%)
  between operations  2.24 us (3%)
  local copies, waits for them, and re-layouts  1.36 us (2%)
  other arithmetic  1.24 us (2%)
    pallas_call x15, Pallas kernels, call(): pl.pallas_call(kernel, out_shape=out_shape, in_specs=[SMEM] * len(scalars...  19.3 us
    ppermute x12, starting transfers between devices, exchange(): lax.ppermute(values[k], 'grid', [(d, step(d, k)) for d in range(devices)])  15.3 us
    all_to_all x1, blocking collectives, body(): lax.all_to_all(packed, 'band', 0, 0, tiled=True)  11.5 us
    ppermute x12, waiting for transfers between devices, exchange(): lax.ppermute(values[k], 'grid', [(d, step(d, k)) for d in range(devices)])  9.53 us
    all_to_all x1, waiting for transfers between devices, body(): lax.all_to_all(partial_sum, ('grid', 'band'), 0, 0, tiled=True)  6.39 us
    all_to_all x1, starting transfers between devices, body(): lax.all_to_all(partial_sum, ('grid', 'band'), 0, 0, tiled=True)  2.57 us
  transfers between devices with their start and end apart: 13, of which 8 were waited for; matrix products, arithmetic and copies ran while one was open for 4% of the time, Pallas kernels for 8%

profile of v16, /device:TPU:0, one launch (start us, length us, event | category | flops | bytes accessed | tf_op | source)
XLA Modules:
  0.0 69.3 jit_solution(14348301785933011129)
XLA Ops:
  0.6 1.3 %shard_map.131 = (f32[56,512]{1,0:T(8,128)S(1)}, f32[56,512]{1,0:T(8,128)S(1)}, f32[56,512]{1,0:T(8,128)S(1)}, f32[56,512]{1,0:T(8,128)S(1)}) custom-call(s32[1]{0:T(128)} %bitcast.me_ref, f32[2,96,512]{2,1,0:T(8,128)} %bitcast.11, s32[1,512]{1,0:T(1,128)} %bitcast.14, bf16[4,48,336]{2,1,0:T(8,128)(2,1)} %constant.24.clone.refs_2_.refs_6_), custom_call_target="tpu_custom_call" | custom-call | tf_op jit(solution)/shard_map/pallas_call | solution.py:126
  2.0 4.0 %collective-permute-start.2 = (f32[56,512]{1,0:T(8,128)S(1)}, f32[56,512]{1,0:T(8,128)S(1)}, u32[]{:S(2)}, u32[]{:S(2)}) collective-permute-start(f32[56,512]{1,0:T(8,128)S(1)} %get-tuple-element.24), channel_id=1, source_target_pairs={{0,24},{8,16},{16,8},{24,0},{1,25},{9,17},{17,9},{25,1},{2,26},{10... | collective-permute-start | bytes 344072 | tf_op jit(solution)/shard_map/ppermute | solution.py:421
  5.9 0.5 collective-permute-start.1
  6.4 0.1 collective-permute-start
  6.6 1.2 %broadcast_multiply_fusion = f32[24,9216]{1,0:T(8,128)S(1)} fusion(f32[24,9216]{1,0:T(8,128)} %param.14), kind=kLoop, calls=%fused_computation | loop fusion | flops 221184 | bytes 1769472 | tf_op jit(solution)/shard_map/mul | solution.py:436
  7.8 0.8 %shard_map.132.refs_0_ = f32[48,2048]{1,0:T(8,128)S(1)} custom-call(f32[56,512]{1,0:T(8,128)S(1)} %get-tuple-element.25.plane_ref.mark_ref, f32[56,512]{1,0:T(8,128)S(1)} %get-tuple-element.25.plane_ref.mark_ref), custom_call_target="tpu_custom_call" | custom-call | tf_op jit(solution)/shard_map/pallas_call | solution.py:126
  8.6 0.5 reshape.22
  9.1 0.1 pad.4.refs_3_
  9.2 0.0 copy-start.1
  9.2 0.0 copy-start.2
  9.2 0.0 copy-start.5
  9.2 0.0 copy-start.6
  9.2 0.3 collective-permute-done.2.plane_ref.mark_ref.refs_0_
  9.5 0.8 %shard_map.133.refs_0_ = f32[48,2048]{1,0:T(8,128)S(1)} custom-call(f32[56,512]{1,0:T(8,128)S(1)} %collective-permute-done.2.plane_ref.mark_ref.refs_0_, f32[56,512]{1,0:T(8,128)S(1)} %collective-permute-done.2.plane_ref.mark_ref.refs_0_, f32[48,2048]{1,0:T(8,128)S(1)} %shard_map.132.refs_0_), custom_call_target="tpu_custom_call" | custom-call | tf_op jit(solution)/shard_map/pallas_call | solution.py:126
  10.3 1.3 %collective-permute-done.1.plane_ref.mark_ref.refs_1_ = f32[56,512]{1,0:T(8,128)S(1)} collective-permute-done((f32[56,512]{1,0:T(8,128)S(1)}, f32[56,512]{1,0:T(8,128)S(1)}, u32[]{:S(2)}, u32[]{:S(2)}) %collective-permute-start.1) | collective-permute-done | bytes 114720 | tf_op jit(solution)/shard_map/ppermute | solution.py:421
  11.5 0.8 %shard_map.134.before_ref = f32[48,2048]{1,0:T(8,128)S(1)} custom-call(f32[56,512]{1,0:T(8,128)S(1)} %collective-permute-done.1.plane_ref.mark_ref.refs_1_, f32[56,512]{1,0:T(8,128)S(1)} %collective-permute-done.1.plane_ref.mark_ref.refs_1_, f32[48,2048]{1,0:T(8,128)S(1)} %shard_map.133.refs_0_), custom_call_target="tpu_custom_call" | custom-call | tf_op jit(solution)/shard_map/pallas_call | solution.py:126
  12.3 0.0 copy-start
  12.3 0.0 copy-start.3
  12.3 0.0 copy-start.4
  12.3 0.0 copy-start.8
  12.4 0.0 collective-permute-done.plane_ref.refs_2_
  12.4 0.0 copy-done.1
  12.4 0.0 copy-done.2
  12.4 0.0 copy-done.5
  12.4 0.0 copy-done.6
  12.4 4.8 %shard_map.135 = (f32[48,512]{1,0:T(8,128)S(1)}, f32[48,512]{1,0:T(8,128)S(1)}, f32[48,512]{1,0:T(8,128)S(1)}, bf16[96,2048]{1,0:T(8,128)(2,1)S(1)}) custom-call(f32[56,512]{1,0:T(8,128)S(1)} %collective-permute-done.plane_ref.refs_2_, f32[48,2048]{1,0:T(8,128)S(1)} %shard_map.134.before_ref, ...), custom_call_target="tpu_custom_call" | custom-call | tf_op jit(solution)/shard_map/pallas_call | solution.py:126
  17.2 1.7 %collective-permute-start.3 = (f32[48,512]{1,0:T(8,128)S(1)}, f32[48,512]{1,0:T(8,128)S(1)}, u32[]{:S(2)}, u32[]{:S(2)}) collective-permute-start(f32[48,512]{1,0:T(8,128)S(1)} %get-tuple-element.27), channel_id=1, source_target_pairs={{0,8},{8,0},{16,24},{24,16},{1,9},{9,1},{17,25},{25,17},{2,10},{10... | collective-permute-start | bytes 294920 | tf_op jit(solution)/shard_map/ppermute | solution.py:421
  18.9 1.0 %collective-permute-start.4 = (f32[48,512]{1,0:T(8,128)S(1)}, f32[48,512]{1,0:T(8,128)S(1)}, u32[]{:S(2)}, u32[]{:S(2)}) collective-permute-start(f32[48,512]{1,0:T(8,128)S(1)} %get-tuple-element.28), channel_id=1, source_target_pairs={{0,16},{8,24},{16,0},{24,8},{1,17},{9,25},{17,1},{25,9},{2,18},{10... | collective-permute-start | bytes 294920 | tf_op jit(solution)/shard_map/ppermute | solution.py:421
  19.9 0.8 %collective-permute-start.5 = (f32[48,512]{1,0:T(8,128)S(1)}, f32[48,512]{1,0:T(8,128)S(1)}, u32[]{:S(2)}, u32[]{:S(2)}) collective-permute-start(f32[48,512]{1,0:T(8,128)S(1)} %get-tuple-element.29), channel_id=1, source_target_pairs={{0,24},{8,16},{16,8},{24,0},{1,25},{9,17},{17,9},{25,1},{2,26},{10... | collective-permute-start | bytes 294920 | tf_op jit(solution)/shard_map/ppermute | solution.py:421
  22.1 0.5 shard_map.136.refs_0_
  22.5 0.0 collective-permute-done.3.refs_1_
  22.5 3.0 %collective-permute-done.4.refs_2_ = f32[48,512]{1,0:T(8,128)S(1)} collective-permute-done((f32[48,512]{1,0:T(8,128)S(1)}, f32[48,512]{1,0:T(8,128)S(1)}, u32[]{:S(2)}, u32[]{:S(2)}) %collective-permute-start.4) | collective-permute-done | bytes 98336 | tf_op jit(solution)/shard_map/ppermute | solution.py:421
  25.5 0.0 collective-permute-done.5.refs_3_
  25.5 0.0 copy-done
  25.5 0.0 copy-done.3
  25.6 0.0 copy-done.4
  25.6 0.0 copy-done.8
  25.6 0.6 shard_map.137
  26.2 1.5 %collective-permute-start.8 = (f32[48,512]{1,0:T(8,128)S(1)}, f32[48,512]{1,0:T(8,128)S(1)}, u32[]{:S(2)}, u32[]{:S(2)}) collective-permute-start(f32[48,512]{1,0:T(8,128)S(1)} %get-tuple-element.32), channel_id=1, source_target_pairs={{0,24},{8,16},{16,8},{24,0},{1,25},{9,17},{17,9},{25,1},{2,26},{10... | collective-permute-start | bytes 294920 | tf_op jit(solution)/shard_map/ppermute | solution.py:421
  27.7 1.0 %collective-permute-start.7 = (f32[48,512]{1,0:T(8,128)S(1)}, f32[48,512]{1,0:T(8,128)S(1)}, u32[]{:S(2)}, u32[]{:S(2)}) collective-permute-start(f32[48,512]{1,0:T(8,128)S(1)} %get-tuple-element.31), channel_id=1, source_target_pairs={{0,16},{8,24},{16,0},{24,8},{1,17},{9,25},{17,1},{25,9},{2,18},{10... | collective-permute-start | bytes 294920 | tf_op jit(solution)/shard_map/ppermute | solution.py:421
  28.7 1.1 %collective-permute-start.6 = (f32[48,512]{1,0:T(8,128)S(1)}, f32[48,512]{1,0:T(8,128)S(1)}, u32[]{:S(2)}, u32[]{:S(2)}) collective-permute-start(f32[48,512]{1,0:T(8,128)S(1)} %get-tuple-element.30), channel_id=1, source_target_pairs={{0,8},{8,0},{16,24},{24,16},{1,9},{9,1},{17,25},{25,17},{2,10},{10... | collective-permute-start | bytes 294920 | tf_op jit(solution)/shard_map/ppermute | solution.py:421
  29.7 0.8 %shard_map.138.refs_0_ = f32[48,2048]{1,0:T(8,128)S(1)} custom-call(f32[48,512]{1,0:T(8,128)S(1)} %get-tuple-element.33.plane_ref, f32[56,512]{1,0:T(8,128)S(1)} %get-tuple-element.25.plane_ref.mark_ref), custom_call_target="tpu_custom_call" | custom-call | tf_op jit(solution)/shard_map/pallas_call | solution.py:126
  30.5 1.8 %collective-permute-done.8.plane_ref = f32[48,512]{1,0:T(8,128)S(1)} collective-permute-done((f32[48,512]{1,0:T(8,128)S(1)}, f32[48,512]{1,0:T(8,128)S(1)}, u32[]{:S(2)}, u32[]{:S(2)}) %collective-permute-start.8) | collective-permute-done | bytes 98336 | tf_op jit(solution)/shard_map/ppermute | solution.py:421
  32.3 0.8 %shard_map.139.refs_0_ = f32[48,2048]{1,0:T(8,128)S(1)} custom-call(f32[48,512]{1,0:T(8,128)S(1)} %collective-permute-done.8.plane_ref, f32[56,512]{1,0:T(8,128)S(1)} %collective-permute-done.2.plane_ref.mark_ref.refs_0_, f32[48,2048]{1,0:T(8,128)S(1)} %shard_map.138.refs_0_), custom_call_target="tpu_custom_call" | custom-call | tf_op jit(solution)/shard_map/pallas_call | solution.py:126
  33.1 0.0 collective-permute-done.7.plane_ref
  33.1 0.8 %shard_map.140.before_ref = f32[48,2048]{1,0:T(8,128)S(1)} custom-call(f32[48,512]{1,0:T(8,128)S(1)} %collective-permute-done.7.plane_ref, f32[56,512]{1,0:T(8,128)S(1)} %collective-permute-done.1.plane_ref.mark_ref.refs_1_, f32[48,2048]{1,0:T(8,128)S(1)} %shard_map.139.refs_0_), custom_call_target="tpu_custom_call" | custom-call | tf_op jit(solution)/shard_map/pallas_call | solution.py:126
  33.9 0.0 copy-start.7
  33.9 0.0 collective-permute-done.6.plane_ref
  33.9 4.8 %shard_map.141 = (f32[48,512]{1,0:T(8,128)S(1)}, f32[48,512]{1,0:T(8,128)S(1)}, f32[48,512]{1,0:T(8,128)S(1)}, bf16[96,2048]{1,0:T(8,128)(2,1)S(1)}) custom-call(f32[48,512]{1,0:T(8,128)S(1)} %collective-permute-done.6.plane_ref, f32[48,2048]{1,0:T(8,128)S(1)} %shard_map.140.before_ref, f32[56,512]{1,0:T(8,128)S(1)} %collective-permute-done.2.plane_ref.mark_ref.refs_0_, ...), custom_call_target="tpu_custom_call" | custom-call | tf_op jit(solution)/shard_map/pallas_call | solution.py:126
  38.7 0.9 %collective-permute-start.10 = (f32[48,512]{1,0:T(8,128)S(1)}, f32[48,512]{1,0:T(8,128)S(1)}, u32[]{:S(2)}, u32[]{:S(2)}) collective-permute-start(f32[48,512]{1,0:T(8,128)S(1)} %get-tuple-element.36), channel_id=1, source_target_pairs={{0,16},{8,24},{16,0},{24,8},{1,17},{9,25},{17,1},{25,9},{2,18},{10... | collective-permute-start | bytes 294920 | tf_op jit(solution)/shard_map/ppermute | solution.py:421
  39.6 1.3 %collective-permute-start.11 = (f32[48,512]{1,0:T(8,128)S(1)}, f32[48,512]{1,0:T(8,128)S(1)}, u32[]{:S(2)}, u32[]{:S(2)}) collective-permute-start(f32[48,512]{1,0:T(8,128)S(1)} %get-tuple-element.37), channel_id=1, source_target_pairs={{0,24},{8,16},{16,8},{24,0},{1,25},{9,17},{17,9},{25,1},{2,26},{10... | collective-permute-start | bytes 294920 | tf_op jit(solution)/shard_map/ppermute | solution.py:421
  40.9 1.3 %collective-permute-start.9 = (f32[48,512]{1,0:T(8,128)S(1)}, f32[48,512]{1,0:T(8,128)S(1)}, u32[]{:S(2)}, u32[]{:S(2)}) collective-permute-start(f32[48,512]{1,0:T(8,128)S(1)} %get-tuple-element.35), channel_id=1, source_target_pairs={{0,8},{8,0},{16,24},{24,16},{1,9},{9,1},{17,25},{25,17},{2,10},{10... | collective-permute-start | bytes 294920 | tf_op jit(solution)/shard_map/ppermute | solution.py:421
  42.2 0.5 shard_map.142.refs_0_
  42.7 0.7 collective-permute-done.10.refs_2_
  43.4 1.8 %collective-permute-done.11.refs_3_ = f32[48,512]{1,0:T(8,128)S(1)} collective-permute-done((f32[48,512]{1,0:T(8,128)S(1)}, f32[48,512]{1,0:T(8,128)S(1)}, u32[]{:S(2)}, u32[]{:S(2)}) %collective-permute-start.11) | collective-permute-done | bytes 98336 | tf_op jit(solution)/shard_map/ppermute | solution.py:421
  45.1 0.8 %collective-permute-done.9.refs_1_ = f32[48,512]{1,0:T(8,128)S(1)} collective-permute-done((f32[48,512]{1,0:T(8,128)S(1)}, f32[48,512]{1,0:T(8,128)S(1)}, u32[]{:S(2)}, u32[]{:S(2)}) %collective-permute-start.9) | collective-permute-done | bytes 98336 | tf_op jit(solution)/shard_map/ppermute | solution.py:421
  45.9 0.0 copy-done.7
  45.9 0.5 shard_map.143
  46.4 11.5 %all_to_all.10.parts_ref = bf16[8,16,512]{2,1,0:T(8,128)(2,1)S(1)} all-to-all(bf16[8,16,512]{2,1,0:T(8,128)(2,1)S(1)} %get-tuple-element.40), channel_id=1, replica_groups=mesh['grid'=4,'band'=8] {'band'}, dimensions={0} | all-to-all | bytes 262144 | tf_op jit(solution)/shard_map/all_to_all | solution.py:517
  57.9 1.0 %shard_map.144 = (f32[32,1,128]{2,1,0:T(1,128)}, f32[8,128]{1,0:T(8,128)}) custom-call(bf16[8,16,512]{2,1,0:T(8,128)(2,1)S(1)} %all_to_all.10.parts_ref), custom_call_target="tpu_custom_call" | custom-call | tf_op jit(solution)/shard_map/pallas_call | solution.py:126
  58.9 2.6 %all-to-all-start.1 = ((f32[32,1,128]{2,1,0:T(1,128)}), f32[32,1,128]{2,1,0:T(1,128)S(1)}, u32[]{:S(2)}, u32[]{:S(2)}) async-start(f32[32,1,128]{2,1,0:T(1,128)} %get-tuple-element.41), calls=%async_computation.1 | async-start | bytes 32768 | tf_op jit(solution)/shard_map/all_to_all | solution.py:524
  61.5 0.7 %copy.15 = f32[2,1,512,96]{2,3,1,0:T(8,128)} copy(f32[2,1,512,96]{2,3,1,0:T(8,128)S(1)} %bitcast.10) | data formatting | bytes 786432
  62.2 6.4 %all-to-all-done.1.parts_ref = f32[32,1,128]{2,1,0:T(1,128)S(1)} async-done(((f32[32,1,128]{2,1,0:T(1,128)}), f32[32,1,128]{2,1,0:T(1,128)S(1)}, u32[]{:S(2)}, u32[]{:S(2)}) %all-to-all-start.1) | async-done | bytes 16416 | tf_op jit(solution)/shard_map/all_to_all | solution.py:524
  68.6 0.7 %shard_map.145 = f32[2,1,2]{2,1,0:T(1,128)} custom-call(s32[1]{0:T(128)} %bitcast.me_ref, f32[32,1,128]{2,1,0:T(1,128)S(1)} %all-to-all-done.1.parts_ref), custom_call_target="tpu_custom_call" | custom-call | tf_op jit(solution)/shard_map/pallas_call | solution.py:126
Async XLA Ops:
  2.0 7.5 %collective-permute-start.2 = (f32[56,512]{1,0:T(8,128)S(1)}, f32[56,512]{1,0:T(8,128)S(1)}, u32[]{:S(2)}, u32[]{:S(2)}) collective-permute-start(f32[56,512]{1,0:T(8,128)S(1)} %get-tuple-element.24), channel_id=1, source_target_pairs={{0,24},{8,16},{16,8},{24,0},{1,25},{9,17},{17,9},{25,1},{2,26},{10... | collective-permute-start | bytes 344072 | tf_op jit(solution)/shard_map/ppermute | solution.py:421
  5.9 5.6 %collective-permute-start.1 = (f32[56,512]{1,0:T(8,128)S(1)}, f32[56,512]{1,0:T(8,128)S(1)}, u32[]{:S(2)}, u32[]{:S(2)}) collective-permute-start(f32[56,512]{1,0:T(8,128)S(1)} %get-tuple-element.23), channel_id=1, source_target_pairs={{0,16},{8,24},{16,0},{24,8},{1,17},{9,25},{17,1},{25,9},{2,18},{10... | collective-permute-start | bytes 344072 | tf_op jit(solution)/shard_map/ppermute | solution.py:421
  6.4 5.9 %collective-permute-start = (f32[56,512]{1,0:T(8,128)S(1)}, f32[56,512]{1,0:T(8,128)S(1)}, u32[]{:S(2)}, u32[]{:S(2)}) collective-permute-start(f32[56,512]{1,0:T(8,128)S(1)} %get-tuple-element.22), channel_id=1, source_target_pairs={{0,8},{8,0},{16,24},{24,16},{1,9},{9,1},{17,25},{25,17},{2,10},{10... | collective-permute-start | bytes 344072 | tf_op jit(solution)/shard_map/ppermute | solution.py:421
  9.2 3.2 %copy-start.1 = (bf16[384,256]{1,0:T(8,128)(2,1)S(1)}, bf16[384,256]{1,0:T(8,128)(2,1)}, u32[]{:S(2)}) copy-start(bf16[384,256]{1,0:T(8,128)(2,1)} %constant.25.clone.refs_4_) | copy-start | bytes 589828
  9.2 3.2 %copy-start.2 = (bf16[384,224]{1,0:T(8,128)(2,1)S(1)}, bf16[384,224]{1,0:T(8,128)(2,1)}, u32[]{:S(2)}) copy-start(bf16[384,224]{1,0:T(8,128)(2,1)} %constant.26.clone.refs_5_) | copy-start | bytes 516100
  9.2 3.2 %copy-start.5 = (bf16[256,256]{1,0:T(8,128)(2,1)S(1)}, bf16[256,256]{1,0:T(8,128)(2,1)}, u32[]{:S(2)}) copy-start(bf16[256,256]{1,0:T(8,128)(2,1)} %constant.28.clone.refs_7_) | copy-start | bytes 393220
  9.2 3.2 %copy-start.6 = (bf16[224,192]{1,0:T(8,128)(2,1)S(1)}, bf16[224,192]{1,0:T(8,128)(2,1)}, u32[]{:S(2)}) copy-start(bf16[224,192]{1,0:T(8,128)(2,1)} %constant.27.clone.refs_6_) | copy-start | bytes 258052
  12.3 13.2 %copy-start = (f32[2,1,512,96]{2,3,1,0:T(8,128)S(1)}, f32[2,1,512,96]{2,3,1,0:T(8,128)}, u32[]{:S(2)}) copy-start(f32[2,1,512,96]{2,3,1,0:T(8,128)} %param.12) | copy-start | bytes 1179652
  12.3 13.2 %copy-start.3 = (bf16[4,48,336]{2,1,0:T(8,128)(2,1)S(1)}, bf16[4,48,336]{2,1,0:T(8,128)(2,1)}, u32[]{:S(2)}) copy-start(bf16[4,48,336]{2,1,0:T(8,128)(2,1)} %constant.24.clone.refs_2_.refs_6_) | copy-start | bytes 387076
  12.3 13.2 %copy-start.4 = (bf16[112,576]{1,0:T(8,128)(2,1)S(1)}, bf16[112,576]{1,0:T(8,128)(2,1)}, u32[]{:S(2)}) copy-start(bf16[112,576]{1,0:T(8,128)(2,1)} %constant.29.clone.refs_7_) | copy-start | bytes 387076
  12.3 13.2 %copy-start.8 = (s32[512]{0:T(512)S(1)}, s32[512]{0:T(512)}, u32[]{:S(2)}) copy-start(s32[512]{0:T(512)} %param.13) | copy-start | bytes 6148
  17.2 5.3 %collective-permute-start.3 = (f32[48,512]{1,0:T(8,128)S(1)}, f32[48,512]{1,0:T(8,128)S(1)}, u32[]{:S(2)}, u32[]{:S(2)}) collective-permute-start(f32[48,512]{1,0:T(8,128)S(1)} %get-tuple-element.27), channel_id=1, source_target_pairs={{0,8},{8,0},{16,24},{24,16},{1,9},{9,1},{17,25},{25,17},{2,10},{10... | collective-permute-start | bytes 294920 | tf_op jit(solution)/shard_map/ppermute | solution.py:421
  18.9 6.6 %collective-permute-start.4 = (f32[48,512]{1,0:T(8,128)S(1)}, f32[48,512]{1,0:T(8,128)S(1)}, u32[]{:S(2)}, u32[]{:S(2)}) collective-permute-start(f32[48,512]{1,0:T(8,128)S(1)} %get-tuple-element.28), channel_id=1, source_target_pairs={{0,16},{8,24},{16,0},{24,8},{1,17},{9,25},{17,1},{25,9},{2,18},{10... | collective-permute-start | bytes 294920 | tf_op jit(solution)/shard_map/ppermute | solution.py:421
  19.9 5.6 %collective-permute-start.5 = (f32[48,512]{1,0:T(8,128)S(1)}, f32[48,512]{1,0:T(8,128)S(1)}, u32[]{:S(2)}, u32[]{:S(2)}) collective-permute-start(f32[48,512]{1,0:T(8,128)S(1)} %get-tuple-element.29), channel_id=1, source_target_pairs={{0,24},{8,16},{16,8},{24,0},{1,25},{9,17},{17,9},{25,1},{2,26},{10... | collective-permute-start | bytes 294920 | tf_op jit(solution)/shard_map/ppermute | solution.py:421
  26.2 6.1 %collective-permute-start.8 = (f32[48,512]{1,0:T(8,128)S(1)}, f32[48,512]{1,0:T(8,128)S(1)}, u32[]{:S(2)}, u32[]{:S(2)}) collective-permute-start(f32[48,512]{1,0:T(8,128)S(1)} %get-tuple-element.32), channel_id=1, source_target_pairs={{0,24},{8,16},{16,8},{24,0},{1,25},{9,17},{17,9},{25,1},{2,26},{10... | collective-permute-start | bytes 294920 | tf_op jit(solution)/shard_map/ppermute | solution.py:421
  27.7 5.4 %collective-permute-start.7 = (f32[48,512]{1,0:T(8,128)S(1)}, f32[48,512]{1,0:T(8,128)S(1)}, u32[]{:S(2)}, u32[]{:S(2)}) collective-permute-start(f32[48,512]{1,0:T(8,128)S(1)} %get-tuple-element.31), channel_id=1, source_target_pairs={{0,16},{8,24},{16,0},{24,8},{1,17},{9,25},{17,1},{25,9},{2,18},{10... | collective-permute-start | bytes 294920 | tf_op jit(solution)/shard_map/ppermute | solution.py:421
  28.7 5.2 %collective-permute-start.6 = (f32[48,512]{1,0:T(8,128)S(1)}, f32[48,512]{1,0:T(8,128)S(1)}, u32[]{:S(2)}, u32[]{:S(2)}) collective-permute-start(f32[48,512]{1,0:T(8,128)S(1)} %get-tuple-element.30), channel_id=1, source_target_pairs={{0,8},{8,0},{16,24},{24,16},{1,9},{9,1},{17,25},{25,17},{2,10},{10... | collective-permute-start | bytes 294920 | tf_op jit(solution)/shard_map/ppermute | solution.py:421
  33.9 12.0 %copy-start.7 = (bf16[2,128,56]{2,1,0:T(8,128)(2,1)S(1)}, bf16[2,128,56]{2,1,0:T(8,128)(2,1)}, u32[]{:S(2)}) copy-start(bf16[2,128,56]{2,1,0:T(8,128)(2,1)} %constant.30.clone.refs_8_) | copy-start | bytes 86020
  38.7 4.7 %collective-permute-start.10 = (f32[48,512]{1,0:T(8,128)S(1)}, f32[48,512]{1,0:T(8,128)S(1)}, u32[]{:S(2)}, u32[]{:S(2)}) collective-permute-start(f32[48,512]{1,0:T(8,128)S(1)} %get-tuple-element.36), channel_id=1, source_target_pairs={{0,16},{8,24},{16,0},{24,8},{1,17},{9,25},{17,1},{25,9},{2,18},{10... | collective-permute-start | bytes 294920 | tf_op jit(solution)/shard_map/ppermute | solution.py:421
  39.6 5.5 %collective-permute-start.11 = (f32[48,512]{1,0:T(8,128)S(1)}, f32[48,512]{1,0:T(8,128)S(1)}, u32[]{:S(2)}, u32[]{:S(2)}) collective-permute-start(f32[48,512]{1,0:T(8,128)S(1)} %get-tuple-element.37), channel_id=1, source_target_pairs={{0,24},{8,16},{16,8},{24,0},{1,25},{9,17},{17,9},{25,1},{2,26},{10... | collective-permute-start | bytes 294920 | tf_op jit(solution)/shard_map/ppermute | solution.py:421
  40.9 5.0 %collective-permute-start.9 = (f32[48,512]{1,0:T(8,128)S(1)}, f32[48,512]{1,0:T(8,128)S(1)}, u32[]{:S(2)}, u32[]{:S(2)}) collective-permute-start(f32[48,512]{1,0:T(8,128)S(1)} %get-tuple-element.35), channel_id=1, source_target_pairs={{0,8},{8,0},{16,24},{24,16},{1,9},{9,1},{17,25},{25,17},{2,10},{10... | collective-permute-start | bytes 294920 | tf_op jit(solution)/shard_map/ppermute | solution.py:421
  58.9 9.7 %all-to-all-start.1 = ((f32[32,1,128]{2,1,0:T(1,128)}), f32[32,1,128]{2,1,0:T(1,128)S(1)}, u32[]{:S(2)}, u32[]{:S(2)}) async-start(f32[32,1,128]{2,1,0:T(1,128)} %get-tuple-element.41), calls=%async_computation.1 | async-start | bytes 32768 | tf_op jit(solution)/shard_map/all_to_all | solution.py:524
